TPU v7x, 128 devices: a whole 4x4x4 slice. The times are simulated.
128 devices in a mesh: seq: 4 (over x), mod: 2 (over core), tp: 16 (over y, z).
Axes of the slice: x: 4, y: 4, z: 4, core: 2. Of those that a mesh axis runs over, the one named last changes fastest.
Arguments:
- activations: bfloat16 [1536, 8192], P(('seq', 'mod')), may hold values from -12 to 12
- grad_attn: bfloat16 [1536, 6144], P(('seq', 'mod'), 'tp'), may hold values from -6 to 6
- weights: bfloat16 [2, 8192, 3, 6144], P('mod', None, None, 'tp'), may hold values from -0.049718446 to 0.049718446
- modality: int32 [1536], replicated, may hold values from 0 to 1, as said below
Outputs:
- grad_input: bfloat16 [1536, 8192], P(('seq', 'mod'), 'tp')
Inputs may be any that keep to these rules, and one draw needn't show every extreme that they name: Tokens come in runs of 12 of one modality. In each aligned block of 192 tokens (the tokens of one index of seq+mod) each modality has at most 144 tokens. In every draw both blocks of some index of seq hold 144 image tokens each, and both blocks of another index hold 144 text tokens each.
All inputs are finite; a program needn't handle non-finite values.
Results may differ from a plain program's by a relative error of at most 0.013.
Values may be sent and summed in bfloat16 or wider, within the bound.
No kernel may reach another device: no remote copies, remote signals or barrier semaphores. Data moves between devices by JAX's collectives and lax.ppermute only.
A program may use at most 128 MiB of HBM per device.

v0:
```python
import jax
import jax.numpy as jnp
from jax import lax
from jax.sharding import PartitionSpec as P

HD = 128
CAP = 144


def slot_tables(modality, owned_rows, capacity):
    blocks = modality.reshape(-1, owned_rows)
    offsets = jnp.arange(owned_rows, dtype=jnp.int32)
    sources = []
    counts = []
    for section in range(2):
        sort_key = jnp.where(blocks == section, offsets[None, :], owned_rows + offsets[None, :])
        sources.append(jnp.argsort(sort_key, axis=1)[:, :capacity])
        counts.append(jnp.sum((blocks == section).astype(jnp.int32), axis=1))
    sources = jnp.stack(sources)
    counts = jnp.stack(counts)
    filled = jnp.arange(capacity, dtype=jnp.int32)[None, None, :] < counts[:, :, None]
    starts = (jnp.arange(blocks.shape[0], dtype=jnp.int32) * owned_rows)[None, :, None]
    return (sources, filled, sources + starts)


def per_device(activations, grad_attn, weights, modality):
    owned_rows, model_width = activations.shape
    head_cols = grad_attn.shape[1]
    head_count = head_cols // HD
    capacity = CAP
    slot_count = 2 * capacity
    seq_count = lax.axis_size("seq")
    score_scale = HD ** (-0.5)
    shard_id = lax.axis_index("seq")
    section = lax.axis_index("mod")
    own_block = shard_id * 2 + section
    sources, filled, positions = slot_tables(modality, owned_rows, capacity)
    send_index = lax.dynamic_index_in_dim(sources, own_block, 1, keepdims=False)
    send_filled = lax.dynamic_index_in_dim(filled, own_block, 1, keepdims=False)
    act_send = jnp.where(send_filled[:, :, None], jnp.take(activations, send_index, axis=0), 0)
    grad_send = jnp.where(send_filled[:, :, None], jnp.take(grad_attn, send_index, axis=0), 0)
    act_recv, grad_recv = (
        lax.all_to_all(act_send, "mod", split_axis=0, concat_axis=0, tiled=True),
        lax.all_to_all(grad_send, "mod", split_axis=0, concat_axis=0, tiled=True),
    )
    act_rows = act_recv.reshape(slot_count, model_width)
    grad_heads = grad_recv.reshape(slot_count, head_count, HD)
    query_pos = lax.dynamic_slice(positions, (section, 2 * shard_id, 0), (1, 2, capacity)).reshape(
        slot_count
    )
    query_filled = lax.dynamic_slice(filled, (section, 2 * shard_id, 0), (1, 2, capacity)).reshape(
        slot_count
    )
    query_pos = jnp.where(query_filled, query_pos, 2**30)
    key_pos = positions.reshape(2, seq_count, 2, capacity).transpose(1, 0, 2, 3).reshape(-1)
    key_filled = filled.reshape(2, seq_count, 2, capacity).transpose(1, 0, 2, 3).reshape(-1)
    weight_mat = weights[0].reshape(model_width, 3 * head_cols)
    projected = jnp.dot(act_rows, weight_mat, preferred_element_type=jnp.float32).astype(
        jnp.bfloat16
    )
    query_part = projected[:, :head_cols]
    key_part = projected[:, head_cols : 2 * head_cols]
    value_part = projected[:, 2 * head_cols :]
    keys_all, values_all = (
        lax.all_gather(key_part, ("seq", "mod"), axis=0, tiled=True),
        lax.all_gather(value_part, ("seq", "mod"), axis=0, tiled=True),
    )
    query_heads = query_part.reshape(slot_count, head_count, HD)
    key_heads = keys_all.reshape(-1, head_count, HD)
    value_heads = values_all.reshape(-1, head_count, HD)
    scores = (
        jnp.einsum("ihd,jhd->hij", query_heads, key_heads, preferred_element_type=jnp.float32)
        * score_scale
    )
    allowed = key_filled[None, :] & (key_pos[None, :] <= query_pos[:, None])
    scores = jnp.where(allowed[None], scores, -jnp.inf)
    row_max = jnp.max(scores, axis=2, keepdims=True)
    lifted = jnp.exp(scores - row_max)
    attn_probs = lifted / jnp.sum(lifted, axis=2, keepdims=True)
    probs_low = attn_probs.astype(jnp.bfloat16)
    dprobs = jnp.einsum("ihd,jhd->hij", grad_heads, value_heads, preferred_element_type=jnp.float32)
    row_dot = jnp.sum(attn_probs * dprobs, axis=2, keepdims=True)
    dscores = (attn_probs * (dprobs - row_dot)).astype(jnp.bfloat16)
    grad_query = (
        jnp.einsum("hij,jhd->ihd", dscores, key_heads, preferred_element_type=jnp.float32)
        * score_scale
    )
    grad_key = (
        jnp.einsum("hij,ihd->jhd", dscores, query_heads, preferred_element_type=jnp.float32)
        * score_scale
    )
    grad_value = jnp.einsum(
        "hij,ihd->jhd", probs_low, grad_heads, preferred_element_type=jnp.float32
    )
    summed_keys = lax.psum_scatter(
        jnp.concatenate(
            [
                grad_key.reshape(slot_count * lax.axis_size(("seq", "mod")), head_cols),
                grad_value.reshape(slot_count * lax.axis_size(("seq", "mod")), head_cols),
            ],
            axis=1,
        ),
        ("seq", "mod"),
        scatter_dimension=0,
        tiled=True,
    )
    grad_qkv = jnp.concatenate(
        [
            grad_query.reshape(slot_count, head_cols).astype(jnp.bfloat16),
            summed_keys.astype(jnp.bfloat16),
        ],
        axis=1,
    )
    head_partial = lax.dot_general(
        grad_qkv, weight_mat, (((1,), (1,)), ((), ())), preferred_element_type=jnp.float32
    )
    own_modality = lax.dynamic_slice_in_dim(modality, own_block * owned_rows, owned_rows)
    image_rank = jnp.cumsum(own_modality) - 1
    text_rank = jnp.cumsum(1 - own_modality) - 1
    slot_index = own_modality * capacity + jnp.where(own_modality == 1, image_rank, text_rank)
    reduced = lax.psum_scatter(head_partial, "tp", scatter_dimension=1, tiled=True).astype(
        jnp.bfloat16
    )
    returned = lax.all_to_all(
        reduced.reshape(2, capacity, -1), "mod", split_axis=0, concat_axis=0, tiled=True
    )
    result = jnp.take(returned.reshape(slot_count, -1), slot_index, axis=0)
    return result


def solution(mesh):
    in_specs = (P(("seq", "mod"), None), P(("seq", "mod"), "tp"), P("mod", None, None, "tp"), P())
    out_specs = P(("seq", "mod"), "tp")
    return jax.shard_map(
        per_device, mesh=mesh, in_specs=in_specs, out_specs=out_specs, check_vma=False
    )
```

profile of v0, /device:TPU:1, one launch (start us, length us, event | category | flops | bytes accessed | tf_op | source)
XLA Modules:
  0.0 311.9 jit_solution(14911059076030554354)
XLA Ops:
  7.7 3.3 %sort.31 = (s32[8,192]{1,0:T(8,128)}, s32[8,192]{1,0:T(8,128)S(1)}) sort(s32[8,192]{1,0:T(8,128)S(1)} %get-tuple-element.30, s32[8,192]{1,0:T(8,128)S(1)} %iota.47), dimensions={1}, to_apply=%region_6.7 | sort | flops 16896 | bytes 24576 | tf_op jit(solution)/shard_map/jit(argsort)/sort | solution.py:17
  11.0 3.3 %sort.32 = (s32[8,192]{1,0:T(8,128)}, s32[8,192]{1,0:T(8,128)S(1)}) sort(s32[8,192]{1,0:T(8,128)S(1)} %get-tuple-element.23, s32[8,192]{1,0:T(8,128)S(1)} %iota.48), dimensions={1}, to_apply=%region_7.8 | sort | flops 16896 | bytes 24576 | tf_op jit(solution)/shard_map/jit(argsort)/sort | solution.py:17
  14.7 6.7 %gather_fusion = bf16[288,8192]{1,0:T(8,128)(2,1)} fusion(bf16[192,8192]{1,0:T(8,128)(2,1)S(1)} %copy-done, s32[1024]{0:T(1024)S(1)} %pad_clamp_fusion.1), kind=kCustom, calls=%fused_computation | custom fusion | bytes 9438336 | tf_op jit(solution)/shard_map/jit(_take)/gather | solution.py:40
  21.3 5.1 %select_select_fusion = bf16[2,144,8192]{2,1,0:T(8,128)(2,1)} fusion(bf16[2,144,8192]{2,1,0:T(8,128)(2,1)} %bitcast.71, pred[2,144]{1,0:T(4,128)(4,1)S(1)} %get-tuple-element.13, pred[2,144]{1,0:T(4,128)(4,1)S(1)} %dynamic-slice_bitcast_fusion), kind=kLoop, calls=%fused_computation.10 | loop fusion | flops 4718592 | bytes 9437760 | tf_op jit(solution)/shard_map/jit(_where)/select_n | solution.py:40
  26.4 7.2 %all-to-all-start = ((bf16[2,144,8192]{2,1,0:T(8,128)(2,1)}), bf16[2,144,8192]{2,1,0:T(8,128)(2,1)}, u32[]{:S(2)}, u32[]{:S(2)}) async-start(bf16[2,144,8192]{2,1,0:T(8,128)(2,1)} %select_select_fusion), calls=%async_computation | async-start | bytes 9437184 | tf_op jit(solution)/shard_map/all_to_all | solution.py:43
  33.7 23.2 %copy.54 = bf16[1,8192,3,384]{1,3,2,0:T(8,128)(2,1)} copy(bf16[1,8192,3,384]{3,1,2,0:T(8,128)(2,1)} %param.6) | data formatting | bytes 37748736 | tf_op args[2]
  56.8 11.1 %convolution_convert_fusion = bf16[288,1152]{1,0:T(8,128)(2,1)S(1)} fusion(bf16[288,8192]{1,0:T(8,128)(2,1)} %bitcast.10, bf16[8192,1152]{0,1:T(8,128)(2,1)} %bitcast.69), kind=kOutput, calls=%fused_computation.19 | convolution fusion | flops 5436149760 | bytes 24256512 | tf_op jit(solution)/shard_map/dot_general | solution.py:58
  69.6 2.0 gather_fusion.1
  72.4 3.5 %all-to-all-start.1 = ((bf16[2,144,384]{2,1,0:T(8,128)(2,1)}), bf16[2,144,384]{2,1,0:T(8,128)(2,1)S(1)}, u32[]{:S(2)}, u32[]{:S(2)}) async-start(bf16[2,144,384]{2,1,0:T(8,128)(2,1)} %select_select_fusion.1), calls=%async_computation.1 | async-start | bytes 442368 | tf_op jit(solution)/shard_map/all_to_all | solution.py:44
  77.7 18.3 %all-gather.3.cloned.1.call-done = bf16[2304,384]{1,0:T(8,128)(2,1)} async-done(((bf16[288,384]{1,0:T(8,128)(2,1)}), bf16[2304,384]{1,0:T(8,128)(2,1)}) %all-gather.3.cloned.1.call-update) | async-done | bytes 1769488 | tf_op jit(solution)/shard_map/all_gather | solution.py:65
  95.9 2.6 copy.55
  98.6 6.0 %fusion.43 = (f32[3,288]{1,0:T(4,128)S(1)}, f32[3,288,2304]{2,1,0:T(8,128)}) fusion(pred[288,2304]{1,0:T(8,128)(4,1)S(1)} %compare_and_fusion, bf16[2304,3,128]{0,2,1:T(8,128)(2,1)S(1)} %bitcast.77, bf16[36,3,8,128]{3,2,1,0:T(8,128)(2,1)S(1)} %get-tuple-element.16), kind=kOutput, calls=%fused_computation.85 | convolution fusion | flops 517572864 | bytes 10620288 | tf_op jit(solution)/shard_map/sub | solution.py:78
  104.6 5.2 %fusion.2 = f32[3,128,2304]{2,1,0:T(8,128)} fusion(bf16[288,3,128]{2,1,0:T(4,128)(2,1)S(1)} %reshape.200, f32[3,288]{1,0:T(4,128)S(1)} %get-tuple-element.24, pred[288,2304]{1,0:T(8,128)(4,1)S(1)} %compare_and_fusion, bf16[2304,3,128]{0,2,1:T(8,128)(2,1)S(1)} %bitcast.78, bf16[36,3,8,128]{3,2,1,0:T(8,128)(2,1)S(1)} %get-tuple-element.16), kind=kOutput, calls=%fused_computation.12 | convolution fusion | flops 1029172352 | bytes 6417792 | tf_op jit(solution)/shard_map/hij,ihd->jhd/dot_general | solution.py:92
  109.8 12.7 %all-gather.5.cloned.1.call-done = bf16[2304,384]{1,0:T(8,128)(2,1)} async-done(((bf16[288,384]{1,0:T(8,128)(2,1)}), bf16[2304,384]{1,0:T(8,128)(2,1)}) %all-gather.5.cloned.1.call-update) | async-done | bytes 1769488 | tf_op jit(solution)/shard_map/all_gather | solution.py:66
  122.5 3.9 %copy.59 = bf16[2304,384]{0,1:T(8,128)(2,1)} copy(bf16[2304,384]{1,0:T(8,128)(2,1)} %all-gather.5.cloned.1.call-done) | data formatting | bytes 3538944 | tf_op jit(solution)/shard_map/all_gather | solution.py:66
  126.4 5.2 %multiply_reduce_fusion = (f32[3,288]{1,0:T(4,128)S(1)}, f32[3,288,2304]{2,1,0:T(8,128)S(1)}) fusion(f32[3,288,2304]{2,1,0:T(8,128)} %get-tuple-element.25, f32[3,288]{1,0:T(4,128)S(1)} %get-tuple-element.24, bf16[2304,3,128]{0,2,1:T(8,128)(2,1)} %bitcast.80, bf16[288,3,128]{2,1,0:T(4,128)(2,1)S(1)} %reshape.200), kind=kOutput, calls=%fused_computation.5 | convolution fusion | flops 515579040 | bytes 17922816 | tf_op jit(solution)/shard_map/ihd,jhd->hij/dot_general | solution.py:81
  133.8 1.9 copy-done.3
  137.7 3.3 %pad_maximum_fusion = f32[2304,768]{0,1:T(8,128)} fusion(f32[2304,384]{0,1:T(8,128)S(1)} %bitcast.76, f32[2304,384]{0,1:T(8,128)S(1)} %bitcast.72), kind=kLoop, calls=%fused_computation.8 | loop fusion | flops 1769472 | bytes 14155776 | tf_op jit(solution)/shard_map/concatenate | solution.py:96
  141.0 8.0 %copy.71 = f32[2304,768]{1,0:T(8,128)} copy(f32[2304,768]{0,1:T(8,128)} %pad_maximum_fusion) | data formatting | bytes 14155776
  149.4 3.3 %fusion.10 = bf16[288,3,128]{2,0,1:T(8,128)(2,1)S(1)} fusion(bf16[2304,3,128]{0,2,1:T(8,128)(2,1)S(1)} %bitcast.79, bf16[3,288,2304]{2,1,0:T(8,128)(2,1)} %copy-done.3), kind=kOutput, calls=%fused_computation.23 | convolution fusion | flops 509829120 | bytes 5971968 | tf_op jit(solution)/shard_map/hij,jhd->ihd/dot_general | solution.py:85
  152.9 41.8 %reduce-scatter.7.cloned.1.call-done = f32[288,768]{1,0:T(8,128)} async-done(((f32[2304,768]{1,0:T(8,128)}), f32[288,768]{1,0:T(8,128)}) %reduce-scatter.7.cloned.1.call-update) | async-done | bytes 884752
  196.2 12.4 %fusion.11 = f32[288,8192]{1,0:T(8,128)} fusion(bf16[8192,1152]{0,1:T(8,128)(2,1)} %bitcast.70, bf16[288,768]{0,1:T(8,128)(2,1)S(1)} %copy.72, bf16[288,384]{0,1:T(8,128)(2,1)S(1)} %bitcast.82), kind=kOutput, calls=%fused_computation.24 | convolution fusion | flops 5437145088 | bytes 28975104 | tf_op jit(solution)/shard_map/dot_general | solution.py:114
  210.8 84.8 %reduce-scatter.5.cloned.1.call-done = f32[288,512]{1,0:T(8,128)} async-done(((f32[288,8192]{1,0:T(8,128)}), f32[288,512]{1,0:T(8,128)}) %reduce-scatter.5.cloned.1.call-update) | async-done | bytes 589840 | tf_op jit(solution)/shard_map/reduce_scatter | solution.py:121
  296.7 5.3 %all_to_all.15 = bf16[2,144,512]{2,1,0:T(8,128)(2,1)S(1)} all-to-all(bf16[2,144,512]{2,1,0:T(8,128)(2,1)S(1)} %bitcast.81), channel_id=1, replica_groups=mesh['seq'=4,'mod'=2,'tp'=16] {'mod'}, dimensions={0} | all-to-all | bytes 589824 | tf_op jit(solution)/shard_map/all_to_all | solution.py:124
  (81 shorter events, 18.3 us)
Async XLA Ops:
  6.5 8.1 %copy-start = (bf16[192,8192]{1,0:T(8,128)(2,1)S(1)}, bf16[192,8192]{1,0:T(8,128)(2,1)}, u32[]{:S(2)}) copy-start(bf16[192,8192]{1,0:T(8,128)(2,1)} %param.4) | copy-start | bytes 9437188
  26.4 30.4 %all-to-all-start = ((bf16[2,144,8192]{2,1,0:T(8,128)(2,1)}), bf16[2,144,8192]{2,1,0:T(8,128)(2,1)}, u32[]{:S(2)}, u32[]{:S(2)}) async-start(bf16[2,144,8192]{2,1,0:T(8,128)(2,1)} %select_select_fusion), calls=%async_computation | async-start | bytes 9437184 | tf_op jit(solution)/shard_map/all_to_all | solution.py:43
  33.6 62.3 %all-gather.3.cloned.1.call-start = ((), (), s32[]{:S(2)}) async-start(), calls=%async_computation.5 | async-start | bytes 1990656 | tf_op jit(solution)/shard_map/all_gather | solution.py:65
  56.8 12.7 %copy-start.2 = (bf16[192,384]{1,0:T(8,128)(2,1)S(1)}, bf16[192,384]{1,0:T(8,128)(2,1)}, u32[]{:S(2)}) copy-start(bf16[192,384]{1,0:T(8,128)(2,1)} %param.5) | copy-start | bytes 442372
  68.8 53.7 %all-gather.5.cloned.1.call-start = ((), (), s32[]{:S(2)}) async-start(), calls=%async_computation.6 | async-start | bytes 1990656 | tf_op jit(solution)/shard_map/all_gather | solution.py:66
  72.4 4.7 %all-to-all-start.1 = ((bf16[2,144,384]{2,1,0:T(8,128)(2,1)}), bf16[2,144,384]{2,1,0:T(8,128)(2,1)S(1)}, u32[]{:S(2)}, u32[]{:S(2)}) async-start(bf16[2,144,384]{2,1,0:T(8,128)(2,1)} %select_select_fusion.1), calls=%async_computation.1 | async-start | bytes 442368 | tf_op jit(solution)/shard_map/all_to_all | solution.py:44
  75.9 118.8 %reduce-scatter.7.cloned.1.call-start = ((), (), s32[]{:S(2)}) async-start(), calls=%async_computation.8 | async-start | bytes 7962624
  126.4 5.3 %slice-start = ((s8[7962624]{0:T(1024)(128)(4,1)}), s8[4194304]{0:T(1024)(128)(4,1)S(1)}, s32[]{:S(2)}) async-start(s8[7962624]{0:T(1024)(128)(4,1)} %bitcast.74), calls=%async_computation.9 | async-start | bytes 8388608
  126.4 6.1 %slice-start.1 = ((s8[7962624]{0:T(1024)(128)(4,1)}), s8[3768320]{0:T(1024)(128)(4,1)S(1)}, s32[]{:S(2)}) async-start(s8[7962624]{0:T(1024)(128)(4,1)} %bitcast.74), calls=%async_computation.10 | async-start | bytes 7536640
  133.8 1.9 copy-start.3
  135.7 2.0 copy-start.4
  149.1 146.5 %reduce-scatter.5.cloned.1.call-start = ((), (), s32[]{:S(2)}) async-start(), calls=%async_computation.7 | async-start | bytes 10027008 | tf_op jit(solution)/shard_map/reduce_scatter | solution.py:121
  208.7 96.7 %copy-start.1 = (bf16[192,8192]{1,0:T(8,128)(2,1)S(1)}, bf16[192,8192]{1,0:T(8,128)(2,1)}, u32[]{:S(2)}) copy-start(bf16[192,8192]{1,0:T(8,128)(2,1)} %param.4) | copy-start | bytes 9437188
Sparse Core Ops, SparseCore 0:
  68.9 26.9 all-gather.2
  97.6 24.8 all-gather.4
  149.2 45.4 reduce-scatter.6
  208.8 86.7 reduce-scatter.4
where the time goes:
time: 313 us; the launch traced here: 312 us
  waiting for transfers between devices  159 us (51%)
  local copies, waits for them, and re-layouts  55.5 us (18%)
  matrix products  44.5 us (14%)
  other arithmetic  23.6 us (8%)
  between operations  13.4 us (4%)
  starting transfers between devices  11.2 us (4%)
  blocking collectives  5.27 us (2%)
    reduce_scatter x1, waiting for transfers between devices, per_device(): lax.psum_scatter(head_partial, 'tp', scatter_dimension=1, tiled=True)  84.8 us
    unnamed x5, waiting for transfers between devices  42.6 us
    unnamed x17, local copies, waits for them, and re-layouts  36.3 us
    all_gather x1, waiting for transfers between devices, per_device(): lax.all_gather(key_part, ('seq', 'mod'), axis=0, tiled=True)  18.3 us
    all_gather x1, waiting for transfers between devices, per_device(): lax.all_gather(value_part, ('seq', 'mod'), axis=0, tiled=True)  12.7 us
    dot_general x1, matrix products, per_device(): lax.dot_general(grad_qkv, weight_mat, (((1,), (1,)), ((), ())), preferred...  12.4 us
    dot_general x1, matrix products, per_device(): jnp.dot(act_rows, weight_mat, preferred_element_type=jnp.float32)  11.1 us
    all_to_all x1, starting transfers between devices, per_device(): lax.all_to_all(act_send, 'mod', split_axis=0, concat_axis=0, tiled=True)  7.25 us
  transfers between devices with their start and end apart: 6, of which 5 were waited for; matrix products, arithmetic and copies ran while one was open for 15% of the time, Pallas kernels for 0%

commit v1 on v0

v1 whole, which is shorter than its diff:
```python
import functools

import jax
import jax.numpy as jnp
from jax import lax
from jax.experimental import pallas as pl
from jax.experimental.pallas import tpu as pltpu
from jax.sharding import PartitionSpec as P

HD = 128
NH = 3
RING = 4
SCALE = HD**-0.5
AXES = ("seq", "mod", "tp")
MIB = 1024 * 1024


def core_swap(x):
    return lax.ppermute(x, "mod", [(0, 1), (1, 0)])


def project_kernel(a_ref, w_ref, out_ref, acc_ref):
    step = pl.program_id(0)
    w = jnp.concatenate([w_ref[0], w_ref[1], w_ref[2]], axis=1)
    part = jnp.dot(a_ref[...], w, preferred_element_type=jnp.float32)

    @pl.when(step == 0)
    def _():
        acc_ref[...] = part

    @pl.when(step > 0)
    def _():
        acc_ref[...] += part

    @pl.when(step == pl.num_programs(0) - 1)
    def _():
        for h in range(NH):
            for c in range(3):
                lo = c * NH * HD + h * HD
                out_ref[h, :, c * HD : (c + 1) * HD] = acc_ref[:, lo : lo + HD].astype(jnp.bfloat16)


def project(a, w3):
    rows, depth = a.shape
    block = 1024
    return pl.pallas_call(
        project_kernel,
        grid=(depth // block,),
        in_specs=[
            pl.BlockSpec((rows, block), lambda i: (0, i)),
            pl.BlockSpec((3, block, NH * HD), lambda i: (0, i, 0)),
        ],
        out_specs=pl.BlockSpec((NH, rows, 3 * HD), lambda i: (0, 0, 0)),
        out_shape=jax.ShapeDtypeStruct((NH, rows, 3 * HD), jnp.bfloat16),
        scratch_shapes=[pltpu.VMEM((rows, 3 * NH * HD), jnp.float32)],
        compiler_params=pltpu.CompilerParams(vmem_limit_bytes=24 * MIB),
        cost_estimate=pl.CostEstimate(
            flops=2 * rows * depth * 9 * HD, bytes_accessed=depth * 9 * HD * 2, transcendentals=0
        ),
        name="project",
    )(a, w3)


def attention_kernel(where_ref, r0, r1, r2, r3, kvo_ref, own_ref, oth_ref, q_s, g_s, k_s, v_s, dk_s, dv_s):
    chip = where_ref[0]
    core = where_ref[1]
    rows = r0.shape[0]
    both = 2 * rows
    for k, r in enumerate((r0, r1, r2, r3)):
        shard = (chip - k + RING) % RING
        q_s[shard] = r[:, 0:HD]
        g_s[shard] = r[:, 3 * HD : 4 * HD]
        mine = pl.ds(pl.multiple_of((2 * shard + core) * rows, rows), rows)
        other = pl.ds(pl.multiple_of((2 * shard + 1 - core) * rows, rows), rows)
        k_s[mine, :] = r[:, HD : 2 * HD]
        v_s[mine, :] = r[:, 2 * HD : 3 * HD]
        k_s[other, :] = kvo_ref[k, :, 0:HD]
        v_s[other, :] = kvo_ref[k, :, HD : 2 * HD]
    nt = (((1,), (1,)), ((), ()))
    tn = (((0,), (0,)), ((), ()))
    for s in range(RING - 1, -1, -1):
        width = both * (s + 1)
        q = q_s[s]
        g = g_s[s]
        kk = k_s[0:width, :]
        vv = v_s[0:width, :]
        scores = lax.dot_general(q, kk, nt, preferred_element_type=jnp.float32) * SCALE
        row = lax.broadcasted_iota(jnp.int32, (rows, width), 0) + (2 * s + core) * rows
        col = lax.broadcasted_iota(jnp.int32, (rows, width), 1)
        scores = jnp.where(col <= row, scores, -jnp.inf)
        lifted = jnp.exp(scores - jnp.max(scores, axis=1, keepdims=True))
        probs = lifted / jnp.sum(lifted, axis=1, keepdims=True)
        low = probs.astype(jnp.bfloat16)
        dprobs = lax.dot_general(g, vv, nt, preferred_element_type=jnp.float32)
        row_dot = jnp.sum(probs * dprobs, axis=1, keepdims=True)
        ds = (probs * (dprobs - row_dot)).astype(jnp.bfloat16)
        dq = jnp.dot(ds, kk, preferred_element_type=jnp.float32) * SCALE
        dk = lax.dot_general(ds, q, tn, preferred_element_type=jnp.float32) * SCALE
        dv = lax.dot_general(low, g, tn, preferred_element_type=jnp.float32)
        if s == RING - 1:
            dk_s[...] = dk
            dv_s[...] = dv
        else:
            dk_s[0:width, :] += dk
            dv_s[0:width, :] += dv
        own_ref[(chip - s + RING) % RING, :, 0:HD] = dq
    for k in range(RING):
        shard = (chip - k + RING) % RING
        mine = pl.ds(pl.multiple_of((2 * shard + core) * rows, rows), rows)
        other = pl.ds(pl.multiple_of((2 * shard + 1 - core) * rows, rows), rows)
        own_ref[k, :, HD : 2 * HD] = dk_s[mine, :]
        own_ref[k, :, 2 * HD : 3 * HD] = dv_s[mine, :]
        oth_ref[k, :, 0:HD] = dk_s[other, :].astype(jnp.bfloat16)
        oth_ref[k, :, HD : 2 * HD] = dv_s[other, :].astype(jnp.bfloat16)


def attention(where, parts, kv_other):
    rows = parts[0].shape[0]
    total = 2 * RING * rows
    vmem = pl.BlockSpec(memory_space=pltpu.VMEM)
    return pl.pallas_call(
        attention_kernel,
        in_specs=[pl.BlockSpec(memory_space=pltpu.SMEM)] + [vmem] * 5,
        out_specs=[vmem, vmem],
        out_shape=[
            jax.ShapeDtypeStruct((RING, rows, 3 * HD), jnp.float32),
            jax.ShapeDtypeStruct((RING, rows, 2 * HD), jnp.bfloat16),
        ],
        scratch_shapes=[
            pltpu.VMEM((RING, rows, HD), jnp.bfloat16),
            pltpu.VMEM((RING, rows, HD), jnp.bfloat16),
            pltpu.VMEM((total, HD), jnp.bfloat16),
            pltpu.VMEM((total, HD), jnp.bfloat16),
            pltpu.VMEM((total, HD), jnp.float32),
            pltpu.VMEM((total, HD), jnp.float32),
        ],
        compiler_params=pltpu.CompilerParams(vmem_limit_bytes=32 * MIB),
        cost_estimate=pl.CostEstimate(flops=10**9, bytes_accessed=4 * 10**6, transcendentals=10**6),
        name="attention",
    )(where, *parts, kv_other)


def collect_kernel(where_ref, own_ref, oth_ref, r0, r1, r2, r3, mine_ref, send_ref):
    chip = where_ref[0]
    for k, r in enumerate((r0, r1, r2, r3)):
        head = (chip + k) % RING

        @pl.when(head < NH)
        def _():
            x = r[...]
            zero = jnp.zeros_like(x)
            mine_ref[head] = jnp.where(own_ref[...] > 0, x, zero)
            send_ref[head] = jnp.where(oth_ref[...] > 0, x, zero)


def collect(where, own, oth, parts):
    rows, width = parts[0].shape
    vmem = pl.BlockSpec(memory_space=pltpu.VMEM)
    shape = jax.ShapeDtypeStruct((NH, rows, width), jnp.bfloat16)
    return pl.pallas_call(
        collect_kernel,
        in_specs=[pl.BlockSpec(memory_space=pltpu.SMEM)] + [vmem] * 6,
        out_specs=[vmem, vmem],
        out_shape=[shape, shape],
        cost_estimate=pl.CostEstimate(flops=10**6, bytes_accessed=2 * 10**6, transcendentals=0),
        name="collect",
    )(where, own, oth, *parts)


def back_kernel(place_ref, mine_ref, oth_ref, w_ref, own_out, oth_out, g_s):
    rows = mine_ref.shape[1]

    @pl.when(pl.program_id(0) == 0)
    def _():
        for h in range(NH):
            for c in range(3):
                lo = c * NH * HD + h * HD
                g_s[0:rows, lo : lo + HD] = mine_ref[h, :, c * HD : (c + 1) * HD]
                g_s[rows : 2 * rows, lo : lo + HD] = oth_ref[h, :, c * HD : (c + 1) * HD]

    w = jnp.concatenate([w_ref[0, 0, 0], w_ref[1, 0, 0], w_ref[2, 0, 0]], axis=1)
    res = lax.dot_general(
        g_s[...], w, (((1,), (1,)), ((), ())), preferred_element_type=jnp.float32
    ).astype(jnp.bfloat16)
    own_out[0] = res[0:rows]
    oth_out[0] = res[rows : 2 * rows]


def back(place, mine, oth, w3, stream, streams):
    _, rows, _ = mine.shape
    depth = w3.shape[1]
    dests = RING * RING
    cols = depth // dests // streams
    w5 = w3.reshape(3, dests, streams, cols, NH * HD)
    shape = jax.ShapeDtypeStruct((dests, rows, cols), jnp.bfloat16)
    return pl.pallas_call(
        back_kernel,
        grid_spec=pltpu.PrefetchScalarGridSpec(
            num_scalar_prefetch=1,
            grid=(dests,),
            in_specs=[
                pl.BlockSpec((NH, rows, 3 * HD), lambda i, p: (0, 0, 0)),
                pl.BlockSpec((NH, rows, 3 * HD), lambda i, p: (0, 0, 0)),
                pl.BlockSpec((3, 1, 1, cols, NH * HD), lambda i, p: (0, i, stream, 0, 0)),
            ],
            out_specs=[
                pl.BlockSpec((1, rows, cols), lambda i, p: (p[0, i], 0, 0)),
                pl.BlockSpec((1, rows, cols), lambda i, p: (p[1, i], 0, 0)),
            ],
            scratch_shapes=[pltpu.VMEM((2 * rows, 9 * HD), jnp.bfloat16)],
        ),
        out_shape=[shape, shape],
        compiler_params=pltpu.CompilerParams(vmem_limit_bytes=24 * MIB),
        cost_estimate=pl.CostEstimate(
            flops=2 * 2 * rows * dests * cols * 9 * HD,
            bytes_accessed=dests * cols * (9 * HD * 2 + 4 * rows),
            transcendentals=0,
        ),
        name="back",
    )(place, mine, oth, w5)


def ring_perm(first, hop):
    pairs = []
    for s in range(RING):
        for m in range(2):
            for y in range(RING):
                for z in range(RING):
                    if (m == 0) == first:
                        to = (y, (z + hop) % RING)
                    else:
                        to = ((y + hop) % RING, z)
                    base = (s * 2 + m) * RING * RING
                    pairs.append((base + y * RING + z, base + to[0] * RING + to[1]))
    return pairs


def per_device(activations, grad_attn, weights, modality):
    rows, depth = activations.shape
    chip = lax.axis_index("seq")
    core = lax.axis_index("mod")
    tp = lax.axis_index("tp")
    where = jnp.stack([chip, core]).astype(jnp.int32)
    w3 = jnp.transpose(weights[0], (1, 0, 2))

    own_mod = lax.dynamic_slice_in_dim(modality, (2 * chip + core) * rows, rows)
    is_mine = (own_mod == core).astype(jnp.int32)[:, None]
    is_other = 1 - is_mine

    act_other = core_swap(activations)
    proj_own = project(activations, w3)
    proj_other = project(act_other, w3)
    proj_back = core_swap(proj_other)
    g_heads = grad_attn.reshape(rows, NH, HD).transpose(1, 0, 2)
    heads = jnp.where((is_mine > 0)[None], proj_own, proj_back)
    heads = jnp.concatenate([heads, g_heads], axis=2)

    parts = []
    for hop in range(RING):
        head = jnp.minimum((chip + hop) % RING, NH - 1)
        x = lax.dynamic_index_in_dim(heads, head, 0, keepdims=False)
        if hop:
            pairs = [(i, (i + hop) % RING) for i in range(RING) if (i + hop) % RING < NH]
            x = lax.ppermute(x, "seq", pairs)
        parts.append(x)
    kv_mine = jnp.stack([x[:, HD : 3 * HD] for x in parts])
    kv_other = core_swap(kv_mine)
    own, oth = attention(where, parts, kv_other)
    from_other = core_swap(oth)

    grads = []
    for hop in range(RING):
        kv = own[hop, :, HD:] + from_other[hop].astype(jnp.float32)
        x = jnp.concatenate([own[hop, :, :HD], kv], axis=1).astype(jnp.bfloat16)
        if hop:
            pairs = [(i, (i - hop) % RING) for i in range(NH)]
            x = lax.ppermute(x, "seq", pairs)
        grads.append(x)

    mine, send = collect(where, is_mine, is_other, grads)
    other = core_swap(send)

    dest = jnp.arange(RING * RING, dtype=jnp.int32)
    dy = (dest // RING - tp // RING + RING) % RING
    dz = (dest % RING - tp % RING + RING) % RING
    z_first = dz * RING + dy
    y_first = dy * RING + dz
    place = jnp.stack(
        [jnp.where(core == 0, z_first, y_first), jnp.where(core == 0, y_first, z_first)]
    ).astype(jnp.int32)

    streams = 1
    quarter = RING
    seconds = []
    for stream in range(streams):
        own_rows, other_rows = back(place, mine, other, w3, stream, streams)
        returned = core_swap(other_rows)

        def piece(k):
            cut = slice(k * quarter, (k + 1) * quarter)
            return own_rows[cut].astype(jnp.float32) + returned[cut].astype(jnp.float32)

        total = piece(0)
        for hop in (2, 1, 3):
            got = lax.ppermute(piece(hop).astype(jnp.bfloat16), AXES, ring_perm(True, hop))
            total = total + got.astype(jnp.float32)
        seconds.append(total)
    total = jnp.concatenate(seconds, axis=2) if streams > 1 else seconds[0]
    result = total[0]
    for hop in (2, 1, 3):
        got = lax.ppermute(total[hop].astype(jnp.bfloat16), AXES, ring_perm(False, hop))
        result = result + got.astype(jnp.float32)
    return result.astype(jnp.bfloat16)


def solution(mesh):
    in_specs = (P(("seq", "mod"), None), P(("seq", "mod"), "tp"), P("mod", None, None, "tp"), P())
    out_specs = P(("seq", "mod"), "tp")
    return jax.shard_map(
        per_device, mesh=mesh, in_specs=in_specs, out_specs=out_specs, check_vma=False
    )
```

time: 313 us -> 146 us (0.47)
  the two profiles are of different devices: /device:TPU:1 before, /device:TPU:2 now
where the time goes in v1:
time: 146 us; the launch traced here: 145 us
  waiting for transfers between devices  51.8 us (35%)
  Pallas kernels  38.3 us (26%)
  starting transfers between devices  27.2 us (19%)
  local copies, waits for them, and re-layouts  23.3 us (16%)
  other arithmetic  4.25 us (3%)
    unnamed x20, local copies, waits for them, and re-layouts  21.6 us
    ppermute x3, waiting for transfers between devices, per_device(): lax.ppermute(piece(hop).astype(jnp.bfloat16), AXES, ring_perm(True, hop))  17.4 us
    pallas_call x2, Pallas kernels, project(): pl.pallas_call(project_kernel, grid=(depth // block,), in_specs=[pl.Block...  16.9 us
    ppermute x6, waiting for transfers between devices, core_swap(): return lax.ppermute(x, 'mod', [(0, 1), (1, 0)])  15.5 us
    ppermute x6, starting transfers between devices, per_device(): x = lax.ppermute(x, 'seq', pairs)  15.2 us
    pallas_call x1, Pallas kernels, back(): pl.pallas_call(back_kernel, grid_spec=pltpu.PrefetchScalarGridSpec(num_sc...  14.2 us
    ppermute x6, waiting for transfers between devices, per_device(): x = lax.ppermute(x, 'seq', pairs)  13 us
    ppermute x3, starting transfers between devices, per_device(): lax.ppermute(piece(hop).astype(jnp.bfloat16), AXES, ring_perm(True, hop))  6.02 us
  transfers between devices with their start and end apart: 18, of which 14 were waited for; matrix products, arithmetic and copies ran while one was open for 2% of the time, Pallas kernels for 6%

profile of v1, /device:TPU:2, one launch (start us, length us, event | category | flops | bytes accessed | tf_op | source)
XLA Modules:
  0.0 145.2 jit_solution(13535773200953047521)
XLA Ops:
  0.9 4.9 %collective-permute-done.a_ref = bf16[192,8192]{1,0:T(8,128)(2,1)S(1)} collective-permute-done((bf16[192,8192]{1,0:T(8,128)(2,1)}, bf16[192,8192]{1,0:T(8,128)(2,1)S(1)}, u32[]{:S(2)}, u32[]{:S(2)}) %collective-permute-start) | collective-permute-done | bytes 3145760 | tf_op jit(solution)/shard_map/ppermute | solution.py:19
  5.9 6.4 %copy-done.1 = bf16[1,8192,3,384]{3,1,2,0:T(8,128)(2,1)S(1)} copy-done((bf16[1,8192,3,384]{3,1,2,0:T(8,128)(2,1)S(1)}, bf16[1,8192,3,384]{3,1,2,0:T(8,128)(2,1)}, u32[]{:S(2)}) %copy-start.1) | copy-done | bytes 18874392
  12.2 8.4 %project.3 = bf16[3,192,384]{2,1,0:T(8,128)(2,1)S(1)} custom-call(bf16[192,8192]{1,0:T(8,128)(2,1)S(1)} %collective-permute-done.a_ref, bf16[3,8192,384]{2,1,0:T(8,128)(2,1)S(1)} %bitcast.64), custom_call_target="tpu_custom_call" | custom-call | flops 3623878656 | bytes 18874368 | tf_op jit(solution)/shard_map/project/pallas_call | solution.py:46
  21.7 6.4 %copy-done.2 = bf16[1,8192,3,384]{3,1,2,0:T(8,128)(2,1)S(1)} copy-done((bf16[1,8192,3,384]{3,1,2,0:T(8,128)(2,1)S(1)}, bf16[1,8192,3,384]{3,1,2,0:T(8,128)(2,1)}, u32[]{:S(2)}) %copy-start.2) | copy-done | bytes 18874392
  28.1 8.4 %project.2 = bf16[3,192,384]{2,1,0:T(8,128)(2,1)S(1)} custom-call(bf16[192,8192]{1,0:T(8,128)(2,1)S(1)} %copy-done.4, bf16[3,8192,384]{2,1,0:T(8,128)(2,1)S(1)} %bitcast.65), custom_call_target="tpu_custom_call" | custom-call | flops 3623878656 | bytes 18874368 | tf_op jit(solution)/shard_map/project/pallas_call | solution.py:46
  36.7 2.4 %collective-permute-start.4 = (bf16[192,512]{1,0:T(8,128)(2,1)S(1)}, bf16[192,512]{1,0:T(8,128)(2,1)S(1)}, u32[]{:S(2)}, u32[]{:S(2)}) collective-permute-start(bf16[192,512]{1,0:T(8,128)(2,1)S(1)} %get-tuple-element.35), channel_id=1, source_target_pairs={{32,0},{64,32},{96,64},{33,1},{65,33},{97,65},{34,2},{66,34},{98,6... | collective-permute-start | bytes 589832 | tf_op jit(solution)/shard_map/ppermute | solution.py:264
  39.1 3.5 %collective-permute-start.2 = (bf16[192,512]{1,0:T(8,128)(2,1)S(1)}, bf16[192,512]{1,0:T(8,128)(2,1)S(1)}, u32[]{:S(2)}, u32[]{:S(2)}) collective-permute-start(bf16[192,512]{1,0:T(8,128)(2,1)S(1)} %get-tuple-element.37), channel_id=1, source_target_pairs={{0,32},{32,64},{96,0},{1,33},{33,65},{97,1},{2,34},{34,66},{98,2},... | collective-permute-start | bytes 589832 | tf_op jit(solution)/shard_map/ppermute | solution.py:264
  45.8 3.0 %collective-permute-done.2.r1 = bf16[192,512]{1,0:T(8,128)(2,1)S(1)} collective-permute-done((bf16[192,512]{1,0:T(8,128)(2,1)S(1)}, bf16[192,512]{1,0:T(8,128)(2,1)S(1)}, u32[]{:S(2)}, u32[]{:S(2)}) %collective-permute-start.2) | collective-permute-done | bytes 196640 | tf_op jit(solution)/shard_map/ppermute | solution.py:264
  48.8 3.8 %collective-permute-done.3.r2 = bf16[192,512]{1,0:T(8,128)(2,1)S(1)} collective-permute-done((bf16[192,512]{1,0:T(8,128)(2,1)S(1)}, bf16[192,512]{1,0:T(8,128)(2,1)S(1)}, u32[]{:S(2)}, u32[]{:S(2)}) %collective-permute-start.3) | collective-permute-done | bytes 196640 | tf_op jit(solution)/shard_map/ppermute | solution.py:264
  54.5 4.7 %attention.1 = (f32[4,192,384]{2,1,0:T(8,128)S(1)}, bf16[4,192,256]{2,1,0:T(8,128)(2,1)S(1)}) custom-call(s32[2]{0:T(128)S(1)} %pad_add_fusion.1.where_ref, bf16[192,512]{1,0:T(8,128)(2,1)S(1)} %get-tuple-element.36.r0, bf16[192,512]{1,0:T(8,128)(2,1)S(1)} %collective-permute-done.2.r1, bf16[192,512]{1,0:T(8,128)(2,1)S(1)} %collective-permute-done.3.r2, ...), custom_call_target="tpu_custom_call" | custom-call | flops 1000000000 | bytes 4000000 | tf_op jit(solution)/shard_map/attention/pallas_call | solution.py:121
  61.2 2.8 %collective-permute-start.7 = (bf16[192,384]{1,0:T(8,128)(2,1)S(1)}, bf16[192,384]{1,0:T(8,128)(2,1)S(1)}, u32[]{:S(2)}, u32[]{:S(2)}) collective-permute-start(bf16[192,384]{1,0:T(8,128)(2,1)S(1)} %pad_maximum_fusion.2), channel_id=1, source_target_pairs={{0,96},{32,0},{64,32},{1,97},{33,1},{65,33},{2,98},{34,2},{66,34},... | collective-permute-start | bytes 442376 | tf_op jit(solution)/shard_map/ppermute | solution.py:277
  65.3 4.0 %collective-permute-start.9 = (bf16[192,384]{1,0:T(8,128)(2,1)S(1)}, bf16[192,384]{1,0:T(8,128)(2,1)S(1)}, u32[]{:S(2)}, u32[]{:S(2)}) collective-permute-start(bf16[192,384]{1,0:T(8,128)(2,1)S(1)} %pad_maximum_fusion.4), channel_id=1, source_target_pairs={{0,32},{32,64},{64,96},{1,33},{33,65},{65,97},{2,34},{34,66},{66,9... | collective-permute-start | bytes 442376 | tf_op jit(solution)/shard_map/ppermute | solution.py:277
  71.6 4.3 %collective-permute-done.9.r3 = bf16[192,384]{1,0:T(8,128)(2,1)S(1)} collective-permute-done((bf16[192,384]{1,0:T(8,128)(2,1)S(1)}, bf16[192,384]{1,0:T(8,128)(2,1)S(1)}, u32[]{:S(2)}, u32[]{:S(2)}) %collective-permute-start.9) | collective-permute-done | bytes 147488 | tf_op jit(solution)/shard_map/ppermute | solution.py:277
  76.5 2.5 %collect.1 = (bf16[3,192,384]{2,1,0:T(8,128)(2,1)}, bf16[3,192,384]{2,1,0:T(8,128)(2,1)}) custom-call(s32[2]{0:T(128)} %copy-done.5, s32[192,1]{1,0:T(8,128)} %copy.6.own_ref, s32[192,1]{1,0:T(8,128)} %copy.7.oth_ref, bf16[192,384]{1,0:T(8,128)(2,1)} %pad_maximum_fusion.1.r0, bf16[192,384]{1,0:T(8,128)(2,1)} %copy-done.7, bf16[192,384]{1,0:T(8,128)(2,1)} %copy-done.8, ...), custom_call_target="tpu_custom_call" | custom-call | flops 1000000 | bytes 2000000 | tf_op jit(solution)/shard_map/collect/pallas_call | solution.py:160
  79.1 2.0 %collective-permute-done.10.oth_ref = bf16[3,192,384]{2,1,0:T(8,128)(2,1)S(1)} collective-permute-done((bf16[3,192,384]{2,1,0:T(8,128)(2,1)}, bf16[3,192,384]{2,1,0:T(8,128)(2,1)S(1)}, u32[]{:S(2)}, u32[]{:S(2)}) %collective-permute-start.10) | collective-permute-done | bytes 442400 | tf_op jit(solution)/shard_map/ppermute | solution.py:19
  81.1 6.4 %copy-done.3 = bf16[1,8192,3,384]{3,1,2,0:T(8,128)(2,1)S(1)} copy-done((bf16[1,8192,3,384]{3,1,2,0:T(8,128)(2,1)S(1)}, bf16[1,8192,3,384]{3,1,2,0:T(8,128)(2,1)}, u32[]{:S(2)}) %copy-start.3) | copy-done | bytes 18874392
  88.4 14.2 %back.1 = (bf16[16,192,512]{2,1,0:T(8,128)(2,1)S(1)}, bf16[16,192,512]{2,1,0:T(8,128)(2,1)S(1)}) custom-call(s32[2,16]{1,0:T(2,128)S(1)} %pad_add_fusion.place_ref, bf16[3,192,384]{2,1,0:T(8,128)(2,1)S(1)} %copy-done.6, bf16[3,192,384]{2,1,0:T(8,128)(2,1)S(1)} %collective-permute-done.10.oth_ref, bf16[3,16,1,512,384]{4,3,2,1,0:T(8,128)(2,1)S(1)} %bitcast.66), custom_call_target="tpu_custom_call" | custom-call | flops 7247757312 | bytes 25165824 | tf_op jit(solution)/shard_map/back/pallas_call | solution.py:196
  102.8 5.5 %collective-permute-done.11 = bf16[16,192,512]{2,1,0:T(8,128)(2,1)S(1)} collective-permute-done((bf16[16,192,512]{2,1,0:T(8,128)(2,1)S(1)}, bf16[16,192,512]{2,1,0:T(8,128)(2,1)S(1)}, u32[]{:S(2)}, u32[]{:S(2)}) %collective-permute-start.11) | collective-permute-done | bytes 3145760 | tf_op jit(solution)/shard_map/ppermute | solution.py:19
  109.2 4.0 %collective-permute-start.12 = (bf16[4,192,512]{2,1,0:T(8,128)(2,1)S(1)}, bf16[4,192,512]{2,1,0:T(8,128)(2,1)S(1)}, u32[]{:S(2)}, u32[]{:S(2)}) collective-permute-start(bf16[4,192,512]{2,1,0:T(8,128)(2,1)S(1)} %get-tuple-element.21), channel_id=1, source_target_pairs={{0,2},{1,3},{2,0},{3,1},{4,6},{5,7},{6,4},{7,5},{8,10},{9,11},{10,... | collective-permute-start | bytes 2359304 | tf_op jit(solution)/shard_map/ppermute | solution.py:305
  115.2 8.0 %collective-permute-done.12 = bf16[4,192,512]{2,1,0:T(8,128)(2,1)S(1)} collective-permute-done((bf16[4,192,512]{2,1,0:T(8,128)(2,1)S(1)}, bf16[4,192,512]{2,1,0:T(8,128)(2,1)S(1)}, u32[]{:S(2)}, u32[]{:S(2)}) %collective-permute-start.12) | collective-permute-done | bytes 786464 | tf_op jit(solution)/shard_map/ppermute | solution.py:305
  123.2 9.4 %collective-permute-done.14 = bf16[4,192,512]{2,1,0:T(8,128)(2,1)S(1)} collective-permute-done((bf16[4,192,512]{2,1,0:T(8,128)(2,1)S(1)}, bf16[4,192,512]{2,1,0:T(8,128)(2,1)S(1)}, u32[]{:S(2)}, u32[]{:S(2)}) %collective-permute-start.14) | collective-permute-done | bytes 786464 | tf_op jit(solution)/shard_map/ppermute | solution.py:305
  133.2 3.3 %collective-permute-start.15 = (bf16[192,512]{1,0:T(8,128)(2,1)S(1)}, bf16[192,512]{1,0:T(8,128)(2,1)S(1)}, u32[]{:S(2)}, u32[]{:S(2)}) collective-permute-start(bf16[192,512]{1,0:T(8,128)(2,1)S(1)} %get-tuple-element.28), channel_id=1, source_target_pairs={{0,8},{1,9},{2,10},{3,11},{4,12},{5,13},{6,14},{7,15},{8,0},{9,1},... | collective-permute-start | bytes 589832 | tf_op jit(solution)/shard_map/ppermute | solution.py:311
  138.5 2.0 %collective-permute-done.15 = bf16[192,512]{1,0:T(8,128)(2,1)S(1)} collective-permute-done((bf16[192,512]{1,0:T(8,128)(2,1)S(1)}, bf16[192,512]{1,0:T(8,128)(2,1)S(1)}, u32[]{:S(2)}, u32[]{:S(2)}) %collective-permute-start.15) | collective-permute-done | bytes 196640 | tf_op jit(solution)/shard_map/ppermute | solution.py:311
  140.5 2.4 %collective-permute-done.17 = bf16[192,512]{1,0:T(8,128)(2,1)S(1)} collective-permute-done((bf16[192,512]{1,0:T(8,128)(2,1)S(1)}, bf16[192,512]{1,0:T(8,128)(2,1)S(1)}, u32[]{:S(2)}, u32[]{:S(2)}) %collective-permute-start.17) | collective-permute-done | bytes 196640 | tf_op jit(solution)/shard_map/ppermute | solution.py:311
  (63 shorter events, 22.3 us)
Async XLA Ops:
  0.0 5.9 %collective-permute-start = (bf16[192,8192]{1,0:T(8,128)(2,1)}, bf16[192,8192]{1,0:T(8,128)(2,1)S(1)}, u32[]{:S(2)}, u32[]{:S(2)}) collective-permute-start(bf16[192,8192]{1,0:T(8,128)(2,1)} %a_ref.1), channel_id=1, source_target_pairs={{0,16},{16,0},{1,17},{17,1},{2,18},{18,2},{3,19},{19,3},{4,20},{20... | collective-permute-start | bytes 9437192 | tf_op jit(solution)/shard_map/ppermute | solution.py:19
  5.9 6.4 %copy-start.1 = (bf16[1,8192,3,384]{3,1,2,0:T(8,128)(2,1)S(1)}, bf16[1,8192,3,384]{3,1,2,0:T(8,128)(2,1)}, u32[]{:S(2)}) copy-start(bf16[1,8192,3,384]{3,1,2,0:T(8,128)(2,1)} %param.6) | copy-start | bytes 56623108
  12.2 9.4 %copy-start.4 = (bf16[192,8192]{1,0:T(8,128)(2,1)S(1)}, bf16[192,8192]{1,0:T(8,128)(2,1)}, u32[]{:S(2)}) copy-start(bf16[192,8192]{1,0:T(8,128)(2,1)} %a_ref.1) | copy-start | bytes 9437188
  20.7 15.8 %collective-permute-start.1 = (bf16[3,192,384]{2,1,0:T(8,128)(2,1)S(1)}, bf16[3,192,384]{2,1,0:T(8,128)(2,1)S(1)}, u32[]{:S(2)}, u32[]{:S(2)}) collective-permute-start(bf16[3,192,384]{2,1,0:T(8,128)(2,1)S(1)} %project.3), channel_id=1, source_target_pairs={{0,16},{16,0},{1,17},{17,1},{2,18},{18,2},{3,19},{19,3},{4,20},{20... | collective-permute-start | bytes 1327112 | tf_op jit(solution)/shard_map/ppermute | solution.py:19
  21.7 6.4 %copy-start.2 = (bf16[1,8192,3,384]{3,1,2,0:T(8,128)(2,1)S(1)}, bf16[1,8192,3,384]{3,1,2,0:T(8,128)(2,1)}, u32[]{:S(2)}) copy-start(bf16[1,8192,3,384]{3,1,2,0:T(8,128)(2,1)} %param.6) | copy-start | bytes 56623108
  36.7 9.1 %collective-permute-start.4 = (bf16[192,512]{1,0:T(8,128)(2,1)S(1)}, bf16[192,512]{1,0:T(8,128)(2,1)S(1)}, u32[]{:S(2)}, u32[]{:S(2)}) collective-permute-start(bf16[192,512]{1,0:T(8,128)(2,1)S(1)} %get-tuple-element.35), channel_id=1, source_target_pairs={{32,0},{64,32},{96,64},{33,1},{65,33},{97,65},{34,2},{66,34},{98,6... | collective-permute-start | bytes 589832 | tf_op jit(solution)/shard_map/ppermute | solution.py:264
  39.1 9.7 %collective-permute-start.2 = (bf16[192,512]{1,0:T(8,128)(2,1)S(1)}, bf16[192,512]{1,0:T(8,128)(2,1)S(1)}, u32[]{:S(2)}, u32[]{:S(2)}) collective-permute-start(bf16[192,512]{1,0:T(8,128)(2,1)S(1)} %get-tuple-element.37), channel_id=1, source_target_pairs={{0,32},{32,64},{96,0},{1,33},{33,65},{97,1},{2,34},{34,66},{98,2},... | collective-permute-start | bytes 589832 | tf_op jit(solution)/shard_map/ppermute | solution.py:264
  42.6 10.0 %collective-permute-start.3 = (bf16[192,512]{1,0:T(8,128)(2,1)S(1)}, bf16[192,512]{1,0:T(8,128)(2,1)S(1)}, u32[]{:S(2)}, u32[]{:S(2)}) collective-permute-start(bf16[192,512]{1,0:T(8,128)(2,1)S(1)} %get-tuple-element.38), channel_id=1, source_target_pairs={{0,64},{64,0},{96,32},{1,65},{65,1},{97,33},{2,66},{66,2},{98,34},... | collective-permute-start | bytes 589832 | tf_op jit(solution)/shard_map/ppermute | solution.py:264
  52.7 1.8 %collective-permute-start.5 = (bf16[4,192,256]{2,1,0:T(8,128)(2,1)S(1)}, bf16[4,192,256]{2,1,0:T(8,128)(2,1)S(1)}, u32[]{:S(2)}, u32[]{:S(2)}) collective-permute-start(bf16[4,192,256]{2,1,0:T(8,128)(2,1)S(1)} %pad_maximum_fusion), channel_id=1, source_target_pairs={{0,16},{16,0},{1,17},{17,1},{2,18},{18,2},{3,19},{19,3},{4,20},{20... | collective-permute-start | bytes 1179656 | tf_op jit(solution)/shard_map/ppermute | solution.py:19
  52.8 6.4 %copy-start.5 = (s32[2]{0:T(128)}, s32[2]{0:T(128)S(1)}, u32[]{:S(2)}) copy-start(s32[2]{0:T(128)S(1)} %pad_add_fusion.1.where_ref) | copy-start | bytes 28
  59.2 1.8 %collective-permute-start.6 = (bf16[4,192,256]{2,1,0:T(8,128)(2,1)S(1)}, bf16[4,192,256]{2,1,0:T(8,128)(2,1)S(1)}, u32[]{:S(2)}, u32[]{:S(2)}) collective-permute-start(bf16[4,192,256]{2,1,0:T(8,128)(2,1)S(1)} %get-tuple-element.12), channel_id=1, source_target_pairs={{0,16},{16,0},{1,17},{17,1},{2,18},{18,2},{3,19},{19,3},{4,20},{20... | collective-permute-start | bytes 1179656 | tf_op jit(solution)/shard_map/ppermute | solution.py:19
  61.2 10.4 %collective-permute-start.7 = (bf16[192,384]{1,0:T(8,128)(2,1)S(1)}, bf16[192,384]{1,0:T(8,128)(2,1)S(1)}, u32[]{:S(2)}, u32[]{:S(2)}) collective-permute-start(bf16[192,384]{1,0:T(8,128)(2,1)S(1)} %pad_maximum_fusion.2), channel_id=1, source_target_pairs={{0,96},{32,0},{64,32},{1,97},{33,1},{65,33},{2,98},{34,2},{66,34},... | collective-permute-start | bytes 442376 | tf_op jit(solution)/shard_map/ppermute | solution.py:277
  64.0 7.6 %collective-permute-start.8 = (bf16[192,384]{1,0:T(8,128)(2,1)S(1)}, bf16[192,384]{1,0:T(8,128)(2,1)S(1)}, u32[]{:S(2)}, u32[]{:S(2)}) collective-permute-start(bf16[192,384]{1,0:T(8,128)(2,1)S(1)} %pad_maximum_fusion.3), channel_id=1, source_target_pairs={{0,64},{32,96},{64,0},{1,65},{33,97},{65,1},{2,66},{34,98},{66,2},... | collective-permute-start | bytes 442376 | tf_op jit(solution)/shard_map/ppermute | solution.py:277
  65.3 10.5 %collective-permute-start.9 = (bf16[192,384]{1,0:T(8,128)(2,1)S(1)}, bf16[192,384]{1,0:T(8,128)(2,1)S(1)}, u32[]{:S(2)}, u32[]{:S(2)}) collective-permute-start(bf16[192,384]{1,0:T(8,128)(2,1)S(1)} %pad_maximum_fusion.4), channel_id=1, source_target_pairs={{0,32},{32,64},{64,96},{1,33},{33,65},{65,97},{2,34},{34,66},{66,9... | collective-permute-start | bytes 442376 | tf_op jit(solution)/shard_map/ppermute | solution.py:277
  71.5 4.3 %copy-start.7 = (bf16[192,384]{1,0:T(8,128)(2,1)}, bf16[192,384]{1,0:T(8,128)(2,1)S(1)}, u32[]{:S(2)}) copy-start(bf16[192,384]{1,0:T(8,128)(2,1)S(1)} %collective-permute-done.7.r1) | copy-start | bytes 442372
  79.1 2.0 %collective-permute-start.10 = (bf16[3,192,384]{2,1,0:T(8,128)(2,1)}, bf16[3,192,384]{2,1,0:T(8,128)(2,1)S(1)}, u32[]{:S(2)}, u32[]{:S(2)}) collective-permute-start(bf16[3,192,384]{2,1,0:T(8,128)(2,1)} %get-tuple-element.14), channel_id=1, source_target_pairs={{0,16},{16,0},{1,17},{17,1},{2,18},{18,2},{3,19},{19,3},{4,20},{20... | collective-permute-start | bytes 1327112 | tf_op jit(solution)/shard_map/ppermute | solution.py:19
  81.1 6.4 %copy-start.3 = (bf16[1,8192,3,384]{3,1,2,0:T(8,128)(2,1)S(1)}, bf16[1,8192,3,384]{3,1,2,0:T(8,128)(2,1)}, u32[]{:S(2)}) copy-start(bf16[1,8192,3,384]{3,1,2,0:T(8,128)(2,1)} %param.6) | copy-start | bytes 56623108
  102.6 5.7 %collective-permute-start.11 = (bf16[16,192,512]{2,1,0:T(8,128)(2,1)S(1)}, bf16[16,192,512]{2,1,0:T(8,128)(2,1)S(1)}, u32[]{:S(2)}, u32[]{:S(2)}) collective-permute-start(bf16[16,192,512]{2,1,0:T(8,128)(2,1)S(1)} %get-tuple-element.16), channel_id=1, source_target_pairs={{0,16},{16,0},{1,17},{17,1},{2,18},{18,2},{3,19},{19,3},{4,20},{20... | collective-permute-start | bytes 9437192 | tf_op jit(solution)/shard_map/ppermute | solution.py:19
  109.2 14.1 %collective-permute-start.12 = (bf16[4,192,512]{2,1,0:T(8,128)(2,1)S(1)}, bf16[4,192,512]{2,1,0:T(8,128)(2,1)S(1)}, u32[]{:S(2)}, u32[]{:S(2)}) collective-permute-start(bf16[4,192,512]{2,1,0:T(8,128)(2,1)S(1)} %get-tuple-element.21), channel_id=1, source_target_pairs={{0,2},{1,3},{2,0},{3,1},{4,6},{5,7},{6,4},{7,5},{8,10},{9,11},{10,... | collective-permute-start | bytes 2359304 | tf_op jit(solution)/shard_map/ppermute | solution.py:305
  113.2 19.4 %collective-permute-start.14 = (bf16[4,192,512]{2,1,0:T(8,128)(2,1)S(1)}, bf16[4,192,512]{2,1,0:T(8,128)(2,1)S(1)}, u32[]{:S(2)}, u32[]{:S(2)}) collective-permute-start(bf16[4,192,512]{2,1,0:T(8,128)(2,1)S(1)} %get-tuple-element.22), channel_id=1, source_target_pairs={{0,3},{1,0},{2,1},{3,2},{4,7},{5,4},{6,5},{7,6},{8,11},{9,8},{10,9... | collective-permute-start | bytes 2359304 | tf_op jit(solution)/shard_map/ppermute | solution.py:305
  113.9 18.7 %collective-permute-start.13 = (bf16[4,192,512]{2,1,0:T(8,128)(2,1)S(1)}, bf16[4,192,512]{2,1,0:T(8,128)(2,1)S(1)}, u32[]{:S(2)}, u32[]{:S(2)}) collective-permute-start(bf16[4,192,512]{2,1,0:T(8,128)(2,1)S(1)} %get-tuple-element.23), channel_id=1, source_target_pairs={{0,1},{1,2},{2,3},{3,0},{4,5},{5,6},{6,7},{7,4},{8,9},{9,10},{10,1... | collective-permute-start | bytes 2359304 | tf_op jit(solution)/shard_map/ppermute | solution.py:305
  133.2 7.3 %collective-permute-start.15 = (bf16[192,512]{1,0:T(8,128)(2,1)S(1)}, bf16[192,512]{1,0:T(8,128)(2,1)S(1)}, u32[]{:S(2)}, u32[]{:S(2)}) collective-permute-start(bf16[192,512]{1,0:T(8,128)(2,1)S(1)} %get-tuple-element.28), channel_id=1, source_target_pairs={{0,8},{1,9},{2,10},{3,11},{4,12},{5,13},{6,14},{7,15},{8,0},{9,1},... | collective-permute-start | bytes 589832 | tf_op jit(solution)/shard_map/ppermute | solution.py:311
  136.5 6.4 %collective-permute-start.17 = (bf16[192,512]{1,0:T(8,128)(2,1)S(1)}, bf16[192,512]{1,0:T(8,128)(2,1)S(1)}, u32[]{:S(2)}, u32[]{:S(2)}) collective-permute-start(bf16[192,512]{1,0:T(8,128)(2,1)S(1)} %get-tuple-element.29), channel_id=1, source_target_pairs={{0,12},{1,13},{2,14},{3,15},{4,0},{5,1},{6,2},{7,3},{8,4},{9,5},{1... | collective-permute-start | bytes 589832 | tf_op jit(solution)/shard_map/ppermute | solution.py:311
  137.6 6.9 %collective-permute-start.16 = (bf16[192,512]{1,0:T(8,128)(2,1)S(1)}, bf16[192,512]{1,0:T(8,128)(2,1)S(1)}, u32[]{:S(2)}, u32[]{:S(2)}) collective-permute-start(bf16[192,512]{1,0:T(8,128)(2,1)S(1)} %get-tuple-element.30), channel_id=1, source_target_pairs={{0,4},{1,5},{2,6},{3,7},{4,8},{5,9},{6,10},{7,11},{8,12},{9,13},{1... | collective-permute-start | bytes 589832 | tf_op jit(solution)/shard_map/ppermute | solution.py:311
  (4 other events, 6.9 us)

commit v2 on v1

v2 whole, which is shorter than its diff:
```python
import functools

import jax
import jax.numpy as jnp
from jax import lax
from jax.experimental import pallas as pl
from jax.experimental.pallas import tpu as pltpu
from jax.sharding import PartitionSpec as P

HD = 128
NH = 3
RING = 4
SCALE = HD**-0.5
AXES = ("seq", "mod", "tp")
MIB = 1024 * 1024
VMEM = 60 * MIB


def core_swap(x):
    return lax.ppermute(x, "mod", [(0, 1), (1, 0)])


def own_kernel(a_ref, w_ref, out_ref):
    step = pl.program_id(0)
    w = jnp.concatenate([w_ref[0], w_ref[1], w_ref[2]], axis=1)
    part = jnp.dot(a_ref[...], w, preferred_element_type=jnp.float32)

    @pl.when(step == 0)
    def _():
        out_ref[...] = part

    @pl.when(step > 0)
    def _():
        out_ref[...] += part


def project_own(a, w3, steps, block):
    rows = a.shape[0]
    return pl.pallas_call(
        own_kernel,
        grid=(steps,),
        in_specs=[
            pl.BlockSpec((rows, block), lambda i: (0, i)),
            pl.BlockSpec((3, block, NH * HD), lambda i: (0, i, 0)),
        ],
        out_specs=pl.BlockSpec((rows, 9 * HD), lambda i: (0, 0)),
        out_shape=jax.ShapeDtypeStruct((rows, 9 * HD), jnp.float32),
        compiler_params=pltpu.CompilerParams(vmem_limit_bytes=VMEM),
        cost_estimate=pl.CostEstimate(
            flops=2 * rows * steps * block * 9 * HD,
            bytes_accessed=steps * block * 9 * HD * 2,
            transcendentals=0,
        ),
        name="project_own",
    )(a, w3)


def project_kernel(early, part_ref, own_ref, oth_ref, w_ref, own_out, oth_out, acc_ref):
    step = pl.program_id(0)
    rows = own_ref.shape[0]
    w = jnp.concatenate([w_ref[0], w_ref[1], w_ref[2]], axis=1)

    @pl.when(step == 0)
    def _():
        acc_ref[0:rows] = part_ref[...]
        acc_ref[rows:] = jnp.dot(oth_ref[...], w, preferred_element_type=jnp.float32)

    @pl.when((step > 0) & (step < early))
    def _():
        acc_ref[rows:] += jnp.dot(oth_ref[...], w, preferred_element_type=jnp.float32)

    @pl.when(step >= early)
    def _():
        a = jnp.concatenate([own_ref[...], oth_ref[...]], axis=0)
        acc_ref[...] += jnp.dot(a, w, preferred_element_type=jnp.float32)

    @pl.when(step == pl.num_programs(0) - 1)
    def _():
        for h in range(NH):
            for c in range(3):
                lo = c * NH * HD + h * HD
                x = acc_ref[:, lo : lo + HD].astype(jnp.bfloat16)
                own_out[h, :, c * HD : (c + 1) * HD] = x[0:rows]
                oth_out[h, :, c * HD : (c + 1) * HD] = x[rows:]


def project(part, own, other, w3, early, block):
    rows, depth = own.shape
    shape = jax.ShapeDtypeStruct((NH, rows, 3 * HD), jnp.bfloat16)
    out_spec = pl.BlockSpec((NH, rows, 3 * HD), lambda i: (0, 0, 0))
    return pl.pallas_call(
        functools.partial(project_kernel, early),
        grid=(depth // block,),
        in_specs=[
            pl.BlockSpec((rows, 9 * HD), lambda i: (0, 0)),
            pl.BlockSpec((rows, block), lambda i: (0, jnp.maximum(i, early))),
            pl.BlockSpec((rows, block), lambda i: (0, i)),
            pl.BlockSpec((3, block, NH * HD), lambda i: (0, i, 0)),
        ],
        out_specs=[out_spec, out_spec],
        out_shape=[shape, shape],
        scratch_shapes=[pltpu.VMEM((2 * rows, 9 * HD), jnp.float32)],
        compiler_params=pltpu.CompilerParams(vmem_limit_bytes=VMEM),
        cost_estimate=pl.CostEstimate(
            flops=3 * rows * depth * 9 * HD, bytes_accessed=depth * 9 * HD * 2, transcendentals=0
        ),
        name="project",
    )(part, own, other, w3)


def attention_kernel(
    where_ref, a0, a1, a2, a3, b0, b1, b2, b3, g_ref0, g_ref1, g_ref2, g_ref3, own_ref, oth_ref, q_s, g_s, k_s, v_s, dk_s, dv_s
):
    chip = where_ref[0]
    core = where_ref[1]
    rows = a0.shape[0]
    both = 2 * rows
    own = (a0, a1, a2, a3)
    oth = (b0, b1, b2, b3)
    grads = (g_ref0, g_ref1, g_ref2, g_ref3)
    for k, (r, o, g) in enumerate(zip(own, oth, grads)):
        shard = (chip - k + RING) % RING
        q_s[shard] = r[:, 0:HD]
        g_s[shard] = g[...]
        mine = pl.ds(pl.multiple_of((2 * shard + core) * rows, rows), rows)
        other = pl.ds(pl.multiple_of((2 * shard + 1 - core) * rows, rows), rows)
        k_s[mine, :] = r[:, HD : 2 * HD]
        v_s[mine, :] = r[:, 2 * HD : 3 * HD]
        k_s[other, :] = o[:, HD : 2 * HD]
        v_s[other, :] = o[:, 2 * HD : 3 * HD]
    nt = (((1,), (1,)), ((), ()))
    tn = (((0,), (0,)), ((), ()))
    for s in range(RING - 1, -1, -1):
        width = both * (s + 1)
        q = q_s[s]
        g = g_s[s]
        kk = k_s[0:width, :]
        vv = v_s[0:width, :]
        scores = lax.dot_general(q, kk, nt, preferred_element_type=jnp.float32) * SCALE
        row = lax.broadcasted_iota(jnp.int32, (rows, width), 0) + (2 * s + core) * rows
        col = lax.broadcasted_iota(jnp.int32, (rows, width), 1)
        scores = jnp.where(col <= row, scores, -jnp.inf)
        lifted = jnp.exp(scores - jnp.max(scores, axis=1, keepdims=True))
        probs = lifted / jnp.sum(lifted, axis=1, keepdims=True)
        low = probs.astype(jnp.bfloat16)
        dprobs = lax.dot_general(g, vv, nt, preferred_element_type=jnp.float32)
        row_dot = jnp.sum(probs * dprobs, axis=1, keepdims=True)
        ds = (probs * (dprobs - row_dot)).astype(jnp.bfloat16)
        dq = jnp.dot(ds, kk, preferred_element_type=jnp.float32) * SCALE
        dk = lax.dot_general(ds, q, tn, preferred_element_type=jnp.float32) * SCALE
        dv = lax.dot_general(low, g, tn, preferred_element_type=jnp.float32)
        if s == RING - 1:
            dk_s[...] = dk
            dv_s[...] = dv
        else:
            dk_s[0:width, :] += dk
            dv_s[0:width, :] += dv
        own_ref[(chip - s + RING) % RING, :, 0:HD] = dq
    for k in range(RING):
        shard = (chip - k + RING) % RING
        mine = pl.ds(pl.multiple_of((2 * shard + core) * rows, rows), rows)
        other = pl.ds(pl.multiple_of((2 * shard + 1 - core) * rows, rows), rows)
        own_ref[k, :, HD : 2 * HD] = dk_s[mine, :]
        own_ref[k, :, 2 * HD : 3 * HD] = dv_s[mine, :]
        oth_ref[k, :, 0:HD] = dk_s[other, :].astype(jnp.bfloat16)
        oth_ref[k, :, HD : 2 * HD] = dv_s[other, :].astype(jnp.bfloat16)


def attention(where, parts, others, grads):
    rows = parts[0].shape[0]
    total = 2 * RING * rows
    vmem = pl.BlockSpec(memory_space=pltpu.VMEM)
    return pl.pallas_call(
        attention_kernel,
        in_specs=[pl.BlockSpec(memory_space=pltpu.SMEM)] + [vmem] * 12,
        out_specs=[vmem, vmem],
        out_shape=[
            jax.ShapeDtypeStruct((RING, rows, 3 * HD), jnp.float32),
            jax.ShapeDtypeStruct((RING, rows, 2 * HD), jnp.bfloat16),
        ],
        scratch_shapes=[
            pltpu.VMEM((RING, rows, HD), jnp.bfloat16),
            pltpu.VMEM((RING, rows, HD), jnp.bfloat16),
            pltpu.VMEM((total, HD), jnp.bfloat16),
            pltpu.VMEM((total, HD), jnp.bfloat16),
            pltpu.VMEM((total, HD), jnp.float32),
            pltpu.VMEM((total, HD), jnp.float32),
        ],
        compiler_params=pltpu.CompilerParams(vmem_limit_bytes=32 * MIB),
        cost_estimate=pl.CostEstimate(flops=10**9, bytes_accessed=4 * 10**6, transcendentals=10**6),
        name="attention",
    )(where, *parts, *others, *grads)


def back_kernel(
    chunk, place_ref, mask_ref, a0, a1, a2, a3, b0, b1, b2, b3, w_hbm, own_hbm, oth_hbm, w_s, g_s, o_s, w_sem, o_sem
):
    chip = place_ref[2, 0]
    rows = a0.shape[0]
    steps = w_s.shape[0]
    cols = w_s.shape[3]

    def fetch(i):
        return pltpu.make_async_copy(w_hbm.at[:, pl.ds(i * chunk, chunk)], w_s.at[i], w_sem.at[i])

    def put(i, j, side):
        out = (own_hbm, oth_hbm)[side]
        dest = place_ref[side, i * chunk + j]
        return pltpu.make_async_copy(o_s.at[side, i * chunk + j], out.at[dest], o_sem.at[side, i * chunk + j])

    for i in range(steps):
        fetch(i).start()
    for k, (own, oth) in enumerate(((a0, b0), (a1, b1), (a2, b2), (a3, b3))):
        head = (chip + k) % RING

        @pl.when(head < NH)
        def _():
            for side, x_ref in enumerate((own, oth)):
                x = x_ref[...]
                x = jnp.where(mask_ref[side] > 0, x, jnp.zeros_like(x))
                for c in range(3):
                    lo = pl.multiple_of((c * NH + head) * HD, HD)
                    g_s[side * rows : (side + 1) * rows, pl.ds(lo, HD)] = x[:, c * HD : (c + 1) * HD]

    for i in range(steps):
        fetch(i).wait()
        w = jnp.concatenate([w_s[i, c].reshape(chunk * cols, NH * HD) for c in range(3)], axis=1)
        res = lax.dot_general(
            g_s[...], w, (((1,), (1,)), ((), ())), preferred_element_type=jnp.float32
        ).astype(jnp.bfloat16)
        for j in range(chunk):
            for side in range(2):
                o_s[side, i * chunk + j] = res[side * rows : (side + 1) * rows, j * cols : (j + 1) * cols]
                put(i, j, side).start()
    for i in range(steps):
        for j in range(chunk):
            for side in range(2):
                put(i, j, side).wait()


def back(place, masks, own, oth, w3, stream, streams):
    rows, _ = own[0].shape
    depth = w3.shape[1]
    dests = RING * RING
    cols = depth // dests // streams
    chunk = 1024 // cols
    w4 = w3.reshape(3, dests, streams, cols, NH * HD)
    shape = jax.ShapeDtypeStruct((dests, rows, cols), jnp.bfloat16)
    vmem = pl.BlockSpec(memory_space=pltpu.VMEM)
    anywhere = pl.BlockSpec(memory_space=pl.ANY)

    def kernel(place_ref, mask_ref, *refs):
        w_ref = refs[8].at[:, :, stream]
        back_kernel(chunk, place_ref, mask_ref, *refs[:8], w_ref, *refs[9:])

    return pl.pallas_call(
        kernel,
        in_specs=[pl.BlockSpec(memory_space=pltpu.SMEM), vmem] + [vmem] * 8 + [anywhere],
        out_specs=[anywhere, anywhere],
        out_shape=[shape, shape],
        scratch_shapes=[
            pltpu.VMEM((dests // chunk, 3, chunk, cols, NH * HD), jnp.bfloat16),
            pltpu.VMEM((2 * rows, 9 * HD), jnp.bfloat16),
            pltpu.VMEM((2, dests, rows, cols), jnp.bfloat16),
            pltpu.SemaphoreType.DMA((dests // chunk,)),
            pltpu.SemaphoreType.DMA((2, dests)),
        ],
        compiler_params=pltpu.CompilerParams(vmem_limit_bytes=VMEM),
        cost_estimate=pl.CostEstimate(
            flops=2 * 2 * rows * dests * cols * 9 * HD,
            bytes_accessed=dests * cols * (9 * HD * 2 + 4 * rows),
            transcendentals=0,
        ),
        name="back",
    )(place, masks, *own, *oth, w4)


def ring_perm(first, hop):
    pairs = []
    for s in range(RING):
        for m in range(2):
            for y in range(RING):
                for z in range(RING):
                    if (m == 0) == first:
                        to = (y, (z + hop) % RING)
                    else:
                        to = ((y + hop) % RING, z)
                    base = (s * 2 + m) * RING * RING
                    pairs.append((base + y * RING + z, base + to[0] * RING + to[1]))
    return pairs


def per_device(activations, grad_attn, weights, modality):
    rows, depth = activations.shape
    chip = lax.axis_index("seq")
    core = lax.axis_index("mod")
    tp = lax.axis_index("tp")
    where = jnp.stack([chip, core]).astype(jnp.int32)
    w3 = jnp.transpose(weights[0], (1, 0, 2))

    own_mod = lax.dynamic_slice_in_dim(modality, (2 * chip + core) * rows, rows)
    other_mod = lax.dynamic_slice_in_dim(modality, (2 * chip + 1 - core) * rows, rows)
    masks = (jnp.stack([own_mod, other_mod]) == core).astype(jnp.int32)[:, :, None]

    def to_heads(hop):
        return [(i, (i + hop) % RING) for i in range(RING) if (i + hop) % RING < NH]

    def head_part(x, hop):
        head = jnp.minimum((chip + hop) % RING, NH - 1)
        return lax.dynamic_index_in_dim(x, head, 0, keepdims=False)

    act_other = core_swap(activations)
    g_heads = grad_attn.reshape(rows, NH, HD).transpose(1, 0, 2)
    g_parts = []
    for hop in (0, 2, 1, 3):
        x = head_part(g_heads, hop)
        g_parts.append(lax.ppermute(x, "seq", to_heads(hop)) if hop else x)
    g_parts = [g_parts[0], g_parts[2], g_parts[1], g_parts[3]]

    block, early = 2048, 2
    part = project_own(activations, w3, early, block)
    proj_own, proj_other = project(part, activations, act_other, w3, early, block)
    proj_back = core_swap(proj_other)
    is_mine = (masks[0] > 0)[None]
    heads = jnp.where(is_mine, proj_own, proj_back)

    parts = [None] * RING
    others = [None] * RING
    for hop in (2, 1, 3, 0):
        x = head_part(heads, hop)
        parts[hop] = lax.ppermute(x, "seq", to_heads(hop)) if hop else x
        others[hop] = core_swap(parts[hop])
    own, oth = attention(where, parts, others, g_parts)
    from_other = core_swap(oth)

    grads = [None] * RING
    other_grads = [None] * RING
    for hop in (2, 1, 3, 0):
        kv = own[hop, :, HD:] + from_other[hop].astype(jnp.float32)
        x = jnp.concatenate([own[hop, :, :HD], kv], axis=1).astype(jnp.bfloat16)
        if hop:
            x = lax.ppermute(x, "seq", [(i, (i - hop) % RING) for i in range(NH)])
        grads[hop] = x
        other_grads[hop] = core_swap(x)

    dest = jnp.arange(RING * RING, dtype=jnp.int32)
    dy = (dest // RING - tp // RING + RING) % RING
    dz = (dest % RING - tp % RING + RING) % RING
    z_first = dz * RING + dy
    y_first = dy * RING + dz
    place = jnp.stack(
        [
            jnp.where(core == 0, z_first, y_first),
            jnp.where(core == 0, y_first, z_first),
            jnp.full_like(dest, chip),
        ]
    ).astype(jnp.int32)

    streams = 2
    quarter = RING
    seconds = []
    for stream in range(streams):
        own_rows, other_rows = back(place, masks, grads, other_grads, w3, stream, streams)
        returned = core_swap(other_rows)

        def piece(k):
            cut = slice(k * quarter, (k + 1) * quarter)
            return own_rows[cut].astype(jnp.float32) + returned[cut].astype(jnp.float32)

        total = piece(0)
        for hop in (2, 1, 3):
            got = lax.ppermute(piece(hop).astype(jnp.bfloat16), AXES, ring_perm(True, hop))
            total = total + got.astype(jnp.float32)
        seconds.append(total)
    total = jnp.concatenate(seconds, axis=2) if streams > 1 else seconds[0]
    result = total[0]
    for hop in (2, 1, 3):
        got = lax.ppermute(total[hop].astype(jnp.bfloat16), AXES, ring_perm(False, hop))
        result = result + got.astype(jnp.float32)
    return result.astype(jnp.bfloat16)


def solution(mesh):
    in_specs = (P(("seq", "mod"), None), P(("seq", "mod"), "tp"), P("mod", None, None, "tp"), P())
    out_specs = P(("seq", "mod"), "tp")
    return jax.shard_map(
        per_device, mesh=mesh, in_specs=in_specs, out_specs=out_specs, check_vma=False
    )
```

time: 146 us -> 127 us (0.87)
  waiting for transfers between devices: 51.8 us -> 31.1 us
  local copies, waits for them, and re-layouts: 23.3 us -> 4.04 us
  starting transfers between devices: 27.2 us -> 43.6 us
  Pallas kernels: 38.3 us -> 42.7 us
    unnamed x20 -> x28, local copies, waits for them, and re-layouts: 21.6 us -> 2.32 us
    ppermute x6 -> x13, waiting for transfers between devices: 15.5 us -> 2.91 us  [core_swap(): return lax.ppermute(x, 'mod', [(0, 1), (1, 0)])]
    ppermute x6 -> x9, starting transfers between devices: 15.2 us -> 24.4 us  [the longest x3 9.27 us: per_device(): x = lax.ppermute(x, 'seq', [(i, (i - hop) % RING) for i in range(NH)])]
    ppermute x3 -> x6, waiting for transfers between devices: 17.4 us -> 11.8 us  [per_device(): lax.ppermute(piece(hop).astype(jnp.bfloat16), AXES, ring_perm(True, hop))]
    ppermute x3 -> x6, starting transfers between devices: 6.02 us -> 11 us  [per_device(): lax.ppermute(piece(hop).astype(jnp.bfloat16), AXES, ring_perm(True, hop))]
    pallas_call x4, Pallas kernels: 33.6 us -> 37.9 us  [the longest x2 18.2 us: back(): pl.pallas_call(kernel, in_specs=[pl.BlockSpec(memory_space=pltpu.SMEM), v...]
    ppermute x6 -> x9, waiting for transfers between devices: 13 us -> 10.5 us  [the longest x3 6.87 us: per_device(): g_parts.append(lax.ppermute(x, 'seq', to_heads(hop)) if hop else x)]
    ppermute x6 -> x13, starting transfers between devices: 0.74 us -> 2.89 us  [core_swap(): return lax.ppermute(x, 'mod', [(0, 1), (1, 0)])]
  transfers between devices with their start and end apart: 18 -> 31, of which waited for: 14 -> 13; matrix products, arithmetic and copies ran while one was open for 2% -> 3% of each run, Pallas kernels for 6% -> 12%
where the time goes in v2:
time: 127 us
  starting transfers between devices  43.6 us (34%)
  Pallas kernels  42.7 us (34%)
  waiting for transfers between devices  31.1 us (24%)
  other arithmetic  4.88 us (4%)
  local copies, waits for them, and re-layouts  4.04 us (3%)
    pallas_call x2, Pallas kernels, back(): pl.pallas_call(kernel, in_specs=[pl.BlockSpec(memory_space=pltpu.SMEM), v...  18.2 us
    pallas_call x1, Pallas kernels, project(): pl.pallas_call(functools.partial(project_kernel, early), grid=(depth // b...  13.3 us
    ppermute x6, waiting for transfers between devices, per_device(): lax.ppermute(piece(hop).astype(jnp.bfloat16), AXES, ring_perm(True, hop))  11.8 us
    ppermute x6, starting transfers between devices, per_device(): lax.ppermute(piece(hop).astype(jnp.bfloat16), AXES, ring_perm(True, hop))  11 us
    ppermute x3, starting transfers between devices, per_device(): x = lax.ppermute(x, 'seq', [(i, (i - hop) % RING) for i in range(NH)])  9.27 us
    ppermute x3, starting transfers between devices, per_device(): parts[hop] = lax.ppermute(x, 'seq', to_heads(hop)) if hop else x  7.78 us
    ppermute x3, starting transfers between devices, per_device(): g_parts.append(lax.ppermute(x, 'seq', to_heads(hop)) if hop else x)  7.36 us
    ppermute x3, waiting for transfers between devices, per_device(): g_parts.append(lax.ppermute(x, 'seq', to_heads(hop)) if hop else x)  6.87 us
  transfers between devices with their start and end apart: 31, of which 13 were waited for; matrix products, arithmetic and copies ran while one was open for 3% of the time, Pallas kernels for 12%

profile of v2, /device:TPU:2, one launch (start us, length us, event | category | flops | bytes accessed | tf_op | source)
XLA Modules:
  0.0 126.7 jit_solution(17197473625007627251)
XLA Ops:
  0.0 6.4 %project_own.1.part_ref = f32[192,1152]{1,0:T(8,128)} custom-call(bf16[192,8192]{1,0:T(8,128)(2,1)} %own_ref.1, bf16[3,8192,384]{2,1,0:T(8,128)(2,1)} %bitcast.69), custom_call_target="tpu_custom_call" | custom-call | flops 1811939328 | bytes 9437184 | tf_op jit(solution)/shard_map/project_own/pallas_call | solution.py:39
  6.5 1.6 %copy-done = bf16[192,8192]{1,0:T(8,128)(2,1)} copy-done((bf16[192,8192]{1,0:T(8,128)(2,1)}, bf16[192,8192]{1,0:T(8,128)(2,1)S(1)}, u32[]{:S(2)}) %copy-start) | copy-done | bytes 3145752
  8.1 13.3 %project.1 = (bf16[3,192,384]{2,1,0:T(8,128)(2,1)}, bf16[3,192,384]{2,1,0:T(8,128)(2,1)}) custom-call(f32[192,1152]{1,0:T(8,128)} %project_own.1.part_ref, bf16[192,8192]{1,0:T(8,128)(2,1)} %own_ref.1, bf16[192,8192]{1,0:T(8,128)(2,1)} %copy-done, bf16[3,8192,384]{2,1,0:T(8,128)(2,1)} %bitcast.70), custom_call_target="tpu_custom_call" | custom-call | flops 5435817984 | bytes 18874368 | tf_op jit(solution)/shard_map/project/pallas_call | solution.py:91
  24.8 2.4 %collective-permute-start.4 = (bf16[192,384]{1,0:T(8,128)(2,1)S(1)}, bf16[192,384]{1,0:T(8,128)(2,1)S(1)}, u32[]{:S(2)}, u32[]{:S(2)}) collective-permute-start(bf16[192,384]{1,0:T(8,128)(2,1)S(1)} %get-tuple-element.38), channel_id=1, source_target_pairs={{32,0},{64,32},{96,64},{33,1},{65,33},{97,65},{34,2},{66,34},{98,6... | collective-permute-start | bytes 442376 | tf_op jit(solution)/shard_map/ppermute | solution.py:331
  28.4 4.1 %collective-permute-start.2 = (bf16[192,384]{1,0:T(8,128)(2,1)S(1)}, bf16[192,384]{1,0:T(8,128)(2,1)S(1)}, u32[]{:S(2)}, u32[]{:S(2)}) collective-permute-start(bf16[192,384]{1,0:T(8,128)(2,1)S(1)} %get-tuple-element.40), channel_id=1, source_target_pairs={{0,32},{32,64},{96,0},{1,33},{33,65},{97,1},{2,34},{34,66},{98,2},... | collective-permute-start | bytes 442376 | tf_op jit(solution)/shard_map/ppermute | solution.py:331
  33.0 1.9 %collective-permute-start.9 = (bf16[192,128]{1,0:T(8,128)(2,1)S(1)}, bf16[192,128]{1,0:T(8,128)(2,1)S(1)}, u32[]{:S(2)}, u32[]{:S(2)}) collective-permute-start(bf16[192,128]{1,0:T(8,128)(2,1)S(1)} %bitcast.75), channel_id=1, source_target_pairs={{0,32},{32,64},{96,0},{1,33},{33,65},{97,1},{2,34},{34,66},{98,2},... | collective-permute-start | bytes 147464 | tf_op jit(solution)/shard_map/ppermute | solution.py:317
  36.2 5.0 %collective-permute-done.9.g_ref1 = bf16[192,128]{1,0:T(8,128)(2,1)S(1)} collective-permute-done((bf16[192,128]{1,0:T(8,128)(2,1)S(1)}, bf16[192,128]{1,0:T(8,128)(2,1)S(1)}, u32[]{:S(2)}, u32[]{:S(2)}) %collective-permute-start.9) | collective-permute-done | bytes 49184 | tf_op jit(solution)/shard_map/ppermute | solution.py:317
  42.4 4.1 %collective-permute-start.11 = (bf16[192,128]{1,0:T(8,128)(2,1)S(1)}, bf16[192,128]{1,0:T(8,128)(2,1)S(1)}, u32[]{:S(2)}, u32[]{:S(2)}) collective-permute-start(bf16[192,128]{1,0:T(8,128)(2,1)S(1)} %bitcast.74), channel_id=1, source_target_pairs={{32,0},{64,32},{96,64},{33,1},{65,33},{97,65},{34,2},{66,34},{98,6... | collective-permute-start | bytes 147464 | tf_op jit(solution)/shard_map/ppermute | solution.py:317
  46.7 1.7 %collective-permute-done.11.g_ref3 = bf16[192,128]{1,0:T(8,128)(2,1)S(1)} collective-permute-done((bf16[192,128]{1,0:T(8,128)(2,1)S(1)}, bf16[192,128]{1,0:T(8,128)(2,1)S(1)}, u32[]{:S(2)}, u32[]{:S(2)}) %collective-permute-start.11) | collective-permute-done | bytes 49184 | tf_op jit(solution)/shard_map/ppermute | solution.py:317
  48.4 4.7 %attention.1 = (f32[4,192,384]{2,1,0:T(8,128)S(1)}, bf16[4,192,256]{2,1,0:T(8,128)(2,1)S(1)}) custom-call(s32[2]{0:T(128)S(1)} %pad_add_fusion.1.where_ref, bf16[192,384]{1,0:T(8,128)(2,1)S(1)} %get-tuple-element.41.a0, bf16[192,384]{1,0:T(8,128)(2,1)S(1)} %collective-permute-done.2.a1, bf16[192,384]{1,0:T(8,128)(2,1)S(1)} %collective-permute-done.3.a2, ...), custom_call_target="tpu_custom_call" | custom-call | flops 1000000000 | bytes 4000000 | tf_op jit(solution)/shard_map/attention/pallas_call | solution.py:173
  53.4 1.5 %collective-permute-done.12 = bf16[4,192,256]{2,1,0:T(8,128)(2,1)S(1)} collective-permute-done((bf16[4,192,256]{2,1,0:T(8,128)(2,1)S(1)}, bf16[4,192,256]{2,1,0:T(8,128)(2,1)S(1)}, u32[]{:S(2)}, u32[]{:S(2)}) %collective-permute-start.12) | collective-permute-done | bytes 393248 | tf_op jit(solution)/shard_map/ppermute | solution.py:20
  55.1 4.0 %collective-permute-start.13 = (bf16[192,384]{1,0:T(8,128)(2,1)S(1)}, bf16[192,384]{1,0:T(8,128)(2,1)S(1)}, u32[]{:S(2)}, u32[]{:S(2)}) collective-permute-start(bf16[192,384]{1,0:T(8,128)(2,1)S(1)} %pad_maximum_fusion.2), channel_id=1, source_target_pairs={{0,96},{32,0},{64,32},{1,97},{33,1},{65,33},{2,98},{34,2},{66,34},... | collective-permute-start | bytes 442376 | tf_op jit(solution)/shard_map/ppermute | solution.py:342
  60.4 4.0 %collective-permute-start.15 = (bf16[192,384]{1,0:T(8,128)(2,1)S(1)}, bf16[192,384]{1,0:T(8,128)(2,1)S(1)}, u32[]{:S(2)}, u32[]{:S(2)}) collective-permute-start(bf16[192,384]{1,0:T(8,128)(2,1)S(1)} %pad_maximum_fusion.4), channel_id=1, source_target_pairs={{0,32},{32,64},{64,96},{1,33},{33,65},{65,97},{2,34},{34,66},{66,9... | collective-permute-start | bytes 442376 | tf_op jit(solution)/shard_map/ppermute | solution.py:342
  66.1 3.6 %collective-permute-done.15.refs_3_ = bf16[192,384]{1,0:T(8,128)(2,1)S(1)} collective-permute-done((bf16[192,384]{1,0:T(8,128)(2,1)S(1)}, bf16[192,384]{1,0:T(8,128)(2,1)S(1)}, u32[]{:S(2)}, u32[]{:S(2)}) %collective-permute-start.15) | collective-permute-done | bytes 147488 | tf_op jit(solution)/shard_map/ppermute | solution.py:342
  71.8 9.0 %back.3 = (bf16[16,192,256]{2,1,0:T(8,128)(2,1)}, bf16[16,192,256]{2,1,0:T(8,128)(2,1)}) custom-call(s32[3,16]{1,0:T(4,128)} %add_add_fusion.place_ref, s32[2,192,1]{2,1,0:T(8,128)} %convert_element_type.138.mask_ref, bf16[192,384]{1,0:T(8,128)(2,1)} %copy-done.3, bf16[192,384]{1,0:T(8,128)(2,1)} %copy-done.4, bf16[192,384]{1,0:T(8,128)(2,1)} %copy-done.5, ...), custom_call_target="tpu_custom_call" | custom-call | flops 3623878656 | bytes 12582912 | tf_op jit(solution)/shard_map/back/pallas_call | solution.py:256
  81.1 9.1 %back.2 = (bf16[16,192,256]{2,1,0:T(8,128)(2,1)}, bf16[16,192,256]{2,1,0:T(8,128)(2,1)}) custom-call(s32[3,16]{1,0:T(4,128)} %add_add_fusion.place_ref, s32[2,192,1]{2,1,0:T(8,128)} %convert_element_type.138.mask_ref, bf16[192,384]{1,0:T(8,128)(2,1)} %copy-done.3, bf16[192,384]{1,0:T(8,128)(2,1)} %copy-done.4, bf16[192,384]{1,0:T(8,128)(2,1)} %copy-done.5, ...), custom_call_target="tpu_custom_call" | custom-call | flops 3623878656 | bytes 12582912 | tf_op jit(solution)/shard_map/back/pallas_call | solution.py:256
  90.9 4.0 %collective-permute-start.25 = (bf16[4,192,256]{2,1,0:T(8,128)(2,1)S(1)}, bf16[4,192,256]{2,1,0:T(8,128)(2,1)S(1)}, u32[]{:S(2)}, u32[]{:S(2)}) collective-permute-start(bf16[4,192,256]{2,1,0:T(8,128)(2,1)S(1)} %get-tuple-element.21), channel_id=1, source_target_pairs={{0,2},{1,3},{2,0},{3,1},{4,6},{5,7},{6,4},{7,5},{8,10},{9,11},{10,... | collective-permute-start | bytes 1179656 | tf_op jit(solution)/shard_map/ppermute | solution.py:372
  98.4 2.6 %collective-permute-start.23 = (bf16[4,192,256]{2,1,0:T(8,128)(2,1)S(1)}, bf16[4,192,256]{2,1,0:T(8,128)(2,1)S(1)}, u32[]{:S(2)}, u32[]{:S(2)}) collective-permute-start(bf16[4,192,256]{2,1,0:T(8,128)(2,1)S(1)} %get-tuple-element.25), channel_id=1, source_target_pairs={{0,3},{1,0},{2,1},{3,2},{4,7},{5,4},{6,5},{7,6},{8,11},{9,8},{10,9... | collective-permute-start | bytes 1179656 | tf_op jit(solution)/shard_map/ppermute | solution.py:372
  102.3 3.6 %collective-permute-done.27 = bf16[4,192,256]{2,1,0:T(8,128)(2,1)S(1)} collective-permute-done((bf16[4,192,256]{2,1,0:T(8,128)(2,1)S(1)}, bf16[4,192,256]{2,1,0:T(8,128)(2,1)S(1)}, u32[]{:S(2)}, u32[]{:S(2)}) %collective-permute-start.27) | collective-permute-done | bytes 393248 | tf_op jit(solution)/shard_map/ppermute | solution.py:372
  106.2 3.0 %collective-permute-done.21 = bf16[4,192,256]{2,1,0:T(8,128)(2,1)S(1)} collective-permute-done((bf16[4,192,256]{2,1,0:T(8,128)(2,1)S(1)}, bf16[4,192,256]{2,1,0:T(8,128)(2,1)S(1)}, u32[]{:S(2)}, u32[]{:S(2)}) %collective-permute-start.21) | collective-permute-done | bytes 393248 | tf_op jit(solution)/shard_map/ppermute | solution.py:372
  109.2 5.2 %collective-permute-done.23 = bf16[4,192,256]{2,1,0:T(8,128)(2,1)S(1)} collective-permute-done((bf16[4,192,256]{2,1,0:T(8,128)(2,1)S(1)}, bf16[4,192,256]{2,1,0:T(8,128)(2,1)S(1)}, u32[]{:S(2)}, u32[]{:S(2)}) %collective-permute-start.23) | collective-permute-done | bytes 393248 | tf_op jit(solution)/shard_map/ppermute | solution.py:372
  114.8 3.3 %collective-permute-start.28 = (bf16[192,512]{1,0:T(8,128)(2,1)S(1)}, bf16[192,512]{1,0:T(8,128)(2,1)S(1)}, u32[]{:S(2)}, u32[]{:S(2)}) collective-permute-start(bf16[192,512]{1,0:T(8,128)(2,1)S(1)} %get-tuple-element.31), channel_id=1, source_target_pairs={{0,8},{1,9},{2,10},{3,11},{4,12},{5,13},{6,14},{7,15},{8,0},{9,1},... | collective-permute-start | bytes 589832 | tf_op jit(solution)/shard_map/ppermute | solution.py:378
  120.1 1.9 %collective-permute-done.28 = bf16[192,512]{1,0:T(8,128)(2,1)S(1)} collective-permute-done((bf16[192,512]{1,0:T(8,128)(2,1)S(1)}, bf16[192,512]{1,0:T(8,128)(2,1)S(1)}, u32[]{:S(2)}, u32[]{:S(2)}) %collective-permute-start.28) | collective-permute-done | bytes 196640 | tf_op jit(solution)/shard_map/ppermute | solution.py:378
  122.0 2.5 %collective-permute-done.30 = bf16[192,512]{1,0:T(8,128)(2,1)S(1)} collective-permute-done((bf16[192,512]{1,0:T(8,128)(2,1)S(1)}, bf16[192,512]{1,0:T(8,128)(2,1)S(1)}, u32[]{:S(2)}, u32[]{:S(2)}) %collective-permute-start.30) | collective-permute-done | bytes 196640 | tf_op jit(solution)/shard_map/ppermute | solution.py:378
  (98 shorter events, 23.6 us)
Async XLA Ops:
  0.0 6.4 %collective-permute-start = (bf16[192,8192]{1,0:T(8,128)(2,1)}, bf16[192,8192]{1,0:T(8,128)(2,1)S(1)}, u32[]{:S(2)}, u32[]{:S(2)}) collective-permute-start(bf16[192,8192]{1,0:T(8,128)(2,1)} %own_ref.1), channel_id=1, source_target_pairs={{0,16},{16,0},{1,17},{17,1},{2,18},{18,2},{3,19},{19,3},{4,20},{20... | collective-permute-start | bytes 9437192 | tf_op jit(solution)/shard_map/ppermute | solution.py:20
  24.8 16.5 %collective-permute-start.4 = (bf16[192,384]{1,0:T(8,128)(2,1)S(1)}, bf16[192,384]{1,0:T(8,128)(2,1)S(1)}, u32[]{:S(2)}, u32[]{:S(2)}) collective-permute-start(bf16[192,384]{1,0:T(8,128)(2,1)S(1)} %get-tuple-element.38), channel_id=1, source_target_pairs={{32,0},{64,32},{96,64},{33,1},{65,33},{97,65},{34,2},{66,34},{98,6... | collective-permute-start | bytes 442376 | tf_op jit(solution)/shard_map/ppermute | solution.py:331
  27.1 14.6 %collective-permute-start.3 = (bf16[192,384]{1,0:T(8,128)(2,1)S(1)}, bf16[192,384]{1,0:T(8,128)(2,1)S(1)}, u32[]{:S(2)}, u32[]{:S(2)}) collective-permute-start(bf16[192,384]{1,0:T(8,128)(2,1)S(1)} %get-tuple-element.39), channel_id=1, source_target_pairs={{0,64},{64,0},{96,32},{1,65},{65,1},{97,33},{2,66},{66,2},{98,34},... | collective-permute-start | bytes 442376 | tf_op jit(solution)/shard_map/ppermute | solution.py:331
  28.4 13.4 %collective-permute-start.2 = (bf16[192,384]{1,0:T(8,128)(2,1)S(1)}, bf16[192,384]{1,0:T(8,128)(2,1)S(1)}, u32[]{:S(2)}, u32[]{:S(2)}) collective-permute-start(bf16[192,384]{1,0:T(8,128)(2,1)S(1)} %get-tuple-element.40), channel_id=1, source_target_pairs={{0,32},{32,64},{96,0},{1,33},{33,65},{97,1},{2,34},{34,66},{98,2},... | collective-permute-start | bytes 442376 | tf_op jit(solution)/shard_map/ppermute | solution.py:331
  33.0 8.3 %collective-permute-start.9 = (bf16[192,128]{1,0:T(8,128)(2,1)S(1)}, bf16[192,128]{1,0:T(8,128)(2,1)S(1)}, u32[]{:S(2)}, u32[]{:S(2)}) collective-permute-start(bf16[192,128]{1,0:T(8,128)(2,1)S(1)} %bitcast.75), channel_id=1, source_target_pairs={{0,32},{32,64},{96,0},{1,33},{33,65},{97,1},{2,34},{34,66},{98,2},... | collective-permute-start | bytes 147464 | tf_op jit(solution)/shard_map/ppermute | solution.py:317
  34.9 7.5 %collective-permute-start.10 = (bf16[192,128]{1,0:T(8,128)(2,1)S(1)}, bf16[192,128]{1,0:T(8,128)(2,1)S(1)}, u32[]{:S(2)}, u32[]{:S(2)}) collective-permute-start(bf16[192,128]{1,0:T(8,128)(2,1)S(1)} %bitcast.73), channel_id=1, source_target_pairs={{0,64},{64,0},{96,32},{1,65},{65,1},{97,33},{2,66},{66,2},{98,34},... | collective-permute-start | bytes 147464 | tf_op jit(solution)/shard_map/ppermute | solution.py:317
  41.3 7.1 %collective-permute-start.5 = (bf16[192,384]{1,0:T(8,128)(2,1)S(1)}, bf16[192,384]{1,0:T(8,128)(2,1)S(1)}, u32[]{:S(2)}, u32[]{:S(2)}) collective-permute-start(bf16[192,384]{1,0:T(8,128)(2,1)S(1)} %get-tuple-element.41.a0), channel_id=1, source_target_pairs={{0,16},{16,0},{1,17},{17,1},{2,18},{18,2},{3,19},{19,3},{4,20},{20... | collective-permute-start | bytes 442376 | tf_op jit(solution)/shard_map/ppermute | solution.py:20
  41.3 7.1 %collective-permute-start.8 = (bf16[192,384]{1,0:T(8,128)(2,1)S(1)}, bf16[192,384]{1,0:T(8,128)(2,1)S(1)}, u32[]{:S(2)}, u32[]{:S(2)}) collective-permute-start(bf16[192,384]{1,0:T(8,128)(2,1)S(1)} %collective-permute-done.4.a3), channel_id=1, source_target_pairs={{0,16},{16,0},{1,17},{17,1},{2,18},{18,2},{3,19},{19,3},{4,20},{20... | collective-permute-start | bytes 442376 | tf_op jit(solution)/shard_map/ppermute | solution.py:20
  41.8 6.6 %collective-permute-start.7 = (bf16[192,384]{1,0:T(8,128)(2,1)S(1)}, bf16[192,384]{1,0:T(8,128)(2,1)S(1)}, u32[]{:S(2)}, u32[]{:S(2)}) collective-permute-start(bf16[192,384]{1,0:T(8,128)(2,1)S(1)} %collective-permute-done.3.a2), channel_id=1, source_target_pairs={{0,16},{16,0},{1,17},{17,1},{2,18},{18,2},{3,19},{19,3},{4,20},{20... | collective-permute-start | bytes 442376 | tf_op jit(solution)/shard_map/ppermute | solution.py:20
  41.9 6.5 %collective-permute-start.6 = (bf16[192,384]{1,0:T(8,128)(2,1)S(1)}, bf16[192,384]{1,0:T(8,128)(2,1)S(1)}, u32[]{:S(2)}, u32[]{:S(2)}) collective-permute-start(bf16[192,384]{1,0:T(8,128)(2,1)S(1)} %collective-permute-done.2.a1), channel_id=1, source_target_pairs={{0,16},{16,0},{1,17},{17,1},{2,18},{18,2},{3,19},{19,3},{4,20},{20... | collective-permute-start | bytes 442376 | tf_op jit(solution)/shard_map/ppermute | solution.py:20
  55.1 10.5 %collective-permute-start.13 = (bf16[192,384]{1,0:T(8,128)(2,1)S(1)}, bf16[192,384]{1,0:T(8,128)(2,1)S(1)}, u32[]{:S(2)}, u32[]{:S(2)}) collective-permute-start(bf16[192,384]{1,0:T(8,128)(2,1)S(1)} %pad_maximum_fusion.2), channel_id=1, source_target_pairs={{0,96},{32,0},{64,32},{1,97},{33,1},{65,33},{2,98},{34,2},{66,34},... | collective-permute-start | bytes 442376 | tf_op jit(solution)/shard_map/ppermute | solution.py:342
  59.1 6.9 %collective-permute-start.14 = (bf16[192,384]{1,0:T(8,128)(2,1)S(1)}, bf16[192,384]{1,0:T(8,128)(2,1)S(1)}, u32[]{:S(2)}, u32[]{:S(2)}) collective-permute-start(bf16[192,384]{1,0:T(8,128)(2,1)S(1)} %pad_maximum_fusion.3), channel_id=1, source_target_pairs={{0,64},{32,96},{64,0},{1,65},{33,97},{65,1},{2,66},{34,98},{66,2},... | collective-permute-start | bytes 442376 | tf_op jit(solution)/shard_map/ppermute | solution.py:342
  60.4 9.3 %collective-permute-start.15 = (bf16[192,384]{1,0:T(8,128)(2,1)S(1)}, bf16[192,384]{1,0:T(8,128)(2,1)S(1)}, u32[]{:S(2)}, u32[]{:S(2)}) collective-permute-start(bf16[192,384]{1,0:T(8,128)(2,1)S(1)} %pad_maximum_fusion.4), channel_id=1, source_target_pairs={{0,32},{32,64},{64,96},{1,33},{33,65},{65,97},{2,34},{34,66},{66,9... | collective-permute-start | bytes 442376 | tf_op jit(solution)/shard_map/ppermute | solution.py:342
  80.8 9.7 %collective-permute-start.24 = (bf16[16,192,256]{2,1,0:T(8,128)(2,1)}, bf16[16,192,256]{2,1,0:T(8,128)(2,1)S(1)}, u32[]{:S(2)}, u32[]{:S(2)}) collective-permute-start(bf16[16,192,256]{2,1,0:T(8,128)(2,1)} %get-tuple-element.20), channel_id=1, source_target_pairs={{0,16},{16,0},{1,17},{17,1},{2,18},{18,2},{3,19},{19,3},{4,20},{20... | collective-permute-start | bytes 4718600 | tf_op jit(solution)/shard_map/ppermute | solution.py:20
  90.2 6.7 %collective-permute-start.20 = (bf16[16,192,256]{2,1,0:T(8,128)(2,1)}, bf16[16,192,256]{2,1,0:T(8,128)(2,1)S(1)}, u32[]{:S(2)}, u32[]{:S(2)}) collective-permute-start(bf16[16,192,256]{2,1,0:T(8,128)(2,1)} %get-tuple-element.18), channel_id=1, source_target_pairs={{0,16},{16,0},{1,17},{17,1},{2,18},{18,2},{3,19},{19,3},{4,20},{20... | collective-permute-start | bytes 4718600 | tf_op jit(solution)/shard_map/ppermute | solution.py:20
  90.9 10.1 %collective-permute-start.25 = (bf16[4,192,256]{2,1,0:T(8,128)(2,1)S(1)}, bf16[4,192,256]{2,1,0:T(8,128)(2,1)S(1)}, u32[]{:S(2)}, u32[]{:S(2)}) collective-permute-start(bf16[4,192,256]{2,1,0:T(8,128)(2,1)S(1)} %get-tuple-element.21), channel_id=1, source_target_pairs={{0,2},{1,3},{2,0},{3,1},{4,6},{5,7},{6,4},{7,5},{8,10},{9,11},{10,... | collective-permute-start | bytes 1179656 | tf_op jit(solution)/shard_map/ppermute | solution.py:372
  94.9 11.0 %collective-permute-start.27 = (bf16[4,192,256]{2,1,0:T(8,128)(2,1)S(1)}, bf16[4,192,256]{2,1,0:T(8,128)(2,1)S(1)}, u32[]{:S(2)}, u32[]{:S(2)}) collective-permute-start(bf16[4,192,256]{2,1,0:T(8,128)(2,1)S(1)} %get-tuple-element.22), channel_id=1, source_target_pairs={{0,3},{1,0},{2,1},{3,2},{4,7},{5,4},{6,5},{7,6},{8,11},{9,8},{10,9... | collective-permute-start | bytes 1179656 | tf_op jit(solution)/shard_map/ppermute | solution.py:372
  95.6 10.3 %collective-permute-start.26 = (bf16[4,192,256]{2,1,0:T(8,128)(2,1)S(1)}, bf16[4,192,256]{2,1,0:T(8,128)(2,1)S(1)}, u32[]{:S(2)}, u32[]{:S(2)}) collective-permute-start(bf16[4,192,256]{2,1,0:T(8,128)(2,1)S(1)} %get-tuple-element.23), channel_id=1, source_target_pairs={{0,1},{1,2},{2,3},{3,0},{4,5},{5,6},{6,7},{7,4},{8,9},{9,10},{10,1... | collective-permute-start | bytes 1179656 | tf_op jit(solution)/shard_map/ppermute | solution.py:372
  97.3 11.9 %collective-permute-start.21 = (bf16[4,192,256]{2,1,0:T(8,128)(2,1)S(1)}, bf16[4,192,256]{2,1,0:T(8,128)(2,1)S(1)}, u32[]{:S(2)}, u32[]{:S(2)}) collective-permute-start(bf16[4,192,256]{2,1,0:T(8,128)(2,1)S(1)} %get-tuple-element.24), channel_id=1, source_target_pairs={{0,2},{1,3},{2,0},{3,1},{4,6},{5,7},{6,4},{7,5},{8,10},{9,11},{10,... | collective-permute-start | bytes 1179656 | tf_op jit(solution)/shard_map/ppermute | solution.py:372
  98.4 16.0 %collective-permute-start.23 = (bf16[4,192,256]{2,1,0:T(8,128)(2,1)S(1)}, bf16[4,192,256]{2,1,0:T(8,128)(2,1)S(1)}, u32[]{:S(2)}, u32[]{:S(2)}) collective-permute-start(bf16[4,192,256]{2,1,0:T(8,128)(2,1)S(1)} %get-tuple-element.25), channel_id=1, source_target_pairs={{0,3},{1,0},{2,1},{3,2},{4,7},{5,4},{6,5},{7,6},{8,11},{9,8},{10,9... | collective-permute-start | bytes 1179656 | tf_op jit(solution)/shard_map/ppermute | solution.py:372
  101.0 13.3 %collective-permute-start.22 = (bf16[4,192,256]{2,1,0:T(8,128)(2,1)S(1)}, bf16[4,192,256]{2,1,0:T(8,128)(2,1)S(1)}, u32[]{:S(2)}, u32[]{:S(2)}) collective-permute-start(bf16[4,192,256]{2,1,0:T(8,128)(2,1)S(1)} %get-tuple-element.26), channel_id=1, source_target_pairs={{0,1},{1,2},{2,3},{3,0},{4,5},{5,6},{6,7},{7,4},{8,9},{9,10},{10,1... | collective-permute-start | bytes 1179656 | tf_op jit(solution)/shard_map/ppermute | solution.py:372
  114.8 7.3 %collective-permute-start.28 = (bf16[192,512]{1,0:T(8,128)(2,1)S(1)}, bf16[192,512]{1,0:T(8,128)(2,1)S(1)}, u32[]{:S(2)}, u32[]{:S(2)}) collective-permute-start(bf16[192,512]{1,0:T(8,128)(2,1)S(1)} %get-tuple-element.31), channel_id=1, source_target_pairs={{0,8},{1,9},{2,10},{3,11},{4,12},{5,13},{6,14},{7,15},{8,0},{9,1},... | collective-permute-start | bytes 589832 | tf_op jit(solution)/shard_map/ppermute | solution.py:378
  118.0 6.4 %collective-permute-start.30 = (bf16[192,512]{1,0:T(8,128)(2,1)S(1)}, bf16[192,512]{1,0:T(8,128)(2,1)S(1)}, u32[]{:S(2)}, u32[]{:S(2)}) collective-permute-start(bf16[192,512]{1,0:T(8,128)(2,1)S(1)} %get-tuple-element.32), channel_id=1, source_target_pairs={{0,12},{1,13},{2,14},{3,15},{4,0},{5,1},{6,2},{7,3},{8,4},{9,5},{1... | collective-permute-start | bytes 589832 | tf_op jit(solution)/shard_map/ppermute | solution.py:378
  119.1 6.9 %collective-permute-start.29 = (bf16[192,512]{1,0:T(8,128)(2,1)S(1)}, bf16[192,512]{1,0:T(8,128)(2,1)S(1)}, u32[]{:S(2)}, u32[]{:S(2)}) collective-permute-start(bf16[192,512]{1,0:T(8,128)(2,1)S(1)} %get-tuple-element.33), channel_id=1, source_target_pairs={{0,4},{1,5},{2,6},{3,7},{4,8},{5,9},{6,10},{7,11},{8,12},{9,13},{1... | collective-permute-start | bytes 589832 | tf_op jit(solution)/shard_map/ppermute | solution.py:378
  (19 other events, 79.4 us)

commit v3 on v1

v3 whole, which is shorter than its diff:
```python
import functools

import jax
import jax.numpy as jnp
from jax import lax
from jax.experimental import pallas as pl
from jax.experimental.pallas import tpu as pltpu
from jax.sharding import PartitionSpec as P

HD = 128
NH = 3
RING = 4
SCALE = HD**-0.5
AXES = ("seq", "mod", "tp")
MIB = 1024 * 1024


def core_swap(x):
    return lax.ppermute(x, "mod", [(0, 1), (1, 0)])


def own_kernel(early, a_ref, w_hbm, part_ref, w_ref, sem):
    chunks = w_ref.shape[1] // 2
    block = 2 * 2 * w_ref.shape[3]

    def fetch(i):
        return pltpu.make_async_copy(w_hbm.at[:, 2 * i : 2 * i + 2], w_ref.at[:, 2 * i : 2 * i + 2], sem.at[i])

    for i in range(chunks):
        fetch(i).start()
    for i in range(chunks):
        fetch(i).wait()
        if i < early:
            part = jnp.dot(
                a_ref[:, i * block : (i + 1) * block], weight_block(w_ref, i), preferred_element_type=jnp.float32
            )
            if i == 0:
                part_ref[...] = part
            else:
                part_ref[...] += part


def weight_block(w_ref, i):
    size = 4 * w_ref.shape[3]
    return jnp.concatenate([w_ref[c, 2 * i : 2 * i + 2].reshape(size, NH * HD) for c in range(3)], axis=1)


def project_own(a, w5, early):
    rows = a.shape[0]
    vmem = pl.BlockSpec(memory_space=pltpu.VMEM)
    anywhere = pl.BlockSpec(memory_space=pl.ANY)
    return pl.pallas_call(
        functools.partial(own_kernel, early),
        in_specs=[vmem, anywhere],
        out_specs=[vmem, vmem],
        out_shape=[
            jax.ShapeDtypeStruct((rows, 9 * HD), jnp.float32),
            pltpu.VMEM(w5.shape, jnp.bfloat16),
        ],
        scratch_shapes=[pltpu.SemaphoreType.DMA((w5.shape[1] // 2,))],
        compiler_params=pltpu.CompilerParams(vmem_limit_bytes=44 * MIB),
        cost_estimate=pl.CostEstimate(flops=4 * 10**9, bytes_accessed=2 * 10**7, transcendentals=0),
        name="project_own",
    )(a, w5)


def project_kernel(early, where_ref, part_ref, own_hbm, oth_hbm, w_ref, own_out, oth_out, half_hbm, a_s, acc_ref, sem, half_sem):
    rows = part_ref.shape[0]
    chunks = w_ref.shape[1] // 2
    block = 2 * 2 * w_ref.shape[3]

    def fetch(i):
        cut = pl.ds(i * block, block)
        return pltpu.make_async_copy(oth_hbm.at[:, cut], a_s.at[i, rows : 2 * rows], sem.at[1, i])

    def fetch_own(i):
        cut = pl.ds(i * block, block)
        return pltpu.make_async_copy(own_hbm.at[:, cut], a_s.at[i, 0:rows], sem.at[0, i])

    half = pltpu.make_async_copy(w_ref.at[:, :, 1 - where_ref[1]], half_hbm, half_sem)
    for i in range(chunks):
        fetch(i).start()
        if i >= early:
            fetch_own(i).start()
    half.start()
    acc_ref[0:rows] = part_ref[...]
    for i in range(chunks):
        fetch(i).wait()
        w = weight_block(w_ref, i)
        if i < early:
            part = jnp.dot(a_s[i, rows:], w, preferred_element_type=jnp.float32)
            if i == 0:
                acc_ref[rows:] = part
            else:
                acc_ref[rows:] += part
        else:
            fetch_own(i).wait()
            acc_ref[...] += jnp.dot(a_s[i], w, preferred_element_type=jnp.float32)
    for h in range(NH):
        for c in range(3):
            lo = c * NH * HD + h * HD
            x = acc_ref[:, lo : lo + HD].astype(jnp.bfloat16)
            own_out[h, :, c * HD : (c + 1) * HD] = x[0:rows]
            oth_out[h, :, c * HD : (c + 1) * HD] = x[rows:]
    half.wait()


def project(where, part, own, other, w5, early):
    rows, depth = own.shape
    chunks = w5.shape[1] // 2
    shape = jax.ShapeDtypeStruct((NH, rows, 3 * HD), jnp.bfloat16)
    vmem = pl.BlockSpec(memory_space=pltpu.VMEM)
    anywhere = pl.BlockSpec(memory_space=pl.ANY)
    return pl.pallas_call(
        functools.partial(project_kernel, early),
        in_specs=[pl.BlockSpec(memory_space=pltpu.SMEM), vmem, anywhere, anywhere, vmem],
        out_specs=[vmem, vmem, anywhere],
        out_shape=[shape, shape, jax.ShapeDtypeStruct((3,) + w5.shape[1:2] + w5.shape[3:], jnp.bfloat16)],
        scratch_shapes=[
            pltpu.VMEM((chunks, 2 * rows, depth // chunks), jnp.bfloat16),
            pltpu.VMEM((2 * rows, 9 * HD), jnp.float32),
            pltpu.SemaphoreType.DMA((2, chunks)),
            pltpu.SemaphoreType.DMA,
        ],
        compiler_params=pltpu.CompilerParams(vmem_limit_bytes=44 * MIB),
        cost_estimate=pl.CostEstimate(flops=7 * 10**9, bytes_accessed=10**7, transcendentals=0),
        name="project",
    )(where, part, own, other, w5)


def attention_kernel(
    where_ref, a0, a1, a2, a3, b0, b1, b2, b3, own_ref, oth_ref, q_s, g_s, k_s, v_s, dk_s, dv_s
):
    chip = where_ref[0]
    core = where_ref[1]
    rows = a0.shape[0]
    both = 2 * rows
    own = (a0, a1, a2, a3)
    oth = (b0, b1, b2, b3)
    for k, (r, o) in enumerate(zip(own, oth)):
        shard = (chip - k + RING) % RING
        q_s[shard] = r[:, 0:HD]
        g_s[shard] = r[:, 3 * HD : 4 * HD]
        mine = pl.ds(pl.multiple_of((2 * shard + core) * rows, rows), rows)
        other = pl.ds(pl.multiple_of((2 * shard + 1 - core) * rows, rows), rows)
        k_s[mine, :] = r[:, HD : 2 * HD]
        v_s[mine, :] = r[:, 2 * HD : 3 * HD]
        k_s[other, :] = o[:, HD : 2 * HD]
        v_s[other, :] = o[:, 2 * HD : 3 * HD]
    nt = (((1,), (1,)), ((), ()))
    tn = (((0,), (0,)), ((), ()))
    for s in range(RING - 1, -1, -1):
        width = both * (s + 1)
        q = q_s[s]
        g = g_s[s]
        kk = k_s[0:width, :]
        vv = v_s[0:width, :]
        scores = lax.dot_general(q, kk, nt, preferred_element_type=jnp.float32) * SCALE
        row = lax.broadcasted_iota(jnp.int32, (rows, width), 0) + (2 * s + core) * rows
        col = lax.broadcasted_iota(jnp.int32, (rows, width), 1)
        scores = jnp.where(col <= row, scores, -jnp.inf)
        lifted = jnp.exp(scores - jnp.max(scores, axis=1, keepdims=True))
        probs = lifted / jnp.sum(lifted, axis=1, keepdims=True)
        low = probs.astype(jnp.bfloat16)
        dprobs = lax.dot_general(g, vv, nt, preferred_element_type=jnp.float32)
        row_dot = jnp.sum(probs * dprobs, axis=1, keepdims=True)
        ds = (probs * (dprobs - row_dot)).astype(jnp.bfloat16)
        dq = jnp.dot(ds, kk, preferred_element_type=jnp.float32) * SCALE
        dk = lax.dot_general(ds, q, tn, preferred_element_type=jnp.float32) * SCALE
        dv = lax.dot_general(low, g, tn, preferred_element_type=jnp.float32)
        if s == RING - 1:
            dk_s[...] = dk
            dv_s[...] = dv
        else:
            dk_s[0:width, :] += dk
            dv_s[0:width, :] += dv
        own_ref[(chip - s + RING) % RING, :, 0:HD] = dq
    for k in range(RING):
        shard = (chip - k + RING) % RING
        mine = pl.ds(pl.multiple_of((2 * shard + core) * rows, rows), rows)
        other = pl.ds(pl.multiple_of((2 * shard + 1 - core) * rows, rows), rows)
        own_ref[k, :, HD : 2 * HD] = dk_s[mine, :]
        own_ref[k, :, 2 * HD : 3 * HD] = dv_s[mine, :]
        oth_ref[k, :, 0:HD] = dk_s[other, :].astype(jnp.bfloat16)
        oth_ref[k, :, HD : 2 * HD] = dv_s[other, :].astype(jnp.bfloat16)


def attention(where, parts, others):
    rows = parts[0].shape[0]
    total = 2 * RING * rows
    vmem = pl.BlockSpec(memory_space=pltpu.VMEM)
    return pl.pallas_call(
        attention_kernel,
        in_specs=[pl.BlockSpec(memory_space=pltpu.SMEM)] + [vmem] * 8,
        out_specs=[vmem, vmem],
        out_shape=[
            jax.ShapeDtypeStruct((RING, rows, 3 * HD), jnp.float32),
            jax.ShapeDtypeStruct((RING, rows, 2 * HD), jnp.bfloat16),
        ],
        scratch_shapes=[
            pltpu.VMEM((RING, rows, HD), jnp.bfloat16),
            pltpu.VMEM((RING, rows, HD), jnp.bfloat16),
            pltpu.VMEM((total, HD), jnp.bfloat16),
            pltpu.VMEM((total, HD), jnp.bfloat16),
            pltpu.VMEM((total, HD), jnp.float32),
            pltpu.VMEM((total, HD), jnp.float32),
        ],
        compiler_params=pltpu.CompilerParams(vmem_limit_bytes=32 * MIB),
        cost_estimate=pl.CostEstimate(flops=10**9, bytes_accessed=4 * 10**6, transcendentals=10**6),
        name="attention",
    )(where, *parts, *others)


def gather(chip, mask_ref, own, oth, out_ref):
    rows = own[0].shape[0]
    for k in range(RING):
        head = (chip + k) % RING

        @pl.when(head < NH)
        def _():
            for block, x_ref in enumerate((own[k], oth[k])):
                x = x_ref[...]
                zero = jnp.zeros_like(x)
                for side in range(2):
                    kept = jnp.where(mask_ref[block] == 1 - side, x, zero)
                    for c in range(3):
                        lo = pl.multiple_of(((side * 3 + c) * NH + head) * HD, HD)
                        out_ref[block * rows : (block + 1) * rows, pl.ds(lo, HD)] = kept[:, c * HD : (c + 1) * HD]


def back_kernel(hop, first, place_ref, *refs):
    if first:
        mask_ref, *parts, own_hbm, other_hbm, out_ref, token_ref, g_ref, w_s, sem = refs
    else:
        _, g_ref, own_hbm, other_hbm, out_ref, token_ref, w_s, sem = refs
    core = place_ref[RING * RING]
    chip = place_ref[RING * RING + 1]
    cols = w_s.shape[3]

    def fetch(side, j):
        dest = place_ref[hop * RING + j]
        src = other_hbm.at[:, dest] if side else own_hbm.at[:, dest, core]
        return pltpu.make_async_copy(src, w_s.at[side, j], sem.at[side, j])

    for j in range(RING):
        for side in range(2):
            fetch(side, j).start()
    token_ref[...] = jnp.zeros_like(token_ref)
    if first:
        gather(chip, mask_ref, parts[:RING], parts[RING:], g_ref)
    pair = 2
    for j in range(0, RING, pair):
        for side in range(2):
            for i in range(pair):
                fetch(side, j + i).wait()
        w = [w_s[side, j : j + pair, c].reshape(pair * cols, NH * HD) for side in range(2) for c in range(3)]
        res = lax.dot_general(
            g_ref[...], jnp.concatenate(w, axis=1), (((1,), (1,)), ((), ())), preferred_element_type=jnp.float32
        ).astype(jnp.bfloat16)
        for i in range(pair):
            out_ref[j + i] = res[:, i * cols : (i + 1) * cols]


def back(place, w5, other_half, hop, token=None, grads=None, gather_from=None):
    cols = w5.shape[3]
    vmem = pl.BlockSpec(memory_space=pltpu.VMEM)
    anywhere = pl.BlockSpec(memory_space=pl.ANY)
    first = grads is None
    if first:
        masks, own, oth = gather_from
        rows = 2 * own[0].shape[0]
        extra = [masks, *own, *oth]
        extra_specs = [vmem] * 9
    else:
        rows = grads.shape[0]
        extra = [token, grads]
        extra_specs = [anywhere, vmem]
    out_shape = [
        jax.ShapeDtypeStruct((RING, rows, cols), jnp.bfloat16),
        jax.ShapeDtypeStruct((8, HD), jnp.float32),
    ]
    if first:
        out_shape.append(pltpu.VMEM((rows, 18 * HD), jnp.bfloat16))
    return pl.pallas_call(
        functools.partial(back_kernel, hop, first),
        in_specs=[pl.BlockSpec(memory_space=pltpu.SMEM)] + extra_specs + [anywhere, anywhere],
        out_specs=[vmem] * len(out_shape),
        out_shape=out_shape,
        scratch_shapes=[
            pltpu.VMEM((2, RING, 3, cols, NH * HD), jnp.bfloat16),
            pltpu.SemaphoreType.DMA((2, RING)),
        ],
        compiler_params=pltpu.CompilerParams(vmem_limit_bytes=50 * MIB),
        cost_estimate=pl.CostEstimate(flops=10**6, bytes_accessed=10**4, transcendentals=0),
        name="back",
    )(place, *extra, w5, other_half)


def ring_perm(first, hop):
    pairs = []
    for s in range(RING):
        for m in range(2):
            for y in range(RING):
                for z in range(RING):
                    if (m == 0) == first:
                        to = (y, (z + hop) % RING)
                    else:
                        to = ((y + hop) % RING, z)
                    base = (s * 2 + m) * RING * RING
                    pairs.append((base + y * RING + z, base + to[0] * RING + to[1]))
    return pairs


def per_device(activations, grad_attn, weights, modality):
    rows, depth = activations.shape
    chip = lax.axis_index("seq")
    core = lax.axis_index("mod")
    tp = lax.axis_index("tp")
    where = jnp.stack([chip, core]).astype(jnp.int32)
    dests = RING * RING
    cols = depth // dests // 2
    w5 = jnp.transpose(weights[0], (1, 0, 2)).reshape(3, dests, 2, cols, NH * HD)

    own_mod = lax.dynamic_slice_in_dim(modality, (2 * chip + core) * rows, rows)
    other_mod = lax.dynamic_slice_in_dim(modality, (2 * chip + 1 - core) * rows, rows)
    masks = (jnp.stack([own_mod, other_mod]) == core).astype(jnp.int32)[:, :, None]

    act_other = core_swap(activations)
    early = 5
    part, w_vmem = project_own(activations, w5, early)
    w_vmem = pltpu.with_memory_space_constraint(w_vmem, pltpu.VMEM)
    proj_own, proj_other, half = project(where, part, activations, act_other, w_vmem, early)
    proj_back = core_swap(proj_other)
    other_half = core_swap(half)
    g_heads = grad_attn.reshape(rows, NH, HD).transpose(1, 0, 2)
    heads = jnp.concatenate([jnp.where((masks[0] > 0)[None], proj_own, proj_back), g_heads], axis=2)

    parts = [None] * RING
    others = [None] * RING
    for hop in (2, 1, 3, 0):
        head = jnp.minimum((chip + hop) % RING, NH - 1)
        x = lax.dynamic_index_in_dim(heads, head, 0, keepdims=False)
        if hop:
            x = lax.ppermute(x, "seq", [(i, (i + hop) % RING) for i in range(RING) if (i + hop) % RING < NH])
        parts[hop] = x
        others[hop] = core_swap(x)
    own, oth = attention(where, parts, others)
    from_other = core_swap(oth)

    grads = [None] * RING
    other_grads = [None] * RING
    for hop in (2, 1, 3, 0):
        kv = own[hop, :, HD:] + from_other[hop].astype(jnp.float32)
        x = jnp.concatenate([own[hop, :, :HD], kv], axis=1).astype(jnp.bfloat16)
        if hop:
            x = lax.ppermute(x, "seq", [(i, (i - hop) % RING) for i in range(NH)])
        grads[hop] = x
        other_grads[hop] = core_swap(x)
    i = jnp.arange(dests, dtype=jnp.int32) // RING
    j = jnp.arange(dests, dtype=jnp.int32) % RING
    y, z = tp // RING, tp % RING
    place = jnp.where(
        core == 0,
        (y + j) % RING * RING + (z + i) % RING,
        (y + i) % RING * RING + (z + j) % RING,
    )
    place = jnp.concatenate([place, jnp.stack([core, chip])]).astype(jnp.int32)

    pieces = {}
    token = g = None
    for hop in (2, 1, 3, 0):
        if g is None:
            x, token, g = back(place, w5, other_half, hop, gather_from=(masks, grads, other_grads))
            g = pltpu.with_memory_space_constraint(g, pltpu.VMEM)
        else:
            x, token = back(place, w5, other_half, hop, token, g)
        pieces[hop] = lax.ppermute(x, AXES, ring_perm(True, hop)) if hop else x
    total = pieces[0].astype(jnp.float32)
    for hop in (2, 1, 3):
        total = lax.optimization_barrier(total) + pieces[hop].astype(jnp.float32)
    result = total[0]
    for hop in (2, 1, 3):
        got = lax.ppermute(total[hop].astype(jnp.bfloat16), AXES, ring_perm(False, hop))
        result = result + got.astype(jnp.float32)
    result = result.astype(jnp.bfloat16)
    mine = result[:rows]
    theirs = core_swap(result[rows:])
    return jnp.where(
        core == 0, jnp.concatenate([mine, theirs], axis=1), jnp.concatenate([theirs, mine], axis=1)
    )


def solution(mesh):
    in_specs = (P(("seq", "mod"), None), P(("seq", "mod"), "tp"), P("mod", None, None, "tp"), P())
    out_specs = P(("seq", "mod"), "tp")
    return jax.shard_map(
        per_device, mesh=mesh, in_specs=in_specs, out_specs=out_specs, check_vma=False
    )
```

time: 146 us -> 116 us (0.79)
  the two profiles are of different devices: /device:TPU:2 before, /device:TPU:1 now
where the time goes in v3:
time: 116 us
  Pallas kernels  43.3 us (37%)
  starting transfers between devices  41.9 us (36%)
  waiting for transfers between devices  25.3 us (22%)
  other arithmetic  3.85 us (3%)
    pallas_call x4, Pallas kernels, back(): pl.pallas_call(functools.partial(back_kernel, hop, first), in_specs=[pl.B...  17.8 us
    ppermute x13, starting transfers between devices, core_swap(): return lax.ppermute(x, 'mod', [(0, 1), (1, 0)])  11.8 us
    pallas_call x1, Pallas kernels, project(): pl.pallas_call(functools.partial(project_kernel, early), in_specs=[pl.Blo...  11.5 us
    ppermute x3, starting transfers between devices, per_device(): x = lax.ppermute(x, 'seq', [(i, (i - hop) % RING) for i in range(NH)])  10.5 us
    ppermute x13, waiting for transfers between devices, core_swap(): return lax.ppermute(x, 'mod', [(0, 1), (1, 0)])  9.96 us
    pallas_call x1, Pallas kernels, project_own(): pl.pallas_call(functools.partial(own_kernel, early), in_specs=[vmem, anyw...  9.33 us
    ppermute x3, starting transfers between devices, per_device(): lax.ppermute(x, 'seq', [(i, (i + hop) % RING) for i in range(RING) if (i...  7.32 us
    ppermute x3, starting transfers between devices, per_device(): lax.ppermute(total[hop].astype(jnp.bfloat16), AXES, ring_perm(False, hop))  6.67 us
  transfers between devices with their start and end apart: 25, of which 13 were waited for; matrix products, arithmetic and copies ran while one was open for 3% of the time, Pallas kernels for 24%

profile of v3, /device:TPU:1, one launch (start us, length us, event | category | flops | bytes accessed | tf_op | source)
XLA Modules:
  0.0 115.8 jit_solution(17202956886797759258)
XLA Ops:
  2.0 9.3 %project_own.1 = (f32[192,1152]{1,0:T(8,128)}, bf16[3,16,2,256,384]{4,3,2,1,0:T(8,128)(2,1)S(1)}) custom-call(bf16[192,8192]{1,0:T(8,128)(2,1)} %own_hbm.1, bf16[3,16,2,256,384]{4,3,2,1,0:T(8,128)(2,1)} %bitcast.62), custom_call_target="tpu_custom_call" | custom-call | flops 4000000000 | bytes 20000000 | tf_op jit(solution)/shard_map/project_own/pallas_call | solution.py:52
  11.4 11.5 %project.1 = (bf16[3,192,384]{2,1,0:T(8,128)(2,1)}, bf16[3,192,384]{2,1,0:T(8,128)(2,1)}, bf16[3,16,256,384]{3,2,1,0:T(8,128)(2,1)}) custom-call(s32[2]{0:T(128)} %pad_add_fusion.2.where_ref, f32[192,1152]{1,0:T(8,128)} %get-tuple-element.20.part_ref, bf16[192,8192]{1,0:T(8,128)(2,1)} %own_hbm.1, bf16[192,8192]{1,0:T(8,128)(2,1)} %collective-permute-done.oth_hbm, ...), custom_call_target="tpu_custom_call" | custom-call | flops 7000000000 | bytes 10000000 | tf_op jit(solution)/shard_map/project/pallas_call | solution.py:114
  24.4 5.9 %collective-permute-done.1 = bf16[3,192,384]{2,1,0:T(8,128)(2,1)S(1)} collective-permute-done((bf16[3,192,384]{2,1,0:T(8,128)(2,1)}, bf16[3,192,384]{2,1,0:T(8,128)(2,1)S(1)}, u32[]{:S(2)}, u32[]{:S(2)}) %collective-permute-start.1) | collective-permute-done | bytes 442400 | tf_op jit(solution)/shard_map/ppermute | solution.py:19
  31.5 2.8 %collective-permute-start.2 = (bf16[192,512]{1,0:T(8,128)(2,1)S(1)}, bf16[192,512]{1,0:T(8,128)(2,1)S(1)}, u32[]{:S(2)}, u32[]{:S(2)}) collective-permute-start(bf16[192,512]{1,0:T(8,128)(2,1)S(1)} %get-tuple-element.50), channel_id=1, source_target_pairs={{0,32},{32,64},{96,0},{1,33},{33,65},{97,1},{2,34},{34,66},{98,2},... | collective-permute-start | bytes 589832 | tf_op jit(solution)/shard_map/ppermute | solution.py:344
  34.3 3.2 %collective-permute-start.3 = (bf16[192,512]{1,0:T(8,128)(2,1)S(1)}, bf16[192,512]{1,0:T(8,128)(2,1)S(1)}, u32[]{:S(2)}, u32[]{:S(2)}) collective-permute-start(bf16[192,512]{1,0:T(8,128)(2,1)S(1)} %get-tuple-element.51), channel_id=1, source_target_pairs={{0,64},{64,0},{96,32},{1,65},{65,1},{97,33},{2,66},{66,2},{98,34},... | collective-permute-start | bytes 589832 | tf_op jit(solution)/shard_map/ppermute | solution.py:344
  39.6 5.4 %collective-permute-done.2.a1 = bf16[192,512]{1,0:T(8,128)(2,1)S(1)} collective-permute-done((bf16[192,512]{1,0:T(8,128)(2,1)S(1)}, bf16[192,512]{1,0:T(8,128)(2,1)S(1)}, u32[]{:S(2)}, u32[]{:S(2)}) %collective-permute-start.2) | collective-permute-done | bytes 196640 | tf_op jit(solution)/shard_map/ppermute | solution.py:344
  47.9 4.7 %attention.1 = (f32[4,192,384]{2,1,0:T(8,128)S(1)}, bf16[4,192,256]{2,1,0:T(8,128)(2,1)S(1)}) custom-call(s32[2]{0:T(128)S(1)} %copy-done.2, bf16[192,512]{1,0:T(8,128)(2,1)S(1)} %get-tuple-element.49.a0, bf16[192,512]{1,0:T(8,128)(2,1)S(1)} %collective-permute-done.2.a1, bf16[192,512]{1,0:T(8,128)(2,1)S(1)} %collective-permute-done.3.a2, ...), custom_call_target="tpu_custom_call" | custom-call | flops 1000000000 | bytes 4000000 | tf_op jit(solution)/shard_map/attention/pallas_call | solution.py:192
  54.5 6.0 %collective-permute-start.12 = (bf16[192,384]{1,0:T(8,128)(2,1)S(1)}, bf16[192,384]{1,0:T(8,128)(2,1)S(1)}, u32[]{:S(2)}, u32[]{:S(2)}) collective-permute-start(bf16[192,384]{1,0:T(8,128)(2,1)S(1)} %pad_maximum_fusion.3), channel_id=1, source_target_pairs={{0,32},{32,64},{64,96},{1,33},{33,65},{65,97},{2,34},{34,66},{66,9... | collective-permute-start | bytes 442376 | tf_op jit(solution)/shard_map/ppermute | solution.py:356
  60.5 2.6 %collective-permute-start.11 = (bf16[192,384]{1,0:T(8,128)(2,1)S(1)}, bf16[192,384]{1,0:T(8,128)(2,1)S(1)}, u32[]{:S(2)}, u32[]{:S(2)}) collective-permute-start(bf16[192,384]{1,0:T(8,128)(2,1)S(1)} %pad_maximum_fusion.2), channel_id=1, source_target_pairs={{0,64},{32,96},{64,0},{1,65},{33,97},{65,1},{2,66},{34,98},{66,2},... | collective-permute-start | bytes 442376 | tf_op jit(solution)/shard_map/ppermute | solution.py:356
  63.1 1.9 %collective-permute-start.10 = (bf16[192,384]{1,0:T(8,128)(2,1)S(1)}, bf16[192,384]{1,0:T(8,128)(2,1)S(1)}, u32[]{:S(2)}, u32[]{:S(2)}) collective-permute-start(bf16[192,384]{1,0:T(8,128)(2,1)S(1)} %pad_maximum_fusion.1), channel_id=1, source_target_pairs={{0,96},{32,0},{64,32},{1,97},{33,1},{65,33},{2,98},{34,2},{66,34},... | collective-permute-start | bytes 442376 | tf_op jit(solution)/shard_map/ppermute | solution.py:356
  66.0 2.7 %collective-permute-done.11.refs_3_ = bf16[192,384]{1,0:T(8,128)(2,1)S(1)} collective-permute-done((bf16[192,384]{1,0:T(8,128)(2,1)S(1)}, bf16[192,384]{1,0:T(8,128)(2,1)S(1)}, u32[]{:S(2)}, u32[]{:S(2)}) %collective-permute-start.11) | collective-permute-done | bytes 147488 | tf_op jit(solution)/shard_map/ppermute | solution.py:356
  68.7 1.5 %collective-permute-start.15 = (bf16[192,384]{1,0:T(8,128)(2,1)S(1)}, bf16[192,384]{1,0:T(8,128)(2,1)S(1)}, u32[]{:S(2)}, u32[]{:S(2)}) collective-permute-start(bf16[192,384]{1,0:T(8,128)(2,1)S(1)} %collective-permute-done.11.refs_3_), channel_id=1, source_target_pairs={{0,16},{16,0},{1,17},{17,1},{2,18},{18,2},{3,19},{19,3},{4,20},{20... | collective-permute-start | bytes 442376 | tf_op jit(solution)/shard_map/ppermute | solution.py:19
  72.3 4.4 %back.4 = (bf16[4,384,256]{2,1,0:T(8,128)(2,1)S(1)}, f32[8,128]{1,0:T(8,128)S(1)}, bf16[384,2304]{1,0:T(8,128)(2,1)S(1)}) custom-call(s32[18]{0:T(128)S(1)} %pad_add_fusion.1.place_ref, s32[2,192,1]{2,1,0:T(8,128)S(1)} %copy.16.refs_0_, bf16[192,384]{1,0:T(8,128)(2,1)S(1)} %pad_maximum_fusion.refs_1_, bf16[192,384]{1,0:T(8,128)(2,1)S(1)} %collective-permute-done.10.refs_2_, ...), custom_call_target="tpu_custom_call" | custom-call | flops 1000000 | bytes 10000 | tf_op jit(solution)/shard_map/back/pallas_call | solution.py:284
  76.8 2.6 %collective-permute-start.18 = (bf16[4,384,256]{2,1,0:T(8,128)(2,1)S(1)}, bf16[4,384,256]{2,1,0:T(8,128)(2,1)S(1)}, u32[]{:S(2)}, u32[]{:S(2)}) collective-permute-start(bf16[4,384,256]{2,1,0:T(8,128)(2,1)S(1)} %get-tuple-element.32), channel_id=1, source_target_pairs={{0,2},{1,3},{2,0},{3,1},{4,6},{5,7},{6,4},{7,5},{8,10},{9,11},{10,... | collective-permute-start | bytes 2359304 | tf_op jit(solution)/shard_map/ppermute | solution.py:377
  79.4 4.4 %back.5 = (bf16[4,384,256]{2,1,0:T(8,128)(2,1)S(1)}, f32[8,128]{1,0:T(8,128)S(1)}) custom-call(s32[18]{0:T(128)S(1)} %pad_add_fusion.1.place_ref, f32[8,128]{1,0:T(8,128)S(1)} %get-tuple-element.27.refs_0_, bf16[384,2304]{1,0:T(8,128)(2,1)S(1)} %get-tuple-element.28.refs_1_, bf16[3,16,2,256,384]{4,3,2,1,0:T(8,128)(2,1)} %bitcast.64, ...), custom_call_target="tpu_custom_call" | custom-call | flops 1000000 | bytes 10000 | tf_op jit(solution)/shard_map/back/pallas_call | solution.py:284
  84.3 4.4 %back.6 = (bf16[4,384,256]{2,1,0:T(8,128)(2,1)S(1)}, f32[8,128]{1,0:T(8,128)S(1)}) custom-call(s32[18]{0:T(128)S(1)} %pad_add_fusion.1.place_ref, f32[8,128]{1,0:T(8,128)S(1)} %get-tuple-element.29.refs_0_, bf16[384,2304]{1,0:T(8,128)(2,1)S(1)} %get-tuple-element.28.refs_1_, bf16[3,16,2,256,384]{4,3,2,1,0:T(8,128)(2,1)} %bitcast.65, ...), custom_call_target="tpu_custom_call" | custom-call | flops 1000000 | bytes 10000 | tf_op jit(solution)/shard_map/back/pallas_call | solution.py:284
  88.7 2.6 %collective-permute-start.20 = (bf16[4,384,256]{2,1,0:T(8,128)(2,1)S(1)}, bf16[4,384,256]{2,1,0:T(8,128)(2,1)S(1)}, u32[]{:S(2)}, u32[]{:S(2)}) collective-permute-start(bf16[4,384,256]{2,1,0:T(8,128)(2,1)S(1)} %get-tuple-element.34), channel_id=1, source_target_pairs={{0,3},{1,0},{2,1},{3,2},{4,7},{5,4},{6,5},{7,6},{8,11},{9,8},{10,9... | collective-permute-start | bytes 2359304 | tf_op jit(solution)/shard_map/ppermute | solution.py:377
  91.3 4.4 %back.7 = (bf16[4,384,256]{2,1,0:T(8,128)(2,1)S(1)}, f32[8,128]{1,0:T(8,128)}) custom-call(s32[18]{0:T(128)S(1)} %pad_add_fusion.1.place_ref, f32[8,128]{1,0:T(8,128)S(1)} %get-tuple-element.30.refs_0_, bf16[384,2304]{1,0:T(8,128)(2,1)S(1)} %get-tuple-element.28.refs_1_, bf16[3,16,2,256,384]{4,3,2,1,0:T(8,128)(2,1)} %bitcast.66, ...), custom_call_target="tpu_custom_call" | custom-call | flops 1000000 | bytes 10000 | tf_op jit(solution)/shard_map/back/pallas_call | solution.py:284
  96.1 1.8 %collective-permute-done.19 = bf16[4,384,256]{2,1,0:T(8,128)(2,1)S(1)} collective-permute-done((bf16[4,384,256]{2,1,0:T(8,128)(2,1)S(1)}, bf16[4,384,256]{2,1,0:T(8,128)(2,1)S(1)}, u32[]{:S(2)}, u32[]{:S(2)}) %collective-permute-start.19) | collective-permute-done | bytes 786464 | tf_op jit(solution)/shard_map/ppermute | solution.py:377
  98.1 2.1 %collective-permute-done.20 = bf16[4,384,256]{2,1,0:T(8,128)(2,1)S(1)} collective-permute-done((bf16[4,384,256]{2,1,0:T(8,128)(2,1)S(1)}, bf16[4,384,256]{2,1,0:T(8,128)(2,1)S(1)}, u32[]{:S(2)}, u32[]{:S(2)}) %collective-permute-start.20) | collective-permute-done | bytes 786464 | tf_op jit(solution)/shard_map/ppermute | solution.py:377
  100.6 4.0 %collective-permute-start.21 = (bf16[384,256]{1,0:T(8,128)(2,1)S(1)}, bf16[384,256]{1,0:T(8,128)(2,1)S(1)}, u32[]{:S(2)}, u32[]{:S(2)}) collective-permute-start(bf16[384,256]{1,0:T(8,128)(2,1)S(1)} %get-tuple-element.41), channel_id=1, source_target_pairs={{0,8},{1,9},{2,10},{3,11},{4,12},{5,13},{6,14},{7,15},{8,0},{9,1},... | collective-permute-start | bytes 589832 | tf_op jit(solution)/shard_map/ppermute | solution.py:383
  105.4 1.9 %collective-permute-start.23 = (bf16[384,256]{1,0:T(8,128)(2,1)S(1)}, bf16[384,256]{1,0:T(8,128)(2,1)S(1)}, u32[]{:S(2)}, u32[]{:S(2)}) collective-permute-start(bf16[384,256]{1,0:T(8,128)(2,1)S(1)} %get-tuple-element.42), channel_id=1, source_target_pairs={{0,12},{1,13},{2,14},{3,15},{4,0},{5,1},{6,2},{7,3},{8,4},{9,5},{1... | collective-permute-start | bytes 589832 | tf_op jit(solution)/shard_map/ppermute | solution.py:383
  107.6 2.9 %collective-permute-done.22 = bf16[384,256]{1,0:T(8,128)(2,1)S(1)} collective-permute-done((bf16[384,256]{1,0:T(8,128)(2,1)S(1)}, bf16[384,256]{1,0:T(8,128)(2,1)S(1)}, u32[]{:S(2)}, u32[]{:S(2)}) %collective-permute-start.22) | collective-permute-done | bytes 196640 | tf_op jit(solution)/shard_map/ppermute | solution.py:383
  110.7 3.4 %collective-permute-start.24 = (bf16[192,256]{1,0:T(8,128)(2,1)S(1)}, bf16[192,256]{1,0:T(8,128)(2,1)S(1)}, u32[]{:S(2)}, u32[]{:S(2)}) collective-permute-start(bf16[192,256]{1,0:T(8,128)(2,1)S(1)} %get-tuple-element.53), channel_id=1, source_target_pairs={{0,16},{16,0},{1,17},{17,1},{2,18},{18,2},{3,19},{19,3},{4,20},{20... | collective-permute-start | bytes 294920 | tf_op jit(solution)/shard_map/ppermute | solution.py:19
  (64 shorter events, 18.9 us)
Async XLA Ops:
  0.0 11.4 %collective-permute-start = (bf16[192,8192]{1,0:T(8,128)(2,1)}, bf16[192,8192]{1,0:T(8,128)(2,1)}, u32[]{:S(2)}, u32[]{:S(2)}) collective-permute-start(bf16[192,8192]{1,0:T(8,128)(2,1)} %own_hbm.1), channel_id=1, source_target_pairs={{0,16},{16,0},{1,17},{17,1},{2,18},{18,2},{3,19},{19,3},{4,20},{20... | collective-permute-start | bytes 9437192 | tf_op jit(solution)/shard_map/ppermute | solution.py:19
  22.9 49.5 %collective-permute-start.17 = (bf16[3,16,256,384]{3,2,1,0:T(8,128)(2,1)}, bf16[3,16,256,384]{3,2,1,0:T(8,128)(2,1)}, u32[]{:S(2)}, u32[]{:S(2)}) collective-permute-start(bf16[3,16,256,384]{3,2,1,0:T(8,128)(2,1)} %get-tuple-element.26), channel_id=1, source_target_pairs={{0,16},{16,0},{1,17},{17,1},{2,18},{18,2},{3,19},{19,3},{4,20},{20... | collective-permute-start | bytes 28311560 | tf_op jit(solution)/shard_map/ppermute | solution.py:19
  23.0 7.3 %collective-permute-start.1 = (bf16[3,192,384]{2,1,0:T(8,128)(2,1)}, bf16[3,192,384]{2,1,0:T(8,128)(2,1)S(1)}, u32[]{:S(2)}, u32[]{:S(2)}) collective-permute-start(bf16[3,192,384]{2,1,0:T(8,128)(2,1)} %get-tuple-element.23), channel_id=1, source_target_pairs={{0,16},{16,0},{1,17},{17,1},{2,18},{18,2},{3,19},{19,3},{4,20},{20... | collective-permute-start | bytes 1327112 | tf_op jit(solution)/shard_map/ppermute | solution.py:19
  31.5 13.4 %collective-permute-start.2 = (bf16[192,512]{1,0:T(8,128)(2,1)S(1)}, bf16[192,512]{1,0:T(8,128)(2,1)S(1)}, u32[]{:S(2)}, u32[]{:S(2)}) collective-permute-start(bf16[192,512]{1,0:T(8,128)(2,1)S(1)} %get-tuple-element.50), channel_id=1, source_target_pairs={{0,32},{32,64},{96,0},{1,33},{33,65},{97,1},{2,34},{34,66},{98,2},... | collective-permute-start | bytes 589832 | tf_op jit(solution)/shard_map/ppermute | solution.py:344
  34.3 11.8 %collective-permute-start.3 = (bf16[192,512]{1,0:T(8,128)(2,1)S(1)}, bf16[192,512]{1,0:T(8,128)(2,1)S(1)}, u32[]{:S(2)}, u32[]{:S(2)}) collective-permute-start(bf16[192,512]{1,0:T(8,128)(2,1)S(1)} %get-tuple-element.51), channel_id=1, source_target_pairs={{0,64},{64,0},{96,32},{1,65},{65,1},{97,33},{2,66},{66,2},{98,34},... | collective-permute-start | bytes 589832 | tf_op jit(solution)/shard_map/ppermute | solution.py:344
  37.5 8.6 %collective-permute-start.4 = (bf16[192,512]{1,0:T(8,128)(2,1)S(1)}, bf16[192,512]{1,0:T(8,128)(2,1)S(1)}, u32[]{:S(2)}, u32[]{:S(2)}) collective-permute-start(bf16[192,512]{1,0:T(8,128)(2,1)S(1)} %get-tuple-element.48), channel_id=1, source_target_pairs={{32,0},{64,32},{96,64},{33,1},{65,33},{97,65},{34,2},{66,34},{98,6... | collective-permute-start | bytes 589832 | tf_op jit(solution)/shard_map/ppermute | solution.py:344
  38.8 7.9 %collective-permute-start.5 = (bf16[192,512]{1,0:T(8,128)(2,1)S(1)}, bf16[192,512]{1,0:T(8,128)(2,1)S(1)}, u32[]{:S(2)}, u32[]{:S(2)}) collective-permute-start(bf16[192,512]{1,0:T(8,128)(2,1)S(1)} %get-tuple-element.49.a0), channel_id=1, source_target_pairs={{0,16},{16,0},{1,17},{17,1},{2,18},{18,2},{3,19},{19,3},{4,20},{20... | collective-permute-start | bytes 589832 | tf_op jit(solution)/shard_map/ppermute | solution.py:19
  44.9 2.3 %collective-permute-start.6 = (bf16[192,512]{1,0:T(8,128)(2,1)S(1)}, bf16[192,512]{1,0:T(8,128)(2,1)S(1)}, u32[]{:S(2)}, u32[]{:S(2)}) collective-permute-start(bf16[192,512]{1,0:T(8,128)(2,1)S(1)} %collective-permute-done.2.a1), channel_id=1, source_target_pairs={{0,16},{16,0},{1,17},{17,1},{2,18},{18,2},{3,19},{19,3},{4,20},{20... | collective-permute-start | bytes 589832 | tf_op jit(solution)/shard_map/ppermute | solution.py:19
  46.1 1.7 %collective-permute-start.8 = (bf16[192,512]{1,0:T(8,128)(2,1)S(1)}, bf16[192,512]{1,0:T(8,128)(2,1)S(1)}, u32[]{:S(2)}, u32[]{:S(2)}) collective-permute-start(bf16[192,512]{1,0:T(8,128)(2,1)S(1)} %collective-permute-done.4.a3), channel_id=1, source_target_pairs={{0,16},{16,0},{1,17},{17,1},{2,18},{18,2},{3,19},{19,3},{4,20},{20... | collective-permute-start | bytes 589832 | tf_op jit(solution)/shard_map/ppermute | solution.py:19
  52.6 1.8 %collective-permute-start.9 = (bf16[4,192,256]{2,1,0:T(8,128)(2,1)S(1)}, bf16[4,192,256]{2,1,0:T(8,128)(2,1)S(1)}, u32[]{:S(2)}, u32[]{:S(2)}) collective-permute-start(bf16[4,192,256]{2,1,0:T(8,128)(2,1)S(1)} %get-tuple-element.25), channel_id=1, source_target_pairs={{0,16},{16,0},{1,17},{17,1},{2,18},{18,2},{3,19},{19,3},{4,20},{20... | collective-permute-start | bytes 1179656 | tf_op jit(solution)/shard_map/ppermute | solution.py:19
  54.5 11.3 %collective-permute-start.12 = (bf16[192,384]{1,0:T(8,128)(2,1)S(1)}, bf16[192,384]{1,0:T(8,128)(2,1)S(1)}, u32[]{:S(2)}, u32[]{:S(2)}) collective-permute-start(bf16[192,384]{1,0:T(8,128)(2,1)S(1)} %pad_maximum_fusion.3), channel_id=1, source_target_pairs={{0,32},{32,64},{64,96},{1,33},{33,65},{65,97},{2,34},{34,66},{66,9... | collective-permute-start | bytes 442376 | tf_op jit(solution)/shard_map/ppermute | solution.py:356
  60.5 8.1 %collective-permute-start.11 = (bf16[192,384]{1,0:T(8,128)(2,1)S(1)}, bf16[192,384]{1,0:T(8,128)(2,1)S(1)}, u32[]{:S(2)}, u32[]{:S(2)}) collective-permute-start(bf16[192,384]{1,0:T(8,128)(2,1)S(1)} %pad_maximum_fusion.2), channel_id=1, source_target_pairs={{0,64},{32,96},{64,0},{1,65},{33,97},{65,1},{2,66},{34,98},{66,2},... | collective-permute-start | bytes 442376 | tf_op jit(solution)/shard_map/ppermute | solution.py:356
  63.1 7.1 %collective-permute-start.10 = (bf16[192,384]{1,0:T(8,128)(2,1)S(1)}, bf16[192,384]{1,0:T(8,128)(2,1)S(1)}, u32[]{:S(2)}, u32[]{:S(2)}) collective-permute-start(bf16[192,384]{1,0:T(8,128)(2,1)S(1)} %pad_maximum_fusion.1), channel_id=1, source_target_pairs={{0,96},{32,0},{64,32},{1,97},{33,1},{65,33},{2,98},{34,2},{66,34},... | collective-permute-start | bytes 442376 | tf_op jit(solution)/shard_map/ppermute | solution.py:356
  65.1 6.4 %collective-permute-start.13 = (bf16[192,384]{1,0:T(8,128)(2,1)S(1)}, bf16[192,384]{1,0:T(8,128)(2,1)S(1)}, u32[]{:S(2)}, u32[]{:S(2)}) collective-permute-start(bf16[192,384]{1,0:T(8,128)(2,1)S(1)} %pad_maximum_fusion.refs_1_), channel_id=1, source_target_pairs={{0,16},{16,0},{1,17},{17,1},{2,18},{18,2},{3,19},{19,3},{4,20},{20... | collective-permute-start | bytes 442376 | tf_op jit(solution)/shard_map/ppermute | solution.py:19
  65.9 5.7 %collective-permute-start.16 = (bf16[192,384]{1,0:T(8,128)(2,1)S(1)}, bf16[192,384]{1,0:T(8,128)(2,1)S(1)}, u32[]{:S(2)}, u32[]{:S(2)}) collective-permute-start(bf16[192,384]{1,0:T(8,128)(2,1)S(1)} %collective-permute-done.12.refs_4_), channel_id=1, source_target_pairs={{0,16},{16,0},{1,17},{17,1},{2,18},{18,2},{3,19},{19,3},{4,20},{20... | collective-permute-start | bytes 442376 | tf_op jit(solution)/shard_map/ppermute | solution.py:19
  68.7 2.9 %collective-permute-start.15 = (bf16[192,384]{1,0:T(8,128)(2,1)S(1)}, bf16[192,384]{1,0:T(8,128)(2,1)S(1)}, u32[]{:S(2)}, u32[]{:S(2)}) collective-permute-start(bf16[192,384]{1,0:T(8,128)(2,1)S(1)} %collective-permute-done.11.refs_3_), channel_id=1, source_target_pairs={{0,16},{16,0},{1,17},{17,1},{2,18},{18,2},{3,19},{19,3},{4,20},{20... | collective-permute-start | bytes 442376 | tf_op jit(solution)/shard_map/ppermute | solution.py:19
  70.2 2.1 %collective-permute-start.14 = (bf16[192,384]{1,0:T(8,128)(2,1)S(1)}, bf16[192,384]{1,0:T(8,128)(2,1)S(1)}, u32[]{:S(2)}, u32[]{:S(2)}) collective-permute-start(bf16[192,384]{1,0:T(8,128)(2,1)S(1)} %collective-permute-done.10.refs_2_), channel_id=1, source_target_pairs={{0,16},{16,0},{1,17},{17,1},{2,18},{18,2},{3,19},{19,3},{4,20},{20... | collective-permute-start | bytes 442376 | tf_op jit(solution)/shard_map/ppermute | solution.py:19
  76.8 19.1 %collective-permute-start.18 = (bf16[4,384,256]{2,1,0:T(8,128)(2,1)S(1)}, bf16[4,384,256]{2,1,0:T(8,128)(2,1)S(1)}, u32[]{:S(2)}, u32[]{:S(2)}) collective-permute-start(bf16[4,384,256]{2,1,0:T(8,128)(2,1)S(1)} %get-tuple-element.32), channel_id=1, source_target_pairs={{0,2},{1,3},{2,0},{3,1},{4,6},{5,7},{6,4},{7,5},{8,10},{9,11},{10,... | collective-permute-start | bytes 2359304 | tf_op jit(solution)/shard_map/ppermute | solution.py:377
  83.8 14.1 %collective-permute-start.19 = (bf16[4,384,256]{2,1,0:T(8,128)(2,1)S(1)}, bf16[4,384,256]{2,1,0:T(8,128)(2,1)S(1)}, u32[]{:S(2)}, u32[]{:S(2)}) collective-permute-start(bf16[4,384,256]{2,1,0:T(8,128)(2,1)S(1)} %get-tuple-element.33), channel_id=1, source_target_pairs={{0,1},{1,2},{2,3},{3,0},{4,5},{5,6},{6,7},{7,4},{8,9},{9,10},{10,1... | collective-permute-start | bytes 2359304 | tf_op jit(solution)/shard_map/ppermute | solution.py:377
  88.7 11.5 %collective-permute-start.20 = (bf16[4,384,256]{2,1,0:T(8,128)(2,1)S(1)}, bf16[4,384,256]{2,1,0:T(8,128)(2,1)S(1)}, u32[]{:S(2)}, u32[]{:S(2)}) collective-permute-start(bf16[4,384,256]{2,1,0:T(8,128)(2,1)S(1)} %get-tuple-element.34), channel_id=1, source_target_pairs={{0,3},{1,0},{2,1},{3,2},{4,7},{5,4},{6,5},{7,6},{8,11},{9,8},{10,9... | collective-permute-start | bytes 2359304 | tf_op jit(solution)/shard_map/ppermute | solution.py:377
  100.6 7.1 %collective-permute-start.21 = (bf16[384,256]{1,0:T(8,128)(2,1)S(1)}, bf16[384,256]{1,0:T(8,128)(2,1)S(1)}, u32[]{:S(2)}, u32[]{:S(2)}) collective-permute-start(bf16[384,256]{1,0:T(8,128)(2,1)S(1)} %get-tuple-element.41), channel_id=1, source_target_pairs={{0,8},{1,9},{2,10},{3,11},{4,12},{5,13},{6,14},{7,15},{8,0},{9,1},... | collective-permute-start | bytes 589832 | tf_op jit(solution)/shard_map/ppermute | solution.py:383
  104.6 6.0 %collective-permute-start.22 = (bf16[384,256]{1,0:T(8,128)(2,1)S(1)}, bf16[384,256]{1,0:T(8,128)(2,1)S(1)}, u32[]{:S(2)}, u32[]{:S(2)}) collective-permute-start(bf16[384,256]{1,0:T(8,128)(2,1)S(1)} %get-tuple-element.43), channel_id=1, source_target_pairs={{0,4},{1,5},{2,6},{3,7},{4,8},{5,9},{6,10},{7,11},{8,12},{9,13},{1... | collective-permute-start | bytes 589832 | tf_op jit(solution)/shard_map/ppermute | solution.py:383
  105.4 5.2 %collective-permute-start.23 = (bf16[384,256]{1,0:T(8,128)(2,1)S(1)}, bf16[384,256]{1,0:T(8,128)(2,1)S(1)}, u32[]{:S(2)}, u32[]{:S(2)}) collective-permute-start(bf16[384,256]{1,0:T(8,128)(2,1)S(1)} %get-tuple-element.42), channel_id=1, source_target_pairs={{0,12},{1,13},{2,14},{3,15},{4,0},{5,1},{6,2},{7,3},{8,4},{9,5},{1... | collective-permute-start | bytes 589832 | tf_op jit(solution)/shard_map/ppermute | solution.py:383
  110.7 4.3 %collective-permute-start.24 = (bf16[192,256]{1,0:T(8,128)(2,1)S(1)}, bf16[192,256]{1,0:T(8,128)(2,1)S(1)}, u32[]{:S(2)}, u32[]{:S(2)}) collective-permute-start(bf16[192,256]{1,0:T(8,128)(2,1)S(1)} %get-tuple-element.53), channel_id=1, source_target_pairs={{0,16},{16,0},{1,17},{17,1},{2,18},{18,2},{3,19},{19,3},{4,20},{20... | collective-permute-start | bytes 294920 | tf_op jit(solution)/shard_map/ppermute | solution.py:19
  (4 other events, 65.5 us)

commit v4 on v3

--- a/solution.py
+++ b/solution.py
@@ -19,113 +19,139 @@
     return lax.ppermute(x, "mod", [(0, 1), (1, 0)])
 
 
-def own_kernel(early, a_ref, w_hbm, part_ref, w_ref, sem):
-    chunks = w_ref.shape[1] // 2
-    block = 2 * 2 * w_ref.shape[3]
-
-    def fetch(i):
-        return pltpu.make_async_copy(w_hbm.at[:, 2 * i : 2 * i + 2], w_ref.at[:, 2 * i : 2 * i + 2], sem.at[i])
-
-    for i in range(chunks):
-        fetch(i).start()
-    for i in range(chunks):
-        fetch(i).wait()
-        if i < early:
-            part = jnp.dot(
-                a_ref[:, i * block : (i + 1) * block], weight_block(w_ref, i), preferred_element_type=jnp.float32
-            )
-            if i == 0:
-                part_ref[...] = part
-            else:
-                part_ref[...] += part
-
-
 def weight_block(w_ref, i):
     size = 4 * w_ref.shape[3]
     return jnp.concatenate([w_ref[c, 2 * i : 2 * i + 2].reshape(size, NH * HD) for c in range(3)], axis=1)
 
 
+def own_kernel(a_hbm, w_hbm, part_ref, w_ref, a_s, a_sem, w_sem):
+    chunks = w_ref.shape[1] // 2
+    block = 4 * w_ref.shape[3]
+
+    def fetch(i):
+        pair = slice(2 * i, 2 * i + 2)
+        return (
+            pltpu.make_async_copy(a_hbm.at[:, pl.ds(i * block, block)], a_s.at[i], a_sem.at[i]),
+            pltpu.make_async_copy(w_hbm.at[:, pair], w_ref.at[:, pair], w_sem.at[i]),
+        )
+
+    for i in range(chunks):
+        for copy in fetch(i):
+            copy.start()
+    for i in range(chunks):
+        for copy in fetch(i):
+            copy.wait()
+        part = jnp.dot(a_s[i], weight_block(w_ref, i), preferred_element_type=jnp.float32)
+        if i == 0:
+            part_ref[...] = part
+        else:
+            part_ref[...] += part
+
+
 def project_own(a, w5, early):
     rows = a.shape[0]
+    block = 4 * w5.shape[3]
     vmem = pl.BlockSpec(memory_space=pltpu.VMEM)
-    anywhere = pl.BlockSpec(memory_space=pl.ANY)
+    hbm = pl.BlockSpec(memory_space=pltpu.HBM)
     return pl.pallas_call(
-        functools.partial(own_kernel, early),
-        in_specs=[vmem, anywhere],
+        own_kernel,
+        in_specs=[hbm, hbm],
         out_specs=[vmem, vmem],
         out_shape=[
             jax.ShapeDtypeStruct((rows, 9 * HD), jnp.float32),
-            pltpu.VMEM(w5.shape, jnp.bfloat16),
+            pltpu.VMEM((3, 2 * early) + w5.shape[2:], jnp.bfloat16),
         ],
-        scratch_shapes=[pltpu.SemaphoreType.DMA((w5.shape[1] // 2,))],
-        compiler_params=pltpu.CompilerParams(vmem_limit_bytes=44 * MIB),
-        cost_estimate=pl.CostEstimate(flops=4 * 10**9, bytes_accessed=2 * 10**7, transcendentals=0),
+        scratch_shapes=[
+            pltpu.VMEM((early, rows, block), jnp.bfloat16),
+            pltpu.SemaphoreType.DMA((early,)),
+            pltpu.SemaphoreType.DMA((early,)),
+        ],
+        compiler_params=pltpu.CompilerParams(vmem_limit_bytes=20 * MIB),
+        cost_estimate=pl.CostEstimate(flops=4 * 10**9, bytes_accessed=10**7, transcendentals=0),
         name="project_own",
     )(a, w5)
 
 
-def project_kernel(early, where_ref, part_ref, own_hbm, oth_hbm, w_ref, own_out, oth_out, half_hbm, a_s, acc_ref, sem, half_sem):
+def project_kernel(
+    early, where_ref, part_ref, own_hbm, oth_ref, w_ref, w_hbm, own_out, oth_out, half_hbm, a_s, w_s, acc_ref,
+    own_sem, w_sem, half_sem
+):
     rows = part_ref.shape[0]
-    chunks = w_ref.shape[1] // 2
-    block = 2 * 2 * w_ref.shape[3]
-
-    def fetch(i):
-        cut = pl.ds(i * block, block)
-        return pltpu.make_async_copy(oth_hbm.at[:, cut], a_s.at[i, rows : 2 * rows], sem.at[1, i])
+    chunks = half_hbm.shape[1] // 2
+    block = 4 * w_ref.shape[3]
+    side = 1 - where_ref[1]
 
     def fetch_own(i):
-        cut = pl.ds(i * block, block)
-        return pltpu.make_async_copy(own_hbm.at[:, cut], a_s.at[i, 0:rows], sem.at[0, i])
-
-    half = pltpu.make_async_copy(w_ref.at[:, :, 1 - where_ref[1]], half_hbm, half_sem)
-    for i in range(chunks):
-        fetch(i).start()
-        if i >= early:
-            fetch_own(i).start()
-    half.start()
+        return pltpu.make_async_copy(own_hbm.at[:, pl.ds(i * block, block)], a_s.at[i - early], own_sem.at[i])
+
+    def other(i):
+        return oth_ref[:, i * block : (i + 1) * block]
+
+    def fetch_weights(i):
+        src = w_hbm.at[:, 2 * i : 2 * i + 2]
+        return pltpu.make_async_copy(src, w_s.at[:, 2 * (i - early) : 2 * (i - early) + 2], w_sem.at[i])
+
+    def put_half(i):
+        if i < early:
+            src = w_ref.at[:, 2 * i : 2 * i + 2, side]
+        else:
+            src = w_s.at[:, 2 * (i - early) : 2 * (i - early) + 2, side]
+        return pltpu.make_async_copy(src, half_hbm.at[:, 2 * i : 2 * i + 2], half_sem.at[i])
+
+    for i in range(early, chunks):
+        fetch_weights(i).start()
+        fetch_own(i).start()
+    for i in range(early):
+        put_half(i).start()
     acc_ref[0:rows] = part_ref[...]
     for i in range(chunks):
-        fetch(i).wait()
-        w = weight_block(w_ref, i)
         if i < early:
-            part = jnp.dot(a_s[i, rows:], w, preferred_element_type=jnp.float32)
+            part = jnp.dot(other(i), weight_block(w_ref, i), preferred_element_type=jnp.float32)
             if i == 0:
                 acc_ref[rows:] = part
             else:
                 acc_ref[rows:] += part
         else:
             fetch_own(i).wait()
-            acc_ref[...] += jnp.dot(a_s[i], w, preferred_element_type=jnp.float32)
+            fetch_weights(i).wait()
+            put_half(i).start()
+            a = jnp.concatenate([a_s[i - early], other(i)], axis=0)
+            acc_ref[...] += jnp.dot(a, weight_block(w_s, i - early), preferred_element_type=jnp.float32)
     for h in range(NH):
         for c in range(3):
             lo = c * NH * HD + h * HD
             x = acc_ref[:, lo : lo + HD].astype(jnp.bfloat16)
             own_out[h, :, c * HD : (c + 1) * HD] = x[0:rows]
             oth_out[h, :, c * HD : (c + 1) * HD] = x[rows:]
-    half.wait()
-
-
-def project(where, part, own, other, w5, early):
+    for i in range(chunks):
+        put_half(i).wait()
+
+
+def project(where, part, own, other, w_early, w5):
     rows, depth = own.shape
     chunks = w5.shape[1] // 2
+    early = w_early.shape[1] // 2
     shape = jax.ShapeDtypeStruct((NH, rows, 3 * HD), jnp.bfloat16)
     vmem = pl.BlockSpec(memory_space=pltpu.VMEM)
-    anywhere = pl.BlockSpec(memory_space=pl.ANY)
+    hbm = pl.BlockSpec(memory_space=pltpu.HBM)
+    dma = pltpu.SemaphoreType.DMA((chunks,))
     return pl.pallas_call(
         functools.partial(project_kernel, early),
-        in_specs=[pl.BlockSpec(memory_space=pltpu.SMEM), vmem, anywhere, anywhere, vmem],
-        out_specs=[vmem, vmem, anywhere],
-        out_shape=[shape, shape, jax.ShapeDtypeStruct((3,) + w5.shape[1:2] + w5.shape[3:], jnp.bfloat16)],
+        in_specs=[pl.BlockSpec(memory_space=pltpu.SMEM), vmem, hbm, vmem, vmem, hbm],
+        out_specs=[vmem, vmem, hbm],
+        out_shape=[shape, shape, pltpu.HBM((3,) + w5.shape[1:2] + w5.shape[3:], jnp.bfloat16)],
         scratch_shapes=[
-            pltpu.VMEM((chunks, 2 * rows, depth // chunks), jnp.bfloat16),
+            pltpu.VMEM((chunks - early, rows, depth // chunks), jnp.bfloat16),
+            pltpu.VMEM((3, 2 * (chunks - early)) + w5.shape[2:], jnp.bfloat16),
             pltpu.VMEM((2 * rows, 9 * HD), jnp.float32),
-            pltpu.SemaphoreType.DMA((2, chunks)),
-            pltpu.SemaphoreType.DMA,
+            dma,
+            dma,
+            dma,
         ],
-        compiler_params=pltpu.CompilerParams(vmem_limit_bytes=44 * MIB),
+        compiler_params=pltpu.CompilerParams(vmem_limit_bytes=26 * MIB),
         cost_estimate=pl.CostEstimate(flops=7 * 10**9, bytes_accessed=10**7, transcendentals=0),
         name="project",
-    )(where, part, own, other, w5)
+    )(where, part, own, other, w_early, w5)
 
 
 def attention_kernel(
@@ -228,72 +254,95 @@
                         out_ref[block * rows : (block + 1) * rows, pl.ds(lo, HD)] = kept[:, c * HD : (c + 1) * HD]
 
 
-def back_kernel(hop, first, place_ref, *refs):
+def weight_copies(place_ref, own_hbm, other_hbm, to_ref, sem, hop):
+    core = place_ref[RING * RING]
+    copies = []
+    for j in range(RING):
+        dest = place_ref[hop * RING + j]
+        copies.append(pltpu.make_async_copy(own_hbm.at[:, dest, core], to_ref.at[0, :, j], sem.at[0, j]))
+        copies.append(pltpu.make_async_copy(other_hbm.at[:, dest], to_ref.at[1, :, j], sem.at[1, j]))
+    return copies
+
+
+def fetch_kernel(hop, place_ref, after_ref, own_hbm, other_hbm, w_out, sem):
+    for copy in weight_copies(place_ref, own_hbm, other_hbm, w_out, sem, hop):
+        copy.start()
+    for copy in weight_copies(place_ref, own_hbm, other_hbm, w_out, sem, hop):
+        copy.wait()
+
+
+def fetch_weights(place, after, w5, other_half, hop):
+    vmem = pl.BlockSpec(memory_space=pltpu.VMEM)
+    hbm = pl.BlockSpec(memory_space=pltpu.HBM)
+    anywhere = pl.BlockSpec(memory_space=pl.ANY)
+    return pl.pallas_call(
+        functools.partial(fetch_kernel, hop),
+        in_specs=[pl.BlockSpec(memory_space=pltpu.SMEM), vmem, hbm, anywhere],
+        out_specs=vmem,
+        out_shape=pltpu.VMEM((2, 3, RING) + w5.shape[3:], jnp.bfloat16),
+        scratch_shapes=[pltpu.SemaphoreType.DMA((2, RING))],
+        compiler_params=pltpu.CompilerParams(vmem_limit_bytes=20 * MIB),
+        cost_estimate=pl.CostEstimate(flops=10**6, bytes_accessed=5 * 10**6, transcendentals=0),
+        name="fetch_weights",
+    )(place, after, w5, other_half)
+
+
+def back_kernel(first, following, place_ref, *refs):
     if first:
-        mask_ref, *parts, own_hbm, other_hbm, out_ref, token_ref, g_ref, w_s, sem = refs
+        mask_ref, *parts, w_ref, own_hbm, other_hbm, out_ref, g_ref, w_out, sem = refs
+    elif following is None:
+        g_ref, w_ref, own_hbm, other_hbm, out_ref = refs
     else:
-        _, g_ref, own_hbm, other_hbm, out_ref, token_ref, w_s, sem = refs
-    core = place_ref[RING * RING]
+        g_ref, w_ref, own_hbm, other_hbm, out_ref, w_out, sem = refs
     chip = place_ref[RING * RING + 1]
-    cols = w_s.shape[3]
-
-    def fetch(side, j):
-        dest = place_ref[hop * RING + j]
-        src = other_hbm.at[:, dest] if side else own_hbm.at[:, dest, core]
-        return pltpu.make_async_copy(src, w_s.at[side, j], sem.at[side, j])
-
-    for j in range(RING):
-        for side in range(2):
-            fetch(side, j).start()
-    token_ref[...] = jnp.zeros_like(token_ref)
+    cols = w_ref.shape[3]
+    if following is not None:
+        for copy in weight_copies(place_ref, own_hbm, other_hbm, w_out, sem, following):
+            copy.start()
     if first:
         gather(chip, mask_ref, parts[:RING], parts[RING:], g_ref)
-    pair = 2
-    for j in range(0, RING, pair):
-        for side in range(2):
-            for i in range(pair):
-                fetch(side, j + i).wait()
-        w = [w_s[side, j : j + pair, c].reshape(pair * cols, NH * HD) for side in range(2) for c in range(3)]
-        res = lax.dot_general(
-            g_ref[...], jnp.concatenate(w, axis=1), (((1,), (1,)), ((), ())), preferred_element_type=jnp.float32
-        ).astype(jnp.bfloat16)
-        for i in range(pair):
-            out_ref[j + i] = res[:, i * cols : (i + 1) * cols]
-
-
-def back(place, w5, other_half, hop, token=None, grads=None, gather_from=None):
+    w = [w_ref[side, c].reshape(RING * cols, NH * HD) for side in range(2) for c in range(3)]
+    res = lax.dot_general(
+        g_ref[...], jnp.concatenate(w, axis=1), (((1,), (1,)), ((), ())), preferred_element_type=jnp.float32
+    ).astype(jnp.bfloat16)
+    for j in range(RING):
+        out_ref[j] = res[:, j * cols : (j + 1) * cols]
+    if following is not None:
+        for copy in weight_copies(place_ref, own_hbm, other_hbm, w_out, sem, following):
+            copy.wait()
+
+
+def back(place, w_here, w5, other_half, following, grads=None, gather_from=None):
     cols = w5.shape[3]
     vmem = pl.BlockSpec(memory_space=pltpu.VMEM)
+    hbm = pl.BlockSpec(memory_space=pltpu.HBM)
     anywhere = pl.BlockSpec(memory_space=pl.ANY)
     first = grads is None
     if first:
         masks, own, oth = gather_from
         rows = 2 * own[0].shape[0]
         extra = [masks, *own, *oth]
-        extra_specs = [vmem] * 9
     else:
         rows = grads.shape[0]
-        extra = [token, grads]
-        extra_specs = [anywhere, vmem]
-    out_shape = [
-        jax.ShapeDtypeStruct((RING, rows, cols), jnp.bfloat16),
-        jax.ShapeDtypeStruct((8, HD), jnp.float32),
-    ]
+        extra = [grads]
+    out_shape = [jax.ShapeDtypeStruct((RING, rows, cols), jnp.bfloat16)]
+    scratch = []
     if first:
         out_shape.append(pltpu.VMEM((rows, 18 * HD), jnp.bfloat16))
-    return pl.pallas_call(
-        functools.partial(back_kernel, hop, first),
-        in_specs=[pl.BlockSpec(memory_space=pltpu.SMEM)] + extra_specs + [anywhere, anywhere],
+    if following is not None:
+        out_shape.append(pltpu.VMEM(w_here.shape, jnp.bfloat16))
+        scratch.append(pltpu.SemaphoreType.DMA((2, RING)))
+    out = pl.pallas_call(
+        functools.partial(back_kernel, first, following),
+        in_specs=[pl.BlockSpec(memory_space=pltpu.SMEM)] + [vmem] * (len(extra) + 1) + [hbm, anywhere],
         out_specs=[vmem] * len(out_shape),
         out_shape=out_shape,
-        scratch_shapes=[
-            pltpu.VMEM((2, RING, 3, cols, NH * HD), jnp.bfloat16),
-            pltpu.SemaphoreType.DMA((2, RING)),
-        ],
-        compiler_params=pltpu.CompilerParams(vmem_limit_bytes=50 * MIB),
+        scratch_shapes=scratch,
+        compiler_params=pltpu.CompilerParams(vmem_limit_bytes=24 * MIB),
         cost_estimate=pl.CostEstimate(flops=10**6, bytes_accessed=10**4, transcendentals=0),
         name="back",
-    )(place, *extra, w5, other_half)
+    )(place, *extra, w_here, w5, other_half)
+    return [out[0]] + [pltpu.with_memory_space_constraint(x, pltpu.VMEM) for x in out[1:]]
 
 
 def ring_perm(first, hop):
@@ -325,12 +374,14 @@
     other_mod = lax.dynamic_slice_in_dim(modality, (2 * chip + 1 - core) * rows, rows)
     masks = (jnp.stack([own_mod, other_mod]) == core).astype(jnp.int32)[:, :, None]
 
-    act_other = core_swap(activations)
-    early = 5
-    part, w_vmem = project_own(activations, w5, early)
-    w_vmem = pltpu.with_memory_space_constraint(w_vmem, pltpu.VMEM)
-    proj_own, proj_other, half = project(where, part, activations, act_other, w_vmem, early)
+    w5 = pltpu.with_memory_space_constraint(w5, pltpu.HBM)
+    activations = pltpu.with_memory_space_constraint(activations, pltpu.HBM)
+    act_other = pltpu.with_memory_space_constraint(core_swap(activations), pltpu.VMEM)
+    part, w_early = project_own(activations, w5, 4)
+    w_early = pltpu.with_memory_space_constraint(w_early, pltpu.VMEM)
+    proj_own, proj_other, half = project(where, part, activations, act_other, w_early, w5)
     proj_back = core_swap(proj_other)
+    proj_back, half = lax.optimization_barrier((proj_back, half))
     other_half = core_swap(half)
     g_heads = grad_attn.reshape(rows, NH, HD).transpose(1, 0, 2)
     heads = jnp.concatenate([jnp.where((masks[0] > 0)[None], proj_own, proj_back), g_heads], axis=2)
@@ -367,14 +418,15 @@
     place = jnp.concatenate([place, jnp.stack([core, chip])]).astype(jnp.int32)
 
     pieces = {}
-    token = g = None
-    for hop in (2, 1, 3, 0):
-        if g is None:
-            x, token, g = back(place, w5, other_half, hop, gather_from=(masks, grads, other_grads))
-            g = pltpu.with_memory_space_constraint(g, pltpu.VMEM)
-        else:
-            x, token = back(place, w5, other_half, hop, token, g)
-        pieces[hop] = lax.ppermute(x, AXES, ring_perm(True, hop)) if hop else x
+    w_here = fetch_weights(place, grads[0], w5, other_half, 2)
+    w_here = pltpu.with_memory_space_constraint(w_here, pltpu.VMEM)
+    x, g, w_here = back(place, w_here, w5, other_half, 1, gather_from=(masks, grads, other_grads))
+    pieces[2] = lax.ppermute(x, AXES, ring_perm(True, 2))
+    x, w_here = back(place, w_here, w5, other_half, 3, grads=g)
+    pieces[1] = lax.ppermute(x, AXES, ring_perm(True, 1))
+    x, w_here = back(place, w_here, w5, other_half, 0, grads=g)
+    pieces[3] = lax.ppermute(x, AXES, ring_perm(True, 3))
+    (pieces[0],) = back(place, w_here, w5, other_half, None, grads=g)
     total = pieces[0].astype(jnp.float32)
     for hop in (2, 1, 3):
         total = lax.optimization_barrier(total) + pieces[hop].astype(jnp.float32)

time: 116 us -> 107 us (0.922)
  Pallas kernels: 43.3 us -> 37 us
  waiting for transfers between devices: 25.3 us -> 23.1 us
    ppermute x13, waiting for transfers between devices: 9.96 us -> 5.17 us  [core_swap(): return lax.ppermute(x, 'mod', [(0, 1), (1, 0)])]
    pallas_call x5 -> x6, Pallas kernels: 27.1 us -> 22.5 us  [the longest x4 14.5 us: back(): pl.pallas_call(functools.partial(back_kernel, first, following), in_specs...]
    ppermute x3, waiting for transfers between devices: 3.93 us -> 5.83 us  [the longest x1 3.52 us: per_device(): pieces[1] = lax.ppermute(x, AXES, ring_perm(True, 1))]
    pallas_call x1, Pallas kernels: 11.5 us -> 9.82 us  [project(): pl.pallas_call(functools.partial(project_kernel, early), in_specs=[pl.Blo...]
  transfers between devices with their start and end apart: 25 -> 25, of which waited for: 13 -> 14; matrix products, arithmetic and copies ran while one was open for 3% -> 3% of each run, Pallas kernels for 24% -> 22%
where the time goes in v4:
time: 107 us
  starting transfers between devices  41 us (38%)
  Pallas kernels  37 us (35%)
  waiting for transfers between devices  23.1 us (22%)
  other arithmetic  3.34 us (3%)
  local copies, waits for them, and re-layouts  1.88 us (2%)
    pallas_call x4, Pallas kernels, back(): pl.pallas_call(functools.partial(back_kernel, first, following), in_specs...  14.5 us
    ppermute x13, starting transfers between devices, core_swap(): return lax.ppermute(x, 'mod', [(0, 1), (1, 0)])  10.8 us
    ppermute x3, starting transfers between devices, per_device(): x = lax.ppermute(x, 'seq', [(i, (i - hop) % RING) for i in range(NH)])  10.5 us
    pallas_call x1, Pallas kernels, project(): pl.pallas_call(functools.partial(project_kernel, early), in_specs=[pl.Blo...  9.82 us
    ppermute x3, starting transfers between devices, per_device(): lax.ppermute(x, 'seq', [(i, (i + hop) % RING) for i in range(RING) if (i...  7.32 us
    ppermute x3, starting transfers between devices, per_device(): lax.ppermute(total[hop].astype(jnp.bfloat16), AXES, ring_perm(False, hop))  6.34 us
    ppermute x3, waiting for transfers between devices, per_device(): lax.ppermute(x, 'seq', [(i, (i + hop) % RING) for i in range(RING) if (i...  5.83 us
    ppermute x13, waiting for transfers between devices, core_swap(): return lax.ppermute(x, 'mod', [(0, 1), (1, 0)])  5.17 us
  transfers between devices with their start and end apart: 25, of which 14 were waited for; matrix products, arithmetic and copies ran while one was open for 3% of the time, Pallas kernels for 22%

profile of v4, /device:TPU:1, one launch (start us, length us, event | category | flops | bytes accessed | tf_op | source)
XLA Modules:
  0.0 106.6 jit_solution(18289880830690483360)
XLA Ops:
  1.5 5.0 %project_own.1 = (f32[192,1152]{1,0:T(8,128)S(1)}, bf16[3,8,2,256,384]{4,3,2,1,0:T(8,128)(2,1)S(1)}) custom-call(bf16[192,8192]{1,0:T(8,128)(2,1)} %own_hbm.1, bf16[3,16,2,256,384]{4,3,2,1,0:T(8,128)(2,1)} %bitcast.62), custom_call_target="tpu_custom_call" | custom-call | flops 4000000000 | bytes 10000000 | tf_op jit(solution)/shard_map/project_own/pallas_call | solution.py:56
  6.9 9.8 %project.1 = (bf16[3,192,384]{2,1,0:T(8,128)(2,1)S(1)}, bf16[3,192,384]{2,1,0:T(8,128)(2,1)S(1)}, bf16[3,16,256,384]{3,2,1,0:T(8,128)(2,1)}) custom-call(s32[2]{0:T(128)S(1)} %pad_add_fusion.2.where_ref, f32[192,1152]{1,0:T(8,128)S(1)} %get-tuple-element.21.part_ref, bf16[192,8192]{1,0:T(8,128)(2,1)} %own_hbm.1, ...), custom_call_target="tpu_custom_call" | custom-call | flops 7000000000 | bytes 10000000 | tf_op jit(solution)/shard_map/project/pallas_call | solution.py:138
  21.8 3.2 %collective-permute-start.2 = (bf16[192,512]{1,0:T(8,128)(2,1)S(1)}, bf16[192,512]{1,0:T(8,128)(2,1)S(1)}, u32[]{:S(2)}, u32[]{:S(2)}) collective-permute-start(bf16[192,512]{1,0:T(8,128)(2,1)S(1)} %get-tuple-element.52), channel_id=1, source_target_pairs={{0,32},{32,64},{96,0},{1,33},{33,65},{97,1},{2,34},{34,66},{98,2},... | collective-permute-start | bytes 589832 | tf_op jit(solution)/shard_map/ppermute | solution.py:395
  25.1 2.8 %collective-permute-start.3 = (bf16[192,512]{1,0:T(8,128)(2,1)S(1)}, bf16[192,512]{1,0:T(8,128)(2,1)S(1)}, u32[]{:S(2)}, u32[]{:S(2)}) collective-permute-start(bf16[192,512]{1,0:T(8,128)(2,1)S(1)} %get-tuple-element.53), channel_id=1, source_target_pairs={{0,64},{64,0},{96,32},{1,65},{65,1},{97,33},{2,66},{66,2},{98,34},... | collective-permute-start | bytes 589832 | tf_op jit(solution)/shard_map/ppermute | solution.py:395
  29.7 5.8 %collective-permute-done.2.a1 = bf16[192,512]{1,0:T(8,128)(2,1)S(1)} collective-permute-done((bf16[192,512]{1,0:T(8,128)(2,1)S(1)}, bf16[192,512]{1,0:T(8,128)(2,1)S(1)}, u32[]{:S(2)}, u32[]{:S(2)}) %collective-permute-start.2) | collective-permute-done | bytes 196640 | tf_op jit(solution)/shard_map/ppermute | solution.py:395
  38.2 4.7 %attention.1 = (f32[4,192,384]{2,1,0:T(8,128)S(1)}, bf16[4,192,256]{2,1,0:T(8,128)(2,1)S(1)}) custom-call(s32[2]{0:T(128)S(1)} %pad_add_fusion.2.where_ref, bf16[192,512]{1,0:T(8,128)(2,1)S(1)} %get-tuple-element.51.a0, bf16[192,512]{1,0:T(8,128)(2,1)S(1)} %collective-permute-done.2.a1, bf16[192,512]{1,0:T(8,128)(2,1)S(1)} %collective-permute-done.3.a2, ...), custom_call_target="tpu_custom_call" | custom-call | flops 1000000000 | bytes 4000000 | tf_op jit(solution)/shard_map/attention/pallas_call | solution.py:218
  44.9 6.0 %collective-permute-start.12 = (bf16[192,384]{1,0:T(8,128)(2,1)S(1)}, bf16[192,384]{1,0:T(8,128)(2,1)S(1)}, u32[]{:S(2)}, u32[]{:S(2)}) collective-permute-start(bf16[192,384]{1,0:T(8,128)(2,1)S(1)} %pad_maximum_fusion.3), channel_id=1, source_target_pairs={{0,32},{32,64},{64,96},{1,33},{33,65},{65,97},{2,34},{34,66},{66,9... | collective-permute-start | bytes 442376 | tf_op jit(solution)/shard_map/ppermute | solution.py:407
  50.9 2.6 %collective-permute-start.11 = (bf16[192,384]{1,0:T(8,128)(2,1)S(1)}, bf16[192,384]{1,0:T(8,128)(2,1)S(1)}, u32[]{:S(2)}, u32[]{:S(2)}) collective-permute-start(bf16[192,384]{1,0:T(8,128)(2,1)S(1)} %pad_maximum_fusion.2), channel_id=1, source_target_pairs={{0,64},{32,96},{64,0},{1,65},{33,97},{65,1},{2,66},{34,98},{66,2},... | collective-permute-start | bytes 442376 | tf_op jit(solution)/shard_map/ppermute | solution.py:407
  53.5 1.9 %collective-permute-start.10 = (bf16[192,384]{1,0:T(8,128)(2,1)S(1)}, bf16[192,384]{1,0:T(8,128)(2,1)S(1)}, u32[]{:S(2)}, u32[]{:S(2)}) collective-permute-start(bf16[192,384]{1,0:T(8,128)(2,1)S(1)} %pad_maximum_fusion.1), channel_id=1, source_target_pairs={{0,96},{32,0},{64,32},{1,97},{33,1},{65,33},{2,98},{34,2},{66,34},... | collective-permute-start | bytes 442376 | tf_op jit(solution)/shard_map/ppermute | solution.py:407
  56.3 2.7 %collective-permute-done.11.refs_3_ = bf16[192,384]{1,0:T(8,128)(2,1)S(1)} collective-permute-done((bf16[192,384]{1,0:T(8,128)(2,1)S(1)}, bf16[192,384]{1,0:T(8,128)(2,1)S(1)}, u32[]{:S(2)}, u32[]{:S(2)}) %collective-permute-start.11) | collective-permute-done | bytes 147488 | tf_op jit(solution)/shard_map/ppermute | solution.py:407
  59.0 1.5 %collective-permute-start.15 = (bf16[192,384]{1,0:T(8,128)(2,1)S(1)}, bf16[192,384]{1,0:T(8,128)(2,1)S(1)}, u32[]{:S(2)}, u32[]{:S(2)}) collective-permute-start(bf16[192,384]{1,0:T(8,128)(2,1)S(1)} %collective-permute-done.11.refs_3_), channel_id=1, source_target_pairs={{0,16},{16,0},{1,17},{17,1},{2,18},{18,2},{3,19},{19,3},{4,20},{20... | collective-permute-start | bytes 442376 | tf_op jit(solution)/shard_map/ppermute | solution.py:19
  61.9 2.9 %fetch_weights.1.refs_9_ = bf16[2,3,4,256,384]{4,3,2,1,0:T(8,128)(2,1)S(1)} custom-call(s32[18]{0:T(128)S(1)} %pad_add_fusion.1.place_ref, bf16[192,384]{1,0:T(8,128)(2,1)S(1)} %pad_maximum_fusion.after_ref.refs_1_, bf16[3,16,2,256,384]{4,3,2,1,0:T(8,128)(2,1)} %bitcast.64, bf16[3,16,256,384]{3,2,1,0:T(8,128)(2,1)} %collective-permute-done.17.other_hbm.refs_11_.refs_3_), custom_call_target="tpu_custom_call" | custom-call | flops 1000000 | bytes 5000000 | tf_op jit(solution)/shard_map/fetch_weights/pallas_call | solution.py:278
  64.9 3.3 %back.4 = (bf16[4,384,256]{2,1,0:T(8,128)(2,1)S(1)}, bf16[384,2304]{1,0:T(8,128)(2,1)S(1)}, bf16[2,3,4,256,384]{4,3,2,1,0:T(8,128)(2,1)S(1)}) custom-call(s32[18]{0:T(128)S(1)} %pad_add_fusion.1.place_ref, s32[2,192,1]{2,1,0:T(8,128)S(1)} %copy.16.refs_0_, bf16[192,384]{1,0:T(8,128)(2,1)S(1)} %pad_maximum_fusion.after_ref.refs_1_, ...), custom_call_target="tpu_custom_call" | custom-call | flops 1000000 | bytes 10000 | tf_op jit(solution)/shard_map/back/pallas_call | solution.py:335
  68.2 3.0 %collective-permute-start.18 = (bf16[4,384,256]{2,1,0:T(8,128)(2,1)S(1)}, bf16[4,384,256]{2,1,0:T(8,128)(2,1)S(1)}, u32[]{:S(2)}, u32[]{:S(2)}) collective-permute-start(bf16[4,384,256]{2,1,0:T(8,128)(2,1)S(1)} %get-tuple-element.34), channel_id=1, source_target_pairs={{0,2},{1,3},{2,0},{3,1},{4,6},{5,7},{6,4},{7,5},{8,10},{9,11},{10,... | collective-permute-start | bytes 2359304 | tf_op jit(solution)/shard_map/ppermute | solution.py:424
  71.2 4.3 %back.5 = (bf16[4,384,256]{2,1,0:T(8,128)(2,1)S(1)}, bf16[2,3,4,256,384]{4,3,2,1,0:T(8,128)(2,1)S(1)}) custom-call(s32[18]{0:T(128)S(1)} %pad_add_fusion.1.place_ref, bf16[384,2304]{1,0:T(8,128)(2,1)S(1)} %get-tuple-element.30.refs_0_, bf16[2,3,4,256,384]{4,3,2,1,0:T(8,128)(2,1)S(1)} %get-tuple-element.31.refs_1_, bf16[3,16,2,256,384]{4,3,2,1,0:T(8,128)(2,1)} %bitcast.66, ...), custom_call_target="tpu_custom_call" | custom-call | flops 1000000 | bytes 10000 | tf_op jit(solution)/shard_map/back/pallas_call | solution.py:335
  76.0 4.3 %back.6 = (bf16[4,384,256]{2,1,0:T(8,128)(2,1)S(1)}, bf16[2,3,4,256,384]{4,3,2,1,0:T(8,128)(2,1)S(1)}) custom-call(s32[18]{0:T(128)S(1)} %pad_add_fusion.1.place_ref, bf16[384,2304]{1,0:T(8,128)(2,1)S(1)} %get-tuple-element.30.refs_0_, bf16[2,3,4,256,384]{4,3,2,1,0:T(8,128)(2,1)S(1)} %get-tuple-element.32.refs_1_, bf16[3,16,2,256,384]{4,3,2,1,0:T(8,128)(2,1)} %bitcast.67, ...), custom_call_target="tpu_custom_call" | custom-call | flops 1000000 | bytes 10000 | tf_op jit(solution)/shard_map/back/pallas_call | solution.py:335
  80.3 2.6 %collective-permute-start.20 = (bf16[4,384,256]{2,1,0:T(8,128)(2,1)S(1)}, bf16[4,384,256]{2,1,0:T(8,128)(2,1)S(1)}, u32[]{:S(2)}, u32[]{:S(2)}) collective-permute-start(bf16[4,384,256]{2,1,0:T(8,128)(2,1)S(1)} %get-tuple-element.36), channel_id=1, source_target_pairs={{0,3},{1,0},{2,1},{3,2},{4,7},{5,4},{6,5},{7,6},{8,11},{9,8},{10,9... | collective-permute-start | bytes 2359304 | tf_op jit(solution)/shard_map/ppermute | solution.py:428
  82.9 2.6 %back.7 = bf16[4,384,256]{2,1,0:T(8,128)(2,1)S(1)} custom-call(s32[18]{0:T(128)S(1)} %pad_add_fusion.1.place_ref, bf16[384,2304]{1,0:T(8,128)(2,1)S(1)} %get-tuple-element.30.refs_0_, bf16[2,3,4,256,384]{4,3,2,1,0:T(8,128)(2,1)S(1)} %get-tuple-element.33.refs_1_, bf16[3,16,2,256,384]{4,3,2,1,0:T(8,128)(2,1)} %bitcast.68, ...), custom_call_target="tpu_custom_call" | custom-call | flops 1000000 | bytes 10000 | tf_op jit(solution)/shard_map/back/pallas_call | solution.py:335
  85.8 3.5 %collective-permute-done.19 = bf16[4,384,256]{2,1,0:T(8,128)(2,1)S(1)} collective-permute-done((bf16[4,384,256]{2,1,0:T(8,128)(2,1)S(1)}, bf16[4,384,256]{2,1,0:T(8,128)(2,1)S(1)}, u32[]{:S(2)}, u32[]{:S(2)}) %collective-permute-start.19) | collective-permute-done | bytes 786464 | tf_op jit(solution)/shard_map/ppermute | solution.py:426
  89.6 2.3 %collective-permute-done.20 = bf16[4,384,256]{2,1,0:T(8,128)(2,1)S(1)} collective-permute-done((bf16[4,384,256]{2,1,0:T(8,128)(2,1)S(1)}, bf16[4,384,256]{2,1,0:T(8,128)(2,1)S(1)}, u32[]{:S(2)}, u32[]{:S(2)}) %collective-permute-start.20) | collective-permute-done | bytes 786464 | tf_op jit(solution)/shard_map/ppermute | solution.py:428
  92.2 3.7 %collective-permute-start.21 = (bf16[384,256]{1,0:T(8,128)(2,1)S(1)}, bf16[384,256]{1,0:T(8,128)(2,1)S(1)}, u32[]{:S(2)}, u32[]{:S(2)}) collective-permute-start(bf16[384,256]{1,0:T(8,128)(2,1)S(1)} %get-tuple-element.43), channel_id=1, source_target_pairs={{0,8},{1,9},{2,10},{3,11},{4,12},{5,13},{6,14},{7,15},{8,0},{9,1},... | collective-permute-start | bytes 589832 | tf_op jit(solution)/shard_map/ppermute | solution.py:435
  96.6 1.9 %collective-permute-start.23 = (bf16[384,256]{1,0:T(8,128)(2,1)S(1)}, bf16[384,256]{1,0:T(8,128)(2,1)S(1)}, u32[]{:S(2)}, u32[]{:S(2)}) collective-permute-start(bf16[384,256]{1,0:T(8,128)(2,1)S(1)} %get-tuple-element.44), channel_id=1, source_target_pairs={{0,12},{1,13},{2,14},{3,15},{4,0},{5,1},{6,2},{7,3},{8,4},{9,5},{1... | collective-permute-start | bytes 589832 | tf_op jit(solution)/shard_map/ppermute | solution.py:435
  98.9 2.7 %collective-permute-done.22 = bf16[384,256]{1,0:T(8,128)(2,1)S(1)} collective-permute-done((bf16[384,256]{1,0:T(8,128)(2,1)S(1)}, bf16[384,256]{1,0:T(8,128)(2,1)S(1)}, u32[]{:S(2)}, u32[]{:S(2)}) %collective-permute-start.22) | collective-permute-done | bytes 196640 | tf_op jit(solution)/shard_map/ppermute | solution.py:435
  102.2 2.7 %collective-permute-start.24 = (bf16[192,256]{1,0:T(8,128)(2,1)S(1)}, bf16[192,256]{1,0:T(8,128)(2,1)S(1)}, u32[]{:S(2)}, u32[]{:S(2)}) collective-permute-start(bf16[192,256]{1,0:T(8,128)(2,1)S(1)} %get-tuple-element.55), channel_id=1, source_target_pairs={{0,16},{16,0},{1,17},{17,1},{2,18},{18,2},{3,19},{19,3},{4,20},{20... | collective-permute-start | bytes 294920 | tf_op jit(solution)/shard_map/ppermute | solution.py:19
  (65 shorter events, 20.3 us)
Async XLA Ops:
  0.0 6.9 %collective-permute-start = (bf16[192,8192]{1,0:T(8,128)(2,1)}, bf16[192,8192]{1,0:T(8,128)(2,1)S(1)}, u32[]{:S(2)}, u32[]{:S(2)}) collective-permute-start(bf16[192,8192]{1,0:T(8,128)(2,1)} %own_hbm.1), channel_id=1, source_target_pairs={{0,16},{16,0},{1,17},{17,1},{2,18},{18,2},{3,19},{19,3},{4,20},{20... | collective-permute-start | bytes 9437192 | tf_op jit(solution)/shard_map/ppermute | solution.py:19
  17.5 1.8 %collective-permute-start.1 = (bf16[3,192,384]{2,1,0:T(8,128)(2,1)S(1)}, bf16[3,192,384]{2,1,0:T(8,128)(2,1)S(1)}, u32[]{:S(2)}, u32[]{:S(2)}) collective-permute-start(bf16[3,192,384]{2,1,0:T(8,128)(2,1)S(1)} %get-tuple-element.24), channel_id=1, source_target_pairs={{0,16},{16,0},{1,17},{17,1},{2,18},{18,2},{3,19},{19,3},{4,20},{20... | collective-permute-start | bytes 1327112 | tf_op jit(solution)/shard_map/ppermute | solution.py:19
  19.3 42.6 %collective-permute-start.17 = (bf16[3,16,256,384]{3,2,1,0:T(8,128)(2,1)}, bf16[3,16,256,384]{3,2,1,0:T(8,128)(2,1)}, u32[]{:S(2)}, u32[]{:S(2)}) collective-permute-start(bf16[3,16,256,384]{3,2,1,0:T(8,128)(2,1)} %get-tuple-element.29), channel_id=1, source_target_pairs={{0,16},{16,0},{1,17},{17,1},{2,18},{18,2},{3,19},{19,3},{4,20},{20... | collective-permute-start | bytes 28311560 | tf_op jit(solution)/shard_map/ppermute | solution.py:19
  21.8 13.7 %collective-permute-start.2 = (bf16[192,512]{1,0:T(8,128)(2,1)S(1)}, bf16[192,512]{1,0:T(8,128)(2,1)S(1)}, u32[]{:S(2)}, u32[]{:S(2)}) collective-permute-start(bf16[192,512]{1,0:T(8,128)(2,1)S(1)} %get-tuple-element.52), channel_id=1, source_target_pairs={{0,32},{32,64},{96,0},{1,33},{33,65},{97,1},{2,34},{34,66},{98,2},... | collective-permute-start | bytes 589832 | tf_op jit(solution)/shard_map/ppermute | solution.py:395
  25.1 11.4 %collective-permute-start.3 = (bf16[192,512]{1,0:T(8,128)(2,1)S(1)}, bf16[192,512]{1,0:T(8,128)(2,1)S(1)}, u32[]{:S(2)}, u32[]{:S(2)}) collective-permute-start(bf16[192,512]{1,0:T(8,128)(2,1)S(1)} %get-tuple-element.53), channel_id=1, source_target_pairs={{0,64},{64,0},{96,32},{1,65},{65,1},{97,33},{2,66},{66,2},{98,34},... | collective-permute-start | bytes 589832 | tf_op jit(solution)/shard_map/ppermute | solution.py:395
  27.9 8.6 %collective-permute-start.4 = (bf16[192,512]{1,0:T(8,128)(2,1)S(1)}, bf16[192,512]{1,0:T(8,128)(2,1)S(1)}, u32[]{:S(2)}, u32[]{:S(2)}) collective-permute-start(bf16[192,512]{1,0:T(8,128)(2,1)S(1)} %get-tuple-element.50), channel_id=1, source_target_pairs={{32,0},{64,32},{96,64},{33,1},{65,33},{97,65},{34,2},{66,34},{98,6... | collective-permute-start | bytes 589832 | tf_op jit(solution)/shard_map/ppermute | solution.py:395
  29.2 7.9 %collective-permute-start.5 = (bf16[192,512]{1,0:T(8,128)(2,1)S(1)}, bf16[192,512]{1,0:T(8,128)(2,1)S(1)}, u32[]{:S(2)}, u32[]{:S(2)}) collective-permute-start(bf16[192,512]{1,0:T(8,128)(2,1)S(1)} %get-tuple-element.51.a0), channel_id=1, source_target_pairs={{0,16},{16,0},{1,17},{17,1},{2,18},{18,2},{3,19},{19,3},{4,20},{20... | collective-permute-start | bytes 589832 | tf_op jit(solution)/shard_map/ppermute | solution.py:19
  35.5 2.0 %collective-permute-start.6 = (bf16[192,512]{1,0:T(8,128)(2,1)S(1)}, bf16[192,512]{1,0:T(8,128)(2,1)S(1)}, u32[]{:S(2)}, u32[]{:S(2)}) collective-permute-start(bf16[192,512]{1,0:T(8,128)(2,1)S(1)} %collective-permute-done.2.a1), channel_id=1, source_target_pairs={{0,16},{16,0},{1,17},{17,1},{2,18},{18,2},{3,19},{19,3},{4,20},{20... | collective-permute-start | bytes 589832 | tf_op jit(solution)/shard_map/ppermute | solution.py:19
  36.5 1.7 %collective-permute-start.8 = (bf16[192,512]{1,0:T(8,128)(2,1)S(1)}, bf16[192,512]{1,0:T(8,128)(2,1)S(1)}, u32[]{:S(2)}, u32[]{:S(2)}) collective-permute-start(bf16[192,512]{1,0:T(8,128)(2,1)S(1)} %collective-permute-done.4.a3), channel_id=1, source_target_pairs={{0,16},{16,0},{1,17},{17,1},{2,18},{18,2},{3,19},{19,3},{4,20},{20... | collective-permute-start | bytes 589832 | tf_op jit(solution)/shard_map/ppermute | solution.py:19
  42.9 1.8 %collective-permute-start.9 = (bf16[4,192,256]{2,1,0:T(8,128)(2,1)S(1)}, bf16[4,192,256]{2,1,0:T(8,128)(2,1)S(1)}, u32[]{:S(2)}, u32[]{:S(2)}) collective-permute-start(bf16[4,192,256]{2,1,0:T(8,128)(2,1)S(1)} %get-tuple-element.28), channel_id=1, source_target_pairs={{0,16},{16,0},{1,17},{17,1},{2,18},{18,2},{3,19},{19,3},{4,20},{20... | collective-permute-start | bytes 1179656 | tf_op jit(solution)/shard_map/ppermute | solution.py:19
  44.9 11.3 %collective-permute-start.12 = (bf16[192,384]{1,0:T(8,128)(2,1)S(1)}, bf16[192,384]{1,0:T(8,128)(2,1)S(1)}, u32[]{:S(2)}, u32[]{:S(2)}) collective-permute-start(bf16[192,384]{1,0:T(8,128)(2,1)S(1)} %pad_maximum_fusion.3), channel_id=1, source_target_pairs={{0,32},{32,64},{64,96},{1,33},{33,65},{65,97},{2,34},{34,66},{66,9... | collective-permute-start | bytes 442376 | tf_op jit(solution)/shard_map/ppermute | solution.py:407
  50.9 8.1 %collective-permute-start.11 = (bf16[192,384]{1,0:T(8,128)(2,1)S(1)}, bf16[192,384]{1,0:T(8,128)(2,1)S(1)}, u32[]{:S(2)}, u32[]{:S(2)}) collective-permute-start(bf16[192,384]{1,0:T(8,128)(2,1)S(1)} %pad_maximum_fusion.2), channel_id=1, source_target_pairs={{0,64},{32,96},{64,0},{1,65},{33,97},{65,1},{2,66},{34,98},{66,2},... | collective-permute-start | bytes 442376 | tf_op jit(solution)/shard_map/ppermute | solution.py:407
  53.5 7.1 %collective-permute-start.10 = (bf16[192,384]{1,0:T(8,128)(2,1)S(1)}, bf16[192,384]{1,0:T(8,128)(2,1)S(1)}, u32[]{:S(2)}, u32[]{:S(2)}) collective-permute-start(bf16[192,384]{1,0:T(8,128)(2,1)S(1)} %pad_maximum_fusion.1), channel_id=1, source_target_pairs={{0,96},{32,0},{64,32},{1,97},{33,1},{65,33},{2,98},{34,2},{66,34},... | collective-permute-start | bytes 442376 | tf_op jit(solution)/shard_map/ppermute | solution.py:407
  55.5 9.3 %collective-permute-start.13 = (bf16[192,384]{1,0:T(8,128)(2,1)S(1)}, bf16[192,384]{1,0:T(8,128)(2,1)S(1)}, u32[]{:S(2)}, u32[]{:S(2)}) collective-permute-start(bf16[192,384]{1,0:T(8,128)(2,1)S(1)} %pad_maximum_fusion.after_ref.refs_1_), channel_id=1, source_target_pairs={{0,16},{16,0},{1,17},{17,1},{2,18},{18,2},{3,19},{19,3},{4,20},{20... | collective-permute-start | bytes 442376 | tf_op jit(solution)/shard_map/ppermute | solution.py:19
  56.2 8.6 %collective-permute-start.16 = (bf16[192,384]{1,0:T(8,128)(2,1)S(1)}, bf16[192,384]{1,0:T(8,128)(2,1)S(1)}, u32[]{:S(2)}, u32[]{:S(2)}) collective-permute-start(bf16[192,384]{1,0:T(8,128)(2,1)S(1)} %collective-permute-done.12.refs_4_), channel_id=1, source_target_pairs={{0,16},{16,0},{1,17},{17,1},{2,18},{18,2},{3,19},{19,3},{4,20},{20... | collective-permute-start | bytes 442376 | tf_op jit(solution)/shard_map/ppermute | solution.py:19
  59.0 5.8 %collective-permute-start.15 = (bf16[192,384]{1,0:T(8,128)(2,1)S(1)}, bf16[192,384]{1,0:T(8,128)(2,1)S(1)}, u32[]{:S(2)}, u32[]{:S(2)}) collective-permute-start(bf16[192,384]{1,0:T(8,128)(2,1)S(1)} %collective-permute-done.11.refs_3_), channel_id=1, source_target_pairs={{0,16},{16,0},{1,17},{17,1},{2,18},{18,2},{3,19},{19,3},{4,20},{20... | collective-permute-start | bytes 442376 | tf_op jit(solution)/shard_map/ppermute | solution.py:19
  60.6 4.3 %collective-permute-start.14 = (bf16[192,384]{1,0:T(8,128)(2,1)S(1)}, bf16[192,384]{1,0:T(8,128)(2,1)S(1)}, u32[]{:S(2)}, u32[]{:S(2)}) collective-permute-start(bf16[192,384]{1,0:T(8,128)(2,1)S(1)} %collective-permute-done.10.refs_2_), channel_id=1, source_target_pairs={{0,16},{16,0},{1,17},{17,1},{2,18},{18,2},{3,19},{19,3},{4,20},{20... | collective-permute-start | bytes 442376 | tf_op jit(solution)/shard_map/ppermute | solution.py:19
  68.2 17.4 %collective-permute-start.18 = (bf16[4,384,256]{2,1,0:T(8,128)(2,1)S(1)}, bf16[4,384,256]{2,1,0:T(8,128)(2,1)S(1)}, u32[]{:S(2)}, u32[]{:S(2)}) collective-permute-start(bf16[4,384,256]{2,1,0:T(8,128)(2,1)S(1)} %get-tuple-element.34), channel_id=1, source_target_pairs={{0,2},{1,3},{2,0},{3,1},{4,6},{5,7},{6,4},{7,5},{8,10},{9,11},{10,... | collective-permute-start | bytes 2359304 | tf_op jit(solution)/shard_map/ppermute | solution.py:424
  75.5 13.8 %collective-permute-start.19 = (bf16[4,384,256]{2,1,0:T(8,128)(2,1)S(1)}, bf16[4,384,256]{2,1,0:T(8,128)(2,1)S(1)}, u32[]{:S(2)}, u32[]{:S(2)}) collective-permute-start(bf16[4,384,256]{2,1,0:T(8,128)(2,1)S(1)} %get-tuple-element.35), channel_id=1, source_target_pairs={{0,1},{1,2},{2,3},{3,0},{4,5},{5,6},{6,7},{7,4},{8,9},{9,10},{10,1... | collective-permute-start | bytes 2359304 | tf_op jit(solution)/shard_map/ppermute | solution.py:426
  80.3 11.5 %collective-permute-start.20 = (bf16[4,384,256]{2,1,0:T(8,128)(2,1)S(1)}, bf16[4,384,256]{2,1,0:T(8,128)(2,1)S(1)}, u32[]{:S(2)}, u32[]{:S(2)}) collective-permute-start(bf16[4,384,256]{2,1,0:T(8,128)(2,1)S(1)} %get-tuple-element.36), channel_id=1, source_target_pairs={{0,3},{1,0},{2,1},{3,2},{4,7},{5,4},{6,5},{7,6},{8,11},{9,8},{10,9... | collective-permute-start | bytes 2359304 | tf_op jit(solution)/shard_map/ppermute | solution.py:428
  92.2 6.7 %collective-permute-start.21 = (bf16[384,256]{1,0:T(8,128)(2,1)S(1)}, bf16[384,256]{1,0:T(8,128)(2,1)S(1)}, u32[]{:S(2)}, u32[]{:S(2)}) collective-permute-start(bf16[384,256]{1,0:T(8,128)(2,1)S(1)} %get-tuple-element.43), channel_id=1, source_target_pairs={{0,8},{1,9},{2,10},{3,11},{4,12},{5,13},{6,14},{7,15},{8,0},{9,1},... | collective-permute-start | bytes 589832 | tf_op jit(solution)/shard_map/ppermute | solution.py:435
  95.9 5.7 %collective-permute-start.22 = (bf16[384,256]{1,0:T(8,128)(2,1)S(1)}, bf16[384,256]{1,0:T(8,128)(2,1)S(1)}, u32[]{:S(2)}, u32[]{:S(2)}) collective-permute-start(bf16[384,256]{1,0:T(8,128)(2,1)S(1)} %get-tuple-element.45), channel_id=1, source_target_pairs={{0,4},{1,5},{2,6},{3,7},{4,8},{5,9},{6,10},{7,11},{8,12},{9,13},{1... | collective-permute-start | bytes 589832 | tf_op jit(solution)/shard_map/ppermute | solution.py:435
  96.6 5.5 %collective-permute-start.23 = (bf16[384,256]{1,0:T(8,128)(2,1)S(1)}, bf16[384,256]{1,0:T(8,128)(2,1)S(1)}, u32[]{:S(2)}, u32[]{:S(2)}) collective-permute-start(bf16[384,256]{1,0:T(8,128)(2,1)S(1)} %get-tuple-element.44), channel_id=1, source_target_pairs={{0,12},{1,13},{2,14},{3,15},{4,0},{5,1},{6,2},{7,3},{8,4},{9,5},{1... | collective-permute-start | bytes 589832 | tf_op jit(solution)/shard_map/ppermute | solution.py:435
  102.2 3.7 %collective-permute-start.24 = (bf16[192,256]{1,0:T(8,128)(2,1)S(1)}, bf16[192,256]{1,0:T(8,128)(2,1)S(1)}, u32[]{:S(2)}, u32[]{:S(2)}) collective-permute-start(bf16[192,256]{1,0:T(8,128)(2,1)S(1)} %get-tuple-element.55), channel_id=1, source_target_pairs={{0,16},{16,0},{1,17},{17,1},{2,18},{18,2},{3,19},{19,3},{4,20},{20... | collective-permute-start | bytes 294920 | tf_op jit(solution)/shard_map/ppermute | solution.py:19
  (4 other events, 37.3 us)

commit v5 on v4

--- a/solution.py
+++ b/solution.py
@@ -155,10 +155,12 @@
 
 
 def attention_kernel(
-    where_ref, a0, a1, a2, a3, b0, b1, b2, b3, own_ref, oth_ref, q_s, g_s, k_s, v_s, dk_s, dv_s
+    where_ref, a0, a1, a2, a3, b0, b1, b2, b3, w_hbm, own_ref, oth_ref, w_ref, q_s, g_s, k_s, v_s, dk_s, dv_s, w_sem
 ):
     chip = where_ref[0]
     core = where_ref[1]
+    fetch = pltpu.make_async_copy(w_hbm.at[:, :, core], w_ref, w_sem)
+    fetch.start()
     rows = a0.shape[0]
     both = 2 * rows
     own = (a0, a1, a2, a3)
@@ -209,19 +211,21 @@
         own_ref[k, :, 2 * HD : 3 * HD] = dv_s[mine, :]
         oth_ref[k, :, 0:HD] = dk_s[other, :].astype(jnp.bfloat16)
         oth_ref[k, :, HD : 2 * HD] = dv_s[other, :].astype(jnp.bfloat16)
-
-
-def attention(where, parts, others):
+    fetch.wait()
+
+
+def attention(where, parts, others, w5):
     rows = parts[0].shape[0]
     total = 2 * RING * rows
     vmem = pl.BlockSpec(memory_space=pltpu.VMEM)
     return pl.pallas_call(
         attention_kernel,
-        in_specs=[pl.BlockSpec(memory_space=pltpu.SMEM)] + [vmem] * 8,
-        out_specs=[vmem, vmem],
+        in_specs=[pl.BlockSpec(memory_space=pltpu.SMEM)] + [vmem] * 8 + [pl.BlockSpec(memory_space=pltpu.HBM)],
+        out_specs=[vmem, vmem, vmem],
         out_shape=[
             jax.ShapeDtypeStruct((RING, rows, 3 * HD), jnp.float32),
             jax.ShapeDtypeStruct((RING, rows, 2 * HD), jnp.bfloat16),
+            pltpu.VMEM(w5.shape[:2] + w5.shape[3:], jnp.bfloat16),
         ],
         scratch_shapes=[
             pltpu.VMEM((RING, rows, HD), jnp.bfloat16),
@@ -230,11 +234,12 @@
             pltpu.VMEM((total, HD), jnp.bfloat16),
             pltpu.VMEM((total, HD), jnp.float32),
             pltpu.VMEM((total, HD), jnp.float32),
+            pltpu.SemaphoreType.DMA,
         ],
-        compiler_params=pltpu.CompilerParams(vmem_limit_bytes=32 * MIB),
+        compiler_params=pltpu.CompilerParams(vmem_limit_bytes=24 * MIB),
         cost_estimate=pl.CostEstimate(flops=10**9, bytes_accessed=4 * 10**6, transcendentals=10**6),
         name="attention",
-    )(where, *parts, *others)
+    )(where, *parts, *others, w5)
 
 
 def gather(chip, mask_ref, own, oth, out_ref):
@@ -254,69 +259,27 @@
                         out_ref[block * rows : (block + 1) * rows, pl.ds(lo, HD)] = kept[:, c * HD : (c + 1) * HD]
 
 
-def weight_copies(place_ref, own_hbm, other_hbm, to_ref, sem, hop):
-    core = place_ref[RING * RING]
-    copies = []
-    for j in range(RING):
-        dest = place_ref[hop * RING + j]
-        copies.append(pltpu.make_async_copy(own_hbm.at[:, dest, core], to_ref.at[0, :, j], sem.at[0, j]))
-        copies.append(pltpu.make_async_copy(other_hbm.at[:, dest], to_ref.at[1, :, j], sem.at[1, j]))
-    return copies
-
-
-def fetch_kernel(hop, place_ref, after_ref, own_hbm, other_hbm, w_out, sem):
-    for copy in weight_copies(place_ref, own_hbm, other_hbm, w_out, sem, hop):
-        copy.start()
-    for copy in weight_copies(place_ref, own_hbm, other_hbm, w_out, sem, hop):
-        copy.wait()
-
-
-def fetch_weights(place, after, w5, other_half, hop):
-    vmem = pl.BlockSpec(memory_space=pltpu.VMEM)
-    hbm = pl.BlockSpec(memory_space=pltpu.HBM)
-    anywhere = pl.BlockSpec(memory_space=pl.ANY)
-    return pl.pallas_call(
-        functools.partial(fetch_kernel, hop),
-        in_specs=[pl.BlockSpec(memory_space=pltpu.SMEM), vmem, hbm, anywhere],
-        out_specs=vmem,
-        out_shape=pltpu.VMEM((2, 3, RING) + w5.shape[3:], jnp.bfloat16),
-        scratch_shapes=[pltpu.SemaphoreType.DMA((2, RING))],
-        compiler_params=pltpu.CompilerParams(vmem_limit_bytes=20 * MIB),
-        cost_estimate=pl.CostEstimate(flops=10**6, bytes_accessed=5 * 10**6, transcendentals=0),
-        name="fetch_weights",
-    )(place, after, w5, other_half)
-
-
-def back_kernel(first, following, place_ref, *refs):
+def back_kernel(hop, first, place_ref, *refs):
     if first:
-        mask_ref, *parts, w_ref, own_hbm, other_hbm, out_ref, g_ref, w_out, sem = refs
-    elif following is None:
-        g_ref, w_ref, own_hbm, other_hbm, out_ref = refs
+        mask_ref, *parts, own_ref, other_ref, out_ref, g_ref = refs
+        gather(place_ref[RING * RING], mask_ref, parts[:RING], parts[RING:], g_ref)
     else:
-        g_ref, w_ref, own_hbm, other_hbm, out_ref, w_out, sem = refs
-    chip = place_ref[RING * RING + 1]
-    cols = w_ref.shape[3]
-    if following is not None:
-        for copy in weight_copies(place_ref, own_hbm, other_hbm, w_out, sem, following):
-            copy.start()
-    if first:
-        gather(chip, mask_ref, parts[:RING], parts[RING:], g_ref)
-    w = [w_ref[side, c].reshape(RING * cols, NH * HD) for side in range(2) for c in range(3)]
+        g_ref, own_ref, other_ref, out_ref = refs
+    cols = own_ref.shape[2]
+    dests = [place_ref[hop * RING + j] for j in range(RING)]
+    w = [
+        jnp.concatenate([w_ref[c, dest] for dest in dests], axis=0) for w_ref in (own_ref, other_ref) for c in range(3)
+    ]
     res = lax.dot_general(
         g_ref[...], jnp.concatenate(w, axis=1), (((1,), (1,)), ((), ())), preferred_element_type=jnp.float32
     ).astype(jnp.bfloat16)
     for j in range(RING):
         out_ref[j] = res[:, j * cols : (j + 1) * cols]
-    if following is not None:
-        for copy in weight_copies(place_ref, own_hbm, other_hbm, w_out, sem, following):
-            copy.wait()
-
-
-def back(place, w_here, w5, other_half, following, grads=None, gather_from=None):
-    cols = w5.shape[3]
+
+
+def back(place, own_half, other_half, hop, grads=None, gather_from=None):
+    cols = own_half.shape[2]
     vmem = pl.BlockSpec(memory_space=pltpu.VMEM)
-    hbm = pl.BlockSpec(memory_space=pltpu.HBM)
-    anywhere = pl.BlockSpec(memory_space=pl.ANY)
     first = grads is None
     if first:
         masks, own, oth = gather_from
@@ -326,23 +289,17 @@
         rows = grads.shape[0]
         extra = [grads]
     out_shape = [jax.ShapeDtypeStruct((RING, rows, cols), jnp.bfloat16)]
-    scratch = []
     if first:
         out_shape.append(pltpu.VMEM((rows, 18 * HD), jnp.bfloat16))
-    if following is not None:
-        out_shape.append(pltpu.VMEM(w_here.shape, jnp.bfloat16))
-        scratch.append(pltpu.SemaphoreType.DMA((2, RING)))
-    out = pl.pallas_call(
-        functools.partial(back_kernel, first, following),
-        in_specs=[pl.BlockSpec(memory_space=pltpu.SMEM)] + [vmem] * (len(extra) + 1) + [hbm, anywhere],
+    return pl.pallas_call(
+        functools.partial(back_kernel, hop, first),
+        in_specs=[pl.BlockSpec(memory_space=pltpu.SMEM)] + [vmem] * (len(extra) + 2),
         out_specs=[vmem] * len(out_shape),
         out_shape=out_shape,
-        scratch_shapes=scratch,
         compiler_params=pltpu.CompilerParams(vmem_limit_bytes=24 * MIB),
         cost_estimate=pl.CostEstimate(flops=10**6, bytes_accessed=10**4, transcendentals=0),
         name="back",
-    )(place, *extra, w_here, w5, other_half)
-    return [out[0]] + [pltpu.with_memory_space_constraint(x, pltpu.VMEM) for x in out[1:]]
+    )(place, *extra, own_half, other_half)
 
 
 def ring_perm(first, hop):
@@ -382,7 +339,7 @@
     proj_own, proj_other, half = project(where, part, activations, act_other, w_early, w5)
     proj_back = core_swap(proj_other)
     proj_back, half = lax.optimization_barrier((proj_back, half))
-    other_half = core_swap(half)
+    other_half = pltpu.with_memory_space_constraint(core_swap(half), pltpu.VMEM)
     g_heads = grad_attn.reshape(rows, NH, HD).transpose(1, 0, 2)
     heads = jnp.concatenate([jnp.where((masks[0] > 0)[None], proj_own, proj_back), g_heads], axis=2)
 
@@ -395,7 +352,8 @@
             x = lax.ppermute(x, "seq", [(i, (i + hop) % RING) for i in range(RING) if (i + hop) % RING < NH])
         parts[hop] = x
         others[hop] = core_swap(x)
-    own, oth = attention(where, parts, others)
+    own, oth, own_half = attention(where, parts, others, w5)
+    own_half = pltpu.with_memory_space_constraint(own_half, pltpu.VMEM)
     from_other = core_swap(oth)
 
     grads = [None] * RING
@@ -415,18 +373,15 @@
         (y + j) % RING * RING + (z + i) % RING,
         (y + i) % RING * RING + (z + j) % RING,
     )
-    place = jnp.concatenate([place, jnp.stack([core, chip])]).astype(jnp.int32)
+    place = jnp.concatenate([place, jnp.stack([chip])]).astype(jnp.int32)
 
     pieces = {}
-    w_here = fetch_weights(place, grads[0], w5, other_half, 2)
-    w_here = pltpu.with_memory_space_constraint(w_here, pltpu.VMEM)
-    x, g, w_here = back(place, w_here, w5, other_half, 1, gather_from=(masks, grads, other_grads))
+    x, g = back(place, own_half, other_half, 2, gather_from=(masks, grads, other_grads))
+    g = pltpu.with_memory_space_constraint(g, pltpu.VMEM)
     pieces[2] = lax.ppermute(x, AXES, ring_perm(True, 2))
-    x, w_here = back(place, w_here, w5, other_half, 3, grads=g)
-    pieces[1] = lax.ppermute(x, AXES, ring_perm(True, 1))
-    x, w_here = back(place, w_here, w5, other_half, 0, grads=g)
-    pieces[3] = lax.ppermute(x, AXES, ring_perm(True, 3))
-    (pieces[0],) = back(place, w_here, w5, other_half, None, grads=g)
+    for hop in (1, 3, 0):
+        (x,) = back(place, own_half, other_half, hop, grads=g)
+        pieces[hop] = lax.ppermute(x, AXES, ring_perm(True, hop)) if hop else x
     total = pieces[0].astype(jnp.float32)
     for hop in (2, 1, 3):
         total = lax.optimization_barrier(total) + pieces[hop].astype(jnp.float32)

time: 107 us -> 121 us (1.13)
  Pallas kernels: 37 us -> 46.7 us
  local copies, waits for them, and re-layouts: 1.88 us -> 9.22 us
  waiting for transfers between devices: 23.1 us -> 17.3 us
  starting transfers between devices: 41 us -> 43.7 us
    unnamed x6 -> x10, local copies, waits for them, and re-layouts: 0.78 us -> 8.12 us
    ppermute x13, starting transfers between devices: 10.8 us -> 16.9 us  [core_swap(): return lax.ppermute(x, 'mod', [(0, 1), (1, 0)])]
    pallas_call x5 -> x4, Pallas kernels: 17.5 us -> 23.5 us  [back(): pl.pallas_call(functools.partial(back_kernel, hop, first), in_specs=[pl.B...]
    ppermute x3, waiting for transfers between devices: 5.83 us -> 2 us  [per_device(): lax.ppermute(x, 'seq', [(i, (i + hop) % RING) for i in range(RING) if (i...]
    pallas_call x1, Pallas kernels: 4.73 us -> 8.42 us  [attention(): pl.pallas_call(attention_kernel, in_specs=[pl.BlockSpec(memory_space=pltp...]
    ppermute x2, waiting for transfers between devices: 5.82 us -> 2.65 us  [per_device(): pieces[hop] = lax.ppermute(x, AXES, ring_perm(True, hop)) if hop else x]
    ppermute x3, starting transfers between devices: 10.5 us -> 7.47 us  [per_device(): x = lax.ppermute(x, 'seq', [(i, (i - hop) % RING) for i in range(NH)])]
  transfers between devices with their start and end apart: 25 -> 25, of which waited for: 14 -> 13; matrix products, arithmetic and copies ran while one was open for 3% -> 3% of each run, Pallas kernels for 22% -> 25%
where the time goes in v5:
time: 121 us
  Pallas kernels  46.7 us (39%)
  starting transfers between devices  43.7 us (36%)
  waiting for transfers between devices  17.3 us (14%)
  local copies, waits for them, and re-layouts  9.22 us (8%)
  other arithmetic  3.34 us (3%)
    pallas_call x4, Pallas kernels, back(): pl.pallas_call(functools.partial(back_kernel, hop, first), in_specs=[pl.B...  23.5 us
    ppermute x13, starting transfers between devices, core_swap(): return lax.ppermute(x, 'mod', [(0, 1), (1, 0)])  16.9 us
    pallas_call x1, Pallas kernels, project(): pl.pallas_call(functools.partial(project_kernel, early), in_specs=[pl.Blo...  9.82 us
    pallas_call x1, Pallas kernels, attention(): pl.pallas_call(attention_kernel, in_specs=[pl.BlockSpec(memory_space=pltp...  8.42 us
    ppermute x3, starting transfers between devices, per_device(): lax.ppermute(x, 'seq', [(i, (i + hop) % RING) for i in range(RING) if (i...  8.19 us
    unnamed x10, local copies, waits for them, and re-layouts  8.12 us
    ppermute x3, starting transfers between devices, per_device(): x = lax.ppermute(x, 'seq', [(i, (i - hop) % RING) for i in range(NH)])  7.47 us
    ppermute x13, waiting for transfers between devices, core_swap(): return lax.ppermute(x, 'mod', [(0, 1), (1, 0)])  6.3 us
  transfers between devices with their start and end apart: 25, of which 13 were waited for; matrix products, arithmetic and copies ran while one was open for 3% of the time, Pallas kernels for 25%

profile of v5, /device:TPU:1, one launch (start us, length us, event | category | flops | bytes accessed | tf_op | source)
XLA Modules:
  0.0 120.7 jit_solution(14637043884415929235)
XLA Ops:
  1.5 5.0 %project_own.1 = (f32[192,1152]{1,0:T(8,128)S(1)}, bf16[3,8,2,256,384]{4,3,2,1,0:T(8,128)(2,1)S(1)}) custom-call(bf16[192,8192]{1,0:T(8,128)(2,1)} %own_hbm.1, bf16[3,16,2,256,384]{4,3,2,1,0:T(8,128)(2,1)} %bitcast.62), custom_call_target="tpu_custom_call" | custom-call | flops 4000000000 | bytes 10000000 | tf_op jit(solution)/shard_map/project_own/pallas_call | solution.py:56
  6.9 9.8 %project.1 = (bf16[3,192,384]{2,1,0:T(8,128)(2,1)S(1)}, bf16[3,192,384]{2,1,0:T(8,128)(2,1)S(1)}, bf16[3,16,256,384]{3,2,1,0:T(8,128)(2,1)}) custom-call(s32[2]{0:T(128)S(1)} %pad_add_fusion.2.where_ref, f32[192,1152]{1,0:T(8,128)S(1)} %get-tuple-element.17.part_ref, bf16[192,8192]{1,0:T(8,128)(2,1)} %own_hbm.1, ...), custom_call_target="tpu_custom_call" | custom-call | flops 7000000000 | bytes 10000000 | tf_op jit(solution)/shard_map/project/pallas_call | solution.py:138
  23.1 4.0 %collective-permute-start.2 = (bf16[192,512]{1,0:T(8,128)(2,1)S(1)}, bf16[192,512]{1,0:T(8,128)(2,1)S(1)}, u32[]{:S(2)}, u32[]{:S(2)}) collective-permute-start(bf16[192,512]{1,0:T(8,128)(2,1)S(1)} %get-tuple-element.44), channel_id=1, source_target_pairs={{0,32},{32,64},{96,0},{1,33},{33,65},{97,1},{2,34},{34,66},{98,2},... | collective-permute-start | bytes 589832 | tf_op jit(solution)/shard_map/ppermute | solution.py:352
  27.1 2.9 %collective-permute-start.3 = (bf16[192,512]{1,0:T(8,128)(2,1)S(1)}, bf16[192,512]{1,0:T(8,128)(2,1)S(1)}, u32[]{:S(2)}, u32[]{:S(2)}) collective-permute-start(bf16[192,512]{1,0:T(8,128)(2,1)S(1)} %get-tuple-element.45), channel_id=1, source_target_pairs={{0,64},{64,0},{96,32},{1,65},{65,1},{97,33},{2,66},{66,2},{98,34},... | collective-permute-start | bytes 589832 | tf_op jit(solution)/shard_map/ppermute | solution.py:352
  31.1 2.0 %collective-permute-done.2.a1 = bf16[192,512]{1,0:T(8,128)(2,1)S(1)} collective-permute-done((bf16[192,512]{1,0:T(8,128)(2,1)S(1)}, bf16[192,512]{1,0:T(8,128)(2,1)S(1)}, u32[]{:S(2)}, u32[]{:S(2)}) %collective-permute-start.2) | collective-permute-done | bytes 196640 | tf_op jit(solution)/shard_map/ppermute | solution.py:352
  33.1 5.2 %collective-permute-start.6 = (bf16[192,512]{1,0:T(8,128)(2,1)S(1)}, bf16[192,512]{1,0:T(8,128)(2,1)S(1)}, u32[]{:S(2)}, u32[]{:S(2)}) collective-permute-start(bf16[192,512]{1,0:T(8,128)(2,1)S(1)} %collective-permute-done.2.a1), channel_id=1, source_target_pairs={{0,16},{16,0},{1,17},{17,1},{2,18},{18,2},{3,19},{19,3},{4,20},{20... | collective-permute-start | bytes 589832 | tf_op jit(solution)/shard_map/ppermute | solution.py:19
  39.7 8.4 %attention.1 = (f32[4,192,384]{2,1,0:T(8,128)S(1)}, bf16[4,192,256]{2,1,0:T(8,128)(2,1)S(1)}, bf16[3,16,256,384]{3,2,1,0:T(8,128)(2,1)S(1)}) custom-call(s32[2]{0:T(128)S(1)} %pad_add_fusion.2.where_ref, bf16[192,512]{1,0:T(8,128)(2,1)S(1)} %get-tuple-element.43.a0, bf16[192,512]{1,0:T(8,128)(2,1)S(1)} %collective-permute-done.2.a1, ...), custom_call_target="tpu_custom_call" | custom-call | flops 1000000000 | bytes 4000000 | tf_op jit(solution)/shard_map/attention/pallas_call | solution.py:221
  48.1 3.7 %copy-done.2 = bf16[3,16,256,384]{3,2,1,0:T(8,128)(2,1)} copy-done((bf16[3,16,256,384]{3,2,1,0:T(8,128)(2,1)}, bf16[3,16,256,384]{3,2,1,0:T(8,128)(2,1)S(1)}, u32[]{:S(2)}) %copy-start.2) | copy-done | bytes 9437208
  53.6 1.9 %collective-permute-start.10 = (bf16[192,384]{1,0:T(8,128)(2,1)S(1)}, bf16[192,384]{1,0:T(8,128)(2,1)S(1)}, u32[]{:S(2)}, u32[]{:S(2)}) collective-permute-start(bf16[192,384]{1,0:T(8,128)(2,1)S(1)} %pad_maximum_fusion.1), channel_id=1, source_target_pairs={{0,96},{32,0},{64,32},{1,97},{33,1},{65,33},{2,98},{34,2},{66,34},... | collective-permute-start | bytes 442376 | tf_op jit(solution)/shard_map/ppermute | solution.py:365
  55.6 4.2 %collective-permute-start.11 = (bf16[192,384]{1,0:T(8,128)(2,1)S(1)}, bf16[192,384]{1,0:T(8,128)(2,1)S(1)}, u32[]{:S(2)}, u32[]{:S(2)}) collective-permute-start(bf16[192,384]{1,0:T(8,128)(2,1)S(1)} %pad_maximum_fusion.2), channel_id=1, source_target_pairs={{0,64},{32,96},{64,0},{1,65},{33,97},{65,1},{2,66},{34,98},{66,2},... | collective-permute-start | bytes 442376 | tf_op jit(solution)/shard_map/ppermute | solution.py:365
  62.5 1.7 %collective-permute-done.11.refs_3_ = bf16[192,384]{1,0:T(8,128)(2,1)S(1)} collective-permute-done((bf16[192,384]{1,0:T(8,128)(2,1)S(1)}, bf16[192,384]{1,0:T(8,128)(2,1)S(1)}, u32[]{:S(2)}, u32[]{:S(2)}) %collective-permute-start.11) | collective-permute-done | bytes 147488 | tf_op jit(solution)/shard_map/ppermute | solution.py:365
  64.1 1.8 %collective-permute-start.15 = (bf16[192,384]{1,0:T(8,128)(2,1)S(1)}, bf16[192,384]{1,0:T(8,128)(2,1)S(1)}, u32[]{:S(2)}, u32[]{:S(2)}) collective-permute-start(bf16[192,384]{1,0:T(8,128)(2,1)S(1)} %collective-permute-done.11.refs_3_), channel_id=1, source_target_pairs={{0,16},{16,0},{1,17},{17,1},{2,18},{18,2},{3,19},{19,3},{4,20},{20... | collective-permute-start | bytes 442376 | tf_op jit(solution)/shard_map/ppermute | solution.py:19
  68.0 3.7 %copy-done.3 = bf16[3,16,256,384]{3,2,1,0:T(8,128)(2,1)S(1)} copy-done((bf16[3,16,256,384]{3,2,1,0:T(8,128)(2,1)S(1)}, bf16[3,16,256,384]{3,2,1,0:T(8,128)(2,1)}, u32[]{:S(2)}) %copy-start.3) | copy-done | bytes 9437208
  71.7 6.4 %back.4 = (bf16[4,384,256]{2,1,0:T(8,128)(2,1)S(1)}, bf16[384,2304]{1,0:T(8,128)(2,1)S(1)}) custom-call(s32[17]{0:T(128)S(1)} %pad_add_fusion.1.place_ref, s32[2,192,1]{2,1,0:T(8,128)S(1)} %copy.16.refs_0_, bf16[192,384]{1,0:T(8,128)(2,1)S(1)} %pad_maximum_fusion.refs_1_, bf16[192,384]{1,0:T(8,128)(2,1)S(1)} %collective-permute-done.10.refs_2_, ...), custom_call_target="tpu_custom_call" | custom-call | flops 1000000 | bytes 10000 | tf_op jit(solution)/shard_map/back/pallas_call | solution.py:294
  78.1 3.0 %collective-permute-start.18 = (bf16[4,384,256]{2,1,0:T(8,128)(2,1)S(1)}, bf16[4,384,256]{2,1,0:T(8,128)(2,1)S(1)}, u32[]{:S(2)}, u32[]{:S(2)}) collective-permute-start(bf16[4,384,256]{2,1,0:T(8,128)(2,1)S(1)} %get-tuple-element.28), channel_id=1, source_target_pairs={{0,2},{1,3},{2,0},{3,1},{4,6},{5,7},{6,4},{7,5},{8,10},{9,11},{10,... | collective-permute-start | bytes 2359304 | tf_op jit(solution)/shard_map/ppermute | solution.py:381
  81.1 5.7 %back.6 = bf16[4,384,256]{2,1,0:T(8,128)(2,1)S(1)} custom-call(s32[17]{0:T(128)S(1)} %pad_add_fusion.1.place_ref, bf16[384,2304]{1,0:T(8,128)(2,1)S(1)} %get-tuple-element.27.refs_0_, bf16[3,16,256,384]{3,2,1,0:T(8,128)(2,1)S(1)} %copy-done.3, bf16[3,16,256,384]{3,2,1,0:T(8,128)(2,1)} %collective-permute-done.17.refs_10_.refs_2_), custom_call_target="tpu_custom_call" | custom-call | flops 1000000 | bytes 10000 | tf_op jit(solution)/shard_map/back/pallas_call | solution.py:294
  87.3 5.7 %back.7 = bf16[4,384,256]{2,1,0:T(8,128)(2,1)S(1)} custom-call(s32[17]{0:T(128)S(1)} %pad_add_fusion.1.place_ref, bf16[384,2304]{1,0:T(8,128)(2,1)S(1)} %get-tuple-element.27.refs_0_, bf16[3,16,256,384]{3,2,1,0:T(8,128)(2,1)S(1)} %copy-done.3, bf16[3,16,256,384]{3,2,1,0:T(8,128)(2,1)} %collective-permute-done.17.refs_10_.refs_2_), custom_call_target="tpu_custom_call" | custom-call | flops 1000000 | bytes 10000 | tf_op jit(solution)/shard_map/back/pallas_call | solution.py:294
  93.0 2.6 %collective-permute-start.20 = (bf16[4,384,256]{2,1,0:T(8,128)(2,1)S(1)}, bf16[4,384,256]{2,1,0:T(8,128)(2,1)S(1)}, u32[]{:S(2)}, u32[]{:S(2)}) collective-permute-start(bf16[4,384,256]{2,1,0:T(8,128)(2,1)S(1)} %back.7), channel_id=1, source_target_pairs={{0,3},{1,0},{2,1},{3,2},{4,7},{5,4},{6,5},{7,6},{8,11},{9,8},{10,9... | collective-permute-start | bytes 2359304 | tf_op jit(solution)/shard_map/ppermute | solution.py:384
  95.6 5.7 %back.5 = bf16[4,384,256]{2,1,0:T(8,128)(2,1)S(1)} custom-call(s32[17]{0:T(128)S(1)} %pad_add_fusion.1.place_ref, bf16[384,2304]{1,0:T(8,128)(2,1)S(1)} %get-tuple-element.27.refs_0_, bf16[3,16,256,384]{3,2,1,0:T(8,128)(2,1)S(1)} %copy-done.3, bf16[3,16,256,384]{3,2,1,0:T(8,128)(2,1)} %collective-permute-done.17.refs_10_.refs_2_), custom_call_target="tpu_custom_call" | custom-call | flops 1000000 | bytes 10000 | tf_op jit(solution)/shard_map/back/pallas_call | solution.py:294
  101.9 2.6 %collective-permute-done.20 = bf16[4,384,256]{2,1,0:T(8,128)(2,1)S(1)} collective-permute-done((bf16[4,384,256]{2,1,0:T(8,128)(2,1)S(1)}, bf16[4,384,256]{2,1,0:T(8,128)(2,1)S(1)}, u32[]{:S(2)}, u32[]{:S(2)}) %collective-permute-start.20) | collective-permute-done | bytes 786464 | tf_op jit(solution)/shard_map/ppermute | solution.py:384
  104.8 3.7 %collective-permute-start.21 = (bf16[384,256]{1,0:T(8,128)(2,1)S(1)}, bf16[384,256]{1,0:T(8,128)(2,1)S(1)}, u32[]{:S(2)}, u32[]{:S(2)}) collective-permute-start(bf16[384,256]{1,0:T(8,128)(2,1)S(1)} %get-tuple-element.35), channel_id=1, source_target_pairs={{0,8},{1,9},{2,10},{3,11},{4,12},{5,13},{6,14},{7,15},{8,0},{9,1},... | collective-permute-start | bytes 589832 | tf_op jit(solution)/shard_map/ppermute | solution.py:390
  110.0 1.6 %collective-permute-done.21 = bf16[384,256]{1,0:T(8,128)(2,1)S(1)} collective-permute-done((bf16[384,256]{1,0:T(8,128)(2,1)S(1)}, bf16[384,256]{1,0:T(8,128)(2,1)S(1)}, u32[]{:S(2)}, u32[]{:S(2)}) %collective-permute-start.21) | collective-permute-done | bytes 196640 | tf_op jit(solution)/shard_map/ppermute | solution.py:390
  111.6 2.9 %collective-permute-done.23 = bf16[384,256]{1,0:T(8,128)(2,1)S(1)} collective-permute-done((bf16[384,256]{1,0:T(8,128)(2,1)S(1)}, bf16[384,256]{1,0:T(8,128)(2,1)S(1)}, u32[]{:S(2)}, u32[]{:S(2)}) %collective-permute-start.23) | collective-permute-done | bytes 196640 | tf_op jit(solution)/shard_map/ppermute | solution.py:390
  114.8 4.2 %collective-permute-start.24 = (bf16[192,256]{1,0:T(8,128)(2,1)S(1)}, bf16[192,256]{1,0:T(8,128)(2,1)S(1)}, u32[]{:S(2)}, u32[]{:S(2)}) collective-permute-start(bf16[192,256]{1,0:T(8,128)(2,1)S(1)} %get-tuple-element.47), channel_id=1, source_target_pairs={{0,16},{16,0},{1,17},{17,1},{2,18},{18,2},{3,19},{19,3},{4,20},{20... | collective-permute-start | bytes 294920 | tf_op jit(solution)/shard_map/ppermute | solution.py:19
  (68 shorter events, 22.0 us)
Async XLA Ops:
  0.0 6.9 %collective-permute-start = (bf16[192,8192]{1,0:T(8,128)(2,1)}, bf16[192,8192]{1,0:T(8,128)(2,1)S(1)}, u32[]{:S(2)}, u32[]{:S(2)}) collective-permute-start(bf16[192,8192]{1,0:T(8,128)(2,1)} %own_hbm.1), channel_id=1, source_target_pairs={{0,16},{16,0},{1,17},{17,1},{2,18},{18,2},{3,19},{19,3},{4,20},{20... | collective-permute-start | bytes 9437192 | tf_op jit(solution)/shard_map/ppermute | solution.py:19
  17.5 1.8 %collective-permute-start.1 = (bf16[3,192,384]{2,1,0:T(8,128)(2,1)S(1)}, bf16[3,192,384]{2,1,0:T(8,128)(2,1)S(1)}, u32[]{:S(2)}, u32[]{:S(2)}) collective-permute-start(bf16[3,192,384]{2,1,0:T(8,128)(2,1)S(1)} %get-tuple-element.20), channel_id=1, source_target_pairs={{0,16},{16,0},{1,17},{17,1},{2,18},{18,2},{3,19},{19,3},{4,20},{20... | collective-permute-start | bytes 1327112 | tf_op jit(solution)/shard_map/ppermute | solution.py:19
  19.3 48.7 %collective-permute-start.17 = (bf16[3,16,256,384]{3,2,1,0:T(8,128)(2,1)}, bf16[3,16,256,384]{3,2,1,0:T(8,128)(2,1)}, u32[]{:S(2)}, u32[]{:S(2)}) collective-permute-start(bf16[3,16,256,384]{3,2,1,0:T(8,128)(2,1)} %get-tuple-element.26), channel_id=1, source_target_pairs={{0,16},{16,0},{1,17},{17,1},{2,18},{18,2},{3,19},{19,3},{4,20},{20... | collective-permute-start | bytes 28311560 | tf_op jit(solution)/shard_map/ppermute | solution.py:19
  21.8 9.0 %collective-permute-start.4 = (bf16[192,512]{1,0:T(8,128)(2,1)S(1)}, bf16[192,512]{1,0:T(8,128)(2,1)S(1)}, u32[]{:S(2)}, u32[]{:S(2)}) collective-permute-start(bf16[192,512]{1,0:T(8,128)(2,1)S(1)} %get-tuple-element.42), channel_id=1, source_target_pairs={{32,0},{64,32},{96,64},{33,1},{65,33},{97,65},{34,2},{66,34},{98,6... | collective-permute-start | bytes 589832 | tf_op jit(solution)/shard_map/ppermute | solution.py:352
  23.1 9.9 %collective-permute-start.2 = (bf16[192,512]{1,0:T(8,128)(2,1)S(1)}, bf16[192,512]{1,0:T(8,128)(2,1)S(1)}, u32[]{:S(2)}, u32[]{:S(2)}) collective-permute-start(bf16[192,512]{1,0:T(8,128)(2,1)S(1)} %get-tuple-element.44), channel_id=1, source_target_pairs={{0,32},{32,64},{96,0},{1,33},{33,65},{97,1},{2,34},{34,66},{98,2},... | collective-permute-start | bytes 589832 | tf_op jit(solution)/shard_map/ppermute | solution.py:352
  27.1 11.1 %collective-permute-start.3 = (bf16[192,512]{1,0:T(8,128)(2,1)S(1)}, bf16[192,512]{1,0:T(8,128)(2,1)S(1)}, u32[]{:S(2)}, u32[]{:S(2)}) collective-permute-start(bf16[192,512]{1,0:T(8,128)(2,1)S(1)} %get-tuple-element.45), channel_id=1, source_target_pairs={{0,64},{64,0},{96,32},{1,65},{65,1},{97,33},{2,66},{66,2},{98,34},... | collective-permute-start | bytes 589832 | tf_op jit(solution)/shard_map/ppermute | solution.py:352
  30.1 8.2 %collective-permute-start.5 = (bf16[192,512]{1,0:T(8,128)(2,1)S(1)}, bf16[192,512]{1,0:T(8,128)(2,1)S(1)}, u32[]{:S(2)}, u32[]{:S(2)}) collective-permute-start(bf16[192,512]{1,0:T(8,128)(2,1)S(1)} %get-tuple-element.43.a0), channel_id=1, source_target_pairs={{0,16},{16,0},{1,17},{17,1},{2,18},{18,2},{3,19},{19,3},{4,20},{20... | collective-permute-start | bytes 589832 | tf_op jit(solution)/shard_map/ppermute | solution.py:19
  30.9 7.4 %collective-permute-start.8 = (bf16[192,512]{1,0:T(8,128)(2,1)S(1)}, bf16[192,512]{1,0:T(8,128)(2,1)S(1)}, u32[]{:S(2)}, u32[]{:S(2)}) collective-permute-start(bf16[192,512]{1,0:T(8,128)(2,1)S(1)} %collective-permute-done.4.a3), channel_id=1, source_target_pairs={{0,16},{16,0},{1,17},{17,1},{2,18},{18,2},{3,19},{19,3},{4,20},{20... | collective-permute-start | bytes 589832 | tf_op jit(solution)/shard_map/ppermute | solution.py:19
  33.1 6.2 %collective-permute-start.6 = (bf16[192,512]{1,0:T(8,128)(2,1)S(1)}, bf16[192,512]{1,0:T(8,128)(2,1)S(1)}, u32[]{:S(2)}, u32[]{:S(2)}) collective-permute-start(bf16[192,512]{1,0:T(8,128)(2,1)S(1)} %collective-permute-done.2.a1), channel_id=1, source_target_pairs={{0,16},{16,0},{1,17},{17,1},{2,18},{18,2},{3,19},{19,3},{4,20},{20... | collective-permute-start | bytes 589832 | tf_op jit(solution)/shard_map/ppermute | solution.py:19
  51.8 1.7 %collective-permute-start.9 = (bf16[4,192,256]{2,1,0:T(8,128)(2,1)S(1)}, bf16[4,192,256]{2,1,0:T(8,128)(2,1)S(1)}, u32[]{:S(2)}, u32[]{:S(2)}) collective-permute-start(bf16[4,192,256]{2,1,0:T(8,128)(2,1)S(1)} %get-tuple-element.24), channel_id=1, source_target_pairs={{0,16},{16,0},{1,17},{17,1},{2,18},{18,2},{3,19},{19,3},{4,20},{20... | collective-permute-start | bytes 1179656 | tf_op jit(solution)/shard_map/ppermute | solution.py:19
  53.6 8.6 %collective-permute-start.10 = (bf16[192,384]{1,0:T(8,128)(2,1)S(1)}, bf16[192,384]{1,0:T(8,128)(2,1)S(1)}, u32[]{:S(2)}, u32[]{:S(2)}) collective-permute-start(bf16[192,384]{1,0:T(8,128)(2,1)S(1)} %pad_maximum_fusion.1), channel_id=1, source_target_pairs={{0,96},{32,0},{64,32},{1,97},{33,1},{65,33},{2,98},{34,2},{66,34},... | collective-permute-start | bytes 442376 | tf_op jit(solution)/shard_map/ppermute | solution.py:365
  55.6 8.6 %collective-permute-start.11 = (bf16[192,384]{1,0:T(8,128)(2,1)S(1)}, bf16[192,384]{1,0:T(8,128)(2,1)S(1)}, u32[]{:S(2)}, u32[]{:S(2)}) collective-permute-start(bf16[192,384]{1,0:T(8,128)(2,1)S(1)} %pad_maximum_fusion.2), channel_id=1, source_target_pairs={{0,64},{32,96},{64,0},{1,65},{33,97},{65,1},{2,66},{34,98},{66,2},... | collective-permute-start | bytes 442376 | tf_op jit(solution)/shard_map/ppermute | solution.py:365
  59.9 6.1 %collective-permute-start.12 = (bf16[192,384]{1,0:T(8,128)(2,1)S(1)}, bf16[192,384]{1,0:T(8,128)(2,1)S(1)}, u32[]{:S(2)}, u32[]{:S(2)}) collective-permute-start(bf16[192,384]{1,0:T(8,128)(2,1)S(1)} %pad_maximum_fusion.3), channel_id=1, source_target_pairs={{0,32},{32,64},{64,96},{1,33},{33,65},{65,97},{2,34},{34,66},{66,9... | collective-permute-start | bytes 442376 | tf_op jit(solution)/shard_map/ppermute | solution.py:365
  61.2 6.0 %collective-permute-start.13 = (bf16[192,384]{1,0:T(8,128)(2,1)S(1)}, bf16[192,384]{1,0:T(8,128)(2,1)S(1)}, u32[]{:S(2)}, u32[]{:S(2)}) collective-permute-start(bf16[192,384]{1,0:T(8,128)(2,1)S(1)} %pad_maximum_fusion.refs_1_), channel_id=1, source_target_pairs={{0,16},{16,0},{1,17},{17,1},{2,18},{18,2},{3,19},{19,3},{4,20},{20... | collective-permute-start | bytes 442376 | tf_op jit(solution)/shard_map/ppermute | solution.py:19
  62.3 5.0 %collective-permute-start.14 = (bf16[192,384]{1,0:T(8,128)(2,1)S(1)}, bf16[192,384]{1,0:T(8,128)(2,1)S(1)}, u32[]{:S(2)}, u32[]{:S(2)}) collective-permute-start(bf16[192,384]{1,0:T(8,128)(2,1)S(1)} %collective-permute-done.10.refs_2_), channel_id=1, source_target_pairs={{0,16},{16,0},{1,17},{17,1},{2,18},{18,2},{3,19},{19,3},{4,20},{20... | collective-permute-start | bytes 442376 | tf_op jit(solution)/shard_map/ppermute | solution.py:19
  64.1 3.1 %collective-permute-start.15 = (bf16[192,384]{1,0:T(8,128)(2,1)S(1)}, bf16[192,384]{1,0:T(8,128)(2,1)S(1)}, u32[]{:S(2)}, u32[]{:S(2)}) collective-permute-start(bf16[192,384]{1,0:T(8,128)(2,1)S(1)} %collective-permute-done.11.refs_3_), channel_id=1, source_target_pairs={{0,16},{16,0},{1,17},{17,1},{2,18},{18,2},{3,19},{19,3},{4,20},{20... | collective-permute-start | bytes 442376 | tf_op jit(solution)/shard_map/ppermute | solution.py:19
  65.9 2.1 %collective-permute-start.16 = (bf16[192,384]{1,0:T(8,128)(2,1)S(1)}, bf16[192,384]{1,0:T(8,128)(2,1)S(1)}, u32[]{:S(2)}, u32[]{:S(2)}) collective-permute-start(bf16[192,384]{1,0:T(8,128)(2,1)S(1)} %collective-permute-done.12.refs_4_), channel_id=1, source_target_pairs={{0,16},{16,0},{1,17},{17,1},{2,18},{18,2},{3,19},{19,3},{4,20},{20... | collective-permute-start | bytes 442376 | tf_op jit(solution)/shard_map/ppermute | solution.py:19
  78.1 23.3 %collective-permute-start.18 = (bf16[4,384,256]{2,1,0:T(8,128)(2,1)S(1)}, bf16[4,384,256]{2,1,0:T(8,128)(2,1)S(1)}, u32[]{:S(2)}, u32[]{:S(2)}) collective-permute-start(bf16[4,384,256]{2,1,0:T(8,128)(2,1)S(1)} %get-tuple-element.28), channel_id=1, source_target_pairs={{0,2},{1,3},{2,0},{3,1},{4,6},{5,7},{6,4},{7,5},{8,10},{9,11},{10,... | collective-permute-start | bytes 2359304 | tf_op jit(solution)/shard_map/ppermute | solution.py:381
  86.8 14.8 %collective-permute-start.19 = (bf16[4,384,256]{2,1,0:T(8,128)(2,1)S(1)}, bf16[4,384,256]{2,1,0:T(8,128)(2,1)S(1)}, u32[]{:S(2)}, u32[]{:S(2)}) collective-permute-start(bf16[4,384,256]{2,1,0:T(8,128)(2,1)S(1)} %back.6), channel_id=1, source_target_pairs={{0,1},{1,2},{2,3},{3,0},{4,5},{5,6},{6,7},{7,4},{8,9},{9,10},{10,1... | collective-permute-start | bytes 2359304 | tf_op jit(solution)/shard_map/ppermute | solution.py:384
  93.0 11.5 %collective-permute-start.20 = (bf16[4,384,256]{2,1,0:T(8,128)(2,1)S(1)}, bf16[4,384,256]{2,1,0:T(8,128)(2,1)S(1)}, u32[]{:S(2)}, u32[]{:S(2)}) collective-permute-start(bf16[4,384,256]{2,1,0:T(8,128)(2,1)S(1)} %back.7), channel_id=1, source_target_pairs={{0,3},{1,0},{2,1},{3,2},{4,7},{5,4},{6,5},{7,6},{8,11},{9,8},{10,9... | collective-permute-start | bytes 2359304 | tf_op jit(solution)/shard_map/ppermute | solution.py:384
  104.8 6.7 %collective-permute-start.21 = (bf16[384,256]{1,0:T(8,128)(2,1)S(1)}, bf16[384,256]{1,0:T(8,128)(2,1)S(1)}, u32[]{:S(2)}, u32[]{:S(2)}) collective-permute-start(bf16[384,256]{1,0:T(8,128)(2,1)S(1)} %get-tuple-element.35), channel_id=1, source_target_pairs={{0,8},{1,9},{2,10},{3,11},{4,12},{5,13},{6,14},{7,15},{8,0},{9,1},... | collective-permute-start | bytes 589832 | tf_op jit(solution)/shard_map/ppermute | solution.py:390
  108.5 6.0 %collective-permute-start.23 = (bf16[384,256]{1,0:T(8,128)(2,1)S(1)}, bf16[384,256]{1,0:T(8,128)(2,1)S(1)}, u32[]{:S(2)}, u32[]{:S(2)}) collective-permute-start(bf16[384,256]{1,0:T(8,128)(2,1)S(1)} %get-tuple-element.36), channel_id=1, source_target_pairs={{0,12},{1,13},{2,14},{3,15},{4,0},{5,1},{6,2},{7,3},{8,4},{9,5},{1... | collective-permute-start | bytes 589832 | tf_op jit(solution)/shard_map/ppermute | solution.py:390
  108.9 5.7 %collective-permute-start.22 = (bf16[384,256]{1,0:T(8,128)(2,1)S(1)}, bf16[384,256]{1,0:T(8,128)(2,1)S(1)}, u32[]{:S(2)}, u32[]{:S(2)}) collective-permute-start(bf16[384,256]{1,0:T(8,128)(2,1)S(1)} %get-tuple-element.37), channel_id=1, source_target_pairs={{0,4},{1,5},{2,6},{3,7},{4,8},{5,9},{6,10},{7,11},{8,12},{9,13},{1... | collective-permute-start | bytes 589832 | tf_op jit(solution)/shard_map/ppermute | solution.py:390
  114.8 5.1 %collective-permute-start.24 = (bf16[192,256]{1,0:T(8,128)(2,1)S(1)}, bf16[192,256]{1,0:T(8,128)(2,1)S(1)}, u32[]{:S(2)}, u32[]{:S(2)}) collective-permute-start(bf16[192,256]{1,0:T(8,128)(2,1)S(1)} %get-tuple-element.47), channel_id=1, source_target_pairs={{0,16},{16,0},{1,17},{17,1},{2,18},{18,2},{3,19},{19,3},{4,20},{20... | collective-permute-start | bytes 294920 | tf_op jit(solution)/shard_map/ppermute | solution.py:19
  (6 other events, 46.1 us)

commit v6 on v4

--- a/solution.py
+++ b/solution.py
@@ -264,85 +264,112 @@
     return copies
 
 
-def fetch_kernel(hop, place_ref, after_ref, own_hbm, other_hbm, w_out, sem):
-    for copy in weight_copies(place_ref, own_hbm, other_hbm, w_out, sem, hop):
+def fetch_kernel(hops, place_ref, after_ref, own_hbm, other_hbm, *refs):
+    copies = []
+    for i, hop in enumerate(hops):
+        copies += weight_copies(place_ref, own_hbm, other_hbm, refs[i], refs[len(hops) + i], hop)
+    for copy in copies:
         copy.start()
-    for copy in weight_copies(place_ref, own_hbm, other_hbm, w_out, sem, hop):
+    for copy in copies:
         copy.wait()
 
 
-def fetch_weights(place, after, w5, other_half, hop):
+def fetch_weights(place, after, w5, other_half, hops):
     vmem = pl.BlockSpec(memory_space=pltpu.VMEM)
     hbm = pl.BlockSpec(memory_space=pltpu.HBM)
     anywhere = pl.BlockSpec(memory_space=pl.ANY)
     return pl.pallas_call(
-        functools.partial(fetch_kernel, hop),
+        functools.partial(fetch_kernel, hops),
         in_specs=[pl.BlockSpec(memory_space=pltpu.SMEM), vmem, hbm, anywhere],
-        out_specs=vmem,
-        out_shape=pltpu.VMEM((2, 3, RING) + w5.shape[3:], jnp.bfloat16),
-        scratch_shapes=[pltpu.SemaphoreType.DMA((2, RING))],
+        out_specs=[vmem for _ in hops],
+        out_shape=[pltpu.VMEM((2, 3, RING) + w5.shape[3:], jnp.bfloat16) for _ in hops],
+        scratch_shapes=[pltpu.SemaphoreType.DMA((2, RING)) for _ in hops],
         compiler_params=pltpu.CompilerParams(vmem_limit_bytes=20 * MIB),
-        cost_estimate=pl.CostEstimate(flops=10**6, bytes_accessed=5 * 10**6, transcendentals=0),
+        cost_estimate=pl.CostEstimate(flops=10**6, bytes_accessed=10**7, transcendentals=0),
         name="fetch_weights",
     )(place, after, w5, other_half)
 
 
-def back_kernel(first, following, place_ref, *refs):
-    if first:
-        mask_ref, *parts, w_ref, own_hbm, other_hbm, out_ref, g_ref, w_out, sem = refs
-    elif following is None:
-        g_ref, w_ref, own_hbm, other_hbm, out_ref = refs
-    else:
-        g_ref, w_ref, own_hbm, other_hbm, out_ref, w_out, sem = refs
-    chip = place_ref[RING * RING + 1]
+def product(g_ref, w_ref, out_ref, j, count):
     cols = w_ref.shape[3]
-    if following is not None:
-        for copy in weight_copies(place_ref, own_hbm, other_hbm, w_out, sem, following):
-            copy.start()
-    if first:
-        gather(chip, mask_ref, parts[:RING], parts[RING:], g_ref)
-    w = [w_ref[side, c].reshape(RING * cols, NH * HD) for side in range(2) for c in range(3)]
+    w = [w_ref[side, c, j : j + count].reshape(count * cols, NH * HD) for side in range(2) for c in range(3)]
     res = lax.dot_general(
         g_ref[...], jnp.concatenate(w, axis=1), (((1,), (1,)), ((), ())), preferred_element_type=jnp.float32
     ).astype(jnp.bfloat16)
-    for j in range(RING):
-        out_ref[j] = res[:, j * cols : (j + 1) * cols]
-    if following is not None:
-        for copy in weight_copies(place_ref, own_hbm, other_hbm, w_out, sem, following):
+    for i in range(count):
+        out_ref[j + i] = res[:, i * cols : (i + 1) * cols]
+
+
+def back_first_kernel(following, place_ref, mask_ref, *refs):
+    *parts, w_ref, own_hbm, other_hbm, out_ref, g_ref, next_ref, sem = refs
+    for copy in weight_copies(place_ref, own_hbm, other_hbm, next_ref, sem, following):
+        copy.start()
+    gather(place_ref[RING * RING + 1], mask_ref, parts[:RING], parts[RING:], g_ref)
+    product(g_ref, w_ref, out_ref, 0, RING)
+    for copy in weight_copies(place_ref, own_hbm, other_hbm, next_ref, sem, following):
+        copy.wait()
+
+
+def back_middle_kernel(g_ref, w_ref, out_ref):
+    product(g_ref, w_ref, out_ref, 0, RING)
+
+
+def back_last_kernel(hop, place_ref, g_ref, own_hbm, other_hbm, out_ref, w_s, sem):
+    copies = weight_copies(place_ref, own_hbm, other_hbm, w_s, sem, hop)
+    for copy in copies:
+        copy.start()
+    for j in range(0, RING, 2):
+        for copy in copies[2 * j : 2 * j + 4]:
             copy.wait()
-
-
-def back(place, w_here, w5, other_half, following, grads=None, gather_from=None):
-    cols = w5.shape[3]
-    vmem = pl.BlockSpec(memory_space=pltpu.VMEM)
-    hbm = pl.BlockSpec(memory_space=pltpu.HBM)
-    anywhere = pl.BlockSpec(memory_space=pl.ANY)
-    first = grads is None
-    if first:
-        masks, own, oth = gather_from
-        rows = 2 * own[0].shape[0]
-        extra = [masks, *own, *oth]
-    else:
-        rows = grads.shape[0]
-        extra = [grads]
-    out_shape = [jax.ShapeDtypeStruct((RING, rows, cols), jnp.bfloat16)]
-    scratch = []
-    if first:
-        out_shape.append(pltpu.VMEM((rows, 18 * HD), jnp.bfloat16))
-    if following is not None:
-        out_shape.append(pltpu.VMEM(w_here.shape, jnp.bfloat16))
-        scratch.append(pltpu.SemaphoreType.DMA((2, RING)))
-    out = pl.pallas_call(
-        functools.partial(back_kernel, first, following),
-        in_specs=[pl.BlockSpec(memory_space=pltpu.SMEM)] + [vmem] * (len(extra) + 1) + [hbm, anywhere],
+        product(g_ref, w_s, out_ref, j, 2)
+
+
+def back_call(kernel, operands, in_specs, out_shape, scratch):
+    vmem = pl.BlockSpec(memory_space=pltpu.VMEM)
+    return pl.pallas_call(
+        kernel,
+        in_specs=in_specs,
         out_specs=[vmem] * len(out_shape),
         out_shape=out_shape,
         scratch_shapes=scratch,
         compiler_params=pltpu.CompilerParams(vmem_limit_bytes=24 * MIB),
         cost_estimate=pl.CostEstimate(flops=10**6, bytes_accessed=10**4, transcendentals=0),
         name="back",
-    )(place, *extra, w_here, w5, other_half)
-    return [out[0]] + [pltpu.with_memory_space_constraint(x, pltpu.VMEM) for x in out[1:]]
+    )(*operands)
+
+
+def back_products(place, masks, own, oth, weights, w5, other_half, send):
+    rows = 2 * own[0].shape[0]
+    cols = w5.shape[3]
+    smem = pl.BlockSpec(memory_space=pltpu.SMEM)
+    vmem = pl.BlockSpec(memory_space=pltpu.VMEM)
+    hbm = pl.BlockSpec(memory_space=pltpu.HBM)
+    anywhere = pl.BlockSpec(memory_space=pl.ANY)
+    piece = jax.ShapeDtypeStruct((RING, rows, cols), jnp.bfloat16)
+    w_shape = (2, 3, RING) + w5.shape[3:]
+    sem = pltpu.SemaphoreType.DMA((2, RING))
+    w_two, w_one = weights
+    x, g, w_three = back_call(
+        functools.partial(back_first_kernel, 3),
+        (place, masks, *own, *oth, w_two, w5, other_half),
+        [smem] + [vmem] * 10 + [hbm, anywhere],
+        [piece, pltpu.VMEM((rows, 18 * HD), jnp.bfloat16), pltpu.VMEM(w_shape, jnp.bfloat16)],
+        [sem],
+    )
+    g = pltpu.with_memory_space_constraint(g, pltpu.VMEM)
+    w_three = pltpu.with_memory_space_constraint(w_three, pltpu.VMEM)
+    pieces = {2: send(x, 2)}
+    for hop, w in ((1, w_one), (3, w_three)):
+        (x,) = back_call(back_middle_kernel, (g, w), [vmem, vmem], [piece], [])
+        pieces[hop] = send(x, hop)
+    (pieces[0],) = back_call(
+        functools.partial(back_last_kernel, 0),
+        (place, g, w5, other_half),
+        [smem, vmem, hbm, anywhere],
+        [piece],
+        [pltpu.VMEM(w_shape, jnp.bfloat16), sem],
+    )
+    return pieces
 
 
 def ring_perm(first, hop):
@@ -376,6 +403,9 @@
 
     w5 = pltpu.with_memory_space_constraint(w5, pltpu.HBM)
     activations = pltpu.with_memory_space_constraint(activations, pltpu.HBM)
+    g_heads = grad_attn.reshape(rows, NH, HD).transpose(1, 0, 2)
+    is_mine = jnp.broadcast_to(masks[0], (rows, HD))
+    where, masks, is_mine, g_heads = lax.optimization_barrier((where, masks, is_mine, g_heads))
     act_other = pltpu.with_memory_space_constraint(core_swap(activations), pltpu.VMEM)
     part, w_early = project_own(activations, w5, 4)
     w_early = pltpu.with_memory_space_constraint(w_early, pltpu.VMEM)
@@ -383,8 +413,7 @@
     proj_back = core_swap(proj_other)
     proj_back, half = lax.optimization_barrier((proj_back, half))
     other_half = core_swap(half)
-    g_heads = grad_attn.reshape(rows, NH, HD).transpose(1, 0, 2)
-    heads = jnp.concatenate([jnp.where((masks[0] > 0)[None], proj_own, proj_back), g_heads], axis=2)
+    heads = jnp.concatenate([jnp.where(jnp.concatenate([is_mine] * 3, axis=1)[None] > 0, proj_own, proj_back), g_heads], axis=2)
 
     parts = [None] * RING
     others = [None] * RING
@@ -398,15 +427,6 @@
     own, oth = attention(where, parts, others)
     from_other = core_swap(oth)
 
-    grads = [None] * RING
-    other_grads = [None] * RING
-    for hop in (2, 1, 3, 0):
-        kv = own[hop, :, HD:] + from_other[hop].astype(jnp.float32)
-        x = jnp.concatenate([own[hop, :, :HD], kv], axis=1).astype(jnp.bfloat16)
-        if hop:
-            x = lax.ppermute(x, "seq", [(i, (i - hop) % RING) for i in range(NH)])
-        grads[hop] = x
-        other_grads[hop] = core_swap(x)
     i = jnp.arange(dests, dtype=jnp.int32) // RING
     j = jnp.arange(dests, dtype=jnp.int32) % RING
     y, z = tp // RING, tp % RING
@@ -417,16 +437,30 @@
     )
     place = jnp.concatenate([place, jnp.stack([core, chip])]).astype(jnp.int32)
 
-    pieces = {}
-    w_here = fetch_weights(place, grads[0], w5, other_half, 2)
-    w_here = pltpu.with_memory_space_constraint(w_here, pltpu.VMEM)
-    x, g, w_here = back(place, w_here, w5, other_half, 1, gather_from=(masks, grads, other_grads))
-    pieces[2] = lax.ppermute(x, AXES, ring_perm(True, 2))
-    x, w_here = back(place, w_here, w5, other_half, 3, grads=g)
-    pieces[1] = lax.ppermute(x, AXES, ring_perm(True, 1))
-    x, w_here = back(place, w_here, w5, other_half, 0, grads=g)
-    pieces[3] = lax.ppermute(x, AXES, ring_perm(True, 3))
-    (pieces[0],) = back(place, w_here, w5, other_half, None, grads=g)
+    grads = [None] * RING
+    for hop in (2, 1, 3, 0):
+        kv = own[hop, :, HD:] + from_other[hop].astype(jnp.float32)
+        x = jnp.concatenate([own[hop, :, :HD], kv], axis=1).astype(jnp.bfloat16)
+        if hop:
+            x = lax.ppermute(x, "seq", [(i, (i - hop) % RING) for i in range(NH)])
+        grads[hop] = x
+    w_first = fetch_weights(place, grads[0], w5, other_half, (2, 1))
+    w_first = [pltpu.with_memory_space_constraint(w, pltpu.VMEM) for w in w_first]
+    grads[1:], w_first = lax.optimization_barrier((grads[1:], w_first))
+    other_grads = [None] * RING
+    for hop in (2, 1, 3, 0):
+        other_grads[hop] = core_swap(grads[hop])
+
+    pieces = back_products(
+        place,
+        masks,
+        grads,
+        other_grads,
+        w_first,
+        w5,
+        other_half,
+        lambda x, hop: lax.ppermute(x, AXES, ring_perm(True, hop)),
+    )
     total = pieces[0].astype(jnp.float32)
     for hop in (2, 1, 3):
         total = lax.optimization_barrier(total) + pieces[hop].astype(jnp.float32)

time: 107 us -> 104 us (0.972)
  waiting for transfers between devices: 23.1 us -> 19.4 us
  local copies, waits for them, and re-layouts: 1.88 us -> 3.32 us
  Pallas kernels: 37 us -> 35.7 us
  other arithmetic: 3.34 us -> 4.42 us
    ppermute x3, waiting for transfers between devices: 5.83 us -> 1.64 us  [per_device(): lax.ppermute(x, 'seq', [(i, (i + hop) % RING) for i in range(RING) if (i...]
    ppermute x13, starting transfers between devices: 10.8 us -> 13.8 us  [core_swap(): return lax.ppermute(x, 'mod', [(0, 1), (1, 0)])]
    ppermute x3, starting transfers between devices: 10.5 us -> 7.46 us  [per_device(): x = lax.ppermute(x, 'seq', [(i, (i - hop) % RING) for i in range(NH)])]
    ppermute x3, waiting for transfers between devices: 2.71 us -> 0.01 us  [per_device(): x = lax.ppermute(x, 'seq', [(i, (i - hop) % RING) for i in range(NH)])]
    ppermute x13, waiting for transfers between devices: 5.17 us -> 6.58 us  [core_swap(): return lax.ppermute(x, 'mod', [(0, 1), (1, 0)])]
    pallas_call x5, Pallas kernels: 17.5 us -> 16.1 us  [the longest x4 11.8 us: back_call(): pl.pallas_call(kernel, in_specs=in_specs, out_specs=[vmem] * len(out_shap...]
    ppermute x3, waiting for transfers between devices: 3.52 us -> 4.77 us  [per_device(): lax.ppermute(total[hop].astype(jnp.bfloat16), AXES, ring_perm(False, hop))]
    ppermute x3, starting transfers between devices: 6.34 us -> 5.15 us  [per_device(): lax.ppermute(total[hop].astype(jnp.bfloat16), AXES, ring_perm(False, hop))]
  transfers between devices with their start and end apart: 25 -> 25, of which waited for: 14 -> 13; matrix products, arithmetic and copies ran while one was open for 3% -> 6% of each run, Pallas kernels for 22% -> 22%
where the time goes in v6:
time: 104 us
  starting transfers between devices  40.7 us (39%)
  Pallas kernels  35.7 us (34%)
  waiting for transfers between devices  19.4 us (19%)
  other arithmetic  4.42 us (4%)
  local copies, waits for them, and re-layouts  3.32 us (3%)
    ppermute x13, starting transfers between devices, core_swap(): return lax.ppermute(x, 'mod', [(0, 1), (1, 0)])  13.8 us
    pallas_call x4, Pallas kernels, back_call(): pl.pallas_call(kernel, in_specs=in_specs, out_specs=[vmem] * len(out_shap...  11.8 us
    pallas_call x1, Pallas kernels, project(): pl.pallas_call(functools.partial(project_kernel, early), in_specs=[pl.Blo...  9.83 us
    ppermute x3, starting transfers between devices, per_device(): lax.ppermute(x, 'seq', [(i, (i + hop) % RING) for i in range(RING) if (i...  8.2 us
    ppermute x3, starting transfers between devices, per_device(): x = lax.ppermute(x, 'seq', [(i, (i - hop) % RING) for i in range(NH)])  7.46 us
    ppermute x13, waiting for transfers between devices, core_swap(): return lax.ppermute(x, 'mod', [(0, 1), (1, 0)])  6.58 us
    ppermute x3, waiting for transfers between devices, per_device(): lax.ppermute(x, AXES, ring_perm(True, hop))  6.36 us
    ppermute x3, starting transfers between devices, per_device(): lax.ppermute(x, AXES, ring_perm(True, hop))  6.03 us
  transfers between devices with their start and end apart: 25, of which 13 were waited for; matrix products, arithmetic and copies ran while one was open for 6% of the time, Pallas kernels for 22%

profile of v6, /device:TPU:1, one launch (start us, length us, event | category | flops | bytes accessed | tf_op | source)
XLA Modules:
  0.0 103.8 jit_solution(380900112008895893)
XLA Ops:
  0.0 1.4 %collective-permute-start = (bf16[192,8192]{1,0:T(8,128)(2,1)}, bf16[192,8192]{1,0:T(8,128)(2,1)S(1)}, u32[]{:S(2)}, u32[]{:S(2)}) collective-permute-start(bf16[192,8192]{1,0:T(8,128)(2,1)} %own_hbm.1), channel_id=1, source_target_pairs={{0,16},{16,0},{1,17},{17,1},{2,18},{18,2},{3,19},{19,3},{4,20},{20... | collective-permute-start | bytes 9437192 | tf_op jit(solution)/shard_map/ppermute | solution.py:19
  4.0 5.0 %project_own.1 = (f32[192,1152]{1,0:T(8,128)S(1)}, bf16[3,8,2,256,384]{4,3,2,1,0:T(8,128)(2,1)S(1)}) custom-call(bf16[192,8192]{1,0:T(8,128)(2,1)} %own_hbm.1, bf16[3,16,2,256,384]{4,3,2,1,0:T(8,128)(2,1)} %bitcast.63), custom_call_target="tpu_custom_call" | custom-call | flops 4000000000 | bytes 10000000 | tf_op jit(solution)/shard_map/project_own/pallas_call | solution.py:56
  9.0 9.8 %project.1 = (bf16[3,192,384]{2,1,0:T(8,128)(2,1)S(1)}, bf16[3,192,384]{2,1,0:T(8,128)(2,1)S(1)}, bf16[3,16,256,384]{3,2,1,0:T(8,128)(2,1)}) custom-call(s32[2]{0:T(128)S(1)} %pad_add_fusion.2.where_ref, f32[192,1152]{1,0:T(8,128)S(1)} %get-tuple-element.31.part_ref, bf16[192,8192]{1,0:T(8,128)(2,1)} %own_hbm.1, ...), custom_call_target="tpu_custom_call" | custom-call | flops 7000000000 | bytes 10000000 | tf_op jit(solution)/shard_map/project/pallas_call | solution.py:138
  19.7 1.8 %collective-permute-done.1 = bf16[3,192,384]{2,1,0:T(8,128)(2,1)S(1)} collective-permute-done((bf16[3,192,384]{2,1,0:T(8,128)(2,1)S(1)}, bf16[3,192,384]{2,1,0:T(8,128)(2,1)S(1)}, u32[]{:S(2)}, u32[]{:S(2)}) %collective-permute-start.1) | collective-permute-done | bytes 442400 | tf_op jit(solution)/shard_map/ppermute | solution.py:19
  25.2 4.0 %collective-permute-start.2 = (bf16[192,512]{1,0:T(8,128)(2,1)S(1)}, bf16[192,512]{1,0:T(8,128)(2,1)S(1)}, u32[]{:S(2)}, u32[]{:S(2)}) collective-permute-start(bf16[192,512]{1,0:T(8,128)(2,1)S(1)} %get-tuple-element.66), channel_id=1, source_target_pairs={{0,32},{32,64},{96,0},{1,33},{33,65},{97,1},{2,34},{34,66},{98,2},... | collective-permute-start | bytes 589832 | tf_op jit(solution)/shard_map/ppermute | solution.py:424
  29.2 2.9 %collective-permute-start.3 = (bf16[192,512]{1,0:T(8,128)(2,1)S(1)}, bf16[192,512]{1,0:T(8,128)(2,1)S(1)}, u32[]{:S(2)}, u32[]{:S(2)}) collective-permute-start(bf16[192,512]{1,0:T(8,128)(2,1)S(1)} %get-tuple-element.67), channel_id=1, source_target_pairs={{0,64},{64,0},{96,32},{1,65},{65,1},{97,33},{2,66},{66,2},{98,34},... | collective-permute-start | bytes 589832 | tf_op jit(solution)/shard_map/ppermute | solution.py:424
  33.2 1.6 %collective-permute-done.2.a1 = bf16[192,512]{1,0:T(8,128)(2,1)S(1)} collective-permute-done((bf16[192,512]{1,0:T(8,128)(2,1)S(1)}, bf16[192,512]{1,0:T(8,128)(2,1)S(1)}, u32[]{:S(2)}, u32[]{:S(2)}) %collective-permute-start.2) | collective-permute-done | bytes 196640 | tf_op jit(solution)/shard_map/ppermute | solution.py:424
  34.8 5.4 %collective-permute-start.6 = (bf16[192,512]{1,0:T(8,128)(2,1)S(1)}, bf16[192,512]{1,0:T(8,128)(2,1)S(1)}, u32[]{:S(2)}, u32[]{:S(2)}) collective-permute-start(bf16[192,512]{1,0:T(8,128)(2,1)S(1)} %collective-permute-done.2.a1), channel_id=1, source_target_pairs={{0,16},{16,0},{1,17},{17,1},{2,18},{18,2},{3,19},{19,3},{4,20},{20... | collective-permute-start | bytes 589832 | tf_op jit(solution)/shard_map/ppermute | solution.py:19
  41.7 4.7 %attention.1 = (f32[4,192,384]{2,1,0:T(8,128)S(1)}, bf16[4,192,256]{2,1,0:T(8,128)(2,1)S(1)}) custom-call(s32[2]{0:T(128)S(1)} %pad_add_fusion.2.where_ref, bf16[192,512]{1,0:T(8,128)(2,1)S(1)} %get-tuple-element.65.a0, bf16[192,512]{1,0:T(8,128)(2,1)S(1)} %collective-permute-done.2.a1, bf16[192,512]{1,0:T(8,128)(2,1)S(1)} %collective-permute-done.3.a2, ...), custom_call_target="tpu_custom_call" | custom-call | flops 1000000000 | bytes 4000000 | tf_op jit(solution)/shard_map/attention/pallas_call | solution.py:218
  46.9 1.3 %collective-permute-done.9 = bf16[4,192,256]{2,1,0:T(8,128)(2,1)S(1)} collective-permute-done((bf16[4,192,256]{2,1,0:T(8,128)(2,1)S(1)}, bf16[4,192,256]{2,1,0:T(8,128)(2,1)S(1)}, u32[]{:S(2)}, u32[]{:S(2)}) %collective-permute-start.9) | collective-permute-done | bytes 393248 | tf_op jit(solution)/shard_map/ppermute | solution.py:19
  48.4 1.9 %collective-permute-start.10 = (bf16[192,384]{1,0:T(8,128)(2,1)S(1)}, bf16[192,384]{1,0:T(8,128)(2,1)S(1)}, u32[]{:S(2)}, u32[]{:S(2)}) collective-permute-start(bf16[192,384]{1,0:T(8,128)(2,1)S(1)} %pad_maximum_fusion.1), channel_id=1, source_target_pairs={{0,96},{32,0},{64,32},{1,97},{33,1},{65,33},{2,98},{34,2},{66,34},... | collective-permute-start | bytes 442376 | tf_op jit(solution)/shard_map/ppermute | solution.py:445
  50.3 4.2 %collective-permute-start.11 = (bf16[192,384]{1,0:T(8,128)(2,1)S(1)}, bf16[192,384]{1,0:T(8,128)(2,1)S(1)}, u32[]{:S(2)}, u32[]{:S(2)}) collective-permute-start(bf16[192,384]{1,0:T(8,128)(2,1)S(1)} %pad_maximum_fusion.2), channel_id=1, source_target_pairs={{0,64},{32,96},{64,0},{1,65},{33,97},{65,1},{2,66},{34,98},{66,2},... | collective-permute-start | bytes 442376 | tf_op jit(solution)/shard_map/ppermute | solution.py:445
  57.0 4.4 %fetch_weights.1 = (bf16[2,3,4,256,384]{4,3,2,1,0:T(8,128)(2,1)S(1)}, bf16[2,3,4,256,384]{4,3,2,1,0:T(8,128)(2,1)S(1)}) custom-call(s32[18]{0:T(128)S(1)} %pad_add_fusion.1.place_ref, bf16[192,384]{1,0:T(8,128)(2,1)S(1)} %pad_maximum_fusion.after_ref.refs_0_, bf16[3,16,2,256,384]{4,3,2,1,0:T(8,128)(2,1)} %bitcast.65, ...), custom_call_target="tpu_custom_call" | custom-call | flops 1000000 | bytes 10000000 | tf_op jit(solution)/shard_map/fetch_weights/pallas_call | solution.py:281
  63.4 3.3 %back.4 = (bf16[4,384,256]{2,1,0:T(8,128)(2,1)S(1)}, bf16[384,2304]{1,0:T(8,128)(2,1)S(1)}, bf16[2,3,4,256,384]{4,3,2,1,0:T(8,128)(2,1)S(1)}) custom-call(s32[18]{0:T(128)S(1)} %pad_add_fusion.1.place_ref, s32[2,192,1]{2,1,0:T(8,128)S(1)} %convert_element_type.66.mask_ref, bf16[192,384]{1,0:T(8,128)(2,1)S(1)} %pad_maximum_fusion.after_ref.refs_0_, ...), custom_call_target="tpu_custom_call" | custom-call | flops 1000000 | bytes 10000 | tf_op jit(solution)/shard_map/back/pallas_call | solution.py:329
  66.7 3.0 %collective-permute-start.18 = (bf16[4,384,256]{2,1,0:T(8,128)(2,1)S(1)}, bf16[4,384,256]{2,1,0:T(8,128)(2,1)S(1)}, u32[]{:S(2)}, u32[]{:S(2)}) collective-permute-start(bf16[4,384,256]{2,1,0:T(8,128)(2,1)S(1)} %get-tuple-element.48), channel_id=1, source_target_pairs={{0,2},{1,3},{2,0},{3,1},{4,6},{5,7},{6,4},{7,5},{8,10},{9,11},{10,... | collective-permute-start | bytes 2359304 | tf_op jit(solution)/shard_map/ppermute | solution.py:462
  69.7 2.0 %back.6 = bf16[4,384,256]{2,1,0:T(8,128)(2,1)S(1)} custom-call(bf16[384,2304]{1,0:T(8,128)(2,1)S(1)} %get-tuple-element.47.g_ref, bf16[2,3,4,256,384]{4,3,2,1,0:T(8,128)(2,1)S(1)} %get-tuple-element.49.w_ref), custom_call_target="tpu_custom_call" | custom-call | flops 1000000 | bytes 10000 | tf_op jit(solution)/shard_map/back/pallas_call | solution.py:329
  72.2 2.0 %back.7 = bf16[4,384,256]{2,1,0:T(8,128)(2,1)S(1)} custom-call(bf16[384,2304]{1,0:T(8,128)(2,1)S(1)} %get-tuple-element.47.g_ref, bf16[2,3,4,256,384]{4,3,2,1,0:T(8,128)(2,1)S(1)} %get-tuple-element.50.w_ref), custom_call_target="tpu_custom_call" | custom-call | flops 1000000 | bytes 10000 | tf_op jit(solution)/shard_map/back/pallas_call | solution.py:329
  74.2 2.6 %collective-permute-start.20 = (bf16[4,384,256]{2,1,0:T(8,128)(2,1)S(1)}, bf16[4,384,256]{2,1,0:T(8,128)(2,1)S(1)}, u32[]{:S(2)}, u32[]{:S(2)}) collective-permute-start(bf16[4,384,256]{2,1,0:T(8,128)(2,1)S(1)} %back.7), channel_id=1, source_target_pairs={{0,3},{1,0},{2,1},{3,2},{4,7},{5,4},{6,5},{7,6},{8,11},{9,8},{10,9... | collective-permute-start | bytes 2359304 | tf_op jit(solution)/shard_map/ppermute | solution.py:462
  76.8 4.4 %back.5 = bf16[4,384,256]{2,1,0:T(8,128)(2,1)S(1)} custom-call(s32[18]{0:T(128)S(1)} %pad_add_fusion.1.place_ref, bf16[384,2304]{1,0:T(8,128)(2,1)S(1)} %get-tuple-element.47.g_ref, bf16[3,16,2,256,384]{4,3,2,1,0:T(8,128)(2,1)} %bitcast.67, bf16[3,16,256,384]{3,2,1,0:T(8,128)(2,1)} %collective-permute-done.13.other_hbm.refs_10_), custom_call_target="tpu_custom_call" | custom-call | flops 1000000 | bytes 10000 | tf_op jit(solution)/shard_map/back/pallas_call | solution.py:329
  81.6 6.2 %collective-permute-done.19 = bf16[4,384,256]{2,1,0:T(8,128)(2,1)S(1)} collective-permute-done((bf16[4,384,256]{2,1,0:T(8,128)(2,1)S(1)}, bf16[4,384,256]{2,1,0:T(8,128)(2,1)S(1)}, u32[]{:S(2)}, u32[]{:S(2)}) %collective-permute-start.19) | collective-permute-done | bytes 786464 | tf_op jit(solution)/shard_map/ppermute | solution.py:462
  88.5 3.7 %collective-permute-start.21 = (bf16[384,256]{1,0:T(8,128)(2,1)S(1)}, bf16[384,256]{1,0:T(8,128)(2,1)S(1)}, u32[]{:S(2)}, u32[]{:S(2)}) collective-permute-start(bf16[384,256]{1,0:T(8,128)(2,1)S(1)} %get-tuple-element.57), channel_id=1, source_target_pairs={{0,8},{1,9},{2,10},{3,11},{4,12},{5,13},{6,14},{7,15},{8,0},{9,1},... | collective-permute-start | bytes 589832 | tf_op jit(solution)/shard_map/ppermute | solution.py:469
  93.7 1.9 %collective-permute-done.21 = bf16[384,256]{1,0:T(8,128)(2,1)S(1)} collective-permute-done((bf16[384,256]{1,0:T(8,128)(2,1)S(1)}, bf16[384,256]{1,0:T(8,128)(2,1)S(1)}, u32[]{:S(2)}, u32[]{:S(2)}) %collective-permute-start.21) | collective-permute-done | bytes 196640 | tf_op jit(solution)/shard_map/ppermute | solution.py:469
  95.6 2.9 %collective-permute-done.23 = bf16[384,256]{1,0:T(8,128)(2,1)S(1)} collective-permute-done((bf16[384,256]{1,0:T(8,128)(2,1)S(1)}, bf16[384,256]{1,0:T(8,128)(2,1)S(1)}, u32[]{:S(2)}, u32[]{:S(2)}) %collective-permute-start.23) | collective-permute-done | bytes 196640 | tf_op jit(solution)/shard_map/ppermute | solution.py:469
  98.6 3.5 %collective-permute-start.24 = (bf16[192,256]{1,0:T(8,128)(2,1)S(1)}, bf16[192,256]{1,0:T(8,128)(2,1)S(1)}, u32[]{:S(2)}, u32[]{:S(2)}) collective-permute-start(bf16[192,256]{1,0:T(8,128)(2,1)S(1)} %get-tuple-element.69), channel_id=1, source_target_pairs={{0,16},{16,0},{1,17},{17,1},{2,18},{18,2},{3,19},{19,3},{4,20},{20... | collective-permute-start | bytes 294920 | tf_op jit(solution)/shard_map/ppermute | solution.py:19
  (70 shorter events, 19.4 us)
Async XLA Ops:
  0.0 9.0 %collective-permute-start = (bf16[192,8192]{1,0:T(8,128)(2,1)}, bf16[192,8192]{1,0:T(8,128)(2,1)S(1)}, u32[]{:S(2)}, u32[]{:S(2)}) collective-permute-start(bf16[192,8192]{1,0:T(8,128)(2,1)} %own_hbm.1), channel_id=1, source_target_pairs={{0,16},{16,0},{1,17},{17,1},{2,18},{18,2},{3,19},{19,3},{4,20},{20... | collective-permute-start | bytes 9437192 | tf_op jit(solution)/shard_map/ppermute | solution.py:19
  19.6 1.8 %collective-permute-start.1 = (bf16[3,192,384]{2,1,0:T(8,128)(2,1)S(1)}, bf16[3,192,384]{2,1,0:T(8,128)(2,1)S(1)}, u32[]{:S(2)}, u32[]{:S(2)}) collective-permute-start(bf16[3,192,384]{2,1,0:T(8,128)(2,1)S(1)} %get-tuple-element.34), channel_id=1, source_target_pairs={{0,16},{16,0},{1,17},{17,1},{2,18},{18,2},{3,19},{19,3},{4,20},{20... | collective-permute-start | bytes 1327112 | tf_op jit(solution)/shard_map/ppermute | solution.py:19
  21.4 35.6 %collective-permute-start.13 = (bf16[3,16,256,384]{3,2,1,0:T(8,128)(2,1)}, bf16[3,16,256,384]{3,2,1,0:T(8,128)(2,1)}, u32[]{:S(2)}, u32[]{:S(2)}) collective-permute-start(bf16[3,16,256,384]{3,2,1,0:T(8,128)(2,1)} %get-tuple-element.40), channel_id=1, source_target_pairs={{0,16},{16,0},{1,17},{17,1},{2,18},{18,2},{3,19},{19,3},{4,20},{20... | collective-permute-start | bytes 28311560 | tf_op jit(solution)/shard_map/ppermute | solution.py:19
  23.9 9.2 %collective-permute-start.4 = (bf16[192,512]{1,0:T(8,128)(2,1)S(1)}, bf16[192,512]{1,0:T(8,128)(2,1)S(1)}, u32[]{:S(2)}, u32[]{:S(2)}) collective-permute-start(bf16[192,512]{1,0:T(8,128)(2,1)S(1)} %get-tuple-element.64), channel_id=1, source_target_pairs={{32,0},{64,32},{96,64},{33,1},{65,33},{97,65},{34,2},{66,34},{98,6... | collective-permute-start | bytes 589832 | tf_op jit(solution)/shard_map/ppermute | solution.py:424
  25.2 9.7 %collective-permute-start.2 = (bf16[192,512]{1,0:T(8,128)(2,1)S(1)}, bf16[192,512]{1,0:T(8,128)(2,1)S(1)}, u32[]{:S(2)}, u32[]{:S(2)}) collective-permute-start(bf16[192,512]{1,0:T(8,128)(2,1)S(1)} %get-tuple-element.66), channel_id=1, source_target_pairs={{0,32},{32,64},{96,0},{1,33},{33,65},{97,1},{2,34},{34,66},{98,2},... | collective-permute-start | bytes 589832 | tf_op jit(solution)/shard_map/ppermute | solution.py:424
  29.2 11.1 %collective-permute-start.3 = (bf16[192,512]{1,0:T(8,128)(2,1)S(1)}, bf16[192,512]{1,0:T(8,128)(2,1)S(1)}, u32[]{:S(2)}, u32[]{:S(2)}) collective-permute-start(bf16[192,512]{1,0:T(8,128)(2,1)S(1)} %get-tuple-element.67), channel_id=1, source_target_pairs={{0,64},{64,0},{96,32},{1,65},{65,1},{97,33},{2,66},{66,2},{98,34},... | collective-permute-start | bytes 589832 | tf_op jit(solution)/shard_map/ppermute | solution.py:424
  32.1 8.2 %collective-permute-start.5 = (bf16[192,512]{1,0:T(8,128)(2,1)S(1)}, bf16[192,512]{1,0:T(8,128)(2,1)S(1)}, u32[]{:S(2)}, u32[]{:S(2)}) collective-permute-start(bf16[192,512]{1,0:T(8,128)(2,1)S(1)} %get-tuple-element.65.a0), channel_id=1, source_target_pairs={{0,16},{16,0},{1,17},{17,1},{2,18},{18,2},{3,19},{19,3},{4,20},{20... | collective-permute-start | bytes 589832 | tf_op jit(solution)/shard_map/ppermute | solution.py:19
  33.1 7.2 %collective-permute-start.8 = (bf16[192,512]{1,0:T(8,128)(2,1)S(1)}, bf16[192,512]{1,0:T(8,128)(2,1)S(1)}, u32[]{:S(2)}, u32[]{:S(2)}) collective-permute-start(bf16[192,512]{1,0:T(8,128)(2,1)S(1)} %collective-permute-done.4.a3), channel_id=1, source_target_pairs={{0,16},{16,0},{1,17},{17,1},{2,18},{18,2},{3,19},{19,3},{4,20},{20... | collective-permute-start | bytes 589832 | tf_op jit(solution)/shard_map/ppermute | solution.py:19
  34.8 6.5 %collective-permute-start.6 = (bf16[192,512]{1,0:T(8,128)(2,1)S(1)}, bf16[192,512]{1,0:T(8,128)(2,1)S(1)}, u32[]{:S(2)}, u32[]{:S(2)}) collective-permute-start(bf16[192,512]{1,0:T(8,128)(2,1)S(1)} %collective-permute-done.2.a1), channel_id=1, source_target_pairs={{0,16},{16,0},{1,17},{17,1},{2,18},{18,2},{3,19},{19,3},{4,20},{20... | collective-permute-start | bytes 589832 | tf_op jit(solution)/shard_map/ppermute | solution.py:19
  40.3 1.4 %collective-permute-start.7 = (bf16[192,512]{1,0:T(8,128)(2,1)S(1)}, bf16[192,512]{1,0:T(8,128)(2,1)S(1)}, u32[]{:S(2)}, u32[]{:S(2)}) collective-permute-start(bf16[192,512]{1,0:T(8,128)(2,1)S(1)} %collective-permute-done.3.a2), channel_id=1, source_target_pairs={{0,16},{16,0},{1,17},{17,1},{2,18},{18,2},{3,19},{19,3},{4,20},{20... | collective-permute-start | bytes 589832 | tf_op jit(solution)/shard_map/ppermute | solution.py:19
  46.4 1.8 %collective-permute-start.9 = (bf16[4,192,256]{2,1,0:T(8,128)(2,1)S(1)}, bf16[4,192,256]{2,1,0:T(8,128)(2,1)S(1)}, u32[]{:S(2)}, u32[]{:S(2)}) collective-permute-start(bf16[4,192,256]{2,1,0:T(8,128)(2,1)S(1)} %get-tuple-element.39), channel_id=1, source_target_pairs={{0,16},{16,0},{1,17},{17,1},{2,18},{18,2},{3,19},{19,3},{4,20},{20... | collective-permute-start | bytes 1179656 | tf_op jit(solution)/shard_map/ppermute | solution.py:19
  48.4 13.0 %collective-permute-start.10 = (bf16[192,384]{1,0:T(8,128)(2,1)S(1)}, bf16[192,384]{1,0:T(8,128)(2,1)S(1)}, u32[]{:S(2)}, u32[]{:S(2)}) collective-permute-start(bf16[192,384]{1,0:T(8,128)(2,1)S(1)} %pad_maximum_fusion.1), channel_id=1, source_target_pairs={{0,96},{32,0},{64,32},{1,97},{33,1},{65,33},{2,98},{34,2},{66,34},... | collective-permute-start | bytes 442376 | tf_op jit(solution)/shard_map/ppermute | solution.py:445
  50.3 11.1 %collective-permute-start.11 = (bf16[192,384]{1,0:T(8,128)(2,1)S(1)}, bf16[192,384]{1,0:T(8,128)(2,1)S(1)}, u32[]{:S(2)}, u32[]{:S(2)}) collective-permute-start(bf16[192,384]{1,0:T(8,128)(2,1)S(1)} %pad_maximum_fusion.2), channel_id=1, source_target_pairs={{0,64},{32,96},{64,0},{1,65},{33,97},{65,1},{2,66},{34,98},{66,2},... | collective-permute-start | bytes 442376 | tf_op jit(solution)/shard_map/ppermute | solution.py:445
  54.6 6.8 %collective-permute-start.12 = (bf16[192,384]{1,0:T(8,128)(2,1)S(1)}, bf16[192,384]{1,0:T(8,128)(2,1)S(1)}, u32[]{:S(2)}, u32[]{:S(2)}) collective-permute-start(bf16[192,384]{1,0:T(8,128)(2,1)S(1)} %pad_maximum_fusion.3), channel_id=1, source_target_pairs={{0,32},{32,64},{64,96},{1,33},{33,65},{65,97},{2,34},{34,66},{66,9... | collective-permute-start | bytes 442376 | tf_op jit(solution)/shard_map/ppermute | solution.py:445
  56.0 6.3 %collective-permute-start.14 = (bf16[192,384]{1,0:T(8,128)(2,1)S(1)}, bf16[192,384]{1,0:T(8,128)(2,1)S(1)}, u32[]{:S(2)}, u32[]{:S(2)}) collective-permute-start(bf16[192,384]{1,0:T(8,128)(2,1)S(1)} %pad_maximum_fusion.after_ref.refs_0_), channel_id=1, source_target_pairs={{0,16},{16,0},{1,17},{17,1},{2,18},{18,2},{3,19},{19,3},{4,20},{20... | collective-permute-start | bytes 442376 | tf_op jit(solution)/shard_map/ppermute | solution.py:19
  61.4 1.5 %collective-permute-start.15 = (bf16[192,384]{1,0:T(8,128)(2,1)S(1)}, bf16[192,384]{1,0:T(8,128)(2,1)S(1)}, u32[]{:S(2)}, u32[]{:S(2)}) collective-permute-start(bf16[192,384]{1,0:T(8,128)(2,1)S(1)} %collective-permute-done.10.refs_1_), channel_id=1, source_target_pairs={{0,16},{16,0},{1,17},{17,1},{2,18},{18,2},{3,19},{19,3},{4,20},{20... | collective-permute-start | bytes 442376 | tf_op jit(solution)/shard_map/ppermute | solution.py:19
  61.8 1.4 %collective-permute-start.16 = (bf16[192,384]{1,0:T(8,128)(2,1)S(1)}, bf16[192,384]{1,0:T(8,128)(2,1)S(1)}, u32[]{:S(2)}, u32[]{:S(2)}) collective-permute-start(bf16[192,384]{1,0:T(8,128)(2,1)S(1)} %collective-permute-done.11.refs_2_), channel_id=1, source_target_pairs={{0,16},{16,0},{1,17},{17,1},{2,18},{18,2},{3,19},{19,3},{4,20},{20... | collective-permute-start | bytes 442376 | tf_op jit(solution)/shard_map/ppermute | solution.py:19
  66.7 14.7 %collective-permute-start.18 = (bf16[4,384,256]{2,1,0:T(8,128)(2,1)S(1)}, bf16[4,384,256]{2,1,0:T(8,128)(2,1)S(1)}, u32[]{:S(2)}, u32[]{:S(2)}) collective-permute-start(bf16[4,384,256]{2,1,0:T(8,128)(2,1)S(1)} %get-tuple-element.48), channel_id=1, source_target_pairs={{0,2},{1,3},{2,0},{3,1},{4,6},{5,7},{6,4},{7,5},{8,10},{9,11},{10,... | collective-permute-start | bytes 2359304 | tf_op jit(solution)/shard_map/ppermute | solution.py:462
  71.7 16.1 %collective-permute-start.19 = (bf16[4,384,256]{2,1,0:T(8,128)(2,1)S(1)}, bf16[4,384,256]{2,1,0:T(8,128)(2,1)S(1)}, u32[]{:S(2)}, u32[]{:S(2)}) collective-permute-start(bf16[4,384,256]{2,1,0:T(8,128)(2,1)S(1)} %back.6), channel_id=1, source_target_pairs={{0,1},{1,2},{2,3},{3,0},{4,5},{5,6},{6,7},{7,4},{8,9},{9,10},{10,1... | collective-permute-start | bytes 2359304 | tf_op jit(solution)/shard_map/ppermute | solution.py:462
  74.2 14.0 %collective-permute-start.20 = (bf16[4,384,256]{2,1,0:T(8,128)(2,1)S(1)}, bf16[4,384,256]{2,1,0:T(8,128)(2,1)S(1)}, u32[]{:S(2)}, u32[]{:S(2)}) collective-permute-start(bf16[4,384,256]{2,1,0:T(8,128)(2,1)S(1)} %back.7), channel_id=1, source_target_pairs={{0,3},{1,0},{2,1},{3,2},{4,7},{5,4},{6,5},{7,6},{8,11},{9,8},{10,9... | collective-permute-start | bytes 2359304 | tf_op jit(solution)/shard_map/ppermute | solution.py:462
  88.5 7.0 %collective-permute-start.21 = (bf16[384,256]{1,0:T(8,128)(2,1)S(1)}, bf16[384,256]{1,0:T(8,128)(2,1)S(1)}, u32[]{:S(2)}, u32[]{:S(2)}) collective-permute-start(bf16[384,256]{1,0:T(8,128)(2,1)S(1)} %get-tuple-element.57), channel_id=1, source_target_pairs={{0,8},{1,9},{2,10},{3,11},{4,12},{5,13},{6,14},{7,15},{8,0},{9,1},... | collective-permute-start | bytes 589832 | tf_op jit(solution)/shard_map/ppermute | solution.py:469
  92.2 6.2 %collective-permute-start.23 = (bf16[384,256]{1,0:T(8,128)(2,1)S(1)}, bf16[384,256]{1,0:T(8,128)(2,1)S(1)}, u32[]{:S(2)}, u32[]{:S(2)}) collective-permute-start(bf16[384,256]{1,0:T(8,128)(2,1)S(1)} %get-tuple-element.58), channel_id=1, source_target_pairs={{0,12},{1,13},{2,14},{3,15},{4,0},{5,1},{6,2},{7,3},{8,4},{9,5},{1... | collective-permute-start | bytes 589832 | tf_op jit(solution)/shard_map/ppermute | solution.py:469
  92.6 5.8 %collective-permute-start.22 = (bf16[384,256]{1,0:T(8,128)(2,1)S(1)}, bf16[384,256]{1,0:T(8,128)(2,1)S(1)}, u32[]{:S(2)}, u32[]{:S(2)}) collective-permute-start(bf16[384,256]{1,0:T(8,128)(2,1)S(1)} %get-tuple-element.59), channel_id=1, source_target_pairs={{0,4},{1,5},{2,6},{3,7},{4,8},{5,9},{6,10},{7,11},{8,12},{9,13},{1... | collective-permute-start | bytes 589832 | tf_op jit(solution)/shard_map/ppermute | solution.py:469
  98.6 4.5 %collective-permute-start.24 = (bf16[192,256]{1,0:T(8,128)(2,1)S(1)}, bf16[192,256]{1,0:T(8,128)(2,1)S(1)}, u32[]{:S(2)}, u32[]{:S(2)}) collective-permute-start(bf16[192,256]{1,0:T(8,128)(2,1)S(1)} %get-tuple-element.69), channel_id=1, source_target_pairs={{0,16},{16,0},{1,17},{17,1},{2,18},{18,2},{3,19},{19,3},{4,20},{20... | collective-permute-start | bytes 294920 | tf_op jit(solution)/shard_map/ppermute | solution.py:19
  (5 other events, 24.2 us)

commit v7 on v6

--- a/solution.py
+++ b/solution.py
@@ -73,7 +73,7 @@
 
 
 def project_kernel(
-    early, where_ref, part_ref, own_hbm, oth_ref, w_ref, w_hbm, own_out, oth_out, half_hbm, a_s, w_s, acc_ref,
+    early, where_ref, part_ref, own_hbm, oth_ref, w_ref, w_hbm, g_ref, own_out, send_out, half_hbm, a_s, w_s, acc_ref,
     own_sem, w_sem, half_sem
 ):
     rows = part_ref.shape[0]
@@ -120,26 +120,33 @@
     for h in range(NH):
         for c in range(3):
             lo = c * NH * HD + h * HD
+            to = slice((h * 3 + c) * HD, (h * 3 + c + 1) * HD)
             x = acc_ref[:, lo : lo + HD].astype(jnp.bfloat16)
-            own_out[h, :, c * HD : (c + 1) * HD] = x[0:rows]
-            oth_out[h, :, c * HD : (c + 1) * HD] = x[rows:]
+            own_out[:, to] = x[0:rows]
+            send_out[:, to] = x[rows:]
+    theirs = pair_head(where_ref[0], side)
+    send_out[:, 9 * HD : 12 * HD] = own_out[:, head_columns(theirs, 3)]
+    send_out[:, 12 * HD :] = g_ref[:, head_columns(theirs, 1)]
     for i in range(chunks):
         put_half(i).wait()
 
 
-def project(where, part, own, other, w_early, w5):
+def project(where, part, own, other, w_early, w5, g):
     rows, depth = own.shape
     chunks = w5.shape[1] // 2
     early = w_early.shape[1] // 2
-    shape = jax.ShapeDtypeStruct((NH, rows, 3 * HD), jnp.bfloat16)
     vmem = pl.BlockSpec(memory_space=pltpu.VMEM)
     hbm = pl.BlockSpec(memory_space=pltpu.HBM)
     dma = pltpu.SemaphoreType.DMA((chunks,))
     return pl.pallas_call(
         functools.partial(project_kernel, early),
-        in_specs=[pl.BlockSpec(memory_space=pltpu.SMEM), vmem, hbm, vmem, vmem, hbm],
+        in_specs=[pl.BlockSpec(memory_space=pltpu.SMEM), vmem, hbm, vmem, vmem, hbm, vmem],
         out_specs=[vmem, vmem, hbm],
-        out_shape=[shape, shape, pltpu.HBM((3,) + w5.shape[1:2] + w5.shape[3:], jnp.bfloat16)],
+        out_shape=[
+            jax.ShapeDtypeStruct((rows, 9 * HD), jnp.bfloat16),
+            jax.ShapeDtypeStruct((rows, 13 * HD), jnp.bfloat16),
+            pltpu.HBM((3,) + w5.shape[1:2] + w5.shape[3:], jnp.bfloat16),
+        ],
         scratch_shapes=[
             pltpu.VMEM((chunks - early, rows, depth // chunks), jnp.bfloat16),
             pltpu.VMEM((3, 2 * (chunks - early)) + w5.shape[2:], jnp.bfloat16),
@@ -151,28 +158,81 @@
         compiler_params=pltpu.CompilerParams(vmem_limit_bytes=26 * MIB),
         cost_estimate=pl.CostEstimate(flops=7 * 10**9, bytes_accessed=10**7, transcendentals=0),
         name="project",
-    )(where, part, own, other, w_early, w5)
+    )(where, part, own, other, w_early, w5, g)
+
+
+def pair_head(chip, core):
+    return jnp.minimum((chip + 1 + 2 * core) % RING, NH - 1)
+
+
+def head_columns(head, width):
+    return pl.ds(pl.multiple_of(head * (width * HD), width * HD), width * HD)
+
+
+def section_rows(mod_ref, block, core):
+    rows = mod_ref.shape[1]
+    mine = (mod_ref[pl.ds(block, 1), :] == core).astype(jnp.float32)
+    row = lax.broadcasted_iota(jnp.int32, (rows, rows), 0)
+    col = lax.broadcasted_iota(jnp.int32, (rows, rows), 1)
+    return jnp.sum(jnp.where(row == col, mine, 0.0), axis=1, keepdims=True)
+
+
+def route_kernel(where_ref, mod_ref, own_ref, sent_ref, got_ref, g_ref, pair_out, far_out, stay_out):
+    chip, core = where_ref[0], where_ref[1]
+    mine = section_rows(mod_ref, 2 * chip + core, core) > 0
+    others = section_rows(mod_ref, 2 * chip + 1 - core, core) > 0
+
+    def own_rows(head):
+        cols = head_columns(head, 3)
+        return jnp.where(mine, own_ref[:, cols], got_ref[:, cols]), g_ref[:, head_columns(head, 1)]
+
+    head = pair_head(chip, core)
+    pair_out[0, :, : 3 * HD], pair_out[0, :, 3 * HD :] = own_rows(head)
+    pair_out[1, :, : 3 * HD] = jnp.where(others, sent_ref[:, head_columns(head, 3)], got_ref[:, 9 * HD : 12 * HD])
+    pair_out[1, :, 3 * HD :] = got_ref[:, 12 * HD :]
+    far_out[:, : 3 * HD], far_out[:, 3 * HD :] = own_rows(jnp.minimum((chip + 2) % RING, NH - 1))
+    stay_out[:, : 3 * HD], stay_out[:, 3 * HD :] = own_rows(jnp.minimum(chip, NH - 1))
+
+
+def small_call(kernel, name, where, operands, out_shape):
+    vmem = pl.BlockSpec(memory_space=pltpu.VMEM)
+    return pl.pallas_call(
+        kernel,
+        in_specs=[pl.BlockSpec(memory_space=pltpu.SMEM)] + [vmem] * len(operands),
+        out_specs=[vmem] * len(out_shape),
+        out_shape=out_shape,
+        compiler_params=pltpu.CompilerParams(vmem_limit_bytes=16 * MIB),
+        cost_estimate=pl.CostEstimate(flops=10**6, bytes_accessed=3 * 10**6, transcendentals=0),
+        name=name,
+    )(where, *operands)
 
 
 def attention_kernel(
-    where_ref, a0, a1, a2, a3, b0, b1, b2, b3, own_ref, oth_ref, q_s, g_s, k_s, v_s, dk_s, dv_s
+    where_ref, stay, far, pair, stay_o, far_o, pair_o, keep_ref, send_ref, q_s, g_s, k_s, v_s, dq_s, dk_s, dv_s
 ):
     chip = where_ref[0]
     core = where_ref[1]
-    rows = a0.shape[0]
+    rows = stay.shape[0]
     both = 2 * rows
-    own = (a0, a1, a2, a3)
-    oth = (b0, b1, b2, b3)
-    for k, (r, o) in enumerate(zip(own, oth)):
-        shard = (chip - k + RING) % RING
+    near = (chip + 3 + 2 * core) % RING
+    across = (chip + 1 + 2 * core) % RING
+    opposite = (chip + 2) % RING
+
+    def block_rows(shard, side):
+        return pl.ds(pl.multiple_of((2 * shard + side) * rows, rows), rows)
+
+    for shard, r, o in (
+        (chip, stay, stay_o),
+        (opposite, far, far_o),
+        (near, pair.at[0], pair.at[1]),
+        (across, pair_o.at[1], pair_o.at[0]),
+    ):
         q_s[shard] = r[:, 0:HD]
         g_s[shard] = r[:, 3 * HD : 4 * HD]
-        mine = pl.ds(pl.multiple_of((2 * shard + core) * rows, rows), rows)
-        other = pl.ds(pl.multiple_of((2 * shard + 1 - core) * rows, rows), rows)
-        k_s[mine, :] = r[:, HD : 2 * HD]
-        v_s[mine, :] = r[:, 2 * HD : 3 * HD]
-        k_s[other, :] = o[:, HD : 2 * HD]
-        v_s[other, :] = o[:, 2 * HD : 3 * HD]
+        k_s[block_rows(shard, core), :] = r[:, HD : 2 * HD]
+        v_s[block_rows(shard, core), :] = r[:, 2 * HD : 3 * HD]
+        k_s[block_rows(shard, 1 - core), :] = o[:, HD : 2 * HD]
+        v_s[block_rows(shard, 1 - core), :] = o[:, 2 * HD : 3 * HD]
     nt = (((1,), (1,)), ((), ()))
     tn = (((0,), (0,)), ((), ()))
     for s in range(RING - 1, -1, -1):
@@ -200,55 +260,85 @@
         else:
             dk_s[0:width, :] += dk
             dv_s[0:width, :] += dv
-        own_ref[(chip - s + RING) % RING, :, 0:HD] = dq
-    for k in range(RING):
-        shard = (chip - k + RING) % RING
-        mine = pl.ds(pl.multiple_of((2 * shard + core) * rows, rows), rows)
-        other = pl.ds(pl.multiple_of((2 * shard + 1 - core) * rows, rows), rows)
-        own_ref[k, :, HD : 2 * HD] = dk_s[mine, :]
-        own_ref[k, :, 2 * HD : 3 * HD] = dv_s[mine, :]
-        oth_ref[k, :, 0:HD] = dk_s[other, :].astype(jnp.bfloat16)
-        oth_ref[k, :, HD : 2 * HD] = dv_s[other, :].astype(jnp.bfloat16)
-
-
-def attention(where, parts, others):
+        dq_s[s] = dq
+    col = 0
+    for shard, whole in ((near, True), (near, False), (chip, True), (opposite, True)):
+        if whole:
+            keep_ref[:, col : col + HD] = dq_s[shard]
+            col += HD
+        side = core if whole else 1 - core
+        keep_ref[:, col : col + HD] = dk_s[block_rows(shard, side), :]
+        keep_ref[:, col + HD : col + 2 * HD] = dv_s[block_rows(shard, side), :]
+        col += 2 * HD
+    col = 0
+    for shard, whole in ((across, True), (across, False), (chip, False), (opposite, False)):
+        if whole:
+            send_ref[:, col : col + HD] = dq_s[shard].astype(jnp.bfloat16)
+            col += HD
+        side = core if whole else 1 - core
+        send_ref[:, col : col + HD] = dk_s[block_rows(shard, side), :].astype(jnp.bfloat16)
+        send_ref[:, col + HD : col + 2 * HD] = dv_s[block_rows(shard, side), :].astype(jnp.bfloat16)
+        col += 2 * HD
+
+
+def attention(where, parts):
     rows = parts[0].shape[0]
     total = 2 * RING * rows
     vmem = pl.BlockSpec(memory_space=pltpu.VMEM)
     return pl.pallas_call(
         attention_kernel,
-        in_specs=[pl.BlockSpec(memory_space=pltpu.SMEM)] + [vmem] * 8,
+        in_specs=[pl.BlockSpec(memory_space=pltpu.SMEM)] + [vmem] * 6,
         out_specs=[vmem, vmem],
         out_shape=[
-            jax.ShapeDtypeStruct((RING, rows, 3 * HD), jnp.float32),
-            jax.ShapeDtypeStruct((RING, rows, 2 * HD), jnp.bfloat16),
+            jax.ShapeDtypeStruct((rows, 11 * HD), jnp.float32),
+            jax.ShapeDtypeStruct((rows, 9 * HD), jnp.bfloat16),
         ],
         scratch_shapes=[
             pltpu.VMEM((RING, rows, HD), jnp.bfloat16),
             pltpu.VMEM((RING, rows, HD), jnp.bfloat16),
             pltpu.VMEM((total, HD), jnp.bfloat16),
             pltpu.VMEM((total, HD), jnp.bfloat16),
+            pltpu.VMEM((RING, rows, HD), jnp.float32),
             pltpu.VMEM((total, HD), jnp.float32),
             pltpu.VMEM((total, HD), jnp.float32),
         ],
         compiler_params=pltpu.CompilerParams(vmem_limit_bytes=32 * MIB),
         cost_estimate=pl.CostEstimate(flops=10**9, bytes_accessed=4 * 10**6, transcendentals=10**6),
         name="attention",
-    )(where, *parts, *others)
-
-
-def gather(chip, mask_ref, own, oth, out_ref):
-    rows = own[0].shape[0]
-    for k in range(RING):
-        head = (chip + k) % RING
+    )(where, *parts)
+
+
+def combine_kernel(where_ref, keep, got, pair_out, far_out, stay_out):
+    def put(out, query, kept, partner):
+        out[:, 0:HD] = query.astype(jnp.bfloat16)
+        kv = keep[:, kept : kept + 2 * HD] + got[:, partner : partner + 2 * HD].astype(jnp.float32)
+        out[:, HD : 3 * HD] = kv.astype(jnp.bfloat16)
+
+    put(pair_out.at[0], keep[:, 0:HD], HD, 3 * HD)
+    put(pair_out.at[1], got[:, 0:HD], 3 * HD, HD)
+    put(stay_out, keep[:, 5 * HD : 6 * HD], 6 * HD, 5 * HD)
+    put(far_out, keep[:, 8 * HD : 9 * HD], 9 * HD, 7 * HD)
+
+
+def gather(where, mod_ref, parts, out_ref):
+    chip, core = where
+    stay, far, pair, stay_o, far_o, pair_o = parts
+    rows = stay.shape[0]
+    mine = [section_rows(mod_ref, 2 * chip + core, core), section_rows(mod_ref, 2 * chip + 1 - core, core)]
+    for head, refs in (
+        (chip, (stay, stay_o)),
+        ((chip + 2) % RING, (far, far_o)),
+        ((chip + 1 + 2 * core) % RING, (pair.at[0], pair.at[1])),
+        ((chip + 3 + 2 * core) % RING, (pair_o.at[1], pair_o.at[0])),
+    ):
 
         @pl.when(head < NH)
         def _():
-            for block, x_ref in enumerate((own[k], oth[k])):
+            for block, x_ref in enumerate(refs):
                 x = x_ref[...]
                 zero = jnp.zeros_like(x)
                 for side in range(2):
-                    kept = jnp.where(mask_ref[block] == 1 - side, x, zero)
+                    kept = jnp.where(mine[block] == 1.0 - side, x, zero)
                     for c in range(3):
                         lo = pl.multiple_of(((side * 3 + c) * NH + head) * HD, HD)
                         out_ref[block * rows : (block + 1) * rows, pl.ds(lo, HD)] = kept[:, c * HD : (c + 1) * HD]
@@ -300,11 +390,11 @@
         out_ref[j + i] = res[:, i * cols : (i + 1) * cols]
 
 
-def back_first_kernel(following, place_ref, mask_ref, *refs):
+def back_first_kernel(following, place_ref, mod_ref, *refs):
     *parts, w_ref, own_hbm, other_hbm, out_ref, g_ref, next_ref, sem = refs
     for copy in weight_copies(place_ref, own_hbm, other_hbm, next_ref, sem, following):
         copy.start()
-    gather(place_ref[RING * RING + 1], mask_ref, parts[:RING], parts[RING:], g_ref)
+    gather((place_ref[RING * RING + 1], place_ref[RING * RING]), mod_ref, parts, g_ref)
     product(g_ref, w_ref, out_ref, 0, RING)
     for copy in weight_copies(place_ref, own_hbm, other_hbm, next_ref, sem, following):
         copy.wait()
@@ -338,8 +428,8 @@
     )(*operands)
 
 
-def back_products(place, masks, own, oth, weights, w5, other_half, send):
-    rows = 2 * own[0].shape[0]
+def back_products(place, mod, parts, weights, w5, other_half, send):
+    rows = 2 * parts[0].shape[0]
     cols = w5.shape[3]
     smem = pl.BlockSpec(memory_space=pltpu.SMEM)
     vmem = pl.BlockSpec(memory_space=pltpu.VMEM)
@@ -351,8 +441,8 @@
     w_two, w_one = weights
     x, g, w_three = back_call(
         functools.partial(back_first_kernel, 3),
-        (place, masks, *own, *oth, w_two, w5, other_half),
-        [smem] + [vmem] * 10 + [hbm, anywhere],
+        (place, mod, *parts, w_two, w5, other_half),
+        [smem] + [vmem] * 8 + [hbm, anywhere],
         [piece, pltpu.VMEM((rows, 18 * HD), jnp.bfloat16), pltpu.VMEM(w_shape, jnp.bfloat16)],
         [sem],
     )
@@ -387,6 +477,18 @@
     return pairs
 
 
+def pair_perm(step):
+    pairs = []
+    for s in range(RING):
+        for m in range(2):
+            head = (s + (1 if m == 0 else -1)) % RING
+            if step > 0 and head < NH:
+                pairs.append((2 * s + m, 2 * head + m))
+            if step < 0 and s < NH:
+                pairs.append((2 * s + m, 2 * ((s + (-1 if m == 0 else 1)) % RING) + m))
+    return pairs
+
+
 def per_device(activations, grad_attn, weights, modality):
     rows, depth = activations.shape
     chip = lax.axis_index("seq")
@@ -397,35 +499,29 @@
     cols = depth // dests // 2
     w5 = jnp.transpose(weights[0], (1, 0, 2)).reshape(3, dests, 2, cols, NH * HD)
 
-    own_mod = lax.dynamic_slice_in_dim(modality, (2 * chip + core) * rows, rows)
-    other_mod = lax.dynamic_slice_in_dim(modality, (2 * chip + 1 - core) * rows, rows)
-    masks = (jnp.stack([own_mod, other_mod]) == core).astype(jnp.int32)[:, :, None]
-
+    mod = modality.reshape(2 * RING, rows)
     w5 = pltpu.with_memory_space_constraint(w5, pltpu.HBM)
     activations = pltpu.with_memory_space_constraint(activations, pltpu.HBM)
-    g_heads = grad_attn.reshape(rows, NH, HD).transpose(1, 0, 2)
-    is_mine = jnp.broadcast_to(masks[0], (rows, HD))
-    where, masks, is_mine, g_heads = lax.optimization_barrier((where, masks, is_mine, g_heads))
     act_other = pltpu.with_memory_space_constraint(core_swap(activations), pltpu.VMEM)
     part, w_early = project_own(activations, w5, 4)
     w_early = pltpu.with_memory_space_constraint(w_early, pltpu.VMEM)
-    proj_own, proj_other, half = project(where, part, activations, act_other, w_early, w5)
-    proj_back = core_swap(proj_other)
-    proj_back, half = lax.optimization_barrier((proj_back, half))
+    proj_own, sent, half = project(where, part, activations, act_other, w_early, w5, grad_attn)
+    got = core_swap(sent)
+    got, half = lax.optimization_barrier((got, half))
     other_half = core_swap(half)
-    heads = jnp.concatenate([jnp.where(jnp.concatenate([is_mine] * 3, axis=1)[None] > 0, proj_own, proj_back), g_heads], axis=2)
-
-    parts = [None] * RING
-    others = [None] * RING
-    for hop in (2, 1, 3, 0):
-        head = jnp.minimum((chip + hop) % RING, NH - 1)
-        x = lax.dynamic_index_in_dim(heads, head, 0, keepdims=False)
-        if hop:
-            x = lax.ppermute(x, "seq", [(i, (i + hop) % RING) for i in range(RING) if (i + hop) % RING < NH])
-        parts[hop] = x
-        others[hop] = core_swap(x)
-    own, oth = attention(where, parts, others)
-    from_other = core_swap(oth)
+
+    def part_shapes(width):
+        block = jax.ShapeDtypeStruct((rows, width), jnp.bfloat16)
+        return [jax.ShapeDtypeStruct((2, rows, width), jnp.bfloat16), block, block]
+
+    pair, far, stay = small_call(
+        route_kernel, "route", where, (mod, proj_own, sent, got, grad_attn), part_shapes(4 * HD)
+    )
+    pair = lax.ppermute(pair, ("seq", "mod"), pair_perm(1))
+    far = lax.ppermute(far, "seq", [(i, (i + 2) % RING) for i in range(RING) if (i + 2) % RING < NH])
+    parts = [stay, far, pair]
+    keep, send = attention(where, parts + [core_swap(x) for x in parts])
+    pair, far, stay = small_call(combine_kernel, "combine", where, (keep, core_swap(send)), part_shapes(3 * HD))
 
     i = jnp.arange(dests, dtype=jnp.int32) // RING
     j = jnp.arange(dests, dtype=jnp.int32) % RING
@@ -437,25 +533,18 @@
     )
     place = jnp.concatenate([place, jnp.stack([core, chip])]).astype(jnp.int32)
 
-    grads = [None] * RING
-    for hop in (2, 1, 3, 0):
-        kv = own[hop, :, HD:] + from_other[hop].astype(jnp.float32)
-        x = jnp.concatenate([own[hop, :, :HD], kv], axis=1).astype(jnp.bfloat16)
-        if hop:
-            x = lax.ppermute(x, "seq", [(i, (i - hop) % RING) for i in range(NH)])
-        grads[hop] = x
-    w_first = fetch_weights(place, grads[0], w5, other_half, (2, 1))
+    w_first = fetch_weights(place, stay, w5, other_half, (2, 1))
     w_first = [pltpu.with_memory_space_constraint(w, pltpu.VMEM) for w in w_first]
-    grads[1:], w_first = lax.optimization_barrier((grads[1:], w_first))
-    other_grads = [None] * RING
-    for hop in (2, 1, 3, 0):
-        other_grads[hop] = core_swap(grads[hop])
+    pair = lax.ppermute(pair, ("seq", "mod"), pair_perm(-1))
+    far = lax.ppermute(far, "seq", [(i, (i + 2) % RING) for i in range(NH)])
+    pair, far, w_first = lax.optimization_barrier((pair, far, w_first))
+    parts = [stay, far, pair]
+    parts += [core_swap(x) for x in parts]
 
     pieces = back_products(
         place,
-        masks,
-        grads,
-        other_grads,
+        mod,
+        parts,
         w_first,
         w5,
         other_half,

time: 104 us -> 101 us (0.971)
  starting transfers between devices: 40.7 us -> 38.1 us
  other arithmetic: 4.42 us -> 1.87 us
  Pallas kernels: 35.7 us -> 37 us
    ppermute x6 -> x4, starting transfers between devices: 15.7 us -> 11.5 us  [the longest x1 5.61 us: per_device(): lax.ppermute(far, 'seq', [(i, (i + 2) % RING) for i in range(RING) if (i...]
    unnamed x8 -> x12, local copies, waits for them, and re-layouts: 0.79 us -> 3.7 us
    ppermute x13 -> x11, starting transfers between devices: 13.8 us -> 15.4 us  [core_swap(): return lax.ppermute(x, 'mod', [(0, 1), (1, 0)])]
    pallas_call x0 -> x2, Pallas kernels: none -> 1.35 us  [small_call(): pl.pallas_call(kernel, in_specs=[pl.BlockSpec(memory_space=pltpu.SMEM)] +...]
    select_n x1 -> x0, other arithmetic: 1.1 us -> none  [per_device(): jnp.where(jnp.concatenate([is_mine] * 3, axis=1)[None] > 0, proj_own, pro...]
    gt x1 -> x0, other arithmetic: 1.08 us -> none  [per_device(): jnp.concatenate([is_mine] * 3, axis=1)[None] > 0]
    ppermute x6 -> x4, waiting for transfers between devices: 1.64 us -> 2.28 us  [the longest x1 1.9 us: per_device(): pair = lax.ppermute(pair, ('seq', 'mod'), pair_perm(1))]
    ppermute x13 -> x11, waiting for transfers between devices: 6.58 us -> 6.12 us  [core_swap(): return lax.ppermute(x, 'mod', [(0, 1), (1, 0)])]
  transfers between devices with their start and end apart: 25 -> 21, of which waited for: 13 -> 14; matrix products, arithmetic and copies ran while one was open for 6% -> 1% of each run, Pallas kernels for 22% -> 24%
where the time goes in v7:
time: 101 us
  starting transfers between devices  38.1 us (38%)
  Pallas kernels  37 us (37%)
  waiting for transfers between devices  19.6 us (19%)
  local copies, waits for them, and re-layouts  3.83 us (4%)
  other arithmetic  1.87 us (2%)
    ppermute x11, starting transfers between devices, core_swap(): return lax.ppermute(x, 'mod', [(0, 1), (1, 0)])  15.4 us
    pallas_call x4, Pallas kernels, back_call(): pl.pallas_call(kernel, in_specs=in_specs, out_specs=[vmem] * len(out_shap...  11.7 us
    pallas_call x1, Pallas kernels, project(): pl.pallas_call(functools.partial(project_kernel, early), in_specs=[pl.Blo...  9.86 us
    ppermute x3, waiting for transfers between devices, per_device(): lax.ppermute(x, AXES, ring_perm(True, hop))  6.38 us
    ppermute x11, waiting for transfers between devices, core_swap(): return lax.ppermute(x, 'mod', [(0, 1), (1, 0)])  6.12 us
    ppermute x3, starting transfers between devices, per_device(): lax.ppermute(x, AXES, ring_perm(True, hop))  6.03 us
    ppermute x1, starting transfers between devices, per_device(): lax.ppermute(far, 'seq', [(i, (i + 2) % RING) for i in range(RING) if (i...  5.61 us
    ppermute x3, starting transfers between devices, per_device(): lax.ppermute(total[hop].astype(jnp.bfloat16), AXES, ring_perm(False, hop))  5.14 us
  transfers between devices with their start and end apart: 21, of which 14 were waited for; matrix products, arithmetic and copies ran while one was open for 1% of the time, Pallas kernels for 24%

profile of v7, /device:TPU:1, one launch (start us, length us, event | category | flops | bytes accessed | tf_op | source)
XLA Modules:
  0.0 100.6 jit_solution(1929328090598532554)
XLA Ops:
  0.0 1.4 %collective-permute-start = (bf16[192,8192]{1,0:T(8,128)(2,1)}, bf16[192,8192]{1,0:T(8,128)(2,1)S(1)}, u32[]{:S(2)}, u32[]{:S(2)}) collective-permute-start(bf16[192,8192]{1,0:T(8,128)(2,1)} %own_hbm.1), channel_id=1, source_target_pairs={{0,16},{16,0},{1,17},{17,1},{2,18},{18,2},{3,19},{19,3},{4,20},{20... | collective-permute-start | bytes 9437192 | tf_op jit(solution)/shard_map/ppermute | solution.py:19
  1.5 5.0 %project_own.1 = (f32[192,1152]{1,0:T(8,128)S(1)}, bf16[3,8,2,256,384]{4,3,2,1,0:T(8,128)(2,1)S(1)}) custom-call(bf16[192,8192]{1,0:T(8,128)(2,1)} %own_hbm.1, bf16[3,16,2,256,384]{4,3,2,1,0:T(8,128)(2,1)} %bitcast.23), custom_call_target="tpu_custom_call" | custom-call | flops 4000000000 | bytes 10000000 | tf_op jit(solution)/shard_map/project_own/pallas_call | solution.py:56
  6.9 9.9 %project.1 = (bf16[192,1152]{1,0:T(8,128)(2,1)S(1)}, bf16[192,1664]{1,0:T(8,128)(2,1)S(1)}, bf16[3,16,256,384]{3,2,1,0:T(8,128)(2,1)}) custom-call(s32[2]{0:T(128)S(1)} %pad_add_fusion.1.where_ref, f32[192,1152]{1,0:T(8,128)S(1)} %get-tuple-element.29.part_ref, bf16[192,8192]{1,0:T(8,128)(2,1)} %own_hbm.1, ...), custom_call_target="tpu_custom_call" | custom-call | flops 7000000000 | bytes 10000000 | tf_op jit(solution)/shard_map/project/pallas_call | solution.py:141
  22.9 1.3 %collective-permute-start.3 = (bf16[2,192,512]{2,1,0:T(8,128)(2,1)S(1)}, bf16[2,192,512]{2,1,0:T(8,128)(2,1)S(1)}, u32[]{:S(2)}, u32[]{:S(2)}) collective-permute-start(bf16[2,192,512]{2,1,0:T(8,128)(2,1)S(1)} %get-tuple-element.37), channel_id=1, source_target_pairs={{0,32},{32,64},{48,16},{80,48},{96,0},{112,80},{1,33},{33,65},{49,... | collective-permute-start | bytes 1179656 | tf_op jit(solution)/shard_map/ppermute | solution.py:520
  24.2 5.6 %collective-permute-start.2 = (bf16[192,512]{1,0:T(8,128)(2,1)S(1)}, bf16[192,512]{1,0:T(8,128)(2,1)S(1)}, u32[]{:S(2)}, u32[]{:S(2)}) collective-permute-start(bf16[192,512]{1,0:T(8,128)(2,1)S(1)} %get-tuple-element.36), channel_id=1, source_target_pairs={{0,64},{64,0},{96,32},{1,65},{65,1},{97,33},{2,66},{66,2},{98,34},... | collective-permute-start | bytes 589832 | tf_op jit(solution)/shard_map/ppermute | solution.py:521
  29.8 1.9 %collective-permute-done.3.pair = bf16[2,192,512]{2,1,0:T(8,128)(2,1)S(1)} collective-permute-done((bf16[2,192,512]{2,1,0:T(8,128)(2,1)S(1)}, bf16[2,192,512]{2,1,0:T(8,128)(2,1)S(1)}, u32[]{:S(2)}, u32[]{:S(2)}) %collective-permute-start.3) | collective-permute-done | bytes 393248 | tf_op jit(solution)/shard_map/ppermute | solution.py:520
  31.7 6.4 %collective-permute-start.6 = (bf16[2,192,512]{2,1,0:T(8,128)(2,1)S(1)}, bf16[2,192,512]{2,1,0:T(8,128)(2,1)S(1)}, u32[]{:S(2)}, u32[]{:S(2)}) collective-permute-start(bf16[2,192,512]{2,1,0:T(8,128)(2,1)S(1)} %collective-permute-done.3.pair), channel_id=1, source_target_pairs={{0,16},{16,0},{1,17},{17,1},{2,18},{18,2},{3,19},{19,3},{4,20},{20... | collective-permute-start | bytes 1179656 | tf_op jit(solution)/shard_map/ppermute | solution.py:19
  40.1 4.7 %attention.1 = (f32[192,1408]{1,0:T(8,128)S(1)}, bf16[192,1152]{1,0:T(8,128)(2,1)S(1)}) custom-call(s32[2]{0:T(128)S(1)} %pad_add_fusion.1.where_ref, bf16[192,512]{1,0:T(8,128)(2,1)S(1)} %get-tuple-element.35.stay, bf16[192,512]{1,0:T(8,128)(2,1)S(1)} %collective-permute-done.2.far, bf16[2,192,512]{2,1,0:T(8,128)(2,1)S(1)} %collective-permute-done.3.pair, ...), custom_call_target="tpu_custom_call" | custom-call | flops 1000000000 | bytes 4000000 | tf_op jit(solution)/shard_map/attention/pallas_call | solution.py:288
  45.3 1.4 %collective-permute-done.7.got = bf16[192,1152]{1,0:T(8,128)(2,1)S(1)} collective-permute-done((bf16[192,1152]{1,0:T(8,128)(2,1)S(1)}, bf16[192,1152]{1,0:T(8,128)(2,1)S(1)}, u32[]{:S(2)}, u32[]{:S(2)}) %collective-permute-start.7) | collective-permute-done | bytes 442400 | tf_op jit(solution)/shard_map/ppermute | solution.py:19
  47.3 1.5 %collective-permute-start.8 = (bf16[2,192,384]{2,1,0:T(8,128)(2,1)S(1)}, bf16[2,192,384]{2,1,0:T(8,128)(2,1)S(1)}, u32[]{:S(2)}, u32[]{:S(2)}) collective-permute-start(bf16[2,192,384]{2,1,0:T(8,128)(2,1)S(1)} %get-tuple-element.41), channel_id=1, source_target_pairs={{0,96},{16,48},{32,0},{48,80},{64,32},{80,112},{1,97},{17,49},{33,... | collective-permute-start | bytes 884744 | tf_op jit(solution)/shard_map/ppermute | solution.py:538
  48.8 3.1 %collective-permute-start.9 = (bf16[192,384]{1,0:T(8,128)(2,1)S(1)}, bf16[192,384]{1,0:T(8,128)(2,1)S(1)}, u32[]{:S(2)}, u32[]{:S(2)}) collective-permute-start(bf16[192,384]{1,0:T(8,128)(2,1)S(1)} %get-tuple-element.42), channel_id=1, source_target_pairs={{0,64},{32,96},{64,0},{1,65},{33,97},{65,1},{2,66},{34,98},{66,2},... | collective-permute-start | bytes 442376 | tf_op jit(solution)/shard_map/ppermute | solution.py:539
  52.1 4.4 %fetch_weights.1 = (bf16[2,3,4,256,384]{4,3,2,1,0:T(8,128)(2,1)S(1)}, bf16[2,3,4,256,384]{4,3,2,1,0:T(8,128)(2,1)S(1)}) custom-call(s32[18]{0:T(128)S(1)} %pad_add_fusion.place_ref, bf16[192,384]{1,0:T(8,128)(2,1)S(1)} %get-tuple-element.40.after_ref.refs_0_, bf16[3,16,2,256,384]{4,3,2,1,0:T(8,128)(2,1)} %bitcast.25, ...), custom_call_target="tpu_custom_call" | custom-call | flops 1000000 | bytes 10000000 | tf_op jit(solution)/shard_map/fetch_weights/pallas_call | solution.py:371
  56.8 1.7 %collective-permute-start.13 = (bf16[2,192,384]{2,1,0:T(8,128)(2,1)S(1)}, bf16[2,192,384]{2,1,0:T(8,128)(2,1)S(1)}, u32[]{:S(2)}, u32[]{:S(2)}) collective-permute-start(bf16[2,192,384]{2,1,0:T(8,128)(2,1)S(1)} %collective-permute-done.8.refs_2_), channel_id=1, source_target_pairs={{0,16},{16,0},{1,17},{17,1},{2,18},{18,2},{3,19},{19,3},{4,20},{20... | collective-permute-start | bytes 884744 | tf_op jit(solution)/shard_map/ppermute | solution.py:19
  60.1 3.2 %back.4 = (bf16[4,384,256]{2,1,0:T(8,128)(2,1)S(1)}, bf16[384,2304]{1,0:T(8,128)(2,1)S(1)}, bf16[2,3,4,256,384]{4,3,2,1,0:T(8,128)(2,1)S(1)}) custom-call(s32[18]{0:T(128)S(1)} %pad_add_fusion.place_ref, s32[8,192]{1,0:T(8,128)S(1)} %reshape.9.mod_ref, bf16[192,384]{1,0:T(8,128)(2,1)S(1)} %get-tuple-element.40.after_ref.refs_0_, ...), custom_call_target="tpu_custom_call" | custom-call | flops 1000000 | bytes 10000 | tf_op jit(solution)/shard_map/back/pallas_call | solution.py:419
  63.4 3.0 %collective-permute-start.14 = (bf16[4,384,256]{2,1,0:T(8,128)(2,1)S(1)}, bf16[4,384,256]{2,1,0:T(8,128)(2,1)S(1)}, u32[]{:S(2)}, u32[]{:S(2)}) collective-permute-start(bf16[4,384,256]{2,1,0:T(8,128)(2,1)S(1)} %get-tuple-element.50), channel_id=1, source_target_pairs={{0,2},{1,3},{2,0},{3,1},{4,6},{5,7},{6,4},{7,5},{8,10},{9,11},{10,... | collective-permute-start | bytes 2359304 | tf_op jit(solution)/shard_map/ppermute | solution.py:551
  66.4 2.0 %back.6 = bf16[4,384,256]{2,1,0:T(8,128)(2,1)S(1)} custom-call(bf16[384,2304]{1,0:T(8,128)(2,1)S(1)} %get-tuple-element.49.g_ref, bf16[2,3,4,256,384]{4,3,2,1,0:T(8,128)(2,1)S(1)} %get-tuple-element.51.w_ref), custom_call_target="tpu_custom_call" | custom-call | flops 1000000 | bytes 10000 | tf_op jit(solution)/shard_map/back/pallas_call | solution.py:419
  68.9 2.0 %back.7 = bf16[4,384,256]{2,1,0:T(8,128)(2,1)S(1)} custom-call(bf16[384,2304]{1,0:T(8,128)(2,1)S(1)} %get-tuple-element.49.g_ref, bf16[2,3,4,256,384]{4,3,2,1,0:T(8,128)(2,1)S(1)} %get-tuple-element.52.w_ref), custom_call_target="tpu_custom_call" | custom-call | flops 1000000 | bytes 10000 | tf_op jit(solution)/shard_map/back/pallas_call | solution.py:419
  70.9 2.6 %collective-permute-start.16 = (bf16[4,384,256]{2,1,0:T(8,128)(2,1)S(1)}, bf16[4,384,256]{2,1,0:T(8,128)(2,1)S(1)}, u32[]{:S(2)}, u32[]{:S(2)}) collective-permute-start(bf16[4,384,256]{2,1,0:T(8,128)(2,1)S(1)} %back.7), channel_id=1, source_target_pairs={{0,3},{1,0},{2,1},{3,2},{4,7},{5,4},{6,5},{7,6},{8,11},{9,8},{10,9... | collective-permute-start | bytes 2359304 | tf_op jit(solution)/shard_map/ppermute | solution.py:551
  73.5 4.4 %back.5 = bf16[4,384,256]{2,1,0:T(8,128)(2,1)S(1)} custom-call(s32[18]{0:T(128)S(1)} %pad_add_fusion.place_ref, bf16[384,2304]{1,0:T(8,128)(2,1)S(1)} %get-tuple-element.49.g_ref, bf16[3,16,2,256,384]{4,3,2,1,0:T(8,128)(2,1)} %bitcast.27, bf16[3,16,256,384]{3,2,1,0:T(8,128)(2,1)} %collective-permute-done.10.other_hbm.refs_8_), custom_call_target="tpu_custom_call" | custom-call | flops 1000000 | bytes 10000 | tf_op jit(solution)/shard_map/back/pallas_call | solution.py:419
  78.3 6.3 %collective-permute-done.15 = bf16[4,384,256]{2,1,0:T(8,128)(2,1)S(1)} collective-permute-done((bf16[4,384,256]{2,1,0:T(8,128)(2,1)S(1)}, bf16[4,384,256]{2,1,0:T(8,128)(2,1)S(1)}, u32[]{:S(2)}, u32[]{:S(2)}) %collective-permute-start.15) | collective-permute-done | bytes 786464 | tf_op jit(solution)/shard_map/ppermute | solution.py:551
  85.2 3.7 %collective-permute-start.17 = (bf16[384,256]{1,0:T(8,128)(2,1)S(1)}, bf16[384,256]{1,0:T(8,128)(2,1)S(1)}, u32[]{:S(2)}, u32[]{:S(2)}) collective-permute-start(bf16[384,256]{1,0:T(8,128)(2,1)S(1)} %get-tuple-element.55), channel_id=1, source_target_pairs={{0,8},{1,9},{2,10},{3,11},{4,12},{5,13},{6,14},{7,15},{8,0},{9,1},... | collective-permute-start | bytes 589832 | tf_op jit(solution)/shard_map/ppermute | solution.py:558
  90.3 1.9 %collective-permute-done.17 = bf16[384,256]{1,0:T(8,128)(2,1)S(1)} collective-permute-done((bf16[384,256]{1,0:T(8,128)(2,1)S(1)}, bf16[384,256]{1,0:T(8,128)(2,1)S(1)}, u32[]{:S(2)}, u32[]{:S(2)}) %collective-permute-start.17) | collective-permute-done | bytes 196640 | tf_op jit(solution)/shard_map/ppermute | solution.py:558
  92.2 2.9 %collective-permute-done.19 = bf16[384,256]{1,0:T(8,128)(2,1)S(1)} collective-permute-done((bf16[384,256]{1,0:T(8,128)(2,1)S(1)}, bf16[384,256]{1,0:T(8,128)(2,1)S(1)}, u32[]{:S(2)}, u32[]{:S(2)}) %collective-permute-start.19) | collective-permute-done | bytes 196640 | tf_op jit(solution)/shard_map/ppermute | solution.py:558
  95.3 3.6 %collective-permute-start.20 = (bf16[192,256]{1,0:T(8,128)(2,1)S(1)}, bf16[192,256]{1,0:T(8,128)(2,1)S(1)}, u32[]{:S(2)}, u32[]{:S(2)}) collective-permute-start(bf16[192,256]{1,0:T(8,128)(2,1)S(1)} %get-tuple-element.59), channel_id=1, source_target_pairs={{0,16},{16,0},{1,17},{17,1},{2,18},{18,2},{3,19},{19,3},{4,20},{20... | collective-permute-start | bytes 294920 | tf_op jit(solution)/shard_map/ppermute | solution.py:19
  (52 shorter events, 16.4 us)
Async XLA Ops:
  0.0 6.9 %collective-permute-start = (bf16[192,8192]{1,0:T(8,128)(2,1)}, bf16[192,8192]{1,0:T(8,128)(2,1)S(1)}, u32[]{:S(2)}, u32[]{:S(2)}) collective-permute-start(bf16[192,8192]{1,0:T(8,128)(2,1)} %own_hbm.1), channel_id=1, source_target_pairs={{0,16},{16,0},{1,17},{17,1},{2,18},{18,2},{3,19},{19,3},{4,20},{20... | collective-permute-start | bytes 9437192 | tf_op jit(solution)/shard_map/ppermute | solution.py:19
  1.5 5.4 %copy-start.2 = (bf16[192,384]{1,0:T(8,128)(2,1)S(1)}, bf16[192,384]{1,0:T(8,128)(2,1)}, u32[]{:S(2)}) copy-start(bf16[192,384]{1,0:T(8,128)(2,1)} %g_ref.3) | copy-start | bytes 442372
  6.9 13.1 %copy-start.5 = (s32[1536]{0:T(1024)S(1)}, s32[1536]{0:T(1024)}, u32[]{:S(2)}) copy-start(s32[1536]{0:T(1024)} %param.7) | copy-start | bytes 18436
  17.6 2.1 %collective-permute-start.1 = (bf16[192,1664]{1,0:T(8,128)(2,1)S(1)}, bf16[192,1664]{1,0:T(8,128)(2,1)S(1)}, u32[]{:S(2)}, u32[]{:S(2)}) collective-permute-start(bf16[192,1664]{1,0:T(8,128)(2,1)S(1)} %get-tuple-element.32.sent_ref), channel_id=1, source_target_pairs={{0,16},{16,0},{1,17},{17,1},{2,18},{18,2},{3,19},{19,3},{4,20},{20... | collective-permute-start | bytes 1916936 | tf_op jit(solution)/shard_map/ppermute | solution.py:19
  19.6 32.4 %collective-permute-start.10 = (bf16[3,16,256,384]{3,2,1,0:T(8,128)(2,1)}, bf16[3,16,256,384]{3,2,1,0:T(8,128)(2,1)}, u32[]{:S(2)}, u32[]{:S(2)}) collective-permute-start(bf16[3,16,256,384]{3,2,1,0:T(8,128)(2,1)} %get-tuple-element.43), channel_id=1, source_target_pairs={{0,16},{16,0},{1,17},{17,1},{2,18},{18,2},{3,19},{19,3},{4,20},{20... | collective-permute-start | bytes 28311560 | tf_op jit(solution)/shard_map/ppermute | solution.py:19
  20.1 1.1 %copy-start.1 = (bf16[192,1664]{1,0:T(8,128)(2,1)S(1)}, bf16[192,1664]{1,0:T(8,128)(2,1)}, u32[]{:S(2)}) copy-start(bf16[192,1664]{1,0:T(8,128)(2,1)} %copy-done) | copy-start | bytes 1916932
  22.9 8.8 %collective-permute-start.3 = (bf16[2,192,512]{2,1,0:T(8,128)(2,1)S(1)}, bf16[2,192,512]{2,1,0:T(8,128)(2,1)S(1)}, u32[]{:S(2)}, u32[]{:S(2)}) collective-permute-start(bf16[2,192,512]{2,1,0:T(8,128)(2,1)S(1)} %get-tuple-element.37), channel_id=1, source_target_pairs={{0,32},{32,64},{48,16},{80,48},{96,0},{112,80},{1,33},{33,65},{49,... | collective-permute-start | bytes 1179656 | tf_op jit(solution)/shard_map/ppermute | solution.py:520
  24.2 13.9 %collective-permute-start.2 = (bf16[192,512]{1,0:T(8,128)(2,1)S(1)}, bf16[192,512]{1,0:T(8,128)(2,1)S(1)}, u32[]{:S(2)}, u32[]{:S(2)}) collective-permute-start(bf16[192,512]{1,0:T(8,128)(2,1)S(1)} %get-tuple-element.36), channel_id=1, source_target_pairs={{0,64},{64,0},{96,32},{1,65},{65,1},{97,33},{2,66},{66,2},{98,34},... | collective-permute-start | bytes 589832 | tf_op jit(solution)/shard_map/ppermute | solution.py:521
  31.7 8.3 %collective-permute-start.6 = (bf16[2,192,512]{2,1,0:T(8,128)(2,1)S(1)}, bf16[2,192,512]{2,1,0:T(8,128)(2,1)S(1)}, u32[]{:S(2)}, u32[]{:S(2)}) collective-permute-start(bf16[2,192,512]{2,1,0:T(8,128)(2,1)S(1)} %collective-permute-done.3.pair), channel_id=1, source_target_pairs={{0,16},{16,0},{1,17},{17,1},{2,18},{18,2},{3,19},{19,3},{4,20},{20... | collective-permute-start | bytes 1179656 | tf_op jit(solution)/shard_map/ppermute | solution.py:19
  38.2 1.6 %collective-permute-start.4 = (bf16[192,512]{1,0:T(8,128)(2,1)S(1)}, bf16[192,512]{1,0:T(8,128)(2,1)S(1)}, u32[]{:S(2)}, u32[]{:S(2)}) collective-permute-start(bf16[192,512]{1,0:T(8,128)(2,1)S(1)} %get-tuple-element.35.stay), channel_id=1, source_target_pairs={{0,16},{16,0},{1,17},{17,1},{2,18},{18,2},{3,19},{19,3},{4,20},{20... | collective-permute-start | bytes 589832 | tf_op jit(solution)/shard_map/ppermute | solution.py:19
  38.2 1.9 %collective-permute-start.5 = (bf16[192,512]{1,0:T(8,128)(2,1)S(1)}, bf16[192,512]{1,0:T(8,128)(2,1)S(1)}, u32[]{:S(2)}, u32[]{:S(2)}) collective-permute-start(bf16[192,512]{1,0:T(8,128)(2,1)S(1)} %collective-permute-done.2.far), channel_id=1, source_target_pairs={{0,16},{16,0},{1,17},{17,1},{2,18},{18,2},{3,19},{19,3},{4,20},{20... | collective-permute-start | bytes 589832 | tf_op jit(solution)/shard_map/ppermute | solution.py:19
  44.8 1.9 %collective-permute-start.7 = (bf16[192,1152]{1,0:T(8,128)(2,1)S(1)}, bf16[192,1152]{1,0:T(8,128)(2,1)S(1)}, u32[]{:S(2)}, u32[]{:S(2)}) collective-permute-start(bf16[192,1152]{1,0:T(8,128)(2,1)S(1)} %get-tuple-element.39), channel_id=1, source_target_pairs={{0,16},{16,0},{1,17},{17,1},{2,18},{18,2},{3,19},{19,3},{4,20},{20... | collective-permute-start | bytes 1327112 | tf_op jit(solution)/shard_map/ppermute | solution.py:19
  47.3 9.5 %collective-permute-start.8 = (bf16[2,192,384]{2,1,0:T(8,128)(2,1)S(1)}, bf16[2,192,384]{2,1,0:T(8,128)(2,1)S(1)}, u32[]{:S(2)}, u32[]{:S(2)}) collective-permute-start(bf16[2,192,384]{2,1,0:T(8,128)(2,1)S(1)} %get-tuple-element.41), channel_id=1, source_target_pairs={{0,96},{16,48},{32,0},{48,80},{64,32},{80,112},{1,97},{17,49},{33,... | collective-permute-start | bytes 884744 | tf_op jit(solution)/shard_map/ppermute | solution.py:538
  48.8 8.0 %collective-permute-start.9 = (bf16[192,384]{1,0:T(8,128)(2,1)S(1)}, bf16[192,384]{1,0:T(8,128)(2,1)S(1)}, u32[]{:S(2)}, u32[]{:S(2)}) collective-permute-start(bf16[192,384]{1,0:T(8,128)(2,1)S(1)} %get-tuple-element.42), channel_id=1, source_target_pairs={{0,64},{32,96},{64,0},{1,65},{33,97},{65,1},{2,66},{34,98},{66,2},... | collective-permute-start | bytes 442376 | tf_op jit(solution)/shard_map/ppermute | solution.py:539
  56.8 3.3 %collective-permute-start.13 = (bf16[2,192,384]{2,1,0:T(8,128)(2,1)S(1)}, bf16[2,192,384]{2,1,0:T(8,128)(2,1)S(1)}, u32[]{:S(2)}, u32[]{:S(2)}) collective-permute-start(bf16[2,192,384]{2,1,0:T(8,128)(2,1)S(1)} %collective-permute-done.8.refs_2_), channel_id=1, source_target_pairs={{0,16},{16,0},{1,17},{17,1},{2,18},{18,2},{3,19},{19,3},{4,20},{20... | collective-permute-start | bytes 884744 | tf_op jit(solution)/shard_map/ppermute | solution.py:19
  58.5 1.4 %collective-permute-start.11 = (bf16[192,384]{1,0:T(8,128)(2,1)S(1)}, bf16[192,384]{1,0:T(8,128)(2,1)S(1)}, u32[]{:S(2)}, u32[]{:S(2)}) collective-permute-start(bf16[192,384]{1,0:T(8,128)(2,1)S(1)} %get-tuple-element.40.after_ref.refs_0_), channel_id=1, source_target_pairs={{0,16},{16,0},{1,17},{17,1},{2,18},{18,2},{3,19},{19,3},{4,20},{20... | collective-permute-start | bytes 442376 | tf_op jit(solution)/shard_map/ppermute | solution.py:19
  58.5 1.6 %collective-permute-start.12 = (bf16[192,384]{1,0:T(8,128)(2,1)S(1)}, bf16[192,384]{1,0:T(8,128)(2,1)S(1)}, u32[]{:S(2)}, u32[]{:S(2)}) collective-permute-start(bf16[192,384]{1,0:T(8,128)(2,1)S(1)} %collective-permute-done.9.refs_1_), channel_id=1, source_target_pairs={{0,16},{16,0},{1,17},{17,1},{2,18},{18,2},{3,19},{19,3},{4,20},{20... | collective-permute-start | bytes 442376 | tf_op jit(solution)/shard_map/ppermute | solution.py:19
  63.4 14.7 %collective-permute-start.14 = (bf16[4,384,256]{2,1,0:T(8,128)(2,1)S(1)}, bf16[4,384,256]{2,1,0:T(8,128)(2,1)S(1)}, u32[]{:S(2)}, u32[]{:S(2)}) collective-permute-start(bf16[4,384,256]{2,1,0:T(8,128)(2,1)S(1)} %get-tuple-element.50), channel_id=1, source_target_pairs={{0,2},{1,3},{2,0},{3,1},{4,6},{5,7},{6,4},{7,5},{8,10},{9,11},{10,... | collective-permute-start | bytes 2359304 | tf_op jit(solution)/shard_map/ppermute | solution.py:551
  68.4 16.1 %collective-permute-start.15 = (bf16[4,384,256]{2,1,0:T(8,128)(2,1)S(1)}, bf16[4,384,256]{2,1,0:T(8,128)(2,1)S(1)}, u32[]{:S(2)}, u32[]{:S(2)}) collective-permute-start(bf16[4,384,256]{2,1,0:T(8,128)(2,1)S(1)} %back.6), channel_id=1, source_target_pairs={{0,1},{1,2},{2,3},{3,0},{4,5},{5,6},{6,7},{7,4},{8,9},{9,10},{10,1... | collective-permute-start | bytes 2359304 | tf_op jit(solution)/shard_map/ppermute | solution.py:551
  70.9 14.0 %collective-permute-start.16 = (bf16[4,384,256]{2,1,0:T(8,128)(2,1)S(1)}, bf16[4,384,256]{2,1,0:T(8,128)(2,1)S(1)}, u32[]{:S(2)}, u32[]{:S(2)}) collective-permute-start(bf16[4,384,256]{2,1,0:T(8,128)(2,1)S(1)} %back.7), channel_id=1, source_target_pairs={{0,3},{1,0},{2,1},{3,2},{4,7},{5,4},{6,5},{7,6},{8,11},{9,8},{10,9... | collective-permute-start | bytes 2359304 | tf_op jit(solution)/shard_map/ppermute | solution.py:551
  85.2 7.0 %collective-permute-start.17 = (bf16[384,256]{1,0:T(8,128)(2,1)S(1)}, bf16[384,256]{1,0:T(8,128)(2,1)S(1)}, u32[]{:S(2)}, u32[]{:S(2)}) collective-permute-start(bf16[384,256]{1,0:T(8,128)(2,1)S(1)} %get-tuple-element.55), channel_id=1, source_target_pairs={{0,8},{1,9},{2,10},{3,11},{4,12},{5,13},{6,14},{7,15},{8,0},{9,1},... | collective-permute-start | bytes 589832 | tf_op jit(solution)/shard_map/ppermute | solution.py:558
  88.9 6.2 %collective-permute-start.19 = (bf16[384,256]{1,0:T(8,128)(2,1)S(1)}, bf16[384,256]{1,0:T(8,128)(2,1)S(1)}, u32[]{:S(2)}, u32[]{:S(2)}) collective-permute-start(bf16[384,256]{1,0:T(8,128)(2,1)S(1)} %get-tuple-element.56), channel_id=1, source_target_pairs={{0,12},{1,13},{2,14},{3,15},{4,0},{5,1},{6,2},{7,3},{8,4},{9,5},{1... | collective-permute-start | bytes 589832 | tf_op jit(solution)/shard_map/ppermute | solution.py:558
  89.3 5.8 %collective-permute-start.18 = (bf16[384,256]{1,0:T(8,128)(2,1)S(1)}, bf16[384,256]{1,0:T(8,128)(2,1)S(1)}, u32[]{:S(2)}, u32[]{:S(2)}) collective-permute-start(bf16[384,256]{1,0:T(8,128)(2,1)S(1)} %get-tuple-element.57), channel_id=1, source_target_pairs={{0,4},{1,5},{2,6},{3,7},{4,8},{5,9},{6,10},{7,11},{8,12},{9,13},{1... | collective-permute-start | bytes 589832 | tf_op jit(solution)/shard_map/ppermute | solution.py:558
  95.3 4.6 %collective-permute-start.20 = (bf16[192,256]{1,0:T(8,128)(2,1)S(1)}, bf16[192,256]{1,0:T(8,128)(2,1)S(1)}, u32[]{:S(2)}, u32[]{:S(2)}) collective-permute-start(bf16[192,256]{1,0:T(8,128)(2,1)S(1)} %get-tuple-element.59), channel_id=1, source_target_pairs={{0,16},{16,0},{1,17},{17,1},{2,18},{18,2},{3,19},{19,3},{4,20},{20... | collective-permute-start | bytes 294920 | tf_op jit(solution)/shard_map/ppermute | solution.py:19
  (3 other events, 2.6 us)

commit v8 on v7

--- a/solution.py
+++ b/solution.py
@@ -24,7 +24,7 @@
     return jnp.concatenate([w_ref[c, 2 * i : 2 * i + 2].reshape(size, NH * HD) for c in range(3)], axis=1)
 
 
-def own_kernel(a_hbm, w_hbm, part_ref, w_ref, a_s, a_sem, w_sem):
+def own_kernel(where_ref, place_ref, mod_ref, a_hbm, w_hbm, part_ref, w_ref, a_s, a_sem, w_sem):
     chunks = w_ref.shape[1] // 2
     block = 4 * w_ref.shape[3]
 
@@ -48,14 +48,15 @@
             part_ref[...] += part
 
 
-def project_own(a, w5, early):
+def project_own(small, a, w5, early):
     rows = a.shape[0]
     block = 4 * w5.shape[3]
+    smem = pl.BlockSpec(memory_space=pltpu.SMEM)
     vmem = pl.BlockSpec(memory_space=pltpu.VMEM)
     hbm = pl.BlockSpec(memory_space=pltpu.HBM)
     return pl.pallas_call(
         own_kernel,
-        in_specs=[hbm, hbm],
+        in_specs=[smem, smem, vmem, hbm, hbm],
         out_specs=[vmem, vmem],
         out_shape=[
             jax.ShapeDtypeStruct((rows, 9 * HD), jnp.float32),
@@ -69,7 +70,7 @@
         compiler_params=pltpu.CompilerParams(vmem_limit_bytes=20 * MIB),
         cost_estimate=pl.CostEstimate(flops=4 * 10**9, bytes_accessed=10**7, transcendentals=0),
         name="project_own",
-    )(a, w5)
+    )(*small, a, w5)
 
 
 def project_kernel(
@@ -502,27 +503,6 @@
     mod = modality.reshape(2 * RING, rows)
     w5 = pltpu.with_memory_space_constraint(w5, pltpu.HBM)
     activations = pltpu.with_memory_space_constraint(activations, pltpu.HBM)
-    act_other = pltpu.with_memory_space_constraint(core_swap(activations), pltpu.VMEM)
-    part, w_early = project_own(activations, w5, 4)
-    w_early = pltpu.with_memory_space_constraint(w_early, pltpu.VMEM)
-    proj_own, sent, half = project(where, part, activations, act_other, w_early, w5, grad_attn)
-    got = core_swap(sent)
-    got, half = lax.optimization_barrier((got, half))
-    other_half = core_swap(half)
-
-    def part_shapes(width):
-        block = jax.ShapeDtypeStruct((rows, width), jnp.bfloat16)
-        return [jax.ShapeDtypeStruct((2, rows, width), jnp.bfloat16), block, block]
-
-    pair, far, stay = small_call(
-        route_kernel, "route", where, (mod, proj_own, sent, got, grad_attn), part_shapes(4 * HD)
-    )
-    pair = lax.ppermute(pair, ("seq", "mod"), pair_perm(1))
-    far = lax.ppermute(far, "seq", [(i, (i + 2) % RING) for i in range(RING) if (i + 2) % RING < NH])
-    parts = [stay, far, pair]
-    keep, send = attention(where, parts + [core_swap(x) for x in parts])
-    pair, far, stay = small_call(combine_kernel, "combine", where, (keep, core_swap(send)), part_shapes(3 * HD))
-
     i = jnp.arange(dests, dtype=jnp.int32) // RING
     j = jnp.arange(dests, dtype=jnp.int32) % RING
     y, z = tp // RING, tp % RING
@@ -532,6 +512,27 @@
         (y + i) % RING * RING + (z + j) % RING,
     )
     place = jnp.concatenate([place, jnp.stack([core, chip])]).astype(jnp.int32)
+
+    act_other = pltpu.with_memory_space_constraint(core_swap(activations), pltpu.VMEM)
+    part, w_early = project_own((where, place, mod), activations, w5, 4)
+    w_early = pltpu.with_memory_space_constraint(w_early, pltpu.VMEM)
+    proj_own, sent, half = project(where, part, activations, act_other, w_early, w5, grad_attn)
+    got = core_swap(sent)
+    got, half = lax.optimization_barrier((got, half))
+    other_half = core_swap(half)
+
+    def part_shapes(width):
+        block = jax.ShapeDtypeStruct((rows, width), jnp.bfloat16)
+        return [jax.ShapeDtypeStruct((2, rows, width), jnp.bfloat16), block, block]
+
+    pair, far, stay = small_call(
+        route_kernel, "route", where, (mod, proj_own, sent, got, grad_attn), part_shapes(4 * HD)
+    )
+    pair = lax.ppermute(pair, ("seq", "mod"), pair_perm(1))
+    far = lax.ppermute(far, "seq", [(i, (i + 2) % RING) for i in range(RING) if (i + 2) % RING < NH])
+    parts = [stay, far, pair]
+    keep, send = attention(where, parts + [core_swap(x) for x in parts])
+    pair, far, stay = small_call(combine_kernel, "combine", where, (keep, core_swap(send)), part_shapes(3 * HD))
 
     w_first = fetch_weights(place, stay, w5, other_half, (2, 1))
     w_first = [pltpu.with_memory_space_constraint(w, pltpu.VMEM) for w in w_first]

time: 101 us -> 99.1 us (0.981)
  local copies, waits for them, and re-layouts: 3.83 us -> 0.83 us
  waiting for transfers between devices: 19.6 us -> 21.4 us
    unnamed x12 -> x2, local copies, waits for them, and re-layouts: 3.7 us -> 0.01 us
    pallas_call x1, Pallas kernels: 4.37 us -> 3.07 us  [fetch_weights(): pl.pallas_call(functools.partial(fetch_kernel, hops), in_specs=[pl.BlockS...]
  transfers between devices with their start and end apart: 21 -> 21, of which waited for: 14 -> 13; matrix products, arithmetic and copies ran while one was open for 1% -> 1% of each run, Pallas kernels for 24% -> 23%
where the time goes in v8:
time: 99.1 us; the launch traced here: 98.8 us
  starting transfers between devices  38.4 us (39%)
  Pallas kernels  36.1 us (36%)
  waiting for transfers between devices  21.4 us (22%)
  other arithmetic  1.81 us (2%)
    ppermute x11, starting transfers between devices, core_swap(): return lax.ppermute(x, 'mod', [(0, 1), (1, 0)])  15.3 us
    pallas_call x4, Pallas kernels, back_call(): pl.pallas_call(kernel, in_specs=in_specs, out_specs=[vmem] * len(out_shap...  11.5 us
    pallas_call x1, Pallas kernels, project(): pl.pallas_call(functools.partial(project_kernel, early), in_specs=[pl.Blo...  9.87 us
    ppermute x11, waiting for transfers between devices, core_swap(): return lax.ppermute(x, 'mod', [(0, 1), (1, 0)])  6.95 us
    ppermute x3, waiting for transfers between devices, per_device(): lax.ppermute(x, AXES, ring_perm(True, hop))  6.77 us
    ppermute x3, starting transfers between devices, per_device(): lax.ppermute(x, AXES, ring_perm(True, hop))  6.03 us
    ppermute x1, starting transfers between devices, per_device(): lax.ppermute(far, 'seq', [(i, (i + 2) % RING) for i in range(RING) if (i...  5.61 us
    pallas_call x1, Pallas kernels, project_own(): pl.pallas_call(own_kernel, in_specs=[smem, smem, vmem, hbm, hbm], out_spe...  5.54 us
  transfers between devices with their start and end apart: 21, of which 13 were waited for; matrix products, arithmetic and copies ran while one was open for 1% of the time, Pallas kernels for 23%

profile of v8, /device:TPU:1, one launch (start us, length us, event | category | flops | bytes accessed | tf_op | source)
XLA Modules:
  0.0 98.8 jit_solution(6204973583059644626)
XLA Ops:
  0.0 1.4 %collective-permute-start = (bf16[192,8192]{1,0:T(8,128)(2,1)}, bf16[192,8192]{1,0:T(8,128)(2,1)S(1)}, u32[]{:S(2)}, u32[]{:S(2)}) collective-permute-start(bf16[192,8192]{1,0:T(8,128)(2,1)} %own_hbm.1), channel_id=1, source_target_pairs={{0,16},{16,0},{1,17},{17,1},{2,18},{18,2},{3,19},{19,3},{4,20},{20... | collective-permute-start | bytes 9437192 | tf_op jit(solution)/shard_map/ppermute | solution.py:19
  2.4 5.5 %project_own.1 = (f32[192,1152]{1,0:T(8,128)S(1)}, bf16[3,8,2,256,384]{4,3,2,1,0:T(8,128)(2,1)S(1)}) custom-call(s32[2]{0:T(128)S(1)} %pad_add_fusion.1.where_ref, s32[18]{0:T(128)S(1)} %pad_add_fusion.place_ref, s32[8,192]{1,0:T(8,128)S(1)} %reshape.9.mod_ref, bf16[192,8192]{1,0:T(8,128)(2,1)} %own_hbm.1, bf16[3,16,2,256,384]{4,3,2,1,0:T(8,128)(2,1)} %bitcast.23), custom_call_target="tpu_custom_call" | custom-call | flops 4000000000 | bytes 10000000 | tf_op jit(solution)/shard_map/project_own/pallas_call | solution.py:57
  7.9 9.9 %project.1 = (bf16[192,1152]{1,0:T(8,128)(2,1)S(1)}, bf16[192,1664]{1,0:T(8,128)(2,1)S(1)}, bf16[3,16,256,384]{3,2,1,0:T(8,128)(2,1)}) custom-call(s32[2]{0:T(128)S(1)} %pad_add_fusion.1.where_ref, f32[192,1152]{1,0:T(8,128)S(1)} %get-tuple-element.29.part_ref, bf16[192,8192]{1,0:T(8,128)(2,1)} %own_hbm.1, ...), custom_call_target="tpu_custom_call" | custom-call | flops 7000000000 | bytes 10000000 | tf_op jit(solution)/shard_map/project/pallas_call | solution.py:142
  17.9 2.1 %collective-permute-done.1.got_ref = bf16[192,1664]{1,0:T(8,128)(2,1)S(1)} collective-permute-done((bf16[192,1664]{1,0:T(8,128)(2,1)S(1)}, bf16[192,1664]{1,0:T(8,128)(2,1)S(1)}, u32[]{:S(2)}, u32[]{:S(2)}) %collective-permute-start.1) | collective-permute-done | bytes 639008 | tf_op jit(solution)/shard_map/ppermute | solution.py:19
  22.1 5.6 %collective-permute-start.2 = (bf16[192,512]{1,0:T(8,128)(2,1)S(1)}, bf16[192,512]{1,0:T(8,128)(2,1)S(1)}, u32[]{:S(2)}, u32[]{:S(2)}) collective-permute-start(bf16[192,512]{1,0:T(8,128)(2,1)S(1)} %get-tuple-element.36), channel_id=1, source_target_pairs={{0,64},{64,0},{96,32},{1,65},{65,1},{97,33},{2,66},{66,2},{98,34},... | collective-permute-start | bytes 589832 | tf_op jit(solution)/shard_map/ppermute | solution.py:532
  27.8 1.9 %collective-permute-done.3.pair = bf16[2,192,512]{2,1,0:T(8,128)(2,1)S(1)} collective-permute-done((bf16[2,192,512]{2,1,0:T(8,128)(2,1)S(1)}, bf16[2,192,512]{2,1,0:T(8,128)(2,1)S(1)}, u32[]{:S(2)}, u32[]{:S(2)}) %collective-permute-start.3) | collective-permute-done | bytes 393248 | tf_op jit(solution)/shard_map/ppermute | solution.py:531
  29.7 6.7 %collective-permute-start.6 = (bf16[2,192,512]{2,1,0:T(8,128)(2,1)S(1)}, bf16[2,192,512]{2,1,0:T(8,128)(2,1)S(1)}, u32[]{:S(2)}, u32[]{:S(2)}) collective-permute-start(bf16[2,192,512]{2,1,0:T(8,128)(2,1)S(1)} %collective-permute-done.3.pair), channel_id=1, source_target_pairs={{0,16},{16,0},{1,17},{17,1},{2,18},{18,2},{3,19},{19,3},{4,20},{20... | collective-permute-start | bytes 1179656 | tf_op jit(solution)/shard_map/ppermute | solution.py:19
  38.2 4.7 %attention.1 = (f32[192,1408]{1,0:T(8,128)S(1)}, bf16[192,1152]{1,0:T(8,128)(2,1)S(1)}) custom-call(s32[2]{0:T(128)S(1)} %pad_add_fusion.1.where_ref, bf16[192,512]{1,0:T(8,128)(2,1)S(1)} %get-tuple-element.35.stay, bf16[192,512]{1,0:T(8,128)(2,1)S(1)} %collective-permute-done.2.far, bf16[2,192,512]{2,1,0:T(8,128)(2,1)S(1)} %collective-permute-done.3.pair, ...), custom_call_target="tpu_custom_call" | custom-call | flops 1000000000 | bytes 4000000 | tf_op jit(solution)/shard_map/attention/pallas_call | solution.py:289
  43.4 1.4 %collective-permute-done.7.got = bf16[192,1152]{1,0:T(8,128)(2,1)S(1)} collective-permute-done((bf16[192,1152]{1,0:T(8,128)(2,1)S(1)}, bf16[192,1152]{1,0:T(8,128)(2,1)S(1)}, u32[]{:S(2)}, u32[]{:S(2)}) %collective-permute-start.7) | collective-permute-done | bytes 442400 | tf_op jit(solution)/shard_map/ppermute | solution.py:19
  45.5 1.3 %collective-permute-start.8 = (bf16[2,192,384]{2,1,0:T(8,128)(2,1)S(1)}, bf16[2,192,384]{2,1,0:T(8,128)(2,1)S(1)}, u32[]{:S(2)}, u32[]{:S(2)}) collective-permute-start(bf16[2,192,384]{2,1,0:T(8,128)(2,1)S(1)} %get-tuple-element.41), channel_id=1, source_target_pairs={{0,96},{16,48},{32,0},{48,80},{64,32},{80,112},{1,97},{17,49},{33,... | collective-permute-start | bytes 884744 | tf_op jit(solution)/shard_map/ppermute | solution.py:539
  46.8 3.8 %collective-permute-start.9 = (bf16[192,384]{1,0:T(8,128)(2,1)S(1)}, bf16[192,384]{1,0:T(8,128)(2,1)S(1)}, u32[]{:S(2)}, u32[]{:S(2)}) collective-permute-start(bf16[192,384]{1,0:T(8,128)(2,1)S(1)} %get-tuple-element.42), channel_id=1, source_target_pairs={{0,64},{32,96},{64,0},{1,65},{33,97},{65,1},{2,66},{34,98},{66,2},... | collective-permute-start | bytes 442376 | tf_op jit(solution)/shard_map/ppermute | solution.py:540
  50.6 3.1 %fetch_weights.1 = (bf16[2,3,4,256,384]{4,3,2,1,0:T(8,128)(2,1)S(1)}, bf16[2,3,4,256,384]{4,3,2,1,0:T(8,128)(2,1)S(1)}) custom-call(s32[18]{0:T(128)S(1)} %pad_add_fusion.place_ref, bf16[192,384]{1,0:T(8,128)(2,1)S(1)} %get-tuple-element.40.after_ref.refs_0_, bf16[3,16,2,256,384]{4,3,2,1,0:T(8,128)(2,1)} %bitcast.25, ...), custom_call_target="tpu_custom_call" | custom-call | flops 1000000 | bytes 10000000 | tf_op jit(solution)/shard_map/fetch_weights/pallas_call | solution.py:372
  54.7 1.9 %collective-permute-start.13 = (bf16[2,192,384]{2,1,0:T(8,128)(2,1)S(1)}, bf16[2,192,384]{2,1,0:T(8,128)(2,1)S(1)}, u32[]{:S(2)}, u32[]{:S(2)}) collective-permute-start(bf16[2,192,384]{2,1,0:T(8,128)(2,1)S(1)} %collective-permute-done.8.refs_2_), channel_id=1, source_target_pairs={{0,16},{16,0},{1,17},{17,1},{2,18},{18,2},{3,19},{19,3},{4,20},{20... | collective-permute-start | bytes 884744 | tf_op jit(solution)/shard_map/ppermute | solution.py:19
  58.2 3.4 %back.4 = (bf16[4,384,256]{2,1,0:T(8,128)(2,1)S(1)}, bf16[384,2304]{1,0:T(8,128)(2,1)S(1)}, bf16[2,3,4,256,384]{4,3,2,1,0:T(8,128)(2,1)S(1)}) custom-call(s32[18]{0:T(128)S(1)} %pad_add_fusion.place_ref, s32[8,192]{1,0:T(8,128)S(1)} %reshape.9.mod_ref, bf16[192,384]{1,0:T(8,128)(2,1)S(1)} %get-tuple-element.40.after_ref.refs_0_, ...), custom_call_target="tpu_custom_call" | custom-call | flops 1000000 | bytes 10000 | tf_op jit(solution)/shard_map/back/pallas_call | solution.py:420
  61.6 3.0 %collective-permute-start.14 = (bf16[4,384,256]{2,1,0:T(8,128)(2,1)S(1)}, bf16[4,384,256]{2,1,0:T(8,128)(2,1)S(1)}, u32[]{:S(2)}, u32[]{:S(2)}) collective-permute-start(bf16[4,384,256]{2,1,0:T(8,128)(2,1)S(1)} %get-tuple-element.50), channel_id=1, source_target_pairs={{0,2},{1,3},{2,0},{3,1},{4,6},{5,7},{6,4},{7,5},{8,10},{9,11},{10,... | collective-permute-start | bytes 2359304 | tf_op jit(solution)/shard_map/ppermute | solution.py:552
  64.6 2.0 %back.6 = bf16[4,384,256]{2,1,0:T(8,128)(2,1)S(1)} custom-call(bf16[384,2304]{1,0:T(8,128)(2,1)S(1)} %get-tuple-element.49.g_ref, bf16[2,3,4,256,384]{4,3,2,1,0:T(8,128)(2,1)S(1)} %get-tuple-element.51.w_ref), custom_call_target="tpu_custom_call" | custom-call | flops 1000000 | bytes 10000 | tf_op jit(solution)/shard_map/back/pallas_call | solution.py:420
  67.1 2.0 %back.7 = bf16[4,384,256]{2,1,0:T(8,128)(2,1)S(1)} custom-call(bf16[384,2304]{1,0:T(8,128)(2,1)S(1)} %get-tuple-element.49.g_ref, bf16[2,3,4,256,384]{4,3,2,1,0:T(8,128)(2,1)S(1)} %get-tuple-element.52.w_ref), custom_call_target="tpu_custom_call" | custom-call | flops 1000000 | bytes 10000 | tf_op jit(solution)/shard_map/back/pallas_call | solution.py:420
  69.1 2.6 %collective-permute-start.16 = (bf16[4,384,256]{2,1,0:T(8,128)(2,1)S(1)}, bf16[4,384,256]{2,1,0:T(8,128)(2,1)S(1)}, u32[]{:S(2)}, u32[]{:S(2)}) collective-permute-start(bf16[4,384,256]{2,1,0:T(8,128)(2,1)S(1)} %back.7), channel_id=1, source_target_pairs={{0,3},{1,0},{2,1},{3,2},{4,7},{5,4},{6,5},{7,6},{8,11},{9,8},{10,9... | collective-permute-start | bytes 2359304 | tf_op jit(solution)/shard_map/ppermute | solution.py:552
  71.7 4.1 %back.5 = bf16[4,384,256]{2,1,0:T(8,128)(2,1)S(1)} custom-call(s32[18]{0:T(128)S(1)} %pad_add_fusion.place_ref, bf16[384,2304]{1,0:T(8,128)(2,1)S(1)} %get-tuple-element.49.g_ref, bf16[3,16,2,256,384]{4,3,2,1,0:T(8,128)(2,1)} %bitcast.27, bf16[3,16,256,384]{3,2,1,0:T(8,128)(2,1)S(1)} %collective-permute-done.10.other_hbm.refs_8_), custom_call_target="tpu_custom_call" | custom-call | flops 1000000 | bytes 10000 | tf_op jit(solution)/shard_map/back/pallas_call | solution.py:420
  76.1 6.6 %collective-permute-done.15 = bf16[4,384,256]{2,1,0:T(8,128)(2,1)S(1)} collective-permute-done((bf16[4,384,256]{2,1,0:T(8,128)(2,1)S(1)}, bf16[4,384,256]{2,1,0:T(8,128)(2,1)S(1)}, u32[]{:S(2)}, u32[]{:S(2)}) %collective-permute-start.15) | collective-permute-done | bytes 786464 | tf_op jit(solution)/shard_map/ppermute | solution.py:552
  83.4 3.7 %collective-permute-start.17 = (bf16[384,256]{1,0:T(8,128)(2,1)S(1)}, bf16[384,256]{1,0:T(8,128)(2,1)S(1)}, u32[]{:S(2)}, u32[]{:S(2)}) collective-permute-start(bf16[384,256]{1,0:T(8,128)(2,1)S(1)} %get-tuple-element.55), channel_id=1, source_target_pairs={{0,8},{1,9},{2,10},{3,11},{4,12},{5,13},{6,14},{7,15},{8,0},{9,1},... | collective-permute-start | bytes 589832 | tf_op jit(solution)/shard_map/ppermute | solution.py:559
  88.6 1.9 %collective-permute-done.17 = bf16[384,256]{1,0:T(8,128)(2,1)S(1)} collective-permute-done((bf16[384,256]{1,0:T(8,128)(2,1)S(1)}, bf16[384,256]{1,0:T(8,128)(2,1)S(1)}, u32[]{:S(2)}, u32[]{:S(2)}) %collective-permute-start.17) | collective-permute-done | bytes 196640 | tf_op jit(solution)/shard_map/ppermute | solution.py:559
  90.5 2.9 %collective-permute-done.19 = bf16[384,256]{1,0:T(8,128)(2,1)S(1)} collective-permute-done((bf16[384,256]{1,0:T(8,128)(2,1)S(1)}, bf16[384,256]{1,0:T(8,128)(2,1)S(1)}, u32[]{:S(2)}, u32[]{:S(2)}) %collective-permute-start.19) | collective-permute-done | bytes 196640 | tf_op jit(solution)/shard_map/ppermute | solution.py:559
  93.5 3.6 %collective-permute-start.20 = (bf16[192,256]{1,0:T(8,128)(2,1)S(1)}, bf16[192,256]{1,0:T(8,128)(2,1)S(1)}, u32[]{:S(2)}, u32[]{:S(2)}) collective-permute-start(bf16[192,256]{1,0:T(8,128)(2,1)S(1)} %get-tuple-element.59), channel_id=1, source_target_pairs={{0,16},{16,0},{1,17},{17,1},{2,18},{18,2},{3,19},{19,3},{4,20},{20... | collective-permute-start | bytes 294920 | tf_op jit(solution)/shard_map/ppermute | solution.py:19
  (42 shorter events, 13.6 us)
Async XLA Ops:
  0.0 7.9 %collective-permute-start = (bf16[192,8192]{1,0:T(8,128)(2,1)}, bf16[192,8192]{1,0:T(8,128)(2,1)S(1)}, u32[]{:S(2)}, u32[]{:S(2)}) collective-permute-start(bf16[192,8192]{1,0:T(8,128)(2,1)} %own_hbm.1), channel_id=1, source_target_pairs={{0,16},{16,0},{1,17},{17,1},{2,18},{18,2},{3,19},{19,3},{4,20},{20... | collective-permute-start | bytes 9437192 | tf_op jit(solution)/shard_map/ppermute | solution.py:19
  2.4 5.6 %copy-start = (bf16[192,384]{1,0:T(8,128)(2,1)S(1)}, bf16[192,384]{1,0:T(8,128)(2,1)}, u32[]{:S(2)}) copy-start(bf16[192,384]{1,0:T(8,128)(2,1)} %g_ref.3) | copy-start | bytes 442372
  17.8 2.2 %collective-permute-start.1 = (bf16[192,1664]{1,0:T(8,128)(2,1)S(1)}, bf16[192,1664]{1,0:T(8,128)(2,1)S(1)}, u32[]{:S(2)}, u32[]{:S(2)}) collective-permute-start(bf16[192,1664]{1,0:T(8,128)(2,1)S(1)} %get-tuple-element.32.sent_ref), channel_id=1, source_target_pairs={{0,16},{16,0},{1,17},{17,1},{2,18},{18,2},{3,19},{19,3},{4,20},{20... | collective-permute-start | bytes 1916936 | tf_op jit(solution)/shard_map/ppermute | solution.py:19
  20.0 30.6 %collective-permute-start.10 = (bf16[3,16,256,384]{3,2,1,0:T(8,128)(2,1)}, bf16[3,16,256,384]{3,2,1,0:T(8,128)(2,1)S(1)}, u32[]{:S(2)}, u32[]{:S(2)}) collective-permute-start(bf16[3,16,256,384]{3,2,1,0:T(8,128)(2,1)} %get-tuple-element.43), channel_id=1, source_target_pairs={{0,16},{16,0},{1,17},{17,1},{2,18},{18,2},{3,19},{19,3},{4,20},{20... | collective-permute-start | bytes 28311560 | tf_op jit(solution)/shard_map/ppermute | solution.py:19
  20.8 8.8 %collective-permute-start.3 = (bf16[2,192,512]{2,1,0:T(8,128)(2,1)S(1)}, bf16[2,192,512]{2,1,0:T(8,128)(2,1)S(1)}, u32[]{:S(2)}, u32[]{:S(2)}) collective-permute-start(bf16[2,192,512]{2,1,0:T(8,128)(2,1)S(1)} %get-tuple-element.37), channel_id=1, source_target_pairs={{0,32},{32,64},{48,16},{80,48},{96,0},{112,80},{1,33},{33,65},{49,... | collective-permute-start | bytes 1179656 | tf_op jit(solution)/shard_map/ppermute | solution.py:531
  22.1 14.2 %collective-permute-start.2 = (bf16[192,512]{1,0:T(8,128)(2,1)S(1)}, bf16[192,512]{1,0:T(8,128)(2,1)S(1)}, u32[]{:S(2)}, u32[]{:S(2)}) collective-permute-start(bf16[192,512]{1,0:T(8,128)(2,1)S(1)} %get-tuple-element.36), channel_id=1, source_target_pairs={{0,64},{64,0},{96,32},{1,65},{65,1},{97,33},{2,66},{66,2},{98,34},... | collective-permute-start | bytes 589832 | tf_op jit(solution)/shard_map/ppermute | solution.py:532
  29.7 8.6 %collective-permute-start.6 = (bf16[2,192,512]{2,1,0:T(8,128)(2,1)S(1)}, bf16[2,192,512]{2,1,0:T(8,128)(2,1)S(1)}, u32[]{:S(2)}, u32[]{:S(2)}) collective-permute-start(bf16[2,192,512]{2,1,0:T(8,128)(2,1)S(1)} %collective-permute-done.3.pair), channel_id=1, source_target_pairs={{0,16},{16,0},{1,17},{17,1},{2,18},{18,2},{3,19},{19,3},{4,20},{20... | collective-permute-start | bytes 1179656 | tf_op jit(solution)/shard_map/ppermute | solution.py:19
  36.3 1.6 %collective-permute-start.4 = (bf16[192,512]{1,0:T(8,128)(2,1)S(1)}, bf16[192,512]{1,0:T(8,128)(2,1)S(1)}, u32[]{:S(2)}, u32[]{:S(2)}) collective-permute-start(bf16[192,512]{1,0:T(8,128)(2,1)S(1)} %get-tuple-element.35.stay), channel_id=1, source_target_pairs={{0,16},{16,0},{1,17},{17,1},{2,18},{18,2},{3,19},{19,3},{4,20},{20... | collective-permute-start | bytes 589832 | tf_op jit(solution)/shard_map/ppermute | solution.py:19
  36.3 1.9 %collective-permute-start.5 = (bf16[192,512]{1,0:T(8,128)(2,1)S(1)}, bf16[192,512]{1,0:T(8,128)(2,1)S(1)}, u32[]{:S(2)}, u32[]{:S(2)}) collective-permute-start(bf16[192,512]{1,0:T(8,128)(2,1)S(1)} %collective-permute-done.2.far), channel_id=1, source_target_pairs={{0,16},{16,0},{1,17},{17,1},{2,18},{18,2},{3,19},{19,3},{4,20},{20... | collective-permute-start | bytes 589832 | tf_op jit(solution)/shard_map/ppermute | solution.py:19
  43.0 1.9 %collective-permute-start.7 = (bf16[192,1152]{1,0:T(8,128)(2,1)S(1)}, bf16[192,1152]{1,0:T(8,128)(2,1)S(1)}, u32[]{:S(2)}, u32[]{:S(2)}) collective-permute-start(bf16[192,1152]{1,0:T(8,128)(2,1)S(1)} %get-tuple-element.39), channel_id=1, source_target_pairs={{0,16},{16,0},{1,17},{17,1},{2,18},{18,2},{3,19},{19,3},{4,20},{20... | collective-permute-start | bytes 1327112 | tf_op jit(solution)/shard_map/ppermute | solution.py:19
  45.5 9.2 %collective-permute-start.8 = (bf16[2,192,384]{2,1,0:T(8,128)(2,1)S(1)}, bf16[2,192,384]{2,1,0:T(8,128)(2,1)S(1)}, u32[]{:S(2)}, u32[]{:S(2)}) collective-permute-start(bf16[2,192,384]{2,1,0:T(8,128)(2,1)S(1)} %get-tuple-element.41), channel_id=1, source_target_pairs={{0,96},{16,48},{32,0},{48,80},{64,32},{80,112},{1,97},{17,49},{33,... | collective-permute-start | bytes 884744 | tf_op jit(solution)/shard_map/ppermute | solution.py:539
  46.8 7.9 %collective-permute-start.9 = (bf16[192,384]{1,0:T(8,128)(2,1)S(1)}, bf16[192,384]{1,0:T(8,128)(2,1)S(1)}, u32[]{:S(2)}, u32[]{:S(2)}) collective-permute-start(bf16[192,384]{1,0:T(8,128)(2,1)S(1)} %get-tuple-element.42), channel_id=1, source_target_pairs={{0,64},{32,96},{64,0},{1,65},{33,97},{65,1},{2,66},{34,98},{66,2},... | collective-permute-start | bytes 442376 | tf_op jit(solution)/shard_map/ppermute | solution.py:540
  54.7 3.5 %collective-permute-start.13 = (bf16[2,192,384]{2,1,0:T(8,128)(2,1)S(1)}, bf16[2,192,384]{2,1,0:T(8,128)(2,1)S(1)}, u32[]{:S(2)}, u32[]{:S(2)}) collective-permute-start(bf16[2,192,384]{2,1,0:T(8,128)(2,1)S(1)} %collective-permute-done.8.refs_2_), channel_id=1, source_target_pairs={{0,16},{16,0},{1,17},{17,1},{2,18},{18,2},{3,19},{19,3},{4,20},{20... | collective-permute-start | bytes 884744 | tf_op jit(solution)/shard_map/ppermute | solution.py:19
  56.6 1.4 %collective-permute-start.11 = (bf16[192,384]{1,0:T(8,128)(2,1)S(1)}, bf16[192,384]{1,0:T(8,128)(2,1)S(1)}, u32[]{:S(2)}, u32[]{:S(2)}) collective-permute-start(bf16[192,384]{1,0:T(8,128)(2,1)S(1)} %get-tuple-element.40.after_ref.refs_0_), channel_id=1, source_target_pairs={{0,16},{16,0},{1,17},{17,1},{2,18},{18,2},{3,19},{19,3},{4,20},{20... | collective-permute-start | bytes 442376 | tf_op jit(solution)/shard_map/ppermute | solution.py:19
  56.6 1.6 %collective-permute-start.12 = (bf16[192,384]{1,0:T(8,128)(2,1)S(1)}, bf16[192,384]{1,0:T(8,128)(2,1)S(1)}, u32[]{:S(2)}, u32[]{:S(2)}) collective-permute-start(bf16[192,384]{1,0:T(8,128)(2,1)S(1)} %collective-permute-done.9.refs_1_), channel_id=1, source_target_pairs={{0,16},{16,0},{1,17},{17,1},{2,18},{18,2},{3,19},{19,3},{4,20},{20... | collective-permute-start | bytes 442376 | tf_op jit(solution)/shard_map/ppermute | solution.py:19
  61.6 14.3 %collective-permute-start.14 = (bf16[4,384,256]{2,1,0:T(8,128)(2,1)S(1)}, bf16[4,384,256]{2,1,0:T(8,128)(2,1)S(1)}, u32[]{:S(2)}, u32[]{:S(2)}) collective-permute-start(bf16[4,384,256]{2,1,0:T(8,128)(2,1)S(1)} %get-tuple-element.50), channel_id=1, source_target_pairs={{0,2},{1,3},{2,0},{3,1},{4,6},{5,7},{6,4},{7,5},{8,10},{9,11},{10,... | collective-permute-start | bytes 2359304 | tf_op jit(solution)/shard_map/ppermute | solution.py:552
  66.7 16.1 %collective-permute-start.15 = (bf16[4,384,256]{2,1,0:T(8,128)(2,1)S(1)}, bf16[4,384,256]{2,1,0:T(8,128)(2,1)S(1)}, u32[]{:S(2)}, u32[]{:S(2)}) collective-permute-start(bf16[4,384,256]{2,1,0:T(8,128)(2,1)S(1)} %back.6), channel_id=1, source_target_pairs={{0,1},{1,2},{2,3},{3,0},{4,5},{5,6},{6,7},{7,4},{8,9},{9,10},{10,1... | collective-permute-start | bytes 2359304 | tf_op jit(solution)/shard_map/ppermute | solution.py:552
  69.1 14.0 %collective-permute-start.16 = (bf16[4,384,256]{2,1,0:T(8,128)(2,1)S(1)}, bf16[4,384,256]{2,1,0:T(8,128)(2,1)S(1)}, u32[]{:S(2)}, u32[]{:S(2)}) collective-permute-start(bf16[4,384,256]{2,1,0:T(8,128)(2,1)S(1)} %back.7), channel_id=1, source_target_pairs={{0,3},{1,0},{2,1},{3,2},{4,7},{5,4},{6,5},{7,6},{8,11},{9,8},{10,9... | collective-permute-start | bytes 2359304 | tf_op jit(solution)/shard_map/ppermute | solution.py:552
  83.4 7.0 %collective-permute-start.17 = (bf16[384,256]{1,0:T(8,128)(2,1)S(1)}, bf16[384,256]{1,0:T(8,128)(2,1)S(1)}, u32[]{:S(2)}, u32[]{:S(2)}) collective-permute-start(bf16[384,256]{1,0:T(8,128)(2,1)S(1)} %get-tuple-element.55), channel_id=1, source_target_pairs={{0,8},{1,9},{2,10},{3,11},{4,12},{5,13},{6,14},{7,15},{8,0},{9,1},... | collective-permute-start | bytes 589832 | tf_op jit(solution)/shard_map/ppermute | solution.py:559
  87.1 6.2 %collective-permute-start.19 = (bf16[384,256]{1,0:T(8,128)(2,1)S(1)}, bf16[384,256]{1,0:T(8,128)(2,1)S(1)}, u32[]{:S(2)}, u32[]{:S(2)}) collective-permute-start(bf16[384,256]{1,0:T(8,128)(2,1)S(1)} %get-tuple-element.56), channel_id=1, source_target_pairs={{0,12},{1,13},{2,14},{3,15},{4,0},{5,1},{6,2},{7,3},{8,4},{9,5},{1... | collective-permute-start | bytes 589832 | tf_op jit(solution)/shard_map/ppermute | solution.py:559
  87.6 5.8 %collective-permute-start.18 = (bf16[384,256]{1,0:T(8,128)(2,1)S(1)}, bf16[384,256]{1,0:T(8,128)(2,1)S(1)}, u32[]{:S(2)}, u32[]{:S(2)}) collective-permute-start(bf16[384,256]{1,0:T(8,128)(2,1)S(1)} %get-tuple-element.57), channel_id=1, source_target_pairs={{0,4},{1,5},{2,6},{3,7},{4,8},{5,9},{6,10},{7,11},{8,12},{9,13},{1... | collective-permute-start | bytes 589832 | tf_op jit(solution)/shard_map/ppermute | solution.py:559
  93.5 4.6 %collective-permute-start.20 = (bf16[192,256]{1,0:T(8,128)(2,1)S(1)}, bf16[192,256]{1,0:T(8,128)(2,1)S(1)}, u32[]{:S(2)}, u32[]{:S(2)}) collective-permute-start(bf16[192,256]{1,0:T(8,128)(2,1)S(1)} %get-tuple-element.59), channel_id=1, source_target_pairs={{0,16},{16,0},{1,17},{17,1},{2,18},{18,2},{3,19},{19,3},{4,20},{20... | collective-permute-start | bytes 294920 | tf_op jit(solution)/shard_map/ppermute | solution.py:19

commit v9 on v7

--- a/solution.py
+++ b/solution.py
@@ -169,18 +169,24 @@
     return pl.ds(pl.multiple_of(head * (width * HD), width * HD), width * HD)
 
 
-def section_rows(mod_ref, block, core):
-    rows = mod_ref.shape[1]
-    mine = (mod_ref[pl.ds(block, 1), :] == core).astype(jnp.float32)
-    row = lax.broadcasted_iota(jnp.int32, (rows, rows), 0)
-    col = lax.broadcasted_iota(jnp.int32, (rows, rows), 1)
-    return jnp.sum(jnp.where(row == col, mine, 0.0), axis=1, keepdims=True)
+def section_rows(mod_ref, block, core, rows):
+    lines = mod_ref.shape[0]
+    mine = (mod_ref[...] == core).astype(jnp.float32)
+    line = (lax.broadcasted_iota(jnp.int32, (rows, lines), 0) + block * rows) // HD
+    place = (lax.broadcasted_iota(jnp.int32, (rows, HD), 0) + block * rows) % HD
+    spread = jnp.dot(
+        (line == lax.broadcasted_iota(jnp.int32, (rows, lines), 1)).astype(jnp.float32),
+        mine,
+        preferred_element_type=jnp.float32,
+    )
+    return jnp.sum(jnp.where(place == lax.broadcasted_iota(jnp.int32, (rows, HD), 1), spread, 0.0), axis=1, keepdims=True)
 
 
 def route_kernel(where_ref, mod_ref, own_ref, sent_ref, got_ref, g_ref, pair_out, far_out, stay_out):
     chip, core = where_ref[0], where_ref[1]
-    mine = section_rows(mod_ref, 2 * chip + core, core) > 0
-    others = section_rows(mod_ref, 2 * chip + 1 - core, core) > 0
+    rows = own_ref.shape[0]
+    mine = section_rows(mod_ref, 2 * chip + core, core, rows) > 0
+    others = section_rows(mod_ref, 2 * chip + 1 - core, core, rows) > 0
 
     def own_rows(head):
         cols = head_columns(head, 3)
@@ -324,7 +330,7 @@
     chip, core = where
     stay, far, pair, stay_o, far_o, pair_o = parts
     rows = stay.shape[0]
-    mine = [section_rows(mod_ref, 2 * chip + core, core), section_rows(mod_ref, 2 * chip + 1 - core, core)]
+    mine = [section_rows(mod_ref, 2 * chip + side, core, rows) for side in (core, 1 - core)]
     for head, refs in (
         (chip, (stay, stay_o)),
         ((chip + 2) % RING, (far, far_o)),
@@ -344,27 +350,33 @@
                         out_ref[block * rows : (block + 1) * rows, pl.ds(lo, HD)] = kept[:, c * HD : (c + 1) * HD]
 
 
-def weight_copies(place_ref, own_hbm, other_hbm, to_ref, sem, hop):
-    core = place_ref[RING * RING]
+def destination(where_ref, i, j):
+    core, tp = where_ref[1], where_ref[2]
+    dy, dz = jnp.where(core == 0, j, i), jnp.where(core == 0, i, j)
+    return (tp // RING + dy) % RING * RING + (tp % RING + dz) % RING
+
+
+def weight_copies(where_ref, own_hbm, other_hbm, to_ref, sem, hop):
+    core = where_ref[1]
     copies = []
     for j in range(RING):
-        dest = place_ref[hop * RING + j]
+        dest = destination(where_ref, hop, j)
         copies.append(pltpu.make_async_copy(own_hbm.at[:, dest, core], to_ref.at[0, :, j], sem.at[0, j]))
         copies.append(pltpu.make_async_copy(other_hbm.at[:, dest], to_ref.at[1, :, j], sem.at[1, j]))
     return copies
 
 
-def fetch_kernel(hops, place_ref, after_ref, own_hbm, other_hbm, *refs):
+def fetch_kernel(hops, where_ref, after_ref, own_hbm, other_hbm, *refs):
     copies = []
     for i, hop in enumerate(hops):
-        copies += weight_copies(place_ref, own_hbm, other_hbm, refs[i], refs[len(hops) + i], hop)
+        copies += weight_copies(where_ref, own_hbm, other_hbm, refs[i], refs[len(hops) + i], hop)
     for copy in copies:
         copy.start()
     for copy in copies:
         copy.wait()
 
 
-def fetch_weights(place, after, w5, other_half, hops):
+def fetch_weights(where, after, w5, other_half, hops):
     vmem = pl.BlockSpec(memory_space=pltpu.VMEM)
     hbm = pl.BlockSpec(memory_space=pltpu.HBM)
     anywhere = pl.BlockSpec(memory_space=pl.ANY)
@@ -377,41 +389,41 @@
         compiler_params=pltpu.CompilerParams(vmem_limit_bytes=20 * MIB),
         cost_estimate=pl.CostEstimate(flops=10**6, bytes_accessed=10**7, transcendentals=0),
         name="fetch_weights",
-    )(place, after, w5, other_half)
-
-
-def product(g_ref, w_ref, out_ref, j, count):
+    )(where, after, w5, other_half)
+
+
+def product(g_ref, w_ref, outs, first=0, count=RING):
     cols = w_ref.shape[3]
-    w = [w_ref[side, c, j : j + count].reshape(count * cols, NH * HD) for side in range(2) for c in range(3)]
+    w = [w_ref[side, c, first : first + count].reshape(count * cols, NH * HD) for side in range(2) for c in range(3)]
     res = lax.dot_general(
         g_ref[...], jnp.concatenate(w, axis=1), (((1,), (1,)), ((), ())), preferred_element_type=jnp.float32
     ).astype(jnp.bfloat16)
     for i in range(count):
-        out_ref[j + i] = res[:, i * cols : (i + 1) * cols]
-
-
-def back_first_kernel(following, place_ref, mod_ref, *refs):
-    *parts, w_ref, own_hbm, other_hbm, out_ref, g_ref, next_ref, sem = refs
-    for copy in weight_copies(place_ref, own_hbm, other_hbm, next_ref, sem, following):
+        outs[(first + i) // 2][(first + i) % 2] = res[:, i * cols : (i + 1) * cols]
+
+
+def back_first_kernel(following, where_ref, mod_ref, *refs):
+    *parts, w_ref, own_hbm, other_hbm, out_a, out_b, g_ref, next_ref, sem = refs
+    for copy in weight_copies(where_ref, own_hbm, other_hbm, next_ref, sem, following):
         copy.start()
-    gather((place_ref[RING * RING + 1], place_ref[RING * RING]), mod_ref, parts, g_ref)
-    product(g_ref, w_ref, out_ref, 0, RING)
-    for copy in weight_copies(place_ref, own_hbm, other_hbm, next_ref, sem, following):
+    gather((where_ref[0], where_ref[1]), mod_ref, parts, g_ref)
+    product(g_ref, w_ref, (out_a, out_b))
+    for copy in weight_copies(where_ref, own_hbm, other_hbm, next_ref, sem, following):
         copy.wait()
 
 
-def back_middle_kernel(g_ref, w_ref, out_ref):
-    product(g_ref, w_ref, out_ref, 0, RING)
-
-
-def back_last_kernel(hop, place_ref, g_ref, own_hbm, other_hbm, out_ref, w_s, sem):
-    copies = weight_copies(place_ref, own_hbm, other_hbm, w_s, sem, hop)
+def back_middle_kernel(g_ref, w_ref, out_a, out_b):
+    product(g_ref, w_ref, (out_a, out_b))
+
+
+def back_last_kernel(hop, where_ref, after_a, after_b, g_ref, own_hbm, other_hbm, out_a, out_b, w_s, sem):
+    copies = weight_copies(where_ref, own_hbm, other_hbm, w_s, sem, hop)
     for copy in copies:
         copy.start()
     for j in range(0, RING, 2):
         for copy in copies[2 * j : 2 * j + 4]:
             copy.wait()
-        product(g_ref, w_s, out_ref, j, 2)
+        product(g_ref, w_s, (out_a, out_b), j, 2)
 
 
 def back_call(kernel, operands, in_specs, out_shape, scratch):
@@ -428,38 +440,73 @@
     )(*operands)
 
 
-def back_products(place, mod, parts, weights, w5, other_half, send):
+def add_kernel(a_ref, b_ref, out_ref):
+    out_ref[...] = (a_ref[...].astype(jnp.float32) + b_ref[...].astype(jnp.float32)).astype(jnp.bfloat16)
+
+
+def add(a, b):
+    vmem = pl.BlockSpec(memory_space=pltpu.VMEM)
+    return pl.pallas_call(
+        add_kernel,
+        in_specs=[vmem, vmem],
+        out_specs=vmem,
+        out_shape=jax.ShapeDtypeStruct(a.shape, jnp.bfloat16),
+        compiler_params=pltpu.CompilerParams(vmem_limit_bytes=16 * MIB),
+        cost_estimate=pl.CostEstimate(flops=10**5, bytes_accessed=10**4, transcendentals=0),
+        name="add",
+    )(a, b)
+
+
+def back_reduced(where, mod, parts, weights, w5, other_half):
     rows = 2 * parts[0].shape[0]
     cols = w5.shape[3]
     smem = pl.BlockSpec(memory_space=pltpu.SMEM)
     vmem = pl.BlockSpec(memory_space=pltpu.VMEM)
     hbm = pl.BlockSpec(memory_space=pltpu.HBM)
     anywhere = pl.BlockSpec(memory_space=pl.ANY)
-    piece = jax.ShapeDtypeStruct((RING, rows, cols), jnp.bfloat16)
+    halves = [jax.ShapeDtypeStruct((RING // 2, rows, cols), jnp.bfloat16)] * 2
     w_shape = (2, 3, RING) + w5.shape[3:]
     sem = pltpu.SemaphoreType.DMA((2, RING))
+
+    def onward(x):
+        return lax.ppermute(x, AXES, ring_perm(True, 1))
+
+    def backward(x):
+        return lax.ppermute(x, AXES, ring_perm(True, -1))
+
     w_two, w_one = weights
-    x, g, w_three = back_call(
+    two_a, two_b, g, w_three = back_call(
         functools.partial(back_first_kernel, 3),
-        (place, mod, *parts, w_two, w5, other_half),
+        (where, mod, *parts, w_two, w5, other_half),
         [smem] + [vmem] * 8 + [hbm, anywhere],
-        [piece, pltpu.VMEM((rows, 18 * HD), jnp.bfloat16), pltpu.VMEM(w_shape, jnp.bfloat16)],
+        halves + [pltpu.VMEM((rows, 18 * HD), jnp.bfloat16), pltpu.VMEM(w_shape, jnp.bfloat16)],
         [sem],
     )
     g = pltpu.with_memory_space_constraint(g, pltpu.VMEM)
     w_three = pltpu.with_memory_space_constraint(w_three, pltpu.VMEM)
-    pieces = {2: send(x, 2)}
-    for hop, w in ((1, w_one), (3, w_three)):
-        (x,) = back_call(back_middle_kernel, (g, w), [vmem, vmem], [piece], [])
-        pieces[hop] = send(x, hop)
-    (pieces[0],) = back_call(
+    relay_a, relay_b = onward(two_a), backward(two_b)
+    one_a, one_b = back_call(back_middle_kernel, (g, w_one), [vmem, vmem], halves, [])
+    from_one_b = onward(one_b)
+    three_a, three_b = back_call(back_middle_kernel, (g, w_three), [vmem, vmem], halves, [])
+    from_three_a = backward(three_a)
+    one_a = add(one_a, relay_a)
+    three_b = add(three_b, relay_b)
+    from_one_a, from_three_b = onward(one_a), backward(three_b)
+    own_a, own_b = back_call(
         functools.partial(back_last_kernel, 0),
-        (place, g, w5, other_half),
-        [smem, vmem, hbm, anywhere],
-        [piece],
+        (where, one_a, three_b, g, w5, other_half),
+        [smem, anywhere, anywhere, vmem, hbm, anywhere],
+        halves,
         [pltpu.VMEM(w_shape, jnp.bfloat16), sem],
     )
-    return pieces
+    sum_b = own_b.astype(jnp.float32) + from_one_b.astype(jnp.float32)
+    own_a, sum_b = lax.optimization_barrier((own_a, sum_b))
+    sum_a = own_a.astype(jnp.float32) + from_three_a.astype(jnp.float32)
+    sum_a, sum_b = lax.optimization_barrier((sum_a, sum_b))
+    sum_a = sum_a + from_one_a.astype(jnp.float32)
+    sum_a, sum_b = lax.optimization_barrier((sum_a, sum_b))
+    sum_b = sum_b + from_three_b.astype(jnp.float32)
+    return [sum_a[0], sum_a[1], sum_b[0], sum_b[1]]
 
 
 def ring_perm(first, hop):
@@ -494,12 +541,12 @@
     chip = lax.axis_index("seq")
     core = lax.axis_index("mod")
     tp = lax.axis_index("tp")
-    where = jnp.stack([chip, core]).astype(jnp.int32)
+    where = jnp.stack([chip, core, tp]).astype(jnp.int32)
     dests = RING * RING
     cols = depth // dests // 2
     w5 = jnp.transpose(weights[0], (1, 0, 2)).reshape(3, dests, 2, cols, NH * HD)
 
-    mod = modality.reshape(2 * RING, rows)
+    mod = modality.reshape(-1, HD)
     w5 = pltpu.with_memory_space_constraint(w5, pltpu.HBM)
     activations = pltpu.with_memory_space_constraint(activations, pltpu.HBM)
     act_other = pltpu.with_memory_space_constraint(core_swap(activations), pltpu.VMEM)
@@ -523,17 +570,7 @@
     keep, send = attention(where, parts + [core_swap(x) for x in parts])
     pair, far, stay = small_call(combine_kernel, "combine", where, (keep, core_swap(send)), part_shapes(3 * HD))
 
-    i = jnp.arange(dests, dtype=jnp.int32) // RING
-    j = jnp.arange(dests, dtype=jnp.int32) % RING
-    y, z = tp // RING, tp % RING
-    place = jnp.where(
-        core == 0,
-        (y + j) % RING * RING + (z + i) % RING,
-        (y + i) % RING * RING + (z + j) % RING,
-    )
-    place = jnp.concatenate([place, jnp.stack([core, chip])]).astype(jnp.int32)
-
-    w_first = fetch_weights(place, stay, w5, other_half, (2, 1))
+    w_first = fetch_weights(where, stay, w5, other_half, (2, 1))
     w_first = [pltpu.with_memory_space_constraint(w, pltpu.VMEM) for w in w_first]
     pair = lax.ppermute(pair, ("seq", "mod"), pair_perm(-1))
     far = lax.ppermute(far, "seq", [(i, (i + 2) % RING) for i in range(NH)])
@@ -541,22 +578,11 @@
     parts = [stay, far, pair]
     parts += [core_swap(x) for x in parts]
 
-    pieces = back_products(
-        place,
-        mod,
-        parts,
-        w_first,
-        w5,
-        other_half,
-        lambda x, hop: lax.ppermute(x, AXES, ring_perm(True, hop)),
-    )
-    total = pieces[0].astype(jnp.float32)
-    for hop in (2, 1, 3):
-        total = lax.optimization_barrier(total) + pieces[hop].astype(jnp.float32)
+    total = back_reduced(where, mod, parts, w_first, w5, other_half)
     result = total[0]
-    for hop in (2, 1, 3):
+    for hop in (1, 3, 2):
         got = lax.ppermute(total[hop].astype(jnp.bfloat16), AXES, ring_perm(False, hop))
-        result = result + got.astype(jnp.float32)
+        result = lax.optimization_barrier(result) + got.astype(jnp.float32)
     result = result.astype(jnp.bfloat16)
     mine = result[:rows]
     theirs = core_swap(result[rows:])

time: 101 us -> 95.4 us (0.945)
  waiting for transfers between devices: 19.6 us -> 15.5 us
  local copies, waits for them, and re-layouts: 3.83 us -> 0.1 us
  starting transfers between devices: 38.1 us -> 41.7 us
    ppermute x3 -> x6, waiting for transfers between devices: 6.38 us -> 0.97 us  [the longest x3 0.96 us: onward(): return lax.ppermute(x, AXES, ring_perm(True, 1))]
    unnamed x12 -> x4, local copies, waits for them, and re-layouts: 3.7 us -> 0.01 us
    ppermute x3 -> x6, starting transfers between devices: 6.03 us -> 8.71 us  [the longest x3 7.19 us: backward(): return lax.ppermute(x, AXES, ring_perm(True, -1))]
    pallas_call x1, Pallas kernels: 4.37 us -> 3.13 us  [fetch_weights(): pl.pallas_call(functools.partial(fetch_kernel, hops), in_specs=[pl.BlockS...]
  transfers between devices with their start and end apart: 21 -> 24, of which waited for: 14 -> 13; matrix products, arithmetic and copies ran while one was open for 1% -> 1% of each run, Pallas kernels for 24% -> 24%
where the time goes in v9:
time: 95.4 us; the launch traced here: 95.2 us
  starting transfers between devices  41.7 us (44%)
  Pallas kernels  36.3 us (38%)
  waiting for transfers between devices  15.5 us (16%)
  other arithmetic  1.28 us (1%)
    ppermute x11, starting transfers between devices, core_swap(): return lax.ppermute(x, 'mod', [(0, 1), (1, 0)])  15.7 us
    pallas_call x4, Pallas kernels, back_call(): pl.pallas_call(kernel, in_specs=in_specs, out_specs=[vmem] * len(out_shap...  11.8 us
    pallas_call x1, Pallas kernels, project(): pl.pallas_call(functools.partial(project_kernel, early), in_specs=[pl.Blo...  9.87 us
    ppermute x3, starting transfers between devices, backward(): return lax.ppermute(x, AXES, ring_perm(True, -1))  7.19 us
    ppermute x11, waiting for transfers between devices, core_swap(): return lax.ppermute(x, 'mod', [(0, 1), (1, 0)])  6.97 us
    ppermute x1, starting transfers between devices, per_device(): lax.ppermute(far, 'seq', [(i, (i + 2) % RING) for i in range(RING) if (i...  5.61 us
    ppermute x3, starting transfers between devices, per_device(): lax.ppermute(total[hop].astype(jnp.bfloat16), AXES, ring_perm(False, hop))  5.53 us
    pallas_call x1, Pallas kernels, project_own(): pl.pallas_call(own_kernel, in_specs=[hbm, hbm], out_specs=[vmem, vmem], o...  5.03 us
  transfers between devices with their start and end apart: 24, of which 13 were waited for; matrix products, arithmetic and copies ran while one was open for 1% of the time, Pallas kernels for 24%

profile of v9, /device:TPU:1, one launch (start us, length us, event | category | flops | bytes accessed | tf_op | source)
XLA Modules:
  0.0 95.2 jit_solution(7890899112445216755)
XLA Ops:
  0.0 1.4 %collective-permute-start = (bf16[192,8192]{1,0:T(8,128)(2,1)}, bf16[192,8192]{1,0:T(8,128)(2,1)S(1)}, u32[]{:S(2)}, u32[]{:S(2)}) collective-permute-start(bf16[192,8192]{1,0:T(8,128)(2,1)} %own_hbm.1), channel_id=1, source_target_pairs={{0,16},{16,0},{1,17},{17,1},{2,18},{18,2},{3,19},{19,3},{4,20},{20... | collective-permute-start | bytes 9437192 | tf_op jit(solution)/shard_map/ppermute | solution.py:19
  1.5 5.0 %project_own.1 = (f32[192,1152]{1,0:T(8,128)S(1)}, bf16[3,8,2,256,384]{4,3,2,1,0:T(8,128)(2,1)S(1)}) custom-call(bf16[192,8192]{1,0:T(8,128)(2,1)} %own_hbm.1, bf16[3,16,2,256,384]{4,3,2,1,0:T(8,128)(2,1)} %bitcast.19), custom_call_target="tpu_custom_call" | custom-call | flops 4000000000 | bytes 10000000 | tf_op jit(solution)/shard_map/project_own/pallas_call | solution.py:56
  6.9 9.9 %project.1 = (bf16[192,1152]{1,0:T(8,128)(2,1)S(1)}, bf16[192,1664]{1,0:T(8,128)(2,1)S(1)}, bf16[3,16,256,384]{3,2,1,0:T(8,128)(2,1)}) custom-call(s32[3]{0:T(128)S(1)} %pad_add_fusion.where_ref, f32[192,1152]{1,0:T(8,128)S(1)} %get-tuple-element.42.part_ref, bf16[192,8192]{1,0:T(8,128)(2,1)} %own_hbm.1, bf16[192,8192]{1,0:T(8,128)(2,1)S(1)} %collective-permute-done.oth_ref, ...), custom_call_target="tpu_custom_call" | custom-call | flops 7000000000 | bytes 10000000 | tf_op jit(solution)/shard_map/project/pallas_call | solution.py:141
  17.3 1.7 %collective-permute-done.1.got_ref = bf16[192,1664]{1,0:T(8,128)(2,1)S(1)} collective-permute-done((bf16[192,1664]{1,0:T(8,128)(2,1)S(1)}, bf16[192,1664]{1,0:T(8,128)(2,1)S(1)}, u32[]{:S(2)}, u32[]{:S(2)}) %collective-permute-start.1) | collective-permute-done | bytes 639008 | tf_op jit(solution)/shard_map/ppermute | solution.py:19
  21.5 5.6 %collective-permute-start.2 = (bf16[192,512]{1,0:T(8,128)(2,1)S(1)}, bf16[192,512]{1,0:T(8,128)(2,1)S(1)}, u32[]{:S(2)}, u32[]{:S(2)}) collective-permute-start(bf16[192,512]{1,0:T(8,128)(2,1)S(1)} %get-tuple-element.49), channel_id=1, source_target_pairs={{0,64},{64,0},{96,32},{1,65},{65,1},{97,33},{2,66},{66,2},{98,34},... | collective-permute-start | bytes 589832 | tf_op jit(solution)/shard_map/ppermute | solution.py:568
  27.2 1.9 %collective-permute-done.3.pair = bf16[2,192,512]{2,1,0:T(8,128)(2,1)S(1)} collective-permute-done((bf16[2,192,512]{2,1,0:T(8,128)(2,1)S(1)}, bf16[2,192,512]{2,1,0:T(8,128)(2,1)S(1)}, u32[]{:S(2)}, u32[]{:S(2)}) %collective-permute-start.3) | collective-permute-done | bytes 393248 | tf_op jit(solution)/shard_map/ppermute | solution.py:567
  29.1 6.4 %collective-permute-start.6 = (bf16[2,192,512]{2,1,0:T(8,128)(2,1)S(1)}, bf16[2,192,512]{2,1,0:T(8,128)(2,1)S(1)}, u32[]{:S(2)}, u32[]{:S(2)}) collective-permute-start(bf16[2,192,512]{2,1,0:T(8,128)(2,1)S(1)} %collective-permute-done.3.pair), channel_id=1, source_target_pairs={{0,16},{16,0},{1,17},{17,1},{2,18},{18,2},{3,19},{19,3},{4,20},{20... | collective-permute-start | bytes 1179656 | tf_op jit(solution)/shard_map/ppermute | solution.py:19
  37.4 4.7 %attention.1 = (f32[192,1408]{1,0:T(8,128)S(1)}, bf16[192,1152]{1,0:T(8,128)(2,1)S(1)}) custom-call(s32[3]{0:T(128)S(1)} %pad_add_fusion.where_ref, bf16[192,512]{1,0:T(8,128)(2,1)S(1)} %get-tuple-element.48.stay, bf16[192,512]{1,0:T(8,128)(2,1)S(1)} %collective-permute-done.2.far, bf16[2,192,512]{2,1,0:T(8,128)(2,1)S(1)} %collective-permute-done.3.pair, ...), custom_call_target="tpu_custom_call" | custom-call | flops 1000000000 | bytes 4000000 | tf_op jit(solution)/shard_map/attention/pallas_call | solution.py:294
  42.6 1.4 %collective-permute-done.7.got = bf16[192,1152]{1,0:T(8,128)(2,1)S(1)} collective-permute-done((bf16[192,1152]{1,0:T(8,128)(2,1)S(1)}, bf16[192,1152]{1,0:T(8,128)(2,1)S(1)}, u32[]{:S(2)}, u32[]{:S(2)}) %collective-permute-start.7) | collective-permute-done | bytes 442400 | tf_op jit(solution)/shard_map/ppermute | solution.py:19
  44.7 1.5 %collective-permute-start.8 = (bf16[2,192,384]{2,1,0:T(8,128)(2,1)S(1)}, bf16[2,192,384]{2,1,0:T(8,128)(2,1)S(1)}, u32[]{:S(2)}, u32[]{:S(2)}) collective-permute-start(bf16[2,192,384]{2,1,0:T(8,128)(2,1)S(1)} %get-tuple-element.54), channel_id=1, source_target_pairs={{0,96},{16,48},{32,0},{48,80},{64,32},{80,112},{1,97},{17,49},{33,... | collective-permute-start | bytes 884744 | tf_op jit(solution)/shard_map/ppermute | solution.py:575
  46.2 3.4 %collective-permute-start.9 = (bf16[192,384]{1,0:T(8,128)(2,1)S(1)}, bf16[192,384]{1,0:T(8,128)(2,1)S(1)}, u32[]{:S(2)}, u32[]{:S(2)}) collective-permute-start(bf16[192,384]{1,0:T(8,128)(2,1)S(1)} %get-tuple-element.55), channel_id=1, source_target_pairs={{0,64},{32,96},{64,0},{1,65},{33,97},{65,1},{2,66},{34,98},{66,2},... | collective-permute-start | bytes 442376 | tf_op jit(solution)/shard_map/ppermute | solution.py:576
  49.6 3.1 %fetch_weights.1 = (bf16[2,3,4,256,384]{4,3,2,1,0:T(8,128)(2,1)S(1)}, bf16[2,3,4,256,384]{4,3,2,1,0:T(8,128)(2,1)S(1)}) custom-call(s32[3]{0:T(128)S(1)} %pad_add_fusion.where_ref, bf16[192,384]{1,0:T(8,128)(2,1)S(1)} %get-tuple-element.53.after_ref.refs_0_, bf16[3,16,2,256,384]{4,3,2,1,0:T(8,128)(2,1)} %bitcast.21, ...), custom_call_target="tpu_custom_call" | custom-call | flops 1000000 | bytes 10000000 | tf_op jit(solution)/shard_map/fetch_weights/pallas_call | solution.py:383
  53.9 1.9 %collective-permute-start.13 = (bf16[2,192,384]{2,1,0:T(8,128)(2,1)S(1)}, bf16[2,192,384]{2,1,0:T(8,128)(2,1)S(1)}, u32[]{:S(2)}, u32[]{:S(2)}) collective-permute-start(bf16[2,192,384]{2,1,0:T(8,128)(2,1)S(1)} %collective-permute-done.8.refs_2_), channel_id=1, source_target_pairs={{0,16},{16,0},{1,17},{17,1},{2,18},{18,2},{3,19},{19,3},{4,20},{20... | collective-permute-start | bytes 884744 | tf_op jit(solution)/shard_map/ppermute | solution.py:19
  57.5 3.6 %back.4 = (bf16[2,384,256]{2,1,0:T(8,128)(2,1)S(1)}, bf16[2,384,256]{2,1,0:T(8,128)(2,1)S(1)}, bf16[384,2304]{1,0:T(8,128)(2,1)S(1)}, bf16[2,3,4,256,384]{4,3,2,1,0:T(8,128)(2,1)S(1)}) custom-call(s32[3]{0:T(128)S(1)} %pad_add_fusion.where_ref, s32[12,128]{1,0:T(8,128)S(1)} %bitcast.18, bf16[192,384]{1,0:T(8,128)(2,1)S(1)} %get-tuple-element.53.after_ref.refs_0_, ...), custom_call_target="tpu_custom_call" | custom-call | flops 1000000 | bytes 10000 | tf_op jit(solution)/shard_map/back/pallas_call | solution.py:431
  62.5 1.5 %collective-permute-start.15 = (bf16[2,384,256]{2,1,0:T(8,128)(2,1)S(1)}, bf16[2,384,256]{2,1,0:T(8,128)(2,1)S(1)}, u32[]{:S(2)}, u32[]{:S(2)}) collective-permute-start(bf16[2,384,256]{2,1,0:T(8,128)(2,1)S(1)} %get-tuple-element.68), channel_id=1, source_target_pairs={{0,3},{1,0},{2,1},{3,2},{4,7},{5,4},{6,5},{7,6},{8,11},{9,8},{10,9... | collective-permute-start | bytes 1179656 | tf_op jit(solution)/shard_map/ppermute | solution.py:475
  64.0 2.0 %back.5 = (bf16[2,384,256]{2,1,0:T(8,128)(2,1)S(1)}, bf16[2,384,256]{2,1,0:T(8,128)(2,1)S(1)}) custom-call(bf16[384,2304]{1,0:T(8,128)(2,1)S(1)} %get-tuple-element.62.g_ref, bf16[2,3,4,256,384]{4,3,2,1,0:T(8,128)(2,1)S(1)} %get-tuple-element.63.w_ref), custom_call_target="tpu_custom_call" | custom-call | flops 1000000 | bytes 10000 | tf_op jit(solution)/shard_map/back/pallas_call | solution.py:431
  66.1 2.0 %back.6 = (bf16[2,384,256]{2,1,0:T(8,128)(2,1)S(1)}, bf16[2,384,256]{2,1,0:T(8,128)(2,1)S(1)}) custom-call(bf16[384,2304]{1,0:T(8,128)(2,1)S(1)} %get-tuple-element.62.g_ref, bf16[2,3,4,256,384]{4,3,2,1,0:T(8,128)(2,1)S(1)} %get-tuple-element.66.w_ref), custom_call_target="tpu_custom_call" | custom-call | flops 1000000 | bytes 10000 | tf_op jit(solution)/shard_map/back/pallas_call | solution.py:431
  68.1 3.0 %collective-permute-start.17 = (bf16[2,384,256]{2,1,0:T(8,128)(2,1)S(1)}, bf16[2,384,256]{2,1,0:T(8,128)(2,1)S(1)}, u32[]{:S(2)}, u32[]{:S(2)}) collective-permute-start(bf16[2,384,256]{2,1,0:T(8,128)(2,1)S(1)} %get-tuple-element.73), channel_id=1, source_target_pairs={{0,3},{1,0},{2,1},{3,2},{4,7},{5,4},{6,5},{7,6},{8,11},{9,8},{10,9... | collective-permute-start | bytes 1179656 | tf_op jit(solution)/shard_map/ppermute | solution.py:475
  71.4 2.7 %collective-permute-start.20 = (bf16[2,384,256]{2,1,0:T(8,128)(2,1)S(1)}, bf16[2,384,256]{2,1,0:T(8,128)(2,1)S(1)}, u32[]{:S(2)}, u32[]{:S(2)}) collective-permute-start(bf16[2,384,256]{2,1,0:T(8,128)(2,1)S(1)} %add.42.after_b), channel_id=1, source_target_pairs={{0,3},{1,0},{2,1},{3,2},{4,7},{5,4},{6,5},{7,6},{8,11},{9,8},{10,9... | collective-permute-start | bytes 1179656 | tf_op jit(solution)/shard_map/ppermute | solution.py:475
  74.1 4.1 %back.7 = (bf16[2,384,256]{2,1,0:T(8,128)(2,1)S(1)}, bf16[2,384,256]{2,1,0:T(8,128)(2,1)S(1)}) custom-call(s32[3]{0:T(128)S(1)} %pad_add_fusion.where_ref, bf16[2,384,256]{2,1,0:T(8,128)(2,1)S(1)} %add.41.after_a, bf16[2,384,256]{2,1,0:T(8,128)(2,1)S(1)} %add.42.after_b, bf16[384,2304]{1,0:T(8,128)(2,1)S(1)} %get-tuple-element.62.g_ref, ...), custom_call_target="tpu_custom_call" | custom-call | flops 1000000 | bytes 10000 | tf_op jit(solution)/shard_map/back/pallas_call | solution.py:431
  79.5 1.4 %collective-permute-start.19 = (bf16[384,256]{1,0:T(8,128)(2,1)S(1)}, bf16[384,256]{1,0:T(8,128)(2,1)S(1)}, u32[]{:S(2)}, u32[]{:S(2)}) collective-permute-start(bf16[384,256]{1,0:T(8,128)(2,1)S(1)} %fusion), channel_id=1, source_target_pairs={{0,4},{1,5},{2,6},{3,7},{4,8},{5,9},{6,10},{7,11},{8,12},{9,13},{1... | collective-permute-start | bytes 589832 | tf_op jit(solution)/shard_map/ppermute | solution.py:584
  81.1 3.7 %collective-permute-start.22 = (bf16[384,256]{1,0:T(8,128)(2,1)S(1)}, bf16[384,256]{1,0:T(8,128)(2,1)S(1)}, u32[]{:S(2)}, u32[]{:S(2)}) collective-permute-start(bf16[384,256]{1,0:T(8,128)(2,1)S(1)} %get-tuple-element.79), channel_id=1, source_target_pairs={{0,8},{1,9},{2,10},{3,11},{4,12},{5,13},{6,14},{7,15},{8,0},{9,1},... | collective-permute-start | bytes 589832 | tf_op jit(solution)/shard_map/ppermute | solution.py:584
  86.5 3.3 %collective-permute-done.21 = bf16[384,256]{1,0:T(8,128)(2,1)S(1)} collective-permute-done((bf16[384,256]{1,0:T(8,128)(2,1)S(1)}, bf16[384,256]{1,0:T(8,128)(2,1)S(1)}, u32[]{:S(2)}, u32[]{:S(2)}) %collective-permute-start.21) | collective-permute-done | bytes 196640 | tf_op jit(solution)/shard_map/ppermute | solution.py:584
  89.8 3.6 %collective-permute-start.23 = (bf16[192,256]{1,0:T(8,128)(2,1)S(1)}, bf16[192,256]{1,0:T(8,128)(2,1)S(1)}, u32[]{:S(2)}, u32[]{:S(2)}) collective-permute-start(bf16[192,256]{1,0:T(8,128)(2,1)S(1)} %get-tuple-element.82), channel_id=1, source_target_pairs={{0,16},{16,0},{1,17},{17,1},{2,18},{18,2},{3,19},{19,3},{4,20},{20... | collective-permute-start | bytes 294920 | tf_op jit(solution)/shard_map/ppermute | solution.py:19
  (53 shorter events, 15.9 us)
Async XLA Ops:
  0.0 6.9 %collective-permute-start = (bf16[192,8192]{1,0:T(8,128)(2,1)}, bf16[192,8192]{1,0:T(8,128)(2,1)S(1)}, u32[]{:S(2)}, u32[]{:S(2)}) collective-permute-start(bf16[192,8192]{1,0:T(8,128)(2,1)} %own_hbm.1), channel_id=1, source_target_pairs={{0,16},{16,0},{1,17},{17,1},{2,18},{18,2},{3,19},{19,3},{4,20},{20... | collective-permute-start | bytes 9437192 | tf_op jit(solution)/shard_map/ppermute | solution.py:19
  16.8 2.2 %collective-permute-start.1 = (bf16[192,1664]{1,0:T(8,128)(2,1)S(1)}, bf16[192,1664]{1,0:T(8,128)(2,1)S(1)}, u32[]{:S(2)}, u32[]{:S(2)}) collective-permute-start(bf16[192,1664]{1,0:T(8,128)(2,1)S(1)} %get-tuple-element.45.sent_ref), channel_id=1, source_target_pairs={{0,16},{16,0},{1,17},{17,1},{2,18},{18,2},{3,19},{19,3},{4,20},{20... | collective-permute-start | bytes 1916936 | tf_op jit(solution)/shard_map/ppermute | solution.py:19
  19.0 30.7 %collective-permute-start.10 = (bf16[3,16,256,384]{3,2,1,0:T(8,128)(2,1)}, bf16[3,16,256,384]{3,2,1,0:T(8,128)(2,1)S(1)}, u32[]{:S(2)}, u32[]{:S(2)}) collective-permute-start(bf16[3,16,256,384]{3,2,1,0:T(8,128)(2,1)} %get-tuple-element.56), channel_id=1, source_target_pairs={{0,16},{16,0},{1,17},{17,1},{2,18},{18,2},{3,19},{19,3},{4,20},{20... | collective-permute-start | bytes 28311560 | tf_op jit(solution)/shard_map/ppermute | solution.py:19
  20.2 8.8 %collective-permute-start.3 = (bf16[2,192,512]{2,1,0:T(8,128)(2,1)S(1)}, bf16[2,192,512]{2,1,0:T(8,128)(2,1)S(1)}, u32[]{:S(2)}, u32[]{:S(2)}) collective-permute-start(bf16[2,192,512]{2,1,0:T(8,128)(2,1)S(1)} %get-tuple-element.50), channel_id=1, source_target_pairs={{0,32},{32,64},{48,16},{80,48},{96,0},{112,80},{1,33},{33,65},{49,... | collective-permute-start | bytes 1179656 | tf_op jit(solution)/shard_map/ppermute | solution.py:567
  21.5 13.9 %collective-permute-start.2 = (bf16[192,512]{1,0:T(8,128)(2,1)S(1)}, bf16[192,512]{1,0:T(8,128)(2,1)S(1)}, u32[]{:S(2)}, u32[]{:S(2)}) collective-permute-start(bf16[192,512]{1,0:T(8,128)(2,1)S(1)} %get-tuple-element.49), channel_id=1, source_target_pairs={{0,64},{64,0},{96,32},{1,65},{65,1},{97,33},{2,66},{66,2},{98,34},... | collective-permute-start | bytes 589832 | tf_op jit(solution)/shard_map/ppermute | solution.py:568
  29.1 8.3 %collective-permute-start.6 = (bf16[2,192,512]{2,1,0:T(8,128)(2,1)S(1)}, bf16[2,192,512]{2,1,0:T(8,128)(2,1)S(1)}, u32[]{:S(2)}, u32[]{:S(2)}) collective-permute-start(bf16[2,192,512]{2,1,0:T(8,128)(2,1)S(1)} %collective-permute-done.3.pair), channel_id=1, source_target_pairs={{0,16},{16,0},{1,17},{17,1},{2,18},{18,2},{3,19},{19,3},{4,20},{20... | collective-permute-start | bytes 1179656 | tf_op jit(solution)/shard_map/ppermute | solution.py:19
  35.5 1.6 %collective-permute-start.4 = (bf16[192,512]{1,0:T(8,128)(2,1)S(1)}, bf16[192,512]{1,0:T(8,128)(2,1)S(1)}, u32[]{:S(2)}, u32[]{:S(2)}) collective-permute-start(bf16[192,512]{1,0:T(8,128)(2,1)S(1)} %get-tuple-element.48.stay), channel_id=1, source_target_pairs={{0,16},{16,0},{1,17},{17,1},{2,18},{18,2},{3,19},{19,3},{4,20},{20... | collective-permute-start | bytes 589832 | tf_op jit(solution)/shard_map/ppermute | solution.py:19
  35.5 1.9 %collective-permute-start.5 = (bf16[192,512]{1,0:T(8,128)(2,1)S(1)}, bf16[192,512]{1,0:T(8,128)(2,1)S(1)}, u32[]{:S(2)}, u32[]{:S(2)}) collective-permute-start(bf16[192,512]{1,0:T(8,128)(2,1)S(1)} %collective-permute-done.2.far), channel_id=1, source_target_pairs={{0,16},{16,0},{1,17},{17,1},{2,18},{18,2},{3,19},{19,3},{4,20},{20... | collective-permute-start | bytes 589832 | tf_op jit(solution)/shard_map/ppermute | solution.py:19
  42.1 1.9 %collective-permute-start.7 = (bf16[192,1152]{1,0:T(8,128)(2,1)S(1)}, bf16[192,1152]{1,0:T(8,128)(2,1)S(1)}, u32[]{:S(2)}, u32[]{:S(2)}) collective-permute-start(bf16[192,1152]{1,0:T(8,128)(2,1)S(1)} %get-tuple-element.52), channel_id=1, source_target_pairs={{0,16},{16,0},{1,17},{17,1},{2,18},{18,2},{3,19},{19,3},{4,20},{20... | collective-permute-start | bytes 1327112 | tf_op jit(solution)/shard_map/ppermute | solution.py:19
  44.7 9.3 %collective-permute-start.8 = (bf16[2,192,384]{2,1,0:T(8,128)(2,1)S(1)}, bf16[2,192,384]{2,1,0:T(8,128)(2,1)S(1)}, u32[]{:S(2)}, u32[]{:S(2)}) collective-permute-start(bf16[2,192,384]{2,1,0:T(8,128)(2,1)S(1)} %get-tuple-element.54), channel_id=1, source_target_pairs={{0,96},{16,48},{32,0},{48,80},{64,32},{80,112},{1,97},{17,49},{33,... | collective-permute-start | bytes 884744 | tf_op jit(solution)/shard_map/ppermute | solution.py:575
  46.2 7.8 %collective-permute-start.9 = (bf16[192,384]{1,0:T(8,128)(2,1)S(1)}, bf16[192,384]{1,0:T(8,128)(2,1)S(1)}, u32[]{:S(2)}, u32[]{:S(2)}) collective-permute-start(bf16[192,384]{1,0:T(8,128)(2,1)S(1)} %get-tuple-element.55), channel_id=1, source_target_pairs={{0,64},{32,96},{64,0},{1,65},{33,97},{65,1},{2,66},{34,98},{66,2},... | collective-permute-start | bytes 442376 | tf_op jit(solution)/shard_map/ppermute | solution.py:576
  53.9 3.5 %collective-permute-start.13 = (bf16[2,192,384]{2,1,0:T(8,128)(2,1)S(1)}, bf16[2,192,384]{2,1,0:T(8,128)(2,1)S(1)}, u32[]{:S(2)}, u32[]{:S(2)}) collective-permute-start(bf16[2,192,384]{2,1,0:T(8,128)(2,1)S(1)} %collective-permute-done.8.refs_2_), channel_id=1, source_target_pairs={{0,16},{16,0},{1,17},{17,1},{2,18},{18,2},{3,19},{19,3},{4,20},{20... | collective-permute-start | bytes 884744 | tf_op jit(solution)/shard_map/ppermute | solution.py:19
  55.8 1.4 %collective-permute-start.11 = (bf16[192,384]{1,0:T(8,128)(2,1)S(1)}, bf16[192,384]{1,0:T(8,128)(2,1)S(1)}, u32[]{:S(2)}, u32[]{:S(2)}) collective-permute-start(bf16[192,384]{1,0:T(8,128)(2,1)S(1)} %get-tuple-element.53.after_ref.refs_0_), channel_id=1, source_target_pairs={{0,16},{16,0},{1,17},{17,1},{2,18},{18,2},{3,19},{19,3},{4,20},{20... | collective-permute-start | bytes 442376 | tf_op jit(solution)/shard_map/ppermute | solution.py:19
  55.8 1.6 %collective-permute-start.12 = (bf16[192,384]{1,0:T(8,128)(2,1)S(1)}, bf16[192,384]{1,0:T(8,128)(2,1)S(1)}, u32[]{:S(2)}, u32[]{:S(2)}) collective-permute-start(bf16[192,384]{1,0:T(8,128)(2,1)S(1)} %collective-permute-done.9.refs_1_), channel_id=1, source_target_pairs={{0,16},{16,0},{1,17},{17,1},{2,18},{18,2},{3,19},{19,3},{4,20},{20... | collective-permute-start | bytes 442376 | tf_op jit(solution)/shard_map/ppermute | solution.py:19
  61.1 10.0 %collective-permute-start.14 = (bf16[2,384,256]{2,1,0:T(8,128)(2,1)S(1)}, bf16[2,384,256]{2,1,0:T(8,128)(2,1)S(1)}, u32[]{:S(2)}, u32[]{:S(2)}) collective-permute-start(bf16[2,384,256]{2,1,0:T(8,128)(2,1)S(1)} %get-tuple-element.65), channel_id=1, source_target_pairs={{0,1},{1,2},{2,3},{3,0},{4,5},{5,6},{6,7},{7,4},{8,9},{9,10},{10,1... | collective-permute-start | bytes 1179656 | tf_op jit(solution)/shard_map/ppermute | solution.py:472
  62.5 8.8 %collective-permute-start.15 = (bf16[2,384,256]{2,1,0:T(8,128)(2,1)S(1)}, bf16[2,384,256]{2,1,0:T(8,128)(2,1)S(1)}, u32[]{:S(2)}, u32[]{:S(2)}) collective-permute-start(bf16[2,384,256]{2,1,0:T(8,128)(2,1)S(1)} %get-tuple-element.68), channel_id=1, source_target_pairs={{0,3},{1,0},{2,1},{3,2},{4,7},{5,4},{6,5},{7,6},{8,11},{9,8},{10,9... | collective-permute-start | bytes 1179656 | tf_op jit(solution)/shard_map/ppermute | solution.py:475
  66.0 12.2 %collective-permute-start.16 = (bf16[2,384,256]{2,1,0:T(8,128)(2,1)S(1)}, bf16[2,384,256]{2,1,0:T(8,128)(2,1)S(1)}, u32[]{:S(2)}, u32[]{:S(2)}) collective-permute-start(bf16[2,384,256]{2,1,0:T(8,128)(2,1)S(1)} %get-tuple-element.71), channel_id=1, source_target_pairs={{0,1},{1,2},{2,3},{3,0},{4,5},{5,6},{6,7},{7,4},{8,9},{9,10},{10,1... | collective-permute-start | bytes 1179656 | tf_op jit(solution)/shard_map/ppermute | solution.py:472
  68.1 10.2 %collective-permute-start.17 = (bf16[2,384,256]{2,1,0:T(8,128)(2,1)S(1)}, bf16[2,384,256]{2,1,0:T(8,128)(2,1)S(1)}, u32[]{:S(2)}, u32[]{:S(2)}) collective-permute-start(bf16[2,384,256]{2,1,0:T(8,128)(2,1)S(1)} %get-tuple-element.73), channel_id=1, source_target_pairs={{0,3},{1,0},{2,1},{3,2},{4,7},{5,4},{6,5},{7,6},{8,11},{9,8},{10,9... | collective-permute-start | bytes 1179656 | tf_op jit(solution)/shard_map/ppermute | solution.py:475
  71.2 8.2 %collective-permute-start.18 = (bf16[2,384,256]{2,1,0:T(8,128)(2,1)S(1)}, bf16[2,384,256]{2,1,0:T(8,128)(2,1)S(1)}, u32[]{:S(2)}, u32[]{:S(2)}) collective-permute-start(bf16[2,384,256]{2,1,0:T(8,128)(2,1)S(1)} %add.41.after_a), channel_id=1, source_target_pairs={{0,1},{1,2},{2,3},{3,0},{4,5},{5,6},{6,7},{7,4},{8,9},{9,10},{10,1... | collective-permute-start | bytes 1179656 | tf_op jit(solution)/shard_map/ppermute | solution.py:472
  71.4 9.6 %collective-permute-start.20 = (bf16[2,384,256]{2,1,0:T(8,128)(2,1)S(1)}, bf16[2,384,256]{2,1,0:T(8,128)(2,1)S(1)}, u32[]{:S(2)}, u32[]{:S(2)}) collective-permute-start(bf16[2,384,256]{2,1,0:T(8,128)(2,1)S(1)} %add.42.after_b), channel_id=1, source_target_pairs={{0,3},{1,0},{2,1},{3,2},{4,7},{5,4},{6,5},{7,6},{8,11},{9,8},{10,9... | collective-permute-start | bytes 1179656 | tf_op jit(solution)/shard_map/ppermute | solution.py:475
  79.5 6.9 %collective-permute-start.19 = (bf16[384,256]{1,0:T(8,128)(2,1)S(1)}, bf16[384,256]{1,0:T(8,128)(2,1)S(1)}, u32[]{:S(2)}, u32[]{:S(2)}) collective-permute-start(bf16[384,256]{1,0:T(8,128)(2,1)S(1)} %fusion), channel_id=1, source_target_pairs={{0,4},{1,5},{2,6},{3,7},{4,8},{5,9},{6,10},{7,11},{8,12},{9,13},{1... | collective-permute-start | bytes 589832 | tf_op jit(solution)/shard_map/ppermute | solution.py:584
  81.1 8.7 %collective-permute-start.22 = (bf16[384,256]{1,0:T(8,128)(2,1)S(1)}, bf16[384,256]{1,0:T(8,128)(2,1)S(1)}, u32[]{:S(2)}, u32[]{:S(2)}) collective-permute-start(bf16[384,256]{1,0:T(8,128)(2,1)S(1)} %get-tuple-element.79), channel_id=1, source_target_pairs={{0,8},{1,9},{2,10},{3,11},{4,12},{5,13},{6,14},{7,15},{8,0},{9,1},... | collective-permute-start | bytes 589832 | tf_op jit(solution)/shard_map/ppermute | solution.py:584
  84.8 5.0 %collective-permute-start.21 = (bf16[384,256]{1,0:T(8,128)(2,1)S(1)}, bf16[384,256]{1,0:T(8,128)(2,1)S(1)}, u32[]{:S(2)}, u32[]{:S(2)}) collective-permute-start(bf16[384,256]{1,0:T(8,128)(2,1)S(1)} %get-tuple-element.80), channel_id=1, source_target_pairs={{0,12},{1,13},{2,14},{3,15},{4,0},{5,1},{6,2},{7,3},{8,4},{9,5},{1... | collective-permute-start | bytes 589832 | tf_op jit(solution)/shard_map/ppermute | solution.py:584
  89.8 4.6 %collective-permute-start.23 = (bf16[192,256]{1,0:T(8,128)(2,1)S(1)}, bf16[192,256]{1,0:T(8,128)(2,1)S(1)}, u32[]{:S(2)}, u32[]{:S(2)}) collective-permute-start(bf16[192,256]{1,0:T(8,128)(2,1)S(1)} %get-tuple-element.82), channel_id=1, source_target_pairs={{0,16},{16,0},{1,17},{17,1},{2,18},{18,2},{3,19},{19,3},{4,20},{20... | collective-permute-start | bytes 294920 | tf_op jit(solution)/shard_map/ppermute | solution.py:19
  (2 other events, 17.8 us)

commit v10 on v9

--- a/solution.py
+++ b/solution.py
@@ -11,6 +11,7 @@
 NH = 3
 RING = 4
 SCALE = HD**-0.5
+SECOND = (0, 2, 1, 3)
 AXES = ("seq", "mod", "tp")
 MIB = 1024 * 1024
 
@@ -19,9 +20,10 @@
     return lax.ppermute(x, "mod", [(0, 1), (1, 0)])
 
 
-def weight_block(w_ref, i):
-    size = 4 * w_ref.shape[3]
-    return jnp.concatenate([w_ref[c, 2 * i : 2 * i + 2].reshape(size, NH * HD) for c in range(3)], axis=1)
+def weight_block(w_ref, i, count=1):
+    size = 4 * w_ref.shape[3] * count
+    rows = slice(2 * i, 2 * (i + count))
+    return jnp.concatenate([w_ref[c, rows].reshape(size, NH * HD) for c in range(3)], axis=1)
 
 
 def own_kernel(a_hbm, w_hbm, part_ref, w_ref, a_s, a_sem, w_sem):
@@ -82,10 +84,10 @@
     side = 1 - where_ref[1]
 
     def fetch_own(i):
-        return pltpu.make_async_copy(own_hbm.at[:, pl.ds(i * block, block)], a_s.at[i - early], own_sem.at[i])
+        return pltpu.make_async_copy(own_hbm.at[:, pl.ds(i * block, block)], a_s.at[:, pl.ds((i - early) * block, block)], own_sem.at[i])
 
     def other(i):
-        return oth_ref[:, i * block : (i + 1) * block]
+        return oth_ref[:, i * block : (i + 2) * block]
 
     def fetch_weights(i):
         src = w_hbm.at[:, 2 * i : 2 * i + 2]
@@ -104,19 +106,20 @@
     for i in range(early):
         put_half(i).start()
     acc_ref[0:rows] = part_ref[...]
-    for i in range(chunks):
+    for i in range(0, chunks, 2):
         if i < early:
-            part = jnp.dot(other(i), weight_block(w_ref, i), preferred_element_type=jnp.float32)
+            part = jnp.dot(other(i), weight_block(w_ref, i, 2), preferred_element_type=jnp.float32)
             if i == 0:
                 acc_ref[rows:] = part
             else:
                 acc_ref[rows:] += part
         else:
-            fetch_own(i).wait()
-            fetch_weights(i).wait()
-            put_half(i).start()
-            a = jnp.concatenate([a_s[i - early], other(i)], axis=0)
-            acc_ref[...] += jnp.dot(a, weight_block(w_s, i - early), preferred_element_type=jnp.float32)
+            for k in (i, i + 1):
+                fetch_own(k).wait()
+                fetch_weights(k).wait()
+                put_half(k).start()
+            a = jnp.concatenate([a_s[:, (i - early) * block : (i - early + 2) * block], other(i)], axis=0)
+            acc_ref[...] += jnp.dot(a, weight_block(w_s, i - early, 2), preferred_element_type=jnp.float32)
     for h in range(NH):
         for c in range(3):
             lo = c * NH * HD + h * HD
@@ -148,7 +151,7 @@
             pltpu.HBM((3,) + w5.shape[1:2] + w5.shape[3:], jnp.bfloat16),
         ],
         scratch_shapes=[
-            pltpu.VMEM((chunks - early, rows, depth // chunks), jnp.bfloat16),
+            pltpu.VMEM((rows, depth // chunks * (chunks - early)), jnp.bfloat16),
             pltpu.VMEM((3, 2 * (chunks - early)) + w5.shape[2:], jnp.bfloat16),
             pltpu.VMEM((2 * rows, 9 * HD), jnp.float32),
             dma,
@@ -182,11 +185,13 @@
     return jnp.sum(jnp.where(place == lax.broadcasted_iota(jnp.int32, (rows, HD), 1), spread, 0.0), axis=1, keepdims=True)
 
 
-def route_kernel(where_ref, mod_ref, own_ref, sent_ref, got_ref, g_ref, pair_out, far_out, stay_out):
+def route_kernel(where_ref, mod_ref, own_ref, sent_ref, got_ref, g_ref, pair_out, far_out, stay_out, mask_out):
     chip, core = where_ref[0], where_ref[1]
     rows = own_ref.shape[0]
-    mine = section_rows(mod_ref, 2 * chip + core, core, rows) > 0
-    others = section_rows(mod_ref, 2 * chip + 1 - core, core, rows) > 0
+    masks = [section_rows(mod_ref, 2 * chip + side, core, rows) for side in (core, 1 - core)]
+    mine, others = [mask > 0 for mask in masks]
+    for block, mask in enumerate(masks):
+        mask_out[block] = jnp.broadcast_to(mask, (rows, HD)).astype(jnp.bfloat16)
 
     def own_rows(head):
         cols = head_columns(head, 3)
@@ -326,11 +331,10 @@
     put(far_out, keep[:, 8 * HD : 9 * HD], 9 * HD, 7 * HD)
 
 
-def gather(where, mod_ref, parts, out_ref):
+def gather(where, mask_ref, parts, out_ref):
     chip, core = where
     stay, far, pair, stay_o, far_o, pair_o = parts
     rows = stay.shape[0]
-    mine = [section_rows(mod_ref, 2 * chip + side, core, rows) for side in (core, 1 - core)]
     for head, refs in (
         (chip, (stay, stay_o)),
         ((chip + 2) % RING, (far, far_o)),
@@ -341,13 +345,12 @@
         @pl.when(head < NH)
         def _():
             for block, x_ref in enumerate(refs):
-                x = x_ref[...]
-                zero = jnp.zeros_like(x)
-                for side in range(2):
-                    kept = jnp.where(mine[block] == 1.0 - side, x, zero)
-                    for c in range(3):
+                for c in range(3):
+                    x = x_ref[:, c * HD : (c + 1) * HD]
+                    mine = x * mask_ref[block]
+                    for side, kept in enumerate((mine, x - mine)):
                         lo = pl.multiple_of(((side * 3 + c) * NH + head) * HD, HD)
-                        out_ref[block * rows : (block + 1) * rows, pl.ds(lo, HD)] = kept[:, c * HD : (c + 1) * HD]
+                        out_ref[block * rows : (block + 1) * rows, pl.ds(lo, HD)] = kept
 
 
 def destination(where_ref, i, j):
@@ -360,7 +363,7 @@
     core = where_ref[1]
     copies = []
     for j in range(RING):
-        dest = destination(where_ref, hop, j)
+        dest = destination(where_ref, hop, SECOND[j])
         copies.append(pltpu.make_async_copy(own_hbm.at[:, dest, core], to_ref.at[0, :, j], sem.at[0, j]))
         copies.append(pltpu.make_async_copy(other_hbm.at[:, dest], to_ref.at[1, :, j], sem.at[1, j]))
     return copies
@@ -402,11 +405,11 @@
         outs[(first + i) // 2][(first + i) % 2] = res[:, i * cols : (i + 1) * cols]
 
 
-def back_first_kernel(following, where_ref, mod_ref, *refs):
+def back_first_kernel(following, where_ref, mask_ref, *refs):
     *parts, w_ref, own_hbm, other_hbm, out_a, out_b, g_ref, next_ref, sem = refs
     for copy in weight_copies(where_ref, own_hbm, other_hbm, next_ref, sem, following):
         copy.start()
-    gather((where_ref[0], where_ref[1]), mod_ref, parts, g_ref)
+    gather((where_ref[0], where_ref[1]), mask_ref, parts, g_ref)
     product(g_ref, w_ref, (out_a, out_b))
     for copy in weight_copies(where_ref, own_hbm, other_hbm, next_ref, sem, following):
         copy.wait()
@@ -457,7 +460,7 @@
     )(a, b)
 
 
-def back_reduced(where, mod, parts, weights, w5, other_half):
+def back_reduced(where, masks, parts, weights, w5, other_half):
     rows = 2 * parts[0].shape[0]
     cols = w5.shape[3]
     smem = pl.BlockSpec(memory_space=pltpu.SMEM)
@@ -477,7 +480,7 @@
     w_two, w_one = weights
     two_a, two_b, g, w_three = back_call(
         functools.partial(back_first_kernel, 3),
-        (where, mod, *parts, w_two, w5, other_half),
+        (where, masks, *parts, w_two, w5, other_half),
         [smem] + [vmem] * 8 + [hbm, anywhere],
         halves + [pltpu.VMEM((rows, 18 * HD), jnp.bfloat16), pltpu.VMEM(w_shape, jnp.bfloat16)],
         [sem],
@@ -506,7 +509,7 @@
     sum_a = sum_a + from_one_a.astype(jnp.float32)
     sum_a, sum_b = lax.optimization_barrier((sum_a, sum_b))
     sum_b = sum_b + from_three_b.astype(jnp.float32)
-    return [sum_a[0], sum_a[1], sum_b[0], sum_b[1]]
+    return dict(zip(SECOND, (sum_a[0], sum_a[1], sum_b[0], sum_b[1])))
 
 
 def ring_perm(first, hop):
@@ -561,8 +564,12 @@
         block = jax.ShapeDtypeStruct((rows, width), jnp.bfloat16)
         return [jax.ShapeDtypeStruct((2, rows, width), jnp.bfloat16), block, block]
 
-    pair, far, stay = small_call(
-        route_kernel, "route", where, (mod, proj_own, sent, got, grad_attn), part_shapes(4 * HD)
+    pair, far, stay, masks = small_call(
+        route_kernel,
+        "route",
+        where,
+        (mod, proj_own, sent, got, grad_attn),
+        part_shapes(4 * HD) + [jax.ShapeDtypeStruct((2, rows, HD), jnp.bfloat16)],
     )
     pair = lax.ppermute(pair, ("seq", "mod"), pair_perm(1))
     far = lax.ppermute(far, "seq", [(i, (i + 2) % RING) for i in range(RING) if (i + 2) % RING < NH])
@@ -574,13 +581,13 @@
     w_first = [pltpu.with_memory_space_constraint(w, pltpu.VMEM) for w in w_first]
     pair = lax.ppermute(pair, ("seq", "mod"), pair_perm(-1))
     far = lax.ppermute(far, "seq", [(i, (i + 2) % RING) for i in range(NH)])
-    pair, far, w_first = lax.optimization_barrier((pair, far, w_first))
+    far, w_first = lax.optimization_barrier((far, w_first))
     parts = [stay, far, pair]
     parts += [core_swap(x) for x in parts]
 
-    total = back_reduced(where, mod, parts, w_first, w5, other_half)
+    total = back_reduced(where, masks, parts, w_first, w5, other_half)
     result = total[0]
-    for hop in (1, 3, 2):
+    for hop in SECOND[1:]:
         got = lax.ppermute(total[hop].astype(jnp.bfloat16), AXES, ring_perm(False, hop))
         result = lax.optimization_barrier(result) + got.astype(jnp.float32)
     result = result.astype(jnp.bfloat16)

time: 95.4 us -> 100 us (1.048)
  starting transfers between devices: 41.7 us -> 47 us
    ppermute x11, starting transfers between devices: 15.7 us -> 21.6 us  [core_swap(): return lax.ppermute(x, 'mod', [(0, 1), (1, 0)])]
    ppermute x1, waiting for transfers between devices: 1.17 us -> 0.01 us  [per_device(): far = lax.ppermute(far, 'seq', [(i, (i + 2) % RING) for i in range(NH)])]
  transfers between devices with their start and end apart: 24 -> 24, of which waited for: 13 -> 12; matrix products, arithmetic and copies ran while one was open for 1% -> 1% of each run, Pallas kernels for 24% -> 23%
where the time goes in v10:
time: 100 us; the launch traced here: 99.8 us
  starting transfers between devices  47 us (47%)
  Pallas kernels  36.1 us (36%)
  waiting for transfers between devices  15.1 us (15%)
  other arithmetic  1.29 us (1%)
    ppermute x11, starting transfers between devices, core_swap(): return lax.ppermute(x, 'mod', [(0, 1), (1, 0)])  21.6 us
    pallas_call x4, Pallas kernels, back_call(): pl.pallas_call(kernel, in_specs=in_specs, out_specs=[vmem] * len(out_shap...  11.3 us
    pallas_call x1, Pallas kernels, project(): pl.pallas_call(functools.partial(project_kernel, early), in_specs=[pl.Blo...  10.1 us
    ppermute x3, starting transfers between devices, backward(): return lax.ppermute(x, AXES, ring_perm(True, -1))  6.98 us
    ppermute x11, waiting for transfers between devices, core_swap(): return lax.ppermute(x, 'mod', [(0, 1), (1, 0)])  6.86 us
    ppermute x1, starting transfers between devices, per_device(): lax.ppermute(far, 'seq', [(i, (i + 2) % RING) for i in range(RING) if (i...  5.6 us
    ppermute x3, waiting for transfers between devices, per_device(): lax.ppermute(total[hop].astype(jnp.bfloat16), AXES, ring_perm(False, hop))  5.15 us
    pallas_call x1, Pallas kernels, project_own(): pl.pallas_call(own_kernel, in_specs=[hbm, hbm], out_specs=[vmem, vmem], o...  5.03 us
  transfers between devices with their start and end apart: 24, of which 12 were waited for; matrix products, arithmetic and copies ran while one was open for 1% of the time, Pallas kernels for 23%

profile of v10, /device:TPU:1, one launch (start us, length us, event | category | flops | bytes accessed | tf_op | source)
XLA Modules:
  0.0 99.8 jit_solution(9814345281841432565)
XLA Ops:
  0.0 1.4 %collective-permute-start = (bf16[192,8192]{1,0:T(8,128)(2,1)}, bf16[192,8192]{1,0:T(8,128)(2,1)S(1)}, u32[]{:S(2)}, u32[]{:S(2)}) collective-permute-start(bf16[192,8192]{1,0:T(8,128)(2,1)} %own_hbm.1), channel_id=1, source_target_pairs={{0,16},{16,0},{1,17},{17,1},{2,18},{18,2},{3,19},{19,3},{4,20},{20... | collective-permute-start | bytes 9437192 | tf_op jit(solution)/shard_map/ppermute | solution.py:20
  1.5 5.0 %project_own.1 = (f32[192,1152]{1,0:T(8,128)S(1)}, bf16[3,8,2,256,384]{4,3,2,1,0:T(8,128)(2,1)S(1)}) custom-call(bf16[192,8192]{1,0:T(8,128)(2,1)} %own_hbm.1, bf16[3,16,2,256,384]{4,3,2,1,0:T(8,128)(2,1)} %bitcast.18), custom_call_target="tpu_custom_call" | custom-call | flops 4000000000 | bytes 10000000 | tf_op jit(solution)/shard_map/project_own/pallas_call | solution.py:58
  6.9 10.1 %project.1 = (bf16[192,1152]{1,0:T(8,128)(2,1)S(1)}, bf16[192,1664]{1,0:T(8,128)(2,1)S(1)}, bf16[3,16,256,384]{3,2,1,0:T(8,128)(2,1)}) custom-call(s32[3]{0:T(128)S(1)} %pad_add_fusion.where_ref, f32[192,1152]{1,0:T(8,128)S(1)} %get-tuple-element.42.part_ref, bf16[192,8192]{1,0:T(8,128)(2,1)} %own_hbm.1, bf16[192,8192]{1,0:T(8,128)(2,1)S(1)} %collective-permute-done.oth_ref, ...), custom_call_target="tpu_custom_call" | custom-call | flops 7000000000 | bytes 10000000 | tf_op jit(solution)/shard_map/project/pallas_call | solution.py:144
  17.5 1.7 %collective-permute-done.1.got_ref = bf16[192,1664]{1,0:T(8,128)(2,1)S(1)} collective-permute-done((bf16[192,1664]{1,0:T(8,128)(2,1)S(1)}, bf16[192,1664]{1,0:T(8,128)(2,1)S(1)}, u32[]{:S(2)}, u32[]{:S(2)}) %collective-permute-start.1) | collective-permute-done | bytes 639008 | tf_op jit(solution)/shard_map/ppermute | solution.py:20
  21.8 5.6 %collective-permute-start.2 = (bf16[192,512]{1,0:T(8,128)(2,1)S(1)}, bf16[192,512]{1,0:T(8,128)(2,1)S(1)}, u32[]{:S(2)}, u32[]{:S(2)}) collective-permute-start(bf16[192,512]{1,0:T(8,128)(2,1)S(1)} %get-tuple-element.50), channel_id=1, source_target_pairs={{0,64},{64,0},{96,32},{1,65},{65,1},{97,33},{2,66},{66,2},{98,34},... | collective-permute-start | bytes 589832 | tf_op jit(solution)/shard_map/ppermute | solution.py:575
  27.4 1.9 %collective-permute-done.3.pair = bf16[2,192,512]{2,1,0:T(8,128)(2,1)S(1)} collective-permute-done((bf16[2,192,512]{2,1,0:T(8,128)(2,1)S(1)}, bf16[2,192,512]{2,1,0:T(8,128)(2,1)S(1)}, u32[]{:S(2)}, u32[]{:S(2)}) %collective-permute-start.3) | collective-permute-done | bytes 393248 | tf_op jit(solution)/shard_map/ppermute | solution.py:574
  29.3 6.4 %collective-permute-start.6 = (bf16[2,192,512]{2,1,0:T(8,128)(2,1)S(1)}, bf16[2,192,512]{2,1,0:T(8,128)(2,1)S(1)}, u32[]{:S(2)}, u32[]{:S(2)}) collective-permute-start(bf16[2,192,512]{2,1,0:T(8,128)(2,1)S(1)} %collective-permute-done.3.pair), channel_id=1, source_target_pairs={{0,16},{16,0},{1,17},{17,1},{2,18},{18,2},{3,19},{19,3},{4,20},{20... | collective-permute-start | bytes 1179656 | tf_op jit(solution)/shard_map/ppermute | solution.py:20
  37.6 4.7 %attention.1 = (f32[192,1408]{1,0:T(8,128)S(1)}, bf16[192,1152]{1,0:T(8,128)(2,1)S(1)}) custom-call(s32[3]{0:T(128)S(1)} %pad_add_fusion.where_ref, bf16[192,512]{1,0:T(8,128)(2,1)S(1)} %get-tuple-element.49.stay, bf16[192,512]{1,0:T(8,128)(2,1)S(1)} %collective-permute-done.2.far, bf16[2,192,512]{2,1,0:T(8,128)(2,1)S(1)} %collective-permute-done.3.pair, ...), custom_call_target="tpu_custom_call" | custom-call | flops 1000000000 | bytes 4000000 | tf_op jit(solution)/shard_map/attention/pallas_call | solution.py:299
  42.8 1.4 %collective-permute-done.7.got = bf16[192,1152]{1,0:T(8,128)(2,1)S(1)} collective-permute-done((bf16[192,1152]{1,0:T(8,128)(2,1)S(1)}, bf16[192,1152]{1,0:T(8,128)(2,1)S(1)}, u32[]{:S(2)}, u32[]{:S(2)}) %collective-permute-start.7) | collective-permute-done | bytes 442400 | tf_op jit(solution)/shard_map/ppermute | solution.py:20
  44.9 1.5 %collective-permute-start.10 = (bf16[2,192,384]{2,1,0:T(8,128)(2,1)S(1)}, bf16[2,192,384]{2,1,0:T(8,128)(2,1)S(1)}, u32[]{:S(2)}, u32[]{:S(2)}) collective-permute-start(bf16[2,192,384]{2,1,0:T(8,128)(2,1)S(1)} %get-tuple-element.60), channel_id=1, source_target_pairs={{0,96},{16,48},{32,0},{48,80},{64,32},{80,112},{1,97},{17,49},{33,... | collective-permute-start | bytes 884744 | tf_op jit(solution)/shard_map/ppermute | solution.py:582
  46.4 3.4 %collective-permute-start.8 = (bf16[192,384]{1,0:T(8,128)(2,1)S(1)}, bf16[192,384]{1,0:T(8,128)(2,1)S(1)}, u32[]{:S(2)}, u32[]{:S(2)}) collective-permute-start(bf16[192,384]{1,0:T(8,128)(2,1)S(1)} %get-tuple-element.55), channel_id=1, source_target_pairs={{0,64},{32,96},{64,0},{1,65},{33,97},{65,1},{2,66},{34,98},{66,2},... | collective-permute-start | bytes 442376 | tf_op jit(solution)/shard_map/ppermute | solution.py:583
  50.0 4.9 %collective-permute-start.13 = (bf16[2,192,384]{2,1,0:T(8,128)(2,1)S(1)}, bf16[2,192,384]{2,1,0:T(8,128)(2,1)S(1)}, u32[]{:S(2)}, u32[]{:S(2)}) collective-permute-start(bf16[2,192,384]{2,1,0:T(8,128)(2,1)S(1)} %collective-permute-done.10.refs_2_), channel_id=1, source_target_pairs={{0,16},{16,0},{1,17},{17,1},{2,18},{18,2},{3,19},{19,3},{4,20},{20... | collective-permute-start | bytes 884744 | tf_op jit(solution)/shard_map/ppermute | solution.py:20
  55.0 3.1 %fetch_weights.1 = (bf16[2,3,4,256,384]{4,3,2,1,0:T(8,128)(2,1)S(1)}, bf16[2,3,4,256,384]{4,3,2,1,0:T(8,128)(2,1)S(1)}) custom-call(s32[3]{0:T(128)S(1)} %pad_add_fusion.where_ref, bf16[192,384]{1,0:T(8,128)(2,1)S(1)} %get-tuple-element.54.after_ref.refs_0_, bf16[3,16,2,256,384]{4,3,2,1,0:T(8,128)(2,1)} %bitcast.20, ...), custom_call_target="tpu_custom_call" | custom-call | flops 1000000 | bytes 10000000 | tf_op jit(solution)/shard_map/fetch_weights/pallas_call | solution.py:386
  59.7 3.2 %back.4 = (bf16[2,384,256]{2,1,0:T(8,128)(2,1)S(1)}, bf16[2,384,256]{2,1,0:T(8,128)(2,1)S(1)}, bf16[384,2304]{1,0:T(8,128)(2,1)S(1)}, bf16[2,3,4,256,384]{4,3,2,1,0:T(8,128)(2,1)S(1)}) custom-call(s32[3]{0:T(128)S(1)} %pad_add_fusion.where_ref, bf16[2,192,128]{2,1,0:T(8,128)(2,1)S(1)} %get-tuple-element.48.mask_ref, ...), custom_call_target="tpu_custom_call" | custom-call | flops 1000000 | bytes 10000 | tf_op jit(solution)/shard_map/back/pallas_call | solution.py:434
  64.3 1.5 %collective-permute-start.15 = (bf16[2,384,256]{2,1,0:T(8,128)(2,1)S(1)}, bf16[2,384,256]{2,1,0:T(8,128)(2,1)S(1)}, u32[]{:S(2)}, u32[]{:S(2)}) collective-permute-start(bf16[2,384,256]{2,1,0:T(8,128)(2,1)S(1)} %get-tuple-element.68), channel_id=1, source_target_pairs={{0,3},{1,0},{2,1},{3,2},{4,7},{5,4},{6,5},{7,6},{8,11},{9,8},{10,9... | collective-permute-start | bytes 1179656 | tf_op jit(solution)/shard_map/ppermute | solution.py:478
  65.8 2.0 %back.5 = (bf16[2,384,256]{2,1,0:T(8,128)(2,1)S(1)}, bf16[2,384,256]{2,1,0:T(8,128)(2,1)S(1)}) custom-call(bf16[384,2304]{1,0:T(8,128)(2,1)S(1)} %get-tuple-element.62.g_ref, bf16[2,3,4,256,384]{4,3,2,1,0:T(8,128)(2,1)S(1)} %get-tuple-element.63.w_ref), custom_call_target="tpu_custom_call" | custom-call | flops 1000000 | bytes 10000 | tf_op jit(solution)/shard_map/back/pallas_call | solution.py:434
  67.9 2.0 %back.6 = (bf16[2,384,256]{2,1,0:T(8,128)(2,1)S(1)}, bf16[2,384,256]{2,1,0:T(8,128)(2,1)S(1)}) custom-call(bf16[384,2304]{1,0:T(8,128)(2,1)S(1)} %get-tuple-element.62.g_ref, bf16[2,3,4,256,384]{4,3,2,1,0:T(8,128)(2,1)S(1)} %get-tuple-element.66.w_ref), custom_call_target="tpu_custom_call" | custom-call | flops 1000000 | bytes 10000 | tf_op jit(solution)/shard_map/back/pallas_call | solution.py:434
  69.9 2.7 %collective-permute-start.17 = (bf16[2,384,256]{2,1,0:T(8,128)(2,1)S(1)}, bf16[2,384,256]{2,1,0:T(8,128)(2,1)S(1)}, u32[]{:S(2)}, u32[]{:S(2)}) collective-permute-start(bf16[2,384,256]{2,1,0:T(8,128)(2,1)S(1)} %get-tuple-element.73), channel_id=1, source_target_pairs={{0,3},{1,0},{2,1},{3,2},{4,7},{5,4},{6,5},{7,6},{8,11},{9,8},{10,9... | collective-permute-start | bytes 1179656 | tf_op jit(solution)/shard_map/ppermute | solution.py:478
  73.2 2.7 %collective-permute-start.20 = (bf16[2,384,256]{2,1,0:T(8,128)(2,1)S(1)}, bf16[2,384,256]{2,1,0:T(8,128)(2,1)S(1)}, u32[]{:S(2)}, u32[]{:S(2)}) collective-permute-start(bf16[2,384,256]{2,1,0:T(8,128)(2,1)S(1)} %add.42.after_b), channel_id=1, source_target_pairs={{0,3},{1,0},{2,1},{3,2},{4,7},{5,4},{6,5},{7,6},{8,11},{9,8},{10,9... | collective-permute-start | bytes 1179656 | tf_op jit(solution)/shard_map/ppermute | solution.py:478
  75.9 4.1 %back.7 = (bf16[2,384,256]{2,1,0:T(8,128)(2,1)S(1)}, bf16[2,384,256]{2,1,0:T(8,128)(2,1)S(1)}) custom-call(s32[3]{0:T(128)S(1)} %pad_add_fusion.where_ref, bf16[2,384,256]{2,1,0:T(8,128)(2,1)S(1)} %add.41.after_a, bf16[2,384,256]{2,1,0:T(8,128)(2,1)S(1)} %add.42.after_b, bf16[384,2304]{1,0:T(8,128)(2,1)S(1)} %get-tuple-element.62.g_ref, ...), custom_call_target="tpu_custom_call" | custom-call | flops 1000000 | bytes 10000 | tf_op jit(solution)/shard_map/back/pallas_call | solution.py:434
  81.3 3.4 %collective-permute-start.19 = (bf16[384,256]{1,0:T(8,128)(2,1)S(1)}, bf16[384,256]{1,0:T(8,128)(2,1)S(1)}, u32[]{:S(2)}, u32[]{:S(2)}) collective-permute-start(bf16[384,256]{1,0:T(8,128)(2,1)S(1)} %fusion), channel_id=1, source_target_pairs={{0,8},{1,9},{2,10},{3,11},{4,12},{5,13},{6,14},{7,15},{8,0},{9,1},... | collective-permute-start | bytes 589832 | tf_op jit(solution)/shard_map/ppermute | solution.py:591
  86.4 1.4 %collective-permute-done.19 = bf16[384,256]{1,0:T(8,128)(2,1)S(1)} collective-permute-done((bf16[384,256]{1,0:T(8,128)(2,1)S(1)}, bf16[384,256]{1,0:T(8,128)(2,1)S(1)}, u32[]{:S(2)}, u32[]{:S(2)}) %collective-permute-start.19) | collective-permute-done | bytes 196640 | tf_op jit(solution)/shard_map/ppermute | solution.py:591
  87.8 3.8 %collective-permute-done.21 = bf16[384,256]{1,0:T(8,128)(2,1)S(1)} collective-permute-done((bf16[384,256]{1,0:T(8,128)(2,1)S(1)}, bf16[384,256]{1,0:T(8,128)(2,1)S(1)}, u32[]{:S(2)}, u32[]{:S(2)}) %collective-permute-start.21) | collective-permute-done | bytes 196640 | tf_op jit(solution)/shard_map/ppermute | solution.py:591
  91.7 6.4 %collective-permute-start.23 = (bf16[192,256]{1,0:T(8,128)(2,1)S(1)}, bf16[192,256]{1,0:T(8,128)(2,1)S(1)}, u32[]{:S(2)}, u32[]{:S(2)}) collective-permute-start(bf16[192,256]{1,0:T(8,128)(2,1)S(1)} %get-tuple-element.82), channel_id=1, source_target_pairs={{0,16},{16,0},{1,17},{17,1},{2,18},{18,2},{3,19},{19,3},{4,20},{20... | collective-permute-start | bytes 294920 | tf_op jit(solution)/shard_map/ppermute | solution.py:20
  (53 shorter events, 15.0 us)
Async XLA Ops:
  0.0 6.9 %collective-permute-start = (bf16[192,8192]{1,0:T(8,128)(2,1)}, bf16[192,8192]{1,0:T(8,128)(2,1)S(1)}, u32[]{:S(2)}, u32[]{:S(2)}) collective-permute-start(bf16[192,8192]{1,0:T(8,128)(2,1)} %own_hbm.1), channel_id=1, source_target_pairs={{0,16},{16,0},{1,17},{17,1},{2,18},{18,2},{3,19},{19,3},{4,20},{20... | collective-permute-start | bytes 9437192 | tf_op jit(solution)/shard_map/ppermute | solution.py:20
  17.1 2.2 %collective-permute-start.1 = (bf16[192,1664]{1,0:T(8,128)(2,1)S(1)}, bf16[192,1664]{1,0:T(8,128)(2,1)S(1)}, u32[]{:S(2)}, u32[]{:S(2)}) collective-permute-start(bf16[192,1664]{1,0:T(8,128)(2,1)S(1)} %get-tuple-element.45.sent_ref), channel_id=1, source_target_pairs={{0,16},{16,0},{1,17},{17,1},{2,18},{18,2},{3,19},{19,3},{4,20},{20... | collective-permute-start | bytes 1916936 | tf_op jit(solution)/shard_map/ppermute | solution.py:20
  19.2 35.8 %collective-permute-start.9 = (bf16[3,16,256,384]{3,2,1,0:T(8,128)(2,1)}, bf16[3,16,256,384]{3,2,1,0:T(8,128)(2,1)S(1)}, u32[]{:S(2)}, u32[]{:S(2)}) collective-permute-start(bf16[3,16,256,384]{3,2,1,0:T(8,128)(2,1)} %get-tuple-element.56), channel_id=1, source_target_pairs={{0,16},{16,0},{1,17},{17,1},{2,18},{18,2},{3,19},{19,3},{4,20},{20... | collective-permute-start | bytes 28311560 | tf_op jit(solution)/shard_map/ppermute | solution.py:20
  20.5 8.8 %collective-permute-start.3 = (bf16[2,192,512]{2,1,0:T(8,128)(2,1)S(1)}, bf16[2,192,512]{2,1,0:T(8,128)(2,1)S(1)}, u32[]{:S(2)}, u32[]{:S(2)}) collective-permute-start(bf16[2,192,512]{2,1,0:T(8,128)(2,1)S(1)} %get-tuple-element.51), channel_id=1, source_target_pairs={{0,32},{32,64},{48,16},{80,48},{96,0},{112,80},{1,33},{33,65},{49,... | collective-permute-start | bytes 1179656 | tf_op jit(solution)/shard_map/ppermute | solution.py:574
  21.8 13.9 %collective-permute-start.2 = (bf16[192,512]{1,0:T(8,128)(2,1)S(1)}, bf16[192,512]{1,0:T(8,128)(2,1)S(1)}, u32[]{:S(2)}, u32[]{:S(2)}) collective-permute-start(bf16[192,512]{1,0:T(8,128)(2,1)S(1)} %get-tuple-element.50), channel_id=1, source_target_pairs={{0,64},{64,0},{96,32},{1,65},{65,1},{97,33},{2,66},{66,2},{98,34},... | collective-permute-start | bytes 589832 | tf_op jit(solution)/shard_map/ppermute | solution.py:575
  29.3 8.3 %collective-permute-start.6 = (bf16[2,192,512]{2,1,0:T(8,128)(2,1)S(1)}, bf16[2,192,512]{2,1,0:T(8,128)(2,1)S(1)}, u32[]{:S(2)}, u32[]{:S(2)}) collective-permute-start(bf16[2,192,512]{2,1,0:T(8,128)(2,1)S(1)} %collective-permute-done.3.pair), channel_id=1, source_target_pairs={{0,16},{16,0},{1,17},{17,1},{2,18},{18,2},{3,19},{19,3},{4,20},{20... | collective-permute-start | bytes 1179656 | tf_op jit(solution)/shard_map/ppermute | solution.py:20
  35.7 1.6 %collective-permute-start.4 = (bf16[192,512]{1,0:T(8,128)(2,1)S(1)}, bf16[192,512]{1,0:T(8,128)(2,1)S(1)}, u32[]{:S(2)}, u32[]{:S(2)}) collective-permute-start(bf16[192,512]{1,0:T(8,128)(2,1)S(1)} %get-tuple-element.49.stay), channel_id=1, source_target_pairs={{0,16},{16,0},{1,17},{17,1},{2,18},{18,2},{3,19},{19,3},{4,20},{20... | collective-permute-start | bytes 589832 | tf_op jit(solution)/shard_map/ppermute | solution.py:20
  35.7 1.9 %collective-permute-start.5 = (bf16[192,512]{1,0:T(8,128)(2,1)S(1)}, bf16[192,512]{1,0:T(8,128)(2,1)S(1)}, u32[]{:S(2)}, u32[]{:S(2)}) collective-permute-start(bf16[192,512]{1,0:T(8,128)(2,1)S(1)} %collective-permute-done.2.far), channel_id=1, source_target_pairs={{0,16},{16,0},{1,17},{17,1},{2,18},{18,2},{3,19},{19,3},{4,20},{20... | collective-permute-start | bytes 589832 | tf_op jit(solution)/shard_map/ppermute | solution.py:20
  42.4 1.9 %collective-permute-start.7 = (bf16[192,1152]{1,0:T(8,128)(2,1)S(1)}, bf16[192,1152]{1,0:T(8,128)(2,1)S(1)}, u32[]{:S(2)}, u32[]{:S(2)}) collective-permute-start(bf16[192,1152]{1,0:T(8,128)(2,1)S(1)} %get-tuple-element.53), channel_id=1, source_target_pairs={{0,16},{16,0},{1,17},{17,1},{2,18},{18,2},{3,19},{19,3},{4,20},{20... | collective-permute-start | bytes 1327112 | tf_op jit(solution)/shard_map/ppermute | solution.py:20
  44.9 5.1 %collective-permute-start.10 = (bf16[2,192,384]{2,1,0:T(8,128)(2,1)S(1)}, bf16[2,192,384]{2,1,0:T(8,128)(2,1)S(1)}, u32[]{:S(2)}, u32[]{:S(2)}) collective-permute-start(bf16[2,192,384]{2,1,0:T(8,128)(2,1)S(1)} %get-tuple-element.60), channel_id=1, source_target_pairs={{0,96},{16,48},{32,0},{48,80},{64,32},{80,112},{1,97},{17,49},{33,... | collective-permute-start | bytes 884744 | tf_op jit(solution)/shard_map/ppermute | solution.py:582
  46.4 11.7 %collective-permute-start.8 = (bf16[192,384]{1,0:T(8,128)(2,1)S(1)}, bf16[192,384]{1,0:T(8,128)(2,1)S(1)}, u32[]{:S(2)}, u32[]{:S(2)}) collective-permute-start(bf16[192,384]{1,0:T(8,128)(2,1)S(1)} %get-tuple-element.55), channel_id=1, source_target_pairs={{0,64},{32,96},{64,0},{1,65},{33,97},{65,1},{2,66},{34,98},{66,2},... | collective-permute-start | bytes 442376 | tf_op jit(solution)/shard_map/ppermute | solution.py:583
  50.0 8.7 %collective-permute-start.13 = (bf16[2,192,384]{2,1,0:T(8,128)(2,1)S(1)}, bf16[2,192,384]{2,1,0:T(8,128)(2,1)S(1)}, u32[]{:S(2)}, u32[]{:S(2)}) collective-permute-start(bf16[2,192,384]{2,1,0:T(8,128)(2,1)S(1)} %collective-permute-done.10.refs_2_), channel_id=1, source_target_pairs={{0,16},{16,0},{1,17},{17,1},{2,18},{18,2},{3,19},{19,3},{4,20},{20... | collective-permute-start | bytes 884744 | tf_op jit(solution)/shard_map/ppermute | solution.py:20
  55.0 3.7 %collective-permute-start.11 = (bf16[192,384]{1,0:T(8,128)(2,1)S(1)}, bf16[192,384]{1,0:T(8,128)(2,1)S(1)}, u32[]{:S(2)}, u32[]{:S(2)}) collective-permute-start(bf16[192,384]{1,0:T(8,128)(2,1)S(1)} %get-tuple-element.54.after_ref.refs_0_), channel_id=1, source_target_pairs={{0,16},{16,0},{1,17},{17,1},{2,18},{18,2},{3,19},{19,3},{4,20},{20... | collective-permute-start | bytes 442376 | tf_op jit(solution)/shard_map/ppermute | solution.py:20
  58.1 1.6 %collective-permute-start.12 = (bf16[192,384]{1,0:T(8,128)(2,1)S(1)}, bf16[192,384]{1,0:T(8,128)(2,1)S(1)}, u32[]{:S(2)}, u32[]{:S(2)}) collective-permute-start(bf16[192,384]{1,0:T(8,128)(2,1)S(1)} %collective-permute-done.8.refs_1_), channel_id=1, source_target_pairs={{0,16},{16,0},{1,17},{17,1},{2,18},{18,2},{3,19},{19,3},{4,20},{20... | collective-permute-start | bytes 442376 | tf_op jit(solution)/shard_map/ppermute | solution.py:20
  62.9 9.8 %collective-permute-start.14 = (bf16[2,384,256]{2,1,0:T(8,128)(2,1)S(1)}, bf16[2,384,256]{2,1,0:T(8,128)(2,1)S(1)}, u32[]{:S(2)}, u32[]{:S(2)}) collective-permute-start(bf16[2,384,256]{2,1,0:T(8,128)(2,1)S(1)} %get-tuple-element.65), channel_id=1, source_target_pairs={{0,1},{1,2},{2,3},{3,0},{4,5},{5,6},{6,7},{7,4},{8,9},{9,10},{10,1... | collective-permute-start | bytes 1179656 | tf_op jit(solution)/shard_map/ppermute | solution.py:475
  64.3 8.8 %collective-permute-start.15 = (bf16[2,384,256]{2,1,0:T(8,128)(2,1)S(1)}, bf16[2,384,256]{2,1,0:T(8,128)(2,1)S(1)}, u32[]{:S(2)}, u32[]{:S(2)}) collective-permute-start(bf16[2,384,256]{2,1,0:T(8,128)(2,1)S(1)} %get-tuple-element.68), channel_id=1, source_target_pairs={{0,3},{1,0},{2,1},{3,2},{4,7},{5,4},{6,5},{7,6},{8,11},{9,8},{10,9... | collective-permute-start | bytes 1179656 | tf_op jit(solution)/shard_map/ppermute | solution.py:478
  67.8 12.2 %collective-permute-start.16 = (bf16[2,384,256]{2,1,0:T(8,128)(2,1)S(1)}, bf16[2,384,256]{2,1,0:T(8,128)(2,1)S(1)}, u32[]{:S(2)}, u32[]{:S(2)}) collective-permute-start(bf16[2,384,256]{2,1,0:T(8,128)(2,1)S(1)} %get-tuple-element.71), channel_id=1, source_target_pairs={{0,1},{1,2},{2,3},{3,0},{4,5},{5,6},{6,7},{7,4},{8,9},{9,10},{10,1... | collective-permute-start | bytes 1179656 | tf_op jit(solution)/shard_map/ppermute | solution.py:475
  69.9 10.2 %collective-permute-start.17 = (bf16[2,384,256]{2,1,0:T(8,128)(2,1)S(1)}, bf16[2,384,256]{2,1,0:T(8,128)(2,1)S(1)}, u32[]{:S(2)}, u32[]{:S(2)}) collective-permute-start(bf16[2,384,256]{2,1,0:T(8,128)(2,1)S(1)} %get-tuple-element.73), channel_id=1, source_target_pairs={{0,3},{1,0},{2,1},{3,2},{4,7},{5,4},{6,5},{7,6},{8,11},{9,8},{10,9... | collective-permute-start | bytes 1179656 | tf_op jit(solution)/shard_map/ppermute | solution.py:478
  72.8 8.4 %collective-permute-start.18 = (bf16[2,384,256]{2,1,0:T(8,128)(2,1)S(1)}, bf16[2,384,256]{2,1,0:T(8,128)(2,1)S(1)}, u32[]{:S(2)}, u32[]{:S(2)}) collective-permute-start(bf16[2,384,256]{2,1,0:T(8,128)(2,1)S(1)} %add.41.after_a), channel_id=1, source_target_pairs={{0,1},{1,2},{2,3},{3,0},{4,5},{5,6},{6,7},{7,4},{8,9},{9,10},{10,1... | collective-permute-start | bytes 1179656 | tf_op jit(solution)/shard_map/ppermute | solution.py:475
  73.2 11.5 %collective-permute-start.20 = (bf16[2,384,256]{2,1,0:T(8,128)(2,1)S(1)}, bf16[2,384,256]{2,1,0:T(8,128)(2,1)S(1)}, u32[]{:S(2)}, u32[]{:S(2)}) collective-permute-start(bf16[2,384,256]{2,1,0:T(8,128)(2,1)S(1)} %add.42.after_b), channel_id=1, source_target_pairs={{0,3},{1,0},{2,1},{3,2},{4,7},{5,4},{6,5},{7,6},{8,11},{9,8},{10,9... | collective-permute-start | bytes 1179656 | tf_op jit(solution)/shard_map/ppermute | solution.py:478
  81.3 6.4 %collective-permute-start.19 = (bf16[384,256]{1,0:T(8,128)(2,1)S(1)}, bf16[384,256]{1,0:T(8,128)(2,1)S(1)}, u32[]{:S(2)}, u32[]{:S(2)}) collective-permute-start(bf16[384,256]{1,0:T(8,128)(2,1)S(1)} %fusion), channel_id=1, source_target_pairs={{0,8},{1,9},{2,10},{3,11},{4,12},{5,13},{6,14},{7,15},{8,0},{9,1},... | collective-permute-start | bytes 589832 | tf_op jit(solution)/shard_map/ppermute | solution.py:591
  84.8 6.8 %collective-permute-start.22 = (bf16[384,256]{1,0:T(8,128)(2,1)S(1)}, bf16[384,256]{1,0:T(8,128)(2,1)S(1)}, u32[]{:S(2)}, u32[]{:S(2)}) collective-permute-start(bf16[384,256]{1,0:T(8,128)(2,1)S(1)} %get-tuple-element.79), channel_id=1, source_target_pairs={{0,12},{1,13},{2,14},{3,15},{4,0},{5,1},{6,2},{7,3},{8,4},{9,5},{1... | collective-permute-start | bytes 589832 | tf_op jit(solution)/shard_map/ppermute | solution.py:591
  85.5 6.0 %collective-permute-start.21 = (bf16[384,256]{1,0:T(8,128)(2,1)S(1)}, bf16[384,256]{1,0:T(8,128)(2,1)S(1)}, u32[]{:S(2)}, u32[]{:S(2)}) collective-permute-start(bf16[384,256]{1,0:T(8,128)(2,1)S(1)} %get-tuple-element.80), channel_id=1, source_target_pairs={{0,4},{1,5},{2,6},{3,7},{4,8},{5,9},{6,10},{7,11},{8,12},{9,13},{1... | collective-permute-start | bytes 589832 | tf_op jit(solution)/shard_map/ppermute | solution.py:591
  91.7 7.4 %collective-permute-start.23 = (bf16[192,256]{1,0:T(8,128)(2,1)S(1)}, bf16[192,256]{1,0:T(8,128)(2,1)S(1)}, u32[]{:S(2)}, u32[]{:S(2)}) collective-permute-start(bf16[192,256]{1,0:T(8,128)(2,1)S(1)} %get-tuple-element.82), channel_id=1, source_target_pairs={{0,16},{16,0},{1,17},{17,1},{2,18},{18,2},{3,19},{19,3},{4,20},{20... | collective-permute-start | bytes 294920 | tf_op jit(solution)/shard_map/ppermute | solution.py:20
  (2 other events, 18.1 us)

commit v11 on v10

--- a/solution.py
+++ b/solution.py
@@ -11,7 +11,6 @@
 NH = 3
 RING = 4
 SCALE = HD**-0.5
-SECOND = (0, 2, 1, 3)
 AXES = ("seq", "mod", "tp")
 MIB = 1024 * 1024
 
@@ -20,10 +19,9 @@
     return lax.ppermute(x, "mod", [(0, 1), (1, 0)])
 
 
-def weight_block(w_ref, i, count=1):
-    size = 4 * w_ref.shape[3] * count
-    rows = slice(2 * i, 2 * (i + count))
-    return jnp.concatenate([w_ref[c, rows].reshape(size, NH * HD) for c in range(3)], axis=1)
+def weight_block(w_ref, i):
+    size = 4 * w_ref.shape[3]
+    return jnp.concatenate([w_ref[c, 2 * i : 2 * i + 2].reshape(size, NH * HD) for c in range(3)], axis=1)
 
 
 def own_kernel(a_hbm, w_hbm, part_ref, w_ref, a_s, a_sem, w_sem):
@@ -84,10 +82,10 @@
     side = 1 - where_ref[1]
 
     def fetch_own(i):
-        return pltpu.make_async_copy(own_hbm.at[:, pl.ds(i * block, block)], a_s.at[:, pl.ds((i - early) * block, block)], own_sem.at[i])
+        return pltpu.make_async_copy(own_hbm.at[:, pl.ds(i * block, block)], a_s.at[i - early], own_sem.at[i])
 
     def other(i):
-        return oth_ref[:, i * block : (i + 2) * block]
+        return oth_ref[:, i * block : (i + 1) * block]
 
     def fetch_weights(i):
         src = w_hbm.at[:, 2 * i : 2 * i + 2]
@@ -106,20 +104,19 @@
     for i in range(early):
         put_half(i).start()
     acc_ref[0:rows] = part_ref[...]
-    for i in range(0, chunks, 2):
+    for i in range(chunks):
         if i < early:
-            part = jnp.dot(other(i), weight_block(w_ref, i, 2), preferred_element_type=jnp.float32)
+            part = jnp.dot(other(i), weight_block(w_ref, i), preferred_element_type=jnp.float32)
             if i == 0:
                 acc_ref[rows:] = part
             else:
                 acc_ref[rows:] += part
         else:
-            for k in (i, i + 1):
-                fetch_own(k).wait()
-                fetch_weights(k).wait()
-                put_half(k).start()
-            a = jnp.concatenate([a_s[:, (i - early) * block : (i - early + 2) * block], other(i)], axis=0)
-            acc_ref[...] += jnp.dot(a, weight_block(w_s, i - early, 2), preferred_element_type=jnp.float32)
+            fetch_own(i).wait()
+            fetch_weights(i).wait()
+            put_half(i).start()
+            a = jnp.concatenate([a_s[i - early], other(i)], axis=0)
+            acc_ref[...] += jnp.dot(a, weight_block(w_s, i - early), preferred_element_type=jnp.float32)
     for h in range(NH):
         for c in range(3):
             lo = c * NH * HD + h * HD
@@ -151,7 +148,7 @@
             pltpu.HBM((3,) + w5.shape[1:2] + w5.shape[3:], jnp.bfloat16),
         ],
         scratch_shapes=[
-            pltpu.VMEM((rows, depth // chunks * (chunks - early)), jnp.bfloat16),
+            pltpu.VMEM((chunks - early, rows, depth // chunks), jnp.bfloat16),
             pltpu.VMEM((3, 2 * (chunks - early)) + w5.shape[2:], jnp.bfloat16),
             pltpu.VMEM((2 * rows, 9 * HD), jnp.float32),
             dma,
@@ -363,7 +360,7 @@
     core = where_ref[1]
     copies = []
     for j in range(RING):
-        dest = destination(where_ref, hop, SECOND[j])
+        dest = destination(where_ref, hop, j)
         copies.append(pltpu.make_async_copy(own_hbm.at[:, dest, core], to_ref.at[0, :, j], sem.at[0, j]))
         copies.append(pltpu.make_async_copy(other_hbm.at[:, dest], to_ref.at[1, :, j], sem.at[1, j]))
     return copies
@@ -395,14 +392,14 @@
     )(where, after, w5, other_half)
 
 
-def product(g_ref, w_ref, outs, first=0, count=RING):
+def product(g_ref, w_ref, outs):
     cols = w_ref.shape[3]
-    w = [w_ref[side, c, first : first + count].reshape(count * cols, NH * HD) for side in range(2) for c in range(3)]
+    w = [w_ref[side, c].reshape(RING * cols, NH * HD) for side in range(2) for c in range(3)]
     res = lax.dot_general(
         g_ref[...], jnp.concatenate(w, axis=1), (((1,), (1,)), ((), ())), preferred_element_type=jnp.float32
     ).astype(jnp.bfloat16)
-    for i in range(count):
-        outs[(first + i) // 2][(first + i) % 2] = res[:, i * cols : (i + 1) * cols]
+    for i in range(RING):
+        outs[i // 2][i % 2] = res[:, i * cols : (i + 1) * cols]
 
 
 def back_first_kernel(following, where_ref, mask_ref, *refs):
@@ -419,14 +416,8 @@
     product(g_ref, w_ref, (out_a, out_b))
 
 
-def back_last_kernel(hop, where_ref, after_a, after_b, g_ref, own_hbm, other_hbm, out_a, out_b, w_s, sem):
-    copies = weight_copies(where_ref, own_hbm, other_hbm, w_s, sem, hop)
-    for copy in copies:
-        copy.start()
-    for j in range(0, RING, 2):
-        for copy in copies[2 * j : 2 * j + 4]:
-            copy.wait()
-        product(g_ref, w_s, (out_a, out_b), j, 2)
+def back_last_kernel(after_a, after_b, g_ref, w_ref, out_a, out_b):
+    product(g_ref, w_ref, (out_a, out_b))
 
 
 def back_call(kernel, operands, in_specs, out_shape, scratch):
@@ -437,7 +428,7 @@
         out_specs=[vmem] * len(out_shape),
         out_shape=out_shape,
         scratch_shapes=scratch,
-        compiler_params=pltpu.CompilerParams(vmem_limit_bytes=24 * MIB),
+        compiler_params=pltpu.CompilerParams(vmem_limit_bytes=16 * MIB),
         cost_estimate=pl.CostEstimate(flops=10**6, bytes_accessed=10**4, transcendentals=0),
         name="back",
     )(*operands)
@@ -477,7 +468,7 @@
     def backward(x):
         return lax.ppermute(x, AXES, ring_perm(True, -1))
 
-    w_two, w_one = weights
+    w_two, w_one, w_zero = weights
     two_a, two_b, g, w_three = back_call(
         functools.partial(back_first_kernel, 3),
         (where, masks, *parts, w_two, w5, other_half),
@@ -496,11 +487,7 @@
     three_b = add(three_b, relay_b)
     from_one_a, from_three_b = onward(one_a), backward(three_b)
     own_a, own_b = back_call(
-        functools.partial(back_last_kernel, 0),
-        (where, one_a, three_b, g, w5, other_half),
-        [smem, anywhere, anywhere, vmem, hbm, anywhere],
-        halves,
-        [pltpu.VMEM(w_shape, jnp.bfloat16), sem],
+        back_last_kernel, (one_a, three_b, g, w_zero), [anywhere, anywhere, vmem, vmem], halves, []
     )
     sum_b = own_b.astype(jnp.float32) + from_one_b.astype(jnp.float32)
     own_a, sum_b = lax.optimization_barrier((own_a, sum_b))
@@ -509,7 +496,7 @@
     sum_a = sum_a + from_one_a.astype(jnp.float32)
     sum_a, sum_b = lax.optimization_barrier((sum_a, sum_b))
     sum_b = sum_b + from_three_b.astype(jnp.float32)
-    return dict(zip(SECOND, (sum_a[0], sum_a[1], sum_b[0], sum_b[1])))
+    return [sum_a[0], sum_a[1], sum_b[0], sum_b[1]]
 
 
 def ring_perm(first, hop):
@@ -577,17 +564,17 @@
     keep, send = attention(where, parts + [core_swap(x) for x in parts])
     pair, far, stay = small_call(combine_kernel, "combine", where, (keep, core_swap(send)), part_shapes(3 * HD))
 
-    w_first = fetch_weights(where, stay, w5, other_half, (2, 1))
+    w_first = fetch_weights(where, stay, w5, other_half, (2, 1, 0))
     w_first = [pltpu.with_memory_space_constraint(w, pltpu.VMEM) for w in w_first]
     pair = lax.ppermute(pair, ("seq", "mod"), pair_perm(-1))
     far = lax.ppermute(far, "seq", [(i, (i + 2) % RING) for i in range(NH)])
-    far, w_first = lax.optimization_barrier((far, w_first))
+    pair, far, w_first = lax.optimization_barrier((pair, far, w_first))
     parts = [stay, far, pair]
     parts += [core_swap(x) for x in parts]
 
     total = back_reduced(where, masks, parts, w_first, w5, other_half)
     result = total[0]
-    for hop in SECOND[1:]:
+    for hop in (1, 3, 2):
         got = lax.ppermute(total[hop].astype(jnp.bfloat16), AXES, ring_perm(False, hop))
         result = lax.optimization_barrier(result) + got.astype(jnp.float32)
     result = result.astype(jnp.bfloat16)

time: 100 us -> 95 us (0.950)
  starting transfers between devices: 47 us -> 41.8 us
  waiting for transfers between devices: 15.1 us -> 16.8 us
  Pallas kernels: 36.1 us -> 34.5 us
    ppermute x11, starting transfers between devices: 21.6 us -> 15.8 us  [core_swap(): return lax.ppermute(x, 'mod', [(0, 1), (1, 0)])]
    ppermute x3, waiting for transfers between devices: 0.96 us -> 3.07 us  [onward(): return lax.ppermute(x, AXES, ring_perm(True, 1))]
    pallas_call x4, Pallas kernels: 11.3 us -> 9.23 us  [back_call(): pl.pallas_call(kernel, in_specs=in_specs, out_specs=[vmem] * len(out_shap...]
  transfers between devices with their start and end apart: 24 -> 24, of which waited for: 12 -> 14; matrix products, arithmetic and copies ran while one was open for 1% -> 1% of each run, Pallas kernels for 23% -> 23%
where the time goes in v11:
time: 95 us; the launch traced here: 94.7 us
  starting transfers between devices  41.8 us (44%)
  Pallas kernels  34.5 us (36%)
  waiting for transfers between devices  16.8 us (18%)
  other arithmetic  1.27 us (1%)
    ppermute x11, starting transfers between devices, core_swap(): return lax.ppermute(x, 'mod', [(0, 1), (1, 0)])  15.8 us
    pallas_call x1, Pallas kernels, project(): pl.pallas_call(functools.partial(project_kernel, early), in_specs=[pl.Blo...  9.86 us
    pallas_call x4, Pallas kernels, back_call(): pl.pallas_call(kernel, in_specs=in_specs, out_specs=[vmem] * len(out_shap...  9.23 us
    ppermute x11, waiting for transfers between devices, core_swap(): return lax.ppermute(x, 'mod', [(0, 1), (1, 0)])  6.98 us
    ppermute x3, starting transfers between devices, backward(): return lax.ppermute(x, AXES, ring_perm(True, -1))  6.95 us
    ppermute x1, starting transfers between devices, per_device(): lax.ppermute(far, 'seq', [(i, (i + 2) % RING) for i in range(RING) if (i...  5.6 us
    ppermute x3, starting transfers between devices, per_device(): lax.ppermute(total[hop].astype(jnp.bfloat16), AXES, ring_perm(False, hop))  5.53 us
    pallas_call x1, Pallas kernels, project_own(): pl.pallas_call(own_kernel, in_specs=[hbm, hbm], out_specs=[vmem, vmem], o...  5.02 us
  transfers between devices with their start and end apart: 24, of which 14 were waited for; matrix products, arithmetic and copies ran while one was open for 1% of the time, Pallas kernels for 23%

profile of v11, /device:TPU:1, one launch (start us, length us, event | category | flops | bytes accessed | tf_op | source)
XLA Modules:
  0.0 94.7 jit_solution(5775945596815103077)
XLA Ops:
  1.5 5.0 %project_own.1 = (f32[192,1152]{1,0:T(8,128)S(1)}, bf16[3,8,2,256,384]{4,3,2,1,0:T(8,128)(2,1)S(1)}) custom-call(bf16[192,8192]{1,0:T(8,128)(2,1)} %own_hbm.1, bf16[3,16,2,256,384]{4,3,2,1,0:T(8,128)(2,1)} %bitcast.18), custom_call_target="tpu_custom_call" | custom-call | flops 4000000000 | bytes 10000000 | tf_op jit(solution)/shard_map/project_own/pallas_call | solution.py:56
  6.9 9.9 %project.1 = (bf16[192,1152]{1,0:T(8,128)(2,1)S(1)}, bf16[192,1664]{1,0:T(8,128)(2,1)S(1)}, bf16[3,16,256,384]{3,2,1,0:T(8,128)(2,1)}) custom-call(s32[3]{0:T(128)S(1)} %pad_add_fusion.where_ref, f32[192,1152]{1,0:T(8,128)S(1)} %get-tuple-element.45.part_ref, bf16[192,8192]{1,0:T(8,128)(2,1)} %own_hbm.1, bf16[192,8192]{1,0:T(8,128)(2,1)S(1)} %collective-permute-done.oth_ref, ...), custom_call_target="tpu_custom_call" | custom-call | flops 7000000000 | bytes 10000000 | tf_op jit(solution)/shard_map/project/pallas_call | solution.py:141
  17.3 1.7 %collective-permute-done.1.got_ref = bf16[192,1664]{1,0:T(8,128)(2,1)S(1)} collective-permute-done((bf16[192,1664]{1,0:T(8,128)(2,1)S(1)}, bf16[192,1664]{1,0:T(8,128)(2,1)S(1)}, u32[]{:S(2)}, u32[]{:S(2)}) %collective-permute-start.1) | collective-permute-done | bytes 639008 | tf_op jit(solution)/shard_map/ppermute | solution.py:19
  21.5 5.6 %collective-permute-start.2 = (bf16[192,512]{1,0:T(8,128)(2,1)S(1)}, bf16[192,512]{1,0:T(8,128)(2,1)S(1)}, u32[]{:S(2)}, u32[]{:S(2)}) collective-permute-start(bf16[192,512]{1,0:T(8,128)(2,1)S(1)} %get-tuple-element.53), channel_id=1, source_target_pairs={{0,64},{64,0},{96,32},{1,65},{65,1},{97,33},{2,66},{66,2},{98,34},... | collective-permute-start | bytes 589832 | tf_op jit(solution)/shard_map/ppermute | solution.py:562
  27.1 1.9 %collective-permute-done.3.pair = bf16[2,192,512]{2,1,0:T(8,128)(2,1)S(1)} collective-permute-done((bf16[2,192,512]{2,1,0:T(8,128)(2,1)S(1)}, bf16[2,192,512]{2,1,0:T(8,128)(2,1)S(1)}, u32[]{:S(2)}, u32[]{:S(2)}) %collective-permute-start.3) | collective-permute-done | bytes 393248 | tf_op jit(solution)/shard_map/ppermute | solution.py:561
  29.1 6.4 %collective-permute-start.6 = (bf16[2,192,512]{2,1,0:T(8,128)(2,1)S(1)}, bf16[2,192,512]{2,1,0:T(8,128)(2,1)S(1)}, u32[]{:S(2)}, u32[]{:S(2)}) collective-permute-start(bf16[2,192,512]{2,1,0:T(8,128)(2,1)S(1)} %collective-permute-done.3.pair), channel_id=1, source_target_pairs={{0,16},{16,0},{1,17},{17,1},{2,18},{18,2},{3,19},{19,3},{4,20},{20... | collective-permute-start | bytes 1179656 | tf_op jit(solution)/shard_map/ppermute | solution.py:19
  37.4 4.7 %attention.1 = (f32[192,1408]{1,0:T(8,128)S(1)}, bf16[192,1152]{1,0:T(8,128)(2,1)S(1)}) custom-call(s32[3]{0:T(128)S(1)} %pad_add_fusion.where_ref, bf16[192,512]{1,0:T(8,128)(2,1)S(1)} %get-tuple-element.52.stay, bf16[192,512]{1,0:T(8,128)(2,1)S(1)} %collective-permute-done.2.far, bf16[2,192,512]{2,1,0:T(8,128)(2,1)S(1)} %collective-permute-done.3.pair, ...), custom_call_target="tpu_custom_call" | custom-call | flops 1000000000 | bytes 4000000 | tf_op jit(solution)/shard_map/attention/pallas_call | solution.py:296
  42.6 1.4 %collective-permute-done.7.got = bf16[192,1152]{1,0:T(8,128)(2,1)S(1)} collective-permute-done((bf16[192,1152]{1,0:T(8,128)(2,1)S(1)}, bf16[192,1152]{1,0:T(8,128)(2,1)S(1)}, u32[]{:S(2)}, u32[]{:S(2)}) %collective-permute-start.7) | collective-permute-done | bytes 442400 | tf_op jit(solution)/shard_map/ppermute | solution.py:19
  44.6 1.5 %collective-permute-start.8 = (bf16[2,192,384]{2,1,0:T(8,128)(2,1)S(1)}, bf16[2,192,384]{2,1,0:T(8,128)(2,1)S(1)}, u32[]{:S(2)}, u32[]{:S(2)}) collective-permute-start(bf16[2,192,384]{2,1,0:T(8,128)(2,1)S(1)} %get-tuple-element.58), channel_id=1, source_target_pairs={{0,96},{16,48},{32,0},{48,80},{64,32},{80,112},{1,97},{17,49},{33,... | collective-permute-start | bytes 884744 | tf_op jit(solution)/shard_map/ppermute | solution.py:569
  46.1 3.4 %collective-permute-start.9 = (bf16[192,384]{1,0:T(8,128)(2,1)S(1)}, bf16[192,384]{1,0:T(8,128)(2,1)S(1)}, u32[]{:S(2)}, u32[]{:S(2)}) collective-permute-start(bf16[192,384]{1,0:T(8,128)(2,1)S(1)} %get-tuple-element.59), channel_id=1, source_target_pairs={{0,64},{32,96},{64,0},{1,65},{33,97},{65,1},{2,66},{34,98},{66,2},... | collective-permute-start | bytes 442376 | tf_op jit(solution)/shard_map/ppermute | solution.py:570
  49.6 4.0 %fetch_weights.1 = (bf16[2,3,4,256,384]{4,3,2,1,0:T(8,128)(2,1)S(1)}, bf16[2,3,4,256,384]{4,3,2,1,0:T(8,128)(2,1)S(1)}, bf16[2,3,4,256,384]{4,3,2,1,0:T(8,128)(2,1)S(1)}) custom-call(s32[3]{0:T(128)S(1)} %pad_add_fusion.where_ref, bf16[192,384]{1,0:T(8,128)(2,1)S(1)} %get-tuple-element.57.after_ref.refs_0_, bf16[3,16,2,256,384]{4,3,2,1,0:T(8,128)(2,1)} %bitcast.20, ...), custom_call_target="tpu_custom_call" | custom-call | flops 1000000 | bytes 10000000 | tf_op jit(solution)/shard_map/fetch_weights/pallas_call | solution.py:383
  53.9 1.9 %collective-permute-start.13 = (bf16[2,192,384]{2,1,0:T(8,128)(2,1)S(1)}, bf16[2,192,384]{2,1,0:T(8,128)(2,1)S(1)}, u32[]{:S(2)}, u32[]{:S(2)}) collective-permute-start(bf16[2,192,384]{2,1,0:T(8,128)(2,1)S(1)} %collective-permute-done.8.refs_2_), channel_id=1, source_target_pairs={{0,16},{16,0},{1,17},{17,1},{2,18},{18,2},{3,19},{19,3},{4,20},{20... | collective-permute-start | bytes 884744 | tf_op jit(solution)/shard_map/ppermute | solution.py:19
  57.4 3.2 %back.4 = (bf16[2,384,256]{2,1,0:T(8,128)(2,1)S(1)}, bf16[2,384,256]{2,1,0:T(8,128)(2,1)S(1)}, bf16[384,2304]{1,0:T(8,128)(2,1)S(1)}, bf16[2,3,4,256,384]{4,3,2,1,0:T(8,128)(2,1)S(1)}) custom-call(s32[3]{0:T(128)S(1)} %pad_add_fusion.where_ref, bf16[2,192,128]{2,1,0:T(8,128)(2,1)S(1)} %get-tuple-element.51.mask_ref, ...), custom_call_target="tpu_custom_call" | custom-call | flops 1000000 | bytes 10000 | tf_op jit(solution)/shard_map/back/pallas_call | solution.py:425
  62.0 1.5 %collective-permute-start.15 = (bf16[2,384,256]{2,1,0:T(8,128)(2,1)S(1)}, bf16[2,384,256]{2,1,0:T(8,128)(2,1)S(1)}, u32[]{:S(2)}, u32[]{:S(2)}) collective-permute-start(bf16[2,384,256]{2,1,0:T(8,128)(2,1)S(1)} %get-tuple-element.73), channel_id=1, source_target_pairs={{0,3},{1,0},{2,1},{3,2},{4,7},{5,4},{6,5},{7,6},{8,11},{9,8},{10,9... | collective-permute-start | bytes 1179656 | tf_op jit(solution)/shard_map/ppermute | solution.py:469
  63.5 2.0 %back.5 = (bf16[2,384,256]{2,1,0:T(8,128)(2,1)S(1)}, bf16[2,384,256]{2,1,0:T(8,128)(2,1)S(1)}) custom-call(bf16[384,2304]{1,0:T(8,128)(2,1)S(1)} %get-tuple-element.67.g_ref, bf16[2,3,4,256,384]{4,3,2,1,0:T(8,128)(2,1)S(1)} %get-tuple-element.68.w_ref), custom_call_target="tpu_custom_call" | custom-call | flops 1000000 | bytes 10000 | tf_op jit(solution)/shard_map/back/pallas_call | solution.py:425
  65.6 2.0 %back.6 = (bf16[2,384,256]{2,1,0:T(8,128)(2,1)S(1)}, bf16[2,384,256]{2,1,0:T(8,128)(2,1)S(1)}) custom-call(bf16[384,2304]{1,0:T(8,128)(2,1)S(1)} %get-tuple-element.67.g_ref, bf16[2,3,4,256,384]{4,3,2,1,0:T(8,128)(2,1)S(1)} %get-tuple-element.71.w_ref), custom_call_target="tpu_custom_call" | custom-call | flops 1000000 | bytes 10000 | tf_op jit(solution)/shard_map/back/pallas_call | solution.py:425
  67.6 2.7 %collective-permute-start.17 = (bf16[2,384,256]{2,1,0:T(8,128)(2,1)S(1)}, bf16[2,384,256]{2,1,0:T(8,128)(2,1)S(1)}, u32[]{:S(2)}, u32[]{:S(2)}) collective-permute-start(bf16[2,384,256]{2,1,0:T(8,128)(2,1)S(1)} %get-tuple-element.79), channel_id=1, source_target_pairs={{0,3},{1,0},{2,1},{3,2},{4,7},{5,4},{6,5},{7,6},{8,11},{9,8},{10,9... | collective-permute-start | bytes 1179656 | tf_op jit(solution)/shard_map/ppermute | solution.py:469
  70.9 2.7 %collective-permute-start.20 = (bf16[2,384,256]{2,1,0:T(8,128)(2,1)S(1)}, bf16[2,384,256]{2,1,0:T(8,128)(2,1)S(1)}, u32[]{:S(2)}, u32[]{:S(2)}) collective-permute-start(bf16[2,384,256]{2,1,0:T(8,128)(2,1)S(1)} %add.42.after_b), channel_id=1, source_target_pairs={{0,3},{1,0},{2,1},{3,2},{4,7},{5,4},{6,5},{7,6},{8,11},{9,8},{10,9... | collective-permute-start | bytes 1179656 | tf_op jit(solution)/shard_map/ppermute | solution.py:469
  73.6 2.0 %back.7 = (bf16[2,384,256]{2,1,0:T(8,128)(2,1)S(1)}, bf16[2,384,256]{2,1,0:T(8,128)(2,1)S(1)}) custom-call(bf16[2,384,256]{2,1,0:T(8,128)(2,1)S(1)} %add.41.after_a, bf16[2,384,256]{2,1,0:T(8,128)(2,1)S(1)} %add.42.after_b, bf16[384,2304]{1,0:T(8,128)(2,1)S(1)} %get-tuple-element.67.g_ref, bf16[2,3,4,256,384]{4,3,2,1,0:T(8,128)(2,1)S(1)} %get-tuple-element.74.w_ref), custom_call_target="tpu_custom_call" | custom-call | flops 1000000 | bytes 10000 | tf_op jit(solution)/shard_map/back/pallas_call | solution.py:425
  75.8 3.1 %collective-permute-done.18 = bf16[2,384,256]{2,1,0:T(8,128)(2,1)S(1)} collective-permute-done((bf16[2,384,256]{2,1,0:T(8,128)(2,1)S(1)}, bf16[2,384,256]{2,1,0:T(8,128)(2,1)S(1)}, u32[]{:S(2)}, u32[]{:S(2)}) %collective-permute-start.18) | collective-permute-done | bytes 393248 | tf_op jit(solution)/shard_map/ppermute | solution.py:466
  79.0 1.4 %collective-permute-start.19 = (bf16[384,256]{1,0:T(8,128)(2,1)S(1)}, bf16[384,256]{1,0:T(8,128)(2,1)S(1)}, u32[]{:S(2)}, u32[]{:S(2)}) collective-permute-start(bf16[384,256]{1,0:T(8,128)(2,1)S(1)} %fusion), channel_id=1, source_target_pairs={{0,4},{1,5},{2,6},{3,7},{4,8},{5,9},{6,10},{7,11},{8,12},{9,13},{1... | collective-permute-start | bytes 589832 | tf_op jit(solution)/shard_map/ppermute | solution.py:578
  80.6 3.7 %collective-permute-start.22 = (bf16[384,256]{1,0:T(8,128)(2,1)S(1)}, bf16[384,256]{1,0:T(8,128)(2,1)S(1)}, u32[]{:S(2)}, u32[]{:S(2)}) collective-permute-start(bf16[384,256]{1,0:T(8,128)(2,1)S(1)} %get-tuple-element.85), channel_id=1, source_target_pairs={{0,8},{1,9},{2,10},{3,11},{4,12},{5,13},{6,14},{7,15},{8,0},{9,1},... | collective-permute-start | bytes 589832 | tf_op jit(solution)/shard_map/ppermute | solution.py:578
  86.0 3.0 %collective-permute-done.21 = bf16[384,256]{1,0:T(8,128)(2,1)S(1)} collective-permute-done((bf16[384,256]{1,0:T(8,128)(2,1)S(1)}, bf16[384,256]{1,0:T(8,128)(2,1)S(1)}, u32[]{:S(2)}, u32[]{:S(2)}) %collective-permute-start.21) | collective-permute-done | bytes 196640 | tf_op jit(solution)/shard_map/ppermute | solution.py:578
  89.3 3.8 %collective-permute-start.23 = (bf16[192,256]{1,0:T(8,128)(2,1)S(1)}, bf16[192,256]{1,0:T(8,128)(2,1)S(1)}, u32[]{:S(2)}, u32[]{:S(2)}) collective-permute-start(bf16[192,256]{1,0:T(8,128)(2,1)S(1)} %get-tuple-element.88), channel_id=1, source_target_pairs={{0,16},{16,0},{1,17},{17,1},{2,18},{18,2},{3,19},{19,3},{4,20},{20... | collective-permute-start | bytes 294920 | tf_op jit(solution)/shard_map/ppermute | solution.py:19
  (53 shorter events, 15.9 us)
Async XLA Ops:
  0.0 6.9 %collective-permute-start = (bf16[192,8192]{1,0:T(8,128)(2,1)}, bf16[192,8192]{1,0:T(8,128)(2,1)S(1)}, u32[]{:S(2)}, u32[]{:S(2)}) collective-permute-start(bf16[192,8192]{1,0:T(8,128)(2,1)} %own_hbm.1), channel_id=1, source_target_pairs={{0,16},{16,0},{1,17},{17,1},{2,18},{18,2},{3,19},{19,3},{4,20},{20... | collective-permute-start | bytes 9437192 | tf_op jit(solution)/shard_map/ppermute | solution.py:19
  16.8 2.2 %collective-permute-start.1 = (bf16[192,1664]{1,0:T(8,128)(2,1)S(1)}, bf16[192,1664]{1,0:T(8,128)(2,1)S(1)}, u32[]{:S(2)}, u32[]{:S(2)}) collective-permute-start(bf16[192,1664]{1,0:T(8,128)(2,1)S(1)} %get-tuple-element.48.sent_ref), channel_id=1, source_target_pairs={{0,16},{16,0},{1,17},{17,1},{2,18},{18,2},{3,19},{19,3},{4,20},{20... | collective-permute-start | bytes 1916936 | tf_op jit(solution)/shard_map/ppermute | solution.py:19
  19.0 30.6 %collective-permute-start.10 = (bf16[3,16,256,384]{3,2,1,0:T(8,128)(2,1)}, bf16[3,16,256,384]{3,2,1,0:T(8,128)(2,1)S(1)}, u32[]{:S(2)}, u32[]{:S(2)}) collective-permute-start(bf16[3,16,256,384]{3,2,1,0:T(8,128)(2,1)} %get-tuple-element.60), channel_id=1, source_target_pairs={{0,16},{16,0},{1,17},{17,1},{2,18},{18,2},{3,19},{19,3},{4,20},{20... | collective-permute-start | bytes 28311560 | tf_op jit(solution)/shard_map/ppermute | solution.py:19
  20.2 8.8 %collective-permute-start.3 = (bf16[2,192,512]{2,1,0:T(8,128)(2,1)S(1)}, bf16[2,192,512]{2,1,0:T(8,128)(2,1)S(1)}, u32[]{:S(2)}, u32[]{:S(2)}) collective-permute-start(bf16[2,192,512]{2,1,0:T(8,128)(2,1)S(1)} %get-tuple-element.54), channel_id=1, source_target_pairs={{0,32},{32,64},{48,16},{80,48},{96,0},{112,80},{1,33},{33,65},{49,... | collective-permute-start | bytes 1179656 | tf_op jit(solution)/shard_map/ppermute | solution.py:561
  21.5 13.9 %collective-permute-start.2 = (bf16[192,512]{1,0:T(8,128)(2,1)S(1)}, bf16[192,512]{1,0:T(8,128)(2,1)S(1)}, u32[]{:S(2)}, u32[]{:S(2)}) collective-permute-start(bf16[192,512]{1,0:T(8,128)(2,1)S(1)} %get-tuple-element.53), channel_id=1, source_target_pairs={{0,64},{64,0},{96,32},{1,65},{65,1},{97,33},{2,66},{66,2},{98,34},... | collective-permute-start | bytes 589832 | tf_op jit(solution)/shard_map/ppermute | solution.py:562
  29.1 8.3 %collective-permute-start.6 = (bf16[2,192,512]{2,1,0:T(8,128)(2,1)S(1)}, bf16[2,192,512]{2,1,0:T(8,128)(2,1)S(1)}, u32[]{:S(2)}, u32[]{:S(2)}) collective-permute-start(bf16[2,192,512]{2,1,0:T(8,128)(2,1)S(1)} %collective-permute-done.3.pair), channel_id=1, source_target_pairs={{0,16},{16,0},{1,17},{17,1},{2,18},{18,2},{3,19},{19,3},{4,20},{20... | collective-permute-start | bytes 1179656 | tf_op jit(solution)/shard_map/ppermute | solution.py:19
  35.5 1.6 %collective-permute-start.4 = (bf16[192,512]{1,0:T(8,128)(2,1)S(1)}, bf16[192,512]{1,0:T(8,128)(2,1)S(1)}, u32[]{:S(2)}, u32[]{:S(2)}) collective-permute-start(bf16[192,512]{1,0:T(8,128)(2,1)S(1)} %get-tuple-element.52.stay), channel_id=1, source_target_pairs={{0,16},{16,0},{1,17},{17,1},{2,18},{18,2},{3,19},{19,3},{4,20},{20... | collective-permute-start | bytes 589832 | tf_op jit(solution)/shard_map/ppermute | solution.py:19
  35.5 1.9 %collective-permute-start.5 = (bf16[192,512]{1,0:T(8,128)(2,1)S(1)}, bf16[192,512]{1,0:T(8,128)(2,1)S(1)}, u32[]{:S(2)}, u32[]{:S(2)}) collective-permute-start(bf16[192,512]{1,0:T(8,128)(2,1)S(1)} %collective-permute-done.2.far), channel_id=1, source_target_pairs={{0,16},{16,0},{1,17},{17,1},{2,18},{18,2},{3,19},{19,3},{4,20},{20... | collective-permute-start | bytes 589832 | tf_op jit(solution)/shard_map/ppermute | solution.py:19
  42.1 1.9 %collective-permute-start.7 = (bf16[192,1152]{1,0:T(8,128)(2,1)S(1)}, bf16[192,1152]{1,0:T(8,128)(2,1)S(1)}, u32[]{:S(2)}, u32[]{:S(2)}) collective-permute-start(bf16[192,1152]{1,0:T(8,128)(2,1)S(1)} %get-tuple-element.56), channel_id=1, source_target_pairs={{0,16},{16,0},{1,17},{17,1},{2,18},{18,2},{3,19},{19,3},{4,20},{20... | collective-permute-start | bytes 1327112 | tf_op jit(solution)/shard_map/ppermute | solution.py:19
  44.6 9.3 %collective-permute-start.8 = (bf16[2,192,384]{2,1,0:T(8,128)(2,1)S(1)}, bf16[2,192,384]{2,1,0:T(8,128)(2,1)S(1)}, u32[]{:S(2)}, u32[]{:S(2)}) collective-permute-start(bf16[2,192,384]{2,1,0:T(8,128)(2,1)S(1)} %get-tuple-element.58), channel_id=1, source_target_pairs={{0,96},{16,48},{32,0},{48,80},{64,32},{80,112},{1,97},{17,49},{33,... | collective-permute-start | bytes 884744 | tf_op jit(solution)/shard_map/ppermute | solution.py:569
  46.1 7.8 %collective-permute-start.9 = (bf16[192,384]{1,0:T(8,128)(2,1)S(1)}, bf16[192,384]{1,0:T(8,128)(2,1)S(1)}, u32[]{:S(2)}, u32[]{:S(2)}) collective-permute-start(bf16[192,384]{1,0:T(8,128)(2,1)S(1)} %get-tuple-element.59), channel_id=1, source_target_pairs={{0,64},{32,96},{64,0},{1,65},{33,97},{65,1},{2,66},{34,98},{66,2},... | collective-permute-start | bytes 442376 | tf_op jit(solution)/shard_map/ppermute | solution.py:570
  53.9 3.5 %collective-permute-start.13 = (bf16[2,192,384]{2,1,0:T(8,128)(2,1)S(1)}, bf16[2,192,384]{2,1,0:T(8,128)(2,1)S(1)}, u32[]{:S(2)}, u32[]{:S(2)}) collective-permute-start(bf16[2,192,384]{2,1,0:T(8,128)(2,1)S(1)} %collective-permute-done.8.refs_2_), channel_id=1, source_target_pairs={{0,16},{16,0},{1,17},{17,1},{2,18},{18,2},{3,19},{19,3},{4,20},{20... | collective-permute-start | bytes 884744 | tf_op jit(solution)/shard_map/ppermute | solution.py:19
  55.8 1.4 %collective-permute-start.11 = (bf16[192,384]{1,0:T(8,128)(2,1)S(1)}, bf16[192,384]{1,0:T(8,128)(2,1)S(1)}, u32[]{:S(2)}, u32[]{:S(2)}) collective-permute-start(bf16[192,384]{1,0:T(8,128)(2,1)S(1)} %get-tuple-element.57.after_ref.refs_0_), channel_id=1, source_target_pairs={{0,16},{16,0},{1,17},{17,1},{2,18},{18,2},{3,19},{19,3},{4,20},{20... | collective-permute-start | bytes 442376 | tf_op jit(solution)/shard_map/ppermute | solution.py:19
  55.8 1.6 %collective-permute-start.12 = (bf16[192,384]{1,0:T(8,128)(2,1)S(1)}, bf16[192,384]{1,0:T(8,128)(2,1)S(1)}, u32[]{:S(2)}, u32[]{:S(2)}) collective-permute-start(bf16[192,384]{1,0:T(8,128)(2,1)S(1)} %collective-permute-done.9.refs_1_), channel_id=1, source_target_pairs={{0,16},{16,0},{1,17},{17,1},{2,18},{18,2},{3,19},{19,3},{4,20},{20... | collective-permute-start | bytes 442376 | tf_op jit(solution)/shard_map/ppermute | solution.py:19
  60.6 9.7 %collective-permute-start.14 = (bf16[2,384,256]{2,1,0:T(8,128)(2,1)S(1)}, bf16[2,384,256]{2,1,0:T(8,128)(2,1)S(1)}, u32[]{:S(2)}, u32[]{:S(2)}) collective-permute-start(bf16[2,384,256]{2,1,0:T(8,128)(2,1)S(1)} %get-tuple-element.70), channel_id=1, source_target_pairs={{0,1},{1,2},{2,3},{3,0},{4,5},{5,6},{6,7},{7,4},{8,9},{9,10},{10,1... | collective-permute-start | bytes 1179656 | tf_op jit(solution)/shard_map/ppermute | solution.py:466
  62.0 8.8 %collective-permute-start.15 = (bf16[2,384,256]{2,1,0:T(8,128)(2,1)S(1)}, bf16[2,384,256]{2,1,0:T(8,128)(2,1)S(1)}, u32[]{:S(2)}, u32[]{:S(2)}) collective-permute-start(bf16[2,384,256]{2,1,0:T(8,128)(2,1)S(1)} %get-tuple-element.73), channel_id=1, source_target_pairs={{0,3},{1,0},{2,1},{3,2},{4,7},{5,4},{6,5},{7,6},{8,11},{9,8},{10,9... | collective-permute-start | bytes 1179656 | tf_op jit(solution)/shard_map/ppermute | solution.py:469
  65.5 10.1 %collective-permute-start.16 = (bf16[2,384,256]{2,1,0:T(8,128)(2,1)S(1)}, bf16[2,384,256]{2,1,0:T(8,128)(2,1)S(1)}, u32[]{:S(2)}, u32[]{:S(2)}) collective-permute-start(bf16[2,384,256]{2,1,0:T(8,128)(2,1)S(1)} %get-tuple-element.77), channel_id=1, source_target_pairs={{0,1},{1,2},{2,3},{3,0},{4,5},{5,6},{6,7},{7,4},{8,9},{9,10},{10,1... | collective-permute-start | bytes 1179656 | tf_op jit(solution)/shard_map/ppermute | solution.py:466
  67.6 8.1 %collective-permute-start.17 = (bf16[2,384,256]{2,1,0:T(8,128)(2,1)S(1)}, bf16[2,384,256]{2,1,0:T(8,128)(2,1)S(1)}, u32[]{:S(2)}, u32[]{:S(2)}) collective-permute-start(bf16[2,384,256]{2,1,0:T(8,128)(2,1)S(1)} %get-tuple-element.79), channel_id=1, source_target_pairs={{0,3},{1,0},{2,1},{3,2},{4,7},{5,4},{6,5},{7,6},{8,11},{9,8},{10,9... | collective-permute-start | bytes 1179656 | tf_op jit(solution)/shard_map/ppermute | solution.py:469
  70.5 8.4 %collective-permute-start.18 = (bf16[2,384,256]{2,1,0:T(8,128)(2,1)S(1)}, bf16[2,384,256]{2,1,0:T(8,128)(2,1)S(1)}, u32[]{:S(2)}, u32[]{:S(2)}) collective-permute-start(bf16[2,384,256]{2,1,0:T(8,128)(2,1)S(1)} %add.41.after_a), channel_id=1, source_target_pairs={{0,1},{1,2},{2,3},{3,0},{4,5},{5,6},{6,7},{7,4},{8,9},{9,10},{10,1... | collective-permute-start | bytes 1179656 | tf_op jit(solution)/shard_map/ppermute | solution.py:466
  70.9 9.6 %collective-permute-start.20 = (bf16[2,384,256]{2,1,0:T(8,128)(2,1)S(1)}, bf16[2,384,256]{2,1,0:T(8,128)(2,1)S(1)}, u32[]{:S(2)}, u32[]{:S(2)}) collective-permute-start(bf16[2,384,256]{2,1,0:T(8,128)(2,1)S(1)} %add.42.after_b), channel_id=1, source_target_pairs={{0,3},{1,0},{2,1},{3,2},{4,7},{5,4},{6,5},{7,6},{8,11},{9,8},{10,9... | collective-permute-start | bytes 1179656 | tf_op jit(solution)/shard_map/ppermute | solution.py:469
  79.0 6.9 %collective-permute-start.19 = (bf16[384,256]{1,0:T(8,128)(2,1)S(1)}, bf16[384,256]{1,0:T(8,128)(2,1)S(1)}, u32[]{:S(2)}, u32[]{:S(2)}) collective-permute-start(bf16[384,256]{1,0:T(8,128)(2,1)S(1)} %fusion), channel_id=1, source_target_pairs={{0,4},{1,5},{2,6},{3,7},{4,8},{5,9},{6,10},{7,11},{8,12},{9,13},{1... | collective-permute-start | bytes 589832 | tf_op jit(solution)/shard_map/ppermute | solution.py:578
  80.6 8.6 %collective-permute-start.22 = (bf16[384,256]{1,0:T(8,128)(2,1)S(1)}, bf16[384,256]{1,0:T(8,128)(2,1)S(1)}, u32[]{:S(2)}, u32[]{:S(2)}) collective-permute-start(bf16[384,256]{1,0:T(8,128)(2,1)S(1)} %get-tuple-element.85), channel_id=1, source_target_pairs={{0,8},{1,9},{2,10},{3,11},{4,12},{5,13},{6,14},{7,15},{8,0},{9,1},... | collective-permute-start | bytes 589832 | tf_op jit(solution)/shard_map/ppermute | solution.py:578
  84.3 4.7 %collective-permute-start.21 = (bf16[384,256]{1,0:T(8,128)(2,1)S(1)}, bf16[384,256]{1,0:T(8,128)(2,1)S(1)}, u32[]{:S(2)}, u32[]{:S(2)}) collective-permute-start(bf16[384,256]{1,0:T(8,128)(2,1)S(1)} %get-tuple-element.86), channel_id=1, source_target_pairs={{0,12},{1,13},{2,14},{3,15},{4,0},{5,1},{6,2},{7,3},{8,4},{9,5},{1... | collective-permute-start | bytes 589832 | tf_op jit(solution)/shard_map/ppermute | solution.py:578
  89.3 4.7 %collective-permute-start.23 = (bf16[192,256]{1,0:T(8,128)(2,1)S(1)}, bf16[192,256]{1,0:T(8,128)(2,1)S(1)}, u32[]{:S(2)}, u32[]{:S(2)}) collective-permute-start(bf16[192,256]{1,0:T(8,128)(2,1)S(1)} %get-tuple-element.88), channel_id=1, source_target_pairs={{0,16},{16,0},{1,17},{17,1},{2,18},{18,2},{3,19},{19,3},{4,20},{20... | collective-permute-start | bytes 294920 | tf_op jit(solution)/shard_map/ppermute | solution.py:19
  (2 other events, 17.8 us)

commit v12 on v11

--- a/solution.py
+++ b/solution.py
@@ -11,6 +11,7 @@
 NH = 3
 RING = 4
 SCALE = HD**-0.5
+SECOND = (2, 0, 1, 3)
 AXES = ("seq", "mod", "tp")
 MIB = 1024 * 1024
 
@@ -360,7 +361,7 @@
     core = where_ref[1]
     copies = []
     for j in range(RING):
-        dest = destination(where_ref, hop, j)
+        dest = destination(where_ref, hop, SECOND[j])
         copies.append(pltpu.make_async_copy(own_hbm.at[:, dest, core], to_ref.at[0, :, j], sem.at[0, j]))
         copies.append(pltpu.make_async_copy(other_hbm.at[:, dest], to_ref.at[1, :, j], sem.at[1, j]))
     return copies
@@ -496,7 +497,7 @@
     sum_a = sum_a + from_one_a.astype(jnp.float32)
     sum_a, sum_b = lax.optimization_barrier((sum_a, sum_b))
     sum_b = sum_b + from_three_b.astype(jnp.float32)
-    return [sum_a[0], sum_a[1], sum_b[0], sum_b[1]]
+    return dict(zip(SECOND, (sum_a[0], sum_a[1], sum_b[0], sum_b[1])))
 
 
 def ring_perm(first, hop):
@@ -573,10 +574,14 @@
     parts += [core_swap(x) for x in parts]
 
     total = back_reduced(where, masks, parts, w_first, w5, other_half)
-    result = total[0]
-    for hop in (1, 3, 2):
-        got = lax.ppermute(total[hop].astype(jnp.bfloat16), AXES, ring_perm(False, hop))
-        result = lax.optimization_barrier(result) + got.astype(jnp.float32)
+    two = total[2].astype(jnp.bfloat16)
+    relay_a = lax.ppermute(two[:rows], AXES, ring_perm(False, 1))
+    relay_b = lax.ppermute(two[rows:], AXES, ring_perm(False, -1))
+    one = jnp.concatenate([total[1][:rows] + relay_a.astype(jnp.float32), total[1][rows:]], axis=0)
+    three = jnp.concatenate([total[3][:rows], total[3][rows:] + relay_b.astype(jnp.float32)], axis=0)
+    from_one = lax.ppermute(one.astype(jnp.bfloat16), AXES, ring_perm(False, 1))
+    from_three = lax.ppermute(three.astype(jnp.bfloat16), AXES, ring_perm(False, -1))
+    result = total[0] + from_one.astype(jnp.float32) + from_three.astype(jnp.float32)
     result = result.astype(jnp.bfloat16)
     mine = result[:rows]
     theirs = core_swap(result[rows:])

time: 95 us -> 101 us (1.063)
  waiting for transfers between devices: 16.8 us -> 19.8 us
  starting transfers between devices: 41.8 us -> 44.3 us
    ppermute x3 -> x4, waiting for transfers between devices: 4.45 us -> 7.51 us  [the longest x1 3.2 us: per_device(): from_one = lax.ppermute(one.astype(jnp.bfloat16), AXES, ring_perm(False, 1))]
    ppermute x3 -> x4, starting transfers between devices: 5.53 us -> 6.81 us  [the longest x1 2.82 us: per_device(): lax.ppermute(three.astype(jnp.bfloat16), AXES, ring_perm(False, -1))]
    ppermute x11, starting transfers between devices: 15.8 us -> 17 us  [core_swap(): return lax.ppermute(x, 'mod', [(0, 1), (1, 0)])]
  transfers between devices with their start and end apart: 24 -> 25, of which waited for: 14 -> 14; matrix products, arithmetic and copies ran while one was open for 1% -> 0% of each run, Pallas kernels for 23% -> 21%
where the time goes in v12:
time: 101 us; the launch traced here: 100 us
  starting transfers between devices  44.3 us (44%)
  Pallas kernels  34.5 us (34%)
  waiting for transfers between devices  19.8 us (20%)
  other arithmetic  1.34 us (1%)
    ppermute x11, starting transfers between devices, core_swap(): return lax.ppermute(x, 'mod', [(0, 1), (1, 0)])  17 us
    pallas_call x1, Pallas kernels, project(): pl.pallas_call(functools.partial(project_kernel, early), in_specs=[pl.Blo...  9.86 us
    pallas_call x4, Pallas kernels, back_call(): pl.pallas_call(kernel, in_specs=in_specs, out_specs=[vmem] * len(out_shap...  9.23 us
    ppermute x11, waiting for transfers between devices, core_swap(): return lax.ppermute(x, 'mod', [(0, 1), (1, 0)])  6.98 us
    ppermute x3, starting transfers between devices, backward(): return lax.ppermute(x, AXES, ring_perm(True, -1))  6.95 us
    ppermute x1, starting transfers between devices, per_device(): lax.ppermute(far, 'seq', [(i, (i + 2) % RING) for i in range(RING) if (i...  5.6 us
    pallas_call x1, Pallas kernels, project_own(): pl.pallas_call(own_kernel, in_specs=[hbm, hbm], out_specs=[vmem, vmem], o...  5.02 us
    pallas_call x1, Pallas kernels, attention(): pl.pallas_call(attention_kernel, in_specs=[pl.BlockSpec(memory_space=pltp...  4.74 us
  transfers between devices with their start and end apart: 25, of which 14 were waited for; matrix products, arithmetic and copies ran while one was open for 0% of the time, Pallas kernels for 21%

profile of v12, /device:TPU:1, one launch (start us, length us, event | category | flops | bytes accessed | tf_op | source)
XLA Modules:
  0.0 100.4 jit_solution(15752712020721465779)
XLA Ops:
  1.5 5.0 %project_own.1 = (f32[192,1152]{1,0:T(8,128)S(1)}, bf16[3,8,2,256,384]{4,3,2,1,0:T(8,128)(2,1)S(1)}) custom-call(bf16[192,8192]{1,0:T(8,128)(2,1)} %own_hbm.1, bf16[3,16,2,256,384]{4,3,2,1,0:T(8,128)(2,1)} %bitcast.36), custom_call_target="tpu_custom_call" | custom-call | flops 4000000000 | bytes 10000000 | tf_op jit(solution)/shard_map/project_own/pallas_call | solution.py:57
  6.9 9.9 %project.1 = (bf16[192,1152]{1,0:T(8,128)(2,1)S(1)}, bf16[192,1664]{1,0:T(8,128)(2,1)S(1)}, bf16[3,16,256,384]{3,2,1,0:T(8,128)(2,1)}) custom-call(s32[3]{0:T(128)S(1)} %pad_add_fusion.where_ref, f32[192,1152]{1,0:T(8,128)S(1)} %get-tuple-element.45.part_ref, bf16[192,8192]{1,0:T(8,128)(2,1)} %own_hbm.1, bf16[192,8192]{1,0:T(8,128)(2,1)S(1)} %collective-permute-done.oth_ref, ...), custom_call_target="tpu_custom_call" | custom-call | flops 7000000000 | bytes 10000000 | tf_op jit(solution)/shard_map/project/pallas_call | solution.py:142
  17.3 1.7 %collective-permute-done.1.got_ref = bf16[192,1664]{1,0:T(8,128)(2,1)S(1)} collective-permute-done((bf16[192,1664]{1,0:T(8,128)(2,1)S(1)}, bf16[192,1664]{1,0:T(8,128)(2,1)S(1)}, u32[]{:S(2)}, u32[]{:S(2)}) %collective-permute-start.1) | collective-permute-done | bytes 639008 | tf_op jit(solution)/shard_map/ppermute | solution.py:20
  21.5 5.6 %collective-permute-start.2 = (bf16[192,512]{1,0:T(8,128)(2,1)S(1)}, bf16[192,512]{1,0:T(8,128)(2,1)S(1)}, u32[]{:S(2)}, u32[]{:S(2)}) collective-permute-start(bf16[192,512]{1,0:T(8,128)(2,1)S(1)} %get-tuple-element.53), channel_id=1, source_target_pairs={{0,64},{64,0},{96,32},{1,65},{65,1},{97,33},{2,66},{66,2},{98,34},... | collective-permute-start | bytes 589832 | tf_op jit(solution)/shard_map/ppermute | solution.py:563
  27.1 1.9 %collective-permute-done.3.pair = bf16[2,192,512]{2,1,0:T(8,128)(2,1)S(1)} collective-permute-done((bf16[2,192,512]{2,1,0:T(8,128)(2,1)S(1)}, bf16[2,192,512]{2,1,0:T(8,128)(2,1)S(1)}, u32[]{:S(2)}, u32[]{:S(2)}) %collective-permute-start.3) | collective-permute-done | bytes 393248 | tf_op jit(solution)/shard_map/ppermute | solution.py:562
  29.1 6.4 %collective-permute-start.6 = (bf16[2,192,512]{2,1,0:T(8,128)(2,1)S(1)}, bf16[2,192,512]{2,1,0:T(8,128)(2,1)S(1)}, u32[]{:S(2)}, u32[]{:S(2)}) collective-permute-start(bf16[2,192,512]{2,1,0:T(8,128)(2,1)S(1)} %collective-permute-done.3.pair), channel_id=1, source_target_pairs={{0,16},{16,0},{1,17},{17,1},{2,18},{18,2},{3,19},{19,3},{4,20},{20... | collective-permute-start | bytes 1179656 | tf_op jit(solution)/shard_map/ppermute | solution.py:20
  37.4 4.7 %attention.1 = (f32[192,1408]{1,0:T(8,128)S(1)}, bf16[192,1152]{1,0:T(8,128)(2,1)S(1)}) custom-call(s32[3]{0:T(128)S(1)} %pad_add_fusion.where_ref, bf16[192,512]{1,0:T(8,128)(2,1)S(1)} %get-tuple-element.52.stay, bf16[192,512]{1,0:T(8,128)(2,1)S(1)} %collective-permute-done.2.far, bf16[2,192,512]{2,1,0:T(8,128)(2,1)S(1)} %collective-permute-done.3.pair, ...), custom_call_target="tpu_custom_call" | custom-call | flops 1000000000 | bytes 4000000 | tf_op jit(solution)/shard_map/attention/pallas_call | solution.py:297
  46.1 3.4 %collective-permute-start.9 = (bf16[192,384]{1,0:T(8,128)(2,1)S(1)}, bf16[192,384]{1,0:T(8,128)(2,1)S(1)}, u32[]{:S(2)}, u32[]{:S(2)}) collective-permute-start(bf16[192,384]{1,0:T(8,128)(2,1)S(1)} %get-tuple-element.59), channel_id=1, source_target_pairs={{0,64},{32,96},{64,0},{1,65},{33,97},{65,1},{2,66},{34,98},{66,2},... | collective-permute-start | bytes 442376 | tf_op jit(solution)/shard_map/ppermute | solution.py:571
  49.6 4.0 %fetch_weights.1 = (bf16[2,3,4,256,384]{4,3,2,1,0:T(8,128)(2,1)S(1)}, bf16[2,3,4,256,384]{4,3,2,1,0:T(8,128)(2,1)S(1)}, bf16[2,3,4,256,384]{4,3,2,1,0:T(8,128)(2,1)S(1)}) custom-call(s32[3]{0:T(128)S(1)} %pad_add_fusion.where_ref, bf16[192,384]{1,0:T(8,128)(2,1)S(1)} %get-tuple-element.57.after_ref.refs_0_, bf16[3,16,2,256,384]{4,3,2,1,0:T(8,128)(2,1)} %bitcast.38, ...), custom_call_target="tpu_custom_call" | custom-call | flops 1000000 | bytes 10000000 | tf_op jit(solution)/shard_map/fetch_weights/pallas_call | solution.py:384
  53.9 1.9 %collective-permute-start.13 = (bf16[2,192,384]{2,1,0:T(8,128)(2,1)S(1)}, bf16[2,192,384]{2,1,0:T(8,128)(2,1)S(1)}, u32[]{:S(2)}, u32[]{:S(2)}) collective-permute-start(bf16[2,192,384]{2,1,0:T(8,128)(2,1)S(1)} %collective-permute-done.8.refs_2_), channel_id=1, source_target_pairs={{0,16},{16,0},{1,17},{17,1},{2,18},{18,2},{3,19},{19,3},{4,20},{20... | collective-permute-start | bytes 884744 | tf_op jit(solution)/shard_map/ppermute | solution.py:20
  57.4 3.2 %back.4 = (bf16[2,384,256]{2,1,0:T(8,128)(2,1)S(1)}, bf16[2,384,256]{2,1,0:T(8,128)(2,1)S(1)}, bf16[384,2304]{1,0:T(8,128)(2,1)S(1)}, bf16[2,3,4,256,384]{4,3,2,1,0:T(8,128)(2,1)S(1)}) custom-call(s32[3]{0:T(128)S(1)} %pad_add_fusion.where_ref, bf16[2,192,128]{2,1,0:T(8,128)(2,1)S(1)} %get-tuple-element.51.mask_ref, ...), custom_call_target="tpu_custom_call" | custom-call | flops 1000000 | bytes 10000 | tf_op jit(solution)/shard_map/back/pallas_call | solution.py:426
  62.0 1.5 %collective-permute-start.15 = (bf16[2,384,256]{2,1,0:T(8,128)(2,1)S(1)}, bf16[2,384,256]{2,1,0:T(8,128)(2,1)S(1)}, u32[]{:S(2)}, u32[]{:S(2)}) collective-permute-start(bf16[2,384,256]{2,1,0:T(8,128)(2,1)S(1)} %get-tuple-element.73), channel_id=1, source_target_pairs={{0,3},{1,0},{2,1},{3,2},{4,7},{5,4},{6,5},{7,6},{8,11},{9,8},{10,9... | collective-permute-start | bytes 1179656 | tf_op jit(solution)/shard_map/ppermute | solution.py:470
  63.5 2.0 %back.5 = (bf16[2,384,256]{2,1,0:T(8,128)(2,1)S(1)}, bf16[2,384,256]{2,1,0:T(8,128)(2,1)S(1)}) custom-call(bf16[384,2304]{1,0:T(8,128)(2,1)S(1)} %get-tuple-element.67.g_ref, bf16[2,3,4,256,384]{4,3,2,1,0:T(8,128)(2,1)S(1)} %get-tuple-element.68.w_ref), custom_call_target="tpu_custom_call" | custom-call | flops 1000000 | bytes 10000 | tf_op jit(solution)/shard_map/back/pallas_call | solution.py:426
  65.6 2.0 %back.6 = (bf16[2,384,256]{2,1,0:T(8,128)(2,1)S(1)}, bf16[2,384,256]{2,1,0:T(8,128)(2,1)S(1)}) custom-call(bf16[384,2304]{1,0:T(8,128)(2,1)S(1)} %get-tuple-element.67.g_ref, bf16[2,3,4,256,384]{4,3,2,1,0:T(8,128)(2,1)S(1)} %get-tuple-element.71.w_ref), custom_call_target="tpu_custom_call" | custom-call | flops 1000000 | bytes 10000 | tf_op jit(solution)/shard_map/back/pallas_call | solution.py:426
  67.6 2.7 %collective-permute-start.17 = (bf16[2,384,256]{2,1,0:T(8,128)(2,1)S(1)}, bf16[2,384,256]{2,1,0:T(8,128)(2,1)S(1)}, u32[]{:S(2)}, u32[]{:S(2)}) collective-permute-start(bf16[2,384,256]{2,1,0:T(8,128)(2,1)S(1)} %get-tuple-element.79), channel_id=1, source_target_pairs={{0,3},{1,0},{2,1},{3,2},{4,7},{5,4},{6,5},{7,6},{8,11},{9,8},{10,9... | collective-permute-start | bytes 1179656 | tf_op jit(solution)/shard_map/ppermute | solution.py:470
  70.9 2.7 %collective-permute-start.19 = (bf16[2,384,256]{2,1,0:T(8,128)(2,1)S(1)}, bf16[2,384,256]{2,1,0:T(8,128)(2,1)S(1)}, u32[]{:S(2)}, u32[]{:S(2)}) collective-permute-start(bf16[2,384,256]{2,1,0:T(8,128)(2,1)S(1)} %add.58.after_b), channel_id=1, source_target_pairs={{0,3},{1,0},{2,1},{3,2},{4,7},{5,4},{6,5},{7,6},{8,11},{9,8},{10,9... | collective-permute-start | bytes 1179656 | tf_op jit(solution)/shard_map/ppermute | solution.py:470
  73.6 2.0 %back.7 = (bf16[2,384,256]{2,1,0:T(8,128)(2,1)S(1)}, bf16[2,384,256]{2,1,0:T(8,128)(2,1)S(1)}) custom-call(bf16[2,384,256]{2,1,0:T(8,128)(2,1)S(1)} %add.57.after_a, bf16[2,384,256]{2,1,0:T(8,128)(2,1)S(1)} %add.58.after_b, bf16[384,2304]{1,0:T(8,128)(2,1)S(1)} %get-tuple-element.67.g_ref, bf16[2,3,4,256,384]{4,3,2,1,0:T(8,128)(2,1)S(1)} %get-tuple-element.74.w_ref), custom_call_target="tpu_custom_call" | custom-call | flops 1000000 | bytes 10000 | tf_op jit(solution)/shard_map/back/pallas_call | solution.py:426
  75.8 3.1 %collective-permute-done.18 = bf16[2,384,256]{2,1,0:T(8,128)(2,1)S(1)} collective-permute-done((bf16[2,384,256]{2,1,0:T(8,128)(2,1)S(1)}, bf16[2,384,256]{2,1,0:T(8,128)(2,1)S(1)}, u32[]{:S(2)}, u32[]{:S(2)}) %collective-permute-start.18) | collective-permute-done | bytes 393248 | tf_op jit(solution)/shard_map/ppermute | solution.py:467
  80.5 2.5 %collective-permute-start.22 = (bf16[192,256]{1,0:T(8,128)(2,1)S(1)}, bf16[192,256]{1,0:T(8,128)(2,1)S(1)}, u32[]{:S(2)}, u32[]{:S(2)}) collective-permute-start(bf16[192,256]{1,0:T(8,128)(2,1)S(1)} %get-tuple-element.90), channel_id=1, source_target_pairs={{0,12},{1,13},{2,14},{3,15},{4,0},{5,1},{6,2},{7,3},{8,4},{9,5},{1... | collective-permute-start | bytes 294920 | tf_op jit(solution)/shard_map/ppermute | solution.py:579
  83.1 1.8 %collective-permute-done.20 = bf16[192,256]{1,0:T(8,128)(2,1)S(1)} collective-permute-done((bf16[192,256]{1,0:T(8,128)(2,1)S(1)}, bf16[192,256]{1,0:T(8,128)(2,1)S(1)}, u32[]{:S(2)}, u32[]{:S(2)}) %collective-permute-start.20) | collective-permute-done | bytes 98336 | tf_op jit(solution)/shard_map/ppermute | solution.py:578
  85.0 2.8 %collective-permute-start.23 = (bf16[384,256]{1,0:T(8,128)(2,1)S(1)}, bf16[384,256]{1,0:T(8,128)(2,1)S(1)}, u32[]{:S(2)}, u32[]{:S(2)}) collective-permute-start(bf16[384,256]{1,0:T(8,128)(2,1)S(1)} %pad_maximum_fusion.1), channel_id=1, source_target_pairs={{0,12},{1,13},{2,14},{3,15},{4,0},{5,1},{6,2},{7,3},{8,4},{9,5},{1... | collective-permute-start | bytes 589832 | tf_op jit(solution)/shard_map/ppermute | solution.py:583
  87.9 2.5 %collective-permute-done.23 = bf16[384,256]{1,0:T(8,128)(2,1)S(1)} collective-permute-done((bf16[384,256]{1,0:T(8,128)(2,1)S(1)}, bf16[384,256]{1,0:T(8,128)(2,1)S(1)}, u32[]{:S(2)}, u32[]{:S(2)}) %collective-permute-start.23) | collective-permute-done | bytes 196640 | tf_op jit(solution)/shard_map/ppermute | solution.py:583
  90.4 3.2 %collective-permute-done.21 = bf16[384,256]{1,0:T(8,128)(2,1)S(1)} collective-permute-done((bf16[384,256]{1,0:T(8,128)(2,1)S(1)}, bf16[384,256]{1,0:T(8,128)(2,1)S(1)}, u32[]{:S(2)}, u32[]{:S(2)}) %collective-permute-start.21) | collective-permute-done | bytes 196640 | tf_op jit(solution)/shard_map/ppermute | solution.py:582
  93.7 5.0 %collective-permute-start.24 = (bf16[192,256]{1,0:T(8,128)(2,1)S(1)}, bf16[192,256]{1,0:T(8,128)(2,1)S(1)}, u32[]{:S(2)}, u32[]{:S(2)}) collective-permute-start(bf16[192,256]{1,0:T(8,128)(2,1)S(1)} %get-tuple-element.94), channel_id=1, source_target_pairs={{0,16},{16,0},{1,17},{17,1},{2,18},{18,2},{3,19},{19,3},{4,20},{20... | collective-permute-start | bytes 294920 | tf_op jit(solution)/shard_map/ppermute | solution.py:20
  (56 shorter events, 18.5 us)
Async XLA Ops:
  0.0 6.9 %collective-permute-start = (bf16[192,8192]{1,0:T(8,128)(2,1)}, bf16[192,8192]{1,0:T(8,128)(2,1)S(1)}, u32[]{:S(2)}, u32[]{:S(2)}) collective-permute-start(bf16[192,8192]{1,0:T(8,128)(2,1)} %own_hbm.1), channel_id=1, source_target_pairs={{0,16},{16,0},{1,17},{17,1},{2,18},{18,2},{3,19},{19,3},{4,20},{20... | collective-permute-start | bytes 9437192 | tf_op jit(solution)/shard_map/ppermute | solution.py:20
  16.8 2.2 %collective-permute-start.1 = (bf16[192,1664]{1,0:T(8,128)(2,1)S(1)}, bf16[192,1664]{1,0:T(8,128)(2,1)S(1)}, u32[]{:S(2)}, u32[]{:S(2)}) collective-permute-start(bf16[192,1664]{1,0:T(8,128)(2,1)S(1)} %get-tuple-element.48.sent_ref), channel_id=1, source_target_pairs={{0,16},{16,0},{1,17},{17,1},{2,18},{18,2},{3,19},{19,3},{4,20},{20... | collective-permute-start | bytes 1916936 | tf_op jit(solution)/shard_map/ppermute | solution.py:20
  19.0 30.6 %collective-permute-start.10 = (bf16[3,16,256,384]{3,2,1,0:T(8,128)(2,1)}, bf16[3,16,256,384]{3,2,1,0:T(8,128)(2,1)S(1)}, u32[]{:S(2)}, u32[]{:S(2)}) collective-permute-start(bf16[3,16,256,384]{3,2,1,0:T(8,128)(2,1)} %get-tuple-element.60), channel_id=1, source_target_pairs={{0,16},{16,0},{1,17},{17,1},{2,18},{18,2},{3,19},{19,3},{4,20},{20... | collective-permute-start | bytes 28311560 | tf_op jit(solution)/shard_map/ppermute | solution.py:20
  20.2 8.8 %collective-permute-start.3 = (bf16[2,192,512]{2,1,0:T(8,128)(2,1)S(1)}, bf16[2,192,512]{2,1,0:T(8,128)(2,1)S(1)}, u32[]{:S(2)}, u32[]{:S(2)}) collective-permute-start(bf16[2,192,512]{2,1,0:T(8,128)(2,1)S(1)} %get-tuple-element.54), channel_id=1, source_target_pairs={{0,32},{32,64},{48,16},{80,48},{96,0},{112,80},{1,33},{33,65},{49,... | collective-permute-start | bytes 1179656 | tf_op jit(solution)/shard_map/ppermute | solution.py:562
  21.5 13.9 %collective-permute-start.2 = (bf16[192,512]{1,0:T(8,128)(2,1)S(1)}, bf16[192,512]{1,0:T(8,128)(2,1)S(1)}, u32[]{:S(2)}, u32[]{:S(2)}) collective-permute-start(bf16[192,512]{1,0:T(8,128)(2,1)S(1)} %get-tuple-element.53), channel_id=1, source_target_pairs={{0,64},{64,0},{96,32},{1,65},{65,1},{97,33},{2,66},{66,2},{98,34},... | collective-permute-start | bytes 589832 | tf_op jit(solution)/shard_map/ppermute | solution.py:563
  29.1 8.3 %collective-permute-start.6 = (bf16[2,192,512]{2,1,0:T(8,128)(2,1)S(1)}, bf16[2,192,512]{2,1,0:T(8,128)(2,1)S(1)}, u32[]{:S(2)}, u32[]{:S(2)}) collective-permute-start(bf16[2,192,512]{2,1,0:T(8,128)(2,1)S(1)} %collective-permute-done.3.pair), channel_id=1, source_target_pairs={{0,16},{16,0},{1,17},{17,1},{2,18},{18,2},{3,19},{19,3},{4,20},{20... | collective-permute-start | bytes 1179656 | tf_op jit(solution)/shard_map/ppermute | solution.py:20
  35.5 1.6 %collective-permute-start.4 = (bf16[192,512]{1,0:T(8,128)(2,1)S(1)}, bf16[192,512]{1,0:T(8,128)(2,1)S(1)}, u32[]{:S(2)}, u32[]{:S(2)}) collective-permute-start(bf16[192,512]{1,0:T(8,128)(2,1)S(1)} %get-tuple-element.52.stay), channel_id=1, source_target_pairs={{0,16},{16,0},{1,17},{17,1},{2,18},{18,2},{3,19},{19,3},{4,20},{20... | collective-permute-start | bytes 589832 | tf_op jit(solution)/shard_map/ppermute | solution.py:20
  35.5 1.9 %collective-permute-start.5 = (bf16[192,512]{1,0:T(8,128)(2,1)S(1)}, bf16[192,512]{1,0:T(8,128)(2,1)S(1)}, u32[]{:S(2)}, u32[]{:S(2)}) collective-permute-start(bf16[192,512]{1,0:T(8,128)(2,1)S(1)} %collective-permute-done.2.far), channel_id=1, source_target_pairs={{0,16},{16,0},{1,17},{17,1},{2,18},{18,2},{3,19},{19,3},{4,20},{20... | collective-permute-start | bytes 589832 | tf_op jit(solution)/shard_map/ppermute | solution.py:20
  42.1 1.9 %collective-permute-start.7 = (bf16[192,1152]{1,0:T(8,128)(2,1)S(1)}, bf16[192,1152]{1,0:T(8,128)(2,1)S(1)}, u32[]{:S(2)}, u32[]{:S(2)}) collective-permute-start(bf16[192,1152]{1,0:T(8,128)(2,1)S(1)} %get-tuple-element.56), channel_id=1, source_target_pairs={{0,16},{16,0},{1,17},{17,1},{2,18},{18,2},{3,19},{19,3},{4,20},{20... | collective-permute-start | bytes 1327112 | tf_op jit(solution)/shard_map/ppermute | solution.py:20
  44.6 9.3 %collective-permute-start.8 = (bf16[2,192,384]{2,1,0:T(8,128)(2,1)S(1)}, bf16[2,192,384]{2,1,0:T(8,128)(2,1)S(1)}, u32[]{:S(2)}, u32[]{:S(2)}) collective-permute-start(bf16[2,192,384]{2,1,0:T(8,128)(2,1)S(1)} %get-tuple-element.58), channel_id=1, source_target_pairs={{0,96},{16,48},{32,0},{48,80},{64,32},{80,112},{1,97},{17,49},{33,... | collective-permute-start | bytes 884744 | tf_op jit(solution)/shard_map/ppermute | solution.py:570
  46.1 7.8 %collective-permute-start.9 = (bf16[192,384]{1,0:T(8,128)(2,1)S(1)}, bf16[192,384]{1,0:T(8,128)(2,1)S(1)}, u32[]{:S(2)}, u32[]{:S(2)}) collective-permute-start(bf16[192,384]{1,0:T(8,128)(2,1)S(1)} %get-tuple-element.59), channel_id=1, source_target_pairs={{0,64},{32,96},{64,0},{1,65},{33,97},{65,1},{2,66},{34,98},{66,2},... | collective-permute-start | bytes 442376 | tf_op jit(solution)/shard_map/ppermute | solution.py:571
  53.9 3.5 %collective-permute-start.13 = (bf16[2,192,384]{2,1,0:T(8,128)(2,1)S(1)}, bf16[2,192,384]{2,1,0:T(8,128)(2,1)S(1)}, u32[]{:S(2)}, u32[]{:S(2)}) collective-permute-start(bf16[2,192,384]{2,1,0:T(8,128)(2,1)S(1)} %collective-permute-done.8.refs_2_), channel_id=1, source_target_pairs={{0,16},{16,0},{1,17},{17,1},{2,18},{18,2},{3,19},{19,3},{4,20},{20... | collective-permute-start | bytes 884744 | tf_op jit(solution)/shard_map/ppermute | solution.py:20
  55.8 1.6 %collective-permute-start.12 = (bf16[192,384]{1,0:T(8,128)(2,1)S(1)}, bf16[192,384]{1,0:T(8,128)(2,1)S(1)}, u32[]{:S(2)}, u32[]{:S(2)}) collective-permute-start(bf16[192,384]{1,0:T(8,128)(2,1)S(1)} %collective-permute-done.9.refs_1_), channel_id=1, source_target_pairs={{0,16},{16,0},{1,17},{17,1},{2,18},{18,2},{3,19},{19,3},{4,20},{20... | collective-permute-start | bytes 442376 | tf_op jit(solution)/shard_map/ppermute | solution.py:20
  60.6 9.7 %collective-permute-start.14 = (bf16[2,384,256]{2,1,0:T(8,128)(2,1)S(1)}, bf16[2,384,256]{2,1,0:T(8,128)(2,1)S(1)}, u32[]{:S(2)}, u32[]{:S(2)}) collective-permute-start(bf16[2,384,256]{2,1,0:T(8,128)(2,1)S(1)} %get-tuple-element.70), channel_id=1, source_target_pairs={{0,1},{1,2},{2,3},{3,0},{4,5},{5,6},{6,7},{7,4},{8,9},{9,10},{10,1... | collective-permute-start | bytes 1179656 | tf_op jit(solution)/shard_map/ppermute | solution.py:467
  62.0 8.8 %collective-permute-start.15 = (bf16[2,384,256]{2,1,0:T(8,128)(2,1)S(1)}, bf16[2,384,256]{2,1,0:T(8,128)(2,1)S(1)}, u32[]{:S(2)}, u32[]{:S(2)}) collective-permute-start(bf16[2,384,256]{2,1,0:T(8,128)(2,1)S(1)} %get-tuple-element.73), channel_id=1, source_target_pairs={{0,3},{1,0},{2,1},{3,2},{4,7},{5,4},{6,5},{7,6},{8,11},{9,8},{10,9... | collective-permute-start | bytes 1179656 | tf_op jit(solution)/shard_map/ppermute | solution.py:470
  65.5 10.1 %collective-permute-start.16 = (bf16[2,384,256]{2,1,0:T(8,128)(2,1)S(1)}, bf16[2,384,256]{2,1,0:T(8,128)(2,1)S(1)}, u32[]{:S(2)}, u32[]{:S(2)}) collective-permute-start(bf16[2,384,256]{2,1,0:T(8,128)(2,1)S(1)} %get-tuple-element.77), channel_id=1, source_target_pairs={{0,1},{1,2},{2,3},{3,0},{4,5},{5,6},{6,7},{7,4},{8,9},{9,10},{10,1... | collective-permute-start | bytes 1179656 | tf_op jit(solution)/shard_map/ppermute | solution.py:467
  67.6 8.1 %collective-permute-start.17 = (bf16[2,384,256]{2,1,0:T(8,128)(2,1)S(1)}, bf16[2,384,256]{2,1,0:T(8,128)(2,1)S(1)}, u32[]{:S(2)}, u32[]{:S(2)}) collective-permute-start(bf16[2,384,256]{2,1,0:T(8,128)(2,1)S(1)} %get-tuple-element.79), channel_id=1, source_target_pairs={{0,3},{1,0},{2,1},{3,2},{4,7},{5,4},{6,5},{7,6},{8,11},{9,8},{10,9... | collective-permute-start | bytes 1179656 | tf_op jit(solution)/shard_map/ppermute | solution.py:470
  70.5 8.4 %collective-permute-start.18 = (bf16[2,384,256]{2,1,0:T(8,128)(2,1)S(1)}, bf16[2,384,256]{2,1,0:T(8,128)(2,1)S(1)}, u32[]{:S(2)}, u32[]{:S(2)}) collective-permute-start(bf16[2,384,256]{2,1,0:T(8,128)(2,1)S(1)} %add.57.after_a), channel_id=1, source_target_pairs={{0,1},{1,2},{2,3},{3,0},{4,5},{5,6},{6,7},{7,4},{8,9},{9,10},{10,1... | collective-permute-start | bytes 1179656 | tf_op jit(solution)/shard_map/ppermute | solution.py:467
  70.9 12.1 %collective-permute-start.19 = (bf16[2,384,256]{2,1,0:T(8,128)(2,1)S(1)}, bf16[2,384,256]{2,1,0:T(8,128)(2,1)S(1)}, u32[]{:S(2)}, u32[]{:S(2)}) collective-permute-start(bf16[2,384,256]{2,1,0:T(8,128)(2,1)S(1)} %add.58.after_b), channel_id=1, source_target_pairs={{0,3},{1,0},{2,1},{3,2},{4,7},{5,4},{6,5},{7,6},{8,11},{9,8},{10,9... | collective-permute-start | bytes 1179656 | tf_op jit(solution)/shard_map/ppermute | solution.py:470
  79.0 5.8 %collective-permute-start.20 = (bf16[192,256]{1,0:T(8,128)(2,1)S(1)}, bf16[192,256]{1,0:T(8,128)(2,1)S(1)}, u32[]{:S(2)}, u32[]{:S(2)}) collective-permute-start(bf16[192,256]{1,0:T(8,128)(2,1)S(1)} %get-tuple-element.89), channel_id=1, source_target_pairs={{0,4},{1,5},{2,6},{3,7},{4,8},{5,9},{6,10},{7,11},{8,12},{9,13},{1... | collective-permute-start | bytes 294920 | tf_op jit(solution)/shard_map/ppermute | solution.py:578
  80.5 4.4 %collective-permute-start.22 = (bf16[192,256]{1,0:T(8,128)(2,1)S(1)}, bf16[192,256]{1,0:T(8,128)(2,1)S(1)}, u32[]{:S(2)}, u32[]{:S(2)}) collective-permute-start(bf16[192,256]{1,0:T(8,128)(2,1)S(1)} %get-tuple-element.90), channel_id=1, source_target_pairs={{0,12},{1,13},{2,14},{3,15},{4,0},{5,1},{6,2},{7,3},{8,4},{9,5},{1... | collective-permute-start | bytes 294920 | tf_op jit(solution)/shard_map/ppermute | solution.py:579
  85.0 5.4 %collective-permute-start.23 = (bf16[384,256]{1,0:T(8,128)(2,1)S(1)}, bf16[384,256]{1,0:T(8,128)(2,1)S(1)}, u32[]{:S(2)}, u32[]{:S(2)}) collective-permute-start(bf16[384,256]{1,0:T(8,128)(2,1)S(1)} %pad_maximum_fusion.1), channel_id=1, source_target_pairs={{0,12},{1,13},{2,14},{3,15},{4,0},{5,1},{6,2},{7,3},{8,4},{9,5},{1... | collective-permute-start | bytes 589832 | tf_op jit(solution)/shard_map/ppermute | solution.py:583
  87.8 5.8 %collective-permute-start.21 = (bf16[384,256]{1,0:T(8,128)(2,1)S(1)}, bf16[384,256]{1,0:T(8,128)(2,1)S(1)}, u32[]{:S(2)}, u32[]{:S(2)}) collective-permute-start(bf16[384,256]{1,0:T(8,128)(2,1)S(1)} %pad_maximum_fusion), channel_id=1, source_target_pairs={{0,4},{1,5},{2,6},{3,7},{4,8},{5,9},{6,10},{7,11},{8,12},{9,13},{1... | collective-permute-start | bytes 589832 | tf_op jit(solution)/shard_map/ppermute | solution.py:582
  93.7 5.9 %collective-permute-start.24 = (bf16[192,256]{1,0:T(8,128)(2,1)S(1)}, bf16[192,256]{1,0:T(8,128)(2,1)S(1)}, u32[]{:S(2)}, u32[]{:S(2)}) collective-permute-start(bf16[192,256]{1,0:T(8,128)(2,1)S(1)} %get-tuple-element.94), channel_id=1, source_target_pairs={{0,16},{16,0},{1,17},{17,1},{2,18},{18,2},{3,19},{19,3},{4,20},{20... | collective-permute-start | bytes 294920 | tf_op jit(solution)/shard_map/ppermute | solution.py:20
  (3 other events, 19.3 us)

commit v13 on v11

--- a/solution.py
+++ b/solution.py
@@ -540,7 +540,7 @@
     w5 = pltpu.with_memory_space_constraint(w5, pltpu.HBM)
     activations = pltpu.with_memory_space_constraint(activations, pltpu.HBM)
     act_other = pltpu.with_memory_space_constraint(core_swap(activations), pltpu.VMEM)
-    part, w_early = project_own(activations, w5, 4)
+    part, w_early = project_own(activations, w5, 5)
     w_early = pltpu.with_memory_space_constraint(w_early, pltpu.VMEM)
     proj_own, sent, half = project(where, part, activations, act_other, w_early, w5, grad_attn)
     got = core_swap(sent)

time: 95 us -> 94 us (0.989)
    pallas_call x1, Pallas kernels: 9.86 us -> 8.59 us  [project(): pl.pallas_call(functools.partial(project_kernel, early), in_specs=[pl.Blo...]
  transfers between devices with their start and end apart: 24 -> 24, of which waited for: 14 -> 13; matrix products, arithmetic and copies ran while one was open for 1% -> 1% of each run, Pallas kernels for 23% -> 24%
where the time goes in v13:
time: 94 us; the launch traced here: 93.8 us
  starting transfers between devices  41.5 us (44%)
  Pallas kernels  34.1 us (36%)
  waiting for transfers between devices  16.5 us (18%)
  other arithmetic  1.27 us (1%)
    ppermute x11, starting transfers between devices, core_swap(): return lax.ppermute(x, 'mod', [(0, 1), (1, 0)])  15.4 us
    pallas_call x4, Pallas kernels, back_call(): pl.pallas_call(kernel, in_specs=in_specs, out_specs=[vmem] * len(out_shap...  9.24 us
    pallas_call x1, Pallas kernels, project(): pl.pallas_call(functools.partial(project_kernel, early), in_specs=[pl.Blo...  8.59 us
    ppermute x3, starting transfers between devices, backward(): return lax.ppermute(x, AXES, ring_perm(True, -1))  6.97 us
    ppermute x11, waiting for transfers between devices, core_swap(): return lax.ppermute(x, 'mod', [(0, 1), (1, 0)])  6.95 us
    pallas_call x1, Pallas kernels, project_own(): pl.pallas_call(own_kernel, in_specs=[hbm, hbm], out_specs=[vmem, vmem], o...  5.83 us
    ppermute x1, starting transfers between devices, per_device(): lax.ppermute(far, 'seq', [(i, (i + 2) % RING) for i in range(RING) if (i...  5.6 us
    ppermute x3, starting transfers between devices, per_device(): lax.ppermute(total[hop].astype(jnp.bfloat16), AXES, ring_perm(False, hop))  5.51 us
  transfers between devices with their start and end apart: 24, of which 13 were waited for; matrix products, arithmetic and copies ran while one was open for 1% of the time, Pallas kernels for 24%

profile of v13, /device:TPU:1, one launch (start us, length us, event | category | flops | bytes accessed | tf_op | source)
XLA Modules:
  0.0 93.8 jit_solution(2687781482727077544)
XLA Ops:
  0.0 1.4 %collective-permute-start = (bf16[192,8192]{1,0:T(8,128)(2,1)}, bf16[192,8192]{1,0:T(8,128)(2,1)S(1)}, u32[]{:S(2)}, u32[]{:S(2)}) collective-permute-start(bf16[192,8192]{1,0:T(8,128)(2,1)} %own_hbm.1), channel_id=1, source_target_pairs={{0,16},{16,0},{1,17},{17,1},{2,18},{18,2},{3,19},{19,3},{4,20},{20... | collective-permute-start | bytes 9437192 | tf_op jit(solution)/shard_map/ppermute | solution.py:19
  1.5 5.8 %project_own.1 = (f32[192,1152]{1,0:T(8,128)S(1)}, bf16[3,10,2,256,384]{4,3,2,1,0:T(8,128)(2,1)S(1)}) custom-call(bf16[192,8192]{1,0:T(8,128)(2,1)} %own_hbm.1, bf16[3,16,2,256,384]{4,3,2,1,0:T(8,128)(2,1)} %bitcast.18), custom_call_target="tpu_custom_call" | custom-call | flops 4000000000 | bytes 10000000 | tf_op jit(solution)/shard_map/project_own/pallas_call | solution.py:56
  7.4 8.6 %project.1 = (bf16[192,1152]{1,0:T(8,128)(2,1)S(1)}, bf16[192,1664]{1,0:T(8,128)(2,1)S(1)}, bf16[3,16,256,384]{3,2,1,0:T(8,128)(2,1)}) custom-call(s32[3]{0:T(128)S(1)} %pad_add_fusion.where_ref, f32[192,1152]{1,0:T(8,128)S(1)} %get-tuple-element.45.part_ref, bf16[192,8192]{1,0:T(8,128)(2,1)} %own_hbm.1, bf16[192,8192]{1,0:T(8,128)(2,1)S(1)} %collective-permute-done.oth_ref, ...), custom_call_target="tpu_custom_call" | custom-call | flops 7000000000 | bytes 10000000 | tf_op jit(solution)/shard_map/project/pallas_call | solution.py:141
  16.1 2.1 %collective-permute-done.1.got_ref = bf16[192,1664]{1,0:T(8,128)(2,1)S(1)} collective-permute-done((bf16[192,1664]{1,0:T(8,128)(2,1)S(1)}, bf16[192,1664]{1,0:T(8,128)(2,1)S(1)}, u32[]{:S(2)}, u32[]{:S(2)}) %collective-permute-start.1) | collective-permute-done | bytes 639008 | tf_op jit(solution)/shard_map/ppermute | solution.py:19
  20.5 5.6 %collective-permute-start.2 = (bf16[192,512]{1,0:T(8,128)(2,1)S(1)}, bf16[192,512]{1,0:T(8,128)(2,1)S(1)}, u32[]{:S(2)}, u32[]{:S(2)}) collective-permute-start(bf16[192,512]{1,0:T(8,128)(2,1)S(1)} %get-tuple-element.53), channel_id=1, source_target_pairs={{0,64},{64,0},{96,32},{1,65},{65,1},{97,33},{2,66},{66,2},{98,34},... | collective-permute-start | bytes 589832 | tf_op jit(solution)/shard_map/ppermute | solution.py:562
  26.1 1.9 %collective-permute-done.3.pair = bf16[2,192,512]{2,1,0:T(8,128)(2,1)S(1)} collective-permute-done((bf16[2,192,512]{2,1,0:T(8,128)(2,1)S(1)}, bf16[2,192,512]{2,1,0:T(8,128)(2,1)S(1)}, u32[]{:S(2)}, u32[]{:S(2)}) %collective-permute-start.3) | collective-permute-done | bytes 393248 | tf_op jit(solution)/shard_map/ppermute | solution.py:561
  28.0 6.7 %collective-permute-start.6 = (bf16[2,192,512]{2,1,0:T(8,128)(2,1)S(1)}, bf16[2,192,512]{2,1,0:T(8,128)(2,1)S(1)}, u32[]{:S(2)}, u32[]{:S(2)}) collective-permute-start(bf16[2,192,512]{2,1,0:T(8,128)(2,1)S(1)} %collective-permute-done.3.pair), channel_id=1, source_target_pairs={{0,16},{16,0},{1,17},{17,1},{2,18},{18,2},{3,19},{19,3},{4,20},{20... | collective-permute-start | bytes 1179656 | tf_op jit(solution)/shard_map/ppermute | solution.py:19
  36.5 4.7 %attention.1 = (f32[192,1408]{1,0:T(8,128)S(1)}, bf16[192,1152]{1,0:T(8,128)(2,1)S(1)}) custom-call(s32[3]{0:T(128)S(1)} %pad_add_fusion.where_ref, bf16[192,512]{1,0:T(8,128)(2,1)S(1)} %get-tuple-element.52.stay, bf16[192,512]{1,0:T(8,128)(2,1)S(1)} %collective-permute-done.2.far, bf16[2,192,512]{2,1,0:T(8,128)(2,1)S(1)} %collective-permute-done.3.pair, ...), custom_call_target="tpu_custom_call" | custom-call | flops 1000000000 | bytes 4000000 | tf_op jit(solution)/shard_map/attention/pallas_call | solution.py:296
  41.7 1.4 %collective-permute-done.7.got = bf16[192,1152]{1,0:T(8,128)(2,1)S(1)} collective-permute-done((bf16[192,1152]{1,0:T(8,128)(2,1)S(1)}, bf16[192,1152]{1,0:T(8,128)(2,1)S(1)}, u32[]{:S(2)}, u32[]{:S(2)}) %collective-permute-start.7) | collective-permute-done | bytes 442400 | tf_op jit(solution)/shard_map/ppermute | solution.py:19
  45.1 3.6 %collective-permute-start.9 = (bf16[192,384]{1,0:T(8,128)(2,1)S(1)}, bf16[192,384]{1,0:T(8,128)(2,1)S(1)}, u32[]{:S(2)}, u32[]{:S(2)}) collective-permute-start(bf16[192,384]{1,0:T(8,128)(2,1)S(1)} %get-tuple-element.59), channel_id=1, source_target_pairs={{0,64},{32,96},{64,0},{1,65},{33,97},{65,1},{2,66},{34,98},{66,2},... | collective-permute-start | bytes 442376 | tf_op jit(solution)/shard_map/ppermute | solution.py:570
  48.7 4.0 %fetch_weights.1 = (bf16[2,3,4,256,384]{4,3,2,1,0:T(8,128)(2,1)S(1)}, bf16[2,3,4,256,384]{4,3,2,1,0:T(8,128)(2,1)S(1)}, bf16[2,3,4,256,384]{4,3,2,1,0:T(8,128)(2,1)S(1)}) custom-call(s32[3]{0:T(128)S(1)} %pad_add_fusion.where_ref, bf16[192,384]{1,0:T(8,128)(2,1)S(1)} %get-tuple-element.57.after_ref.refs_0_, bf16[3,16,2,256,384]{4,3,2,1,0:T(8,128)(2,1)} %bitcast.20, ...), custom_call_target="tpu_custom_call" | custom-call | flops 1000000 | bytes 10000000 | tf_op jit(solution)/shard_map/fetch_weights/pallas_call | solution.py:383
  52.9 1.9 %collective-permute-start.13 = (bf16[2,192,384]{2,1,0:T(8,128)(2,1)S(1)}, bf16[2,192,384]{2,1,0:T(8,128)(2,1)S(1)}, u32[]{:S(2)}, u32[]{:S(2)}) collective-permute-start(bf16[2,192,384]{2,1,0:T(8,128)(2,1)S(1)} %collective-permute-done.8.refs_2_), channel_id=1, source_target_pairs={{0,16},{16,0},{1,17},{17,1},{2,18},{18,2},{3,19},{19,3},{4,20},{20... | collective-permute-start | bytes 884744 | tf_op jit(solution)/shard_map/ppermute | solution.py:19
  56.4 3.2 %back.4 = (bf16[2,384,256]{2,1,0:T(8,128)(2,1)S(1)}, bf16[2,384,256]{2,1,0:T(8,128)(2,1)S(1)}, bf16[384,2304]{1,0:T(8,128)(2,1)S(1)}, bf16[2,3,4,256,384]{4,3,2,1,0:T(8,128)(2,1)S(1)}) custom-call(s32[3]{0:T(128)S(1)} %pad_add_fusion.where_ref, bf16[2,192,128]{2,1,0:T(8,128)(2,1)S(1)} %get-tuple-element.51.mask_ref, ...), custom_call_target="tpu_custom_call" | custom-call | flops 1000000 | bytes 10000 | tf_op jit(solution)/shard_map/back/pallas_call | solution.py:425
  59.6 1.4 %collective-permute-start.14 = (bf16[2,384,256]{2,1,0:T(8,128)(2,1)S(1)}, bf16[2,384,256]{2,1,0:T(8,128)(2,1)S(1)}, u32[]{:S(2)}, u32[]{:S(2)}) collective-permute-start(bf16[2,384,256]{2,1,0:T(8,128)(2,1)S(1)} %get-tuple-element.70), channel_id=1, source_target_pairs={{0,1},{1,2},{2,3},{3,0},{4,5},{5,6},{6,7},{7,4},{8,9},{9,10},{10,1... | collective-permute-start | bytes 1179656 | tf_op jit(solution)/shard_map/ppermute | solution.py:466
  61.1 1.5 %collective-permute-start.15 = (bf16[2,384,256]{2,1,0:T(8,128)(2,1)S(1)}, bf16[2,384,256]{2,1,0:T(8,128)(2,1)S(1)}, u32[]{:S(2)}, u32[]{:S(2)}) collective-permute-start(bf16[2,384,256]{2,1,0:T(8,128)(2,1)S(1)} %get-tuple-element.73), channel_id=1, source_target_pairs={{0,3},{1,0},{2,1},{3,2},{4,7},{5,4},{6,5},{7,6},{8,11},{9,8},{10,9... | collective-permute-start | bytes 1179656 | tf_op jit(solution)/shard_map/ppermute | solution.py:469
  62.6 2.0 %back.5 = (bf16[2,384,256]{2,1,0:T(8,128)(2,1)S(1)}, bf16[2,384,256]{2,1,0:T(8,128)(2,1)S(1)}) custom-call(bf16[384,2304]{1,0:T(8,128)(2,1)S(1)} %get-tuple-element.67.g_ref, bf16[2,3,4,256,384]{4,3,2,1,0:T(8,128)(2,1)S(1)} %get-tuple-element.68.w_ref), custom_call_target="tpu_custom_call" | custom-call | flops 1000000 | bytes 10000 | tf_op jit(solution)/shard_map/back/pallas_call | solution.py:425
  64.7 2.0 %back.6 = (bf16[2,384,256]{2,1,0:T(8,128)(2,1)S(1)}, bf16[2,384,256]{2,1,0:T(8,128)(2,1)S(1)}) custom-call(bf16[384,2304]{1,0:T(8,128)(2,1)S(1)} %get-tuple-element.67.g_ref, bf16[2,3,4,256,384]{4,3,2,1,0:T(8,128)(2,1)S(1)} %get-tuple-element.71.w_ref), custom_call_target="tpu_custom_call" | custom-call | flops 1000000 | bytes 10000 | tf_op jit(solution)/shard_map/back/pallas_call | solution.py:425
  66.7 2.7 %collective-permute-start.17 = (bf16[2,384,256]{2,1,0:T(8,128)(2,1)S(1)}, bf16[2,384,256]{2,1,0:T(8,128)(2,1)S(1)}, u32[]{:S(2)}, u32[]{:S(2)}) collective-permute-start(bf16[2,384,256]{2,1,0:T(8,128)(2,1)S(1)} %get-tuple-element.79), channel_id=1, source_target_pairs={{0,3},{1,0},{2,1},{3,2},{4,7},{5,4},{6,5},{7,6},{8,11},{9,8},{10,9... | collective-permute-start | bytes 1179656 | tf_op jit(solution)/shard_map/ppermute | solution.py:469
  70.0 2.7 %collective-permute-start.20 = (bf16[2,384,256]{2,1,0:T(8,128)(2,1)S(1)}, bf16[2,384,256]{2,1,0:T(8,128)(2,1)S(1)}, u32[]{:S(2)}, u32[]{:S(2)}) collective-permute-start(bf16[2,384,256]{2,1,0:T(8,128)(2,1)S(1)} %add.42.after_b), channel_id=1, source_target_pairs={{0,3},{1,0},{2,1},{3,2},{4,7},{5,4},{6,5},{7,6},{8,11},{9,8},{10,9... | collective-permute-start | bytes 1179656 | tf_op jit(solution)/shard_map/ppermute | solution.py:469
  72.7 2.0 %back.7 = (bf16[2,384,256]{2,1,0:T(8,128)(2,1)S(1)}, bf16[2,384,256]{2,1,0:T(8,128)(2,1)S(1)}) custom-call(bf16[2,384,256]{2,1,0:T(8,128)(2,1)S(1)} %add.41.after_a, bf16[2,384,256]{2,1,0:T(8,128)(2,1)S(1)} %add.42.after_b, bf16[384,2304]{1,0:T(8,128)(2,1)S(1)} %get-tuple-element.67.g_ref, bf16[2,3,4,256,384]{4,3,2,1,0:T(8,128)(2,1)S(1)} %get-tuple-element.74.w_ref), custom_call_target="tpu_custom_call" | custom-call | flops 1000000 | bytes 10000 | tf_op jit(solution)/shard_map/back/pallas_call | solution.py:425
  74.9 3.1 %collective-permute-done.18 = bf16[2,384,256]{2,1,0:T(8,128)(2,1)S(1)} collective-permute-done((bf16[2,384,256]{2,1,0:T(8,128)(2,1)S(1)}, bf16[2,384,256]{2,1,0:T(8,128)(2,1)S(1)}, u32[]{:S(2)}, u32[]{:S(2)}) %collective-permute-start.18) | collective-permute-done | bytes 393248 | tf_op jit(solution)/shard_map/ppermute | solution.py:466
  79.7 3.7 %collective-permute-start.22 = (bf16[384,256]{1,0:T(8,128)(2,1)S(1)}, bf16[384,256]{1,0:T(8,128)(2,1)S(1)}, u32[]{:S(2)}, u32[]{:S(2)}) collective-permute-start(bf16[384,256]{1,0:T(8,128)(2,1)S(1)} %get-tuple-element.85), channel_id=1, source_target_pairs={{0,8},{1,9},{2,10},{3,11},{4,12},{5,13},{6,14},{7,15},{8,0},{9,1},... | collective-permute-start | bytes 589832 | tf_op jit(solution)/shard_map/ppermute | solution.py:578
  85.0 3.0 %collective-permute-done.21 = bf16[384,256]{1,0:T(8,128)(2,1)S(1)} collective-permute-done((bf16[384,256]{1,0:T(8,128)(2,1)S(1)}, bf16[384,256]{1,0:T(8,128)(2,1)S(1)}, u32[]{:S(2)}, u32[]{:S(2)}) %collective-permute-start.21) | collective-permute-done | bytes 196640 | tf_op jit(solution)/shard_map/ppermute | solution.py:578
  88.4 3.7 %collective-permute-start.23 = (bf16[192,256]{1,0:T(8,128)(2,1)S(1)}, bf16[192,256]{1,0:T(8,128)(2,1)S(1)}, u32[]{:S(2)}, u32[]{:S(2)}) collective-permute-start(bf16[192,256]{1,0:T(8,128)(2,1)S(1)} %get-tuple-element.88), channel_id=1, source_target_pairs={{0,16},{16,0},{1,17},{17,1},{2,18},{18,2},{3,19},{19,3},{4,20},{20... | collective-permute-start | bytes 294920 | tf_op jit(solution)/shard_map/ppermute | solution.py:19
  (53 shorter events, 14.6 us)
Async XLA Ops:
  0.0 7.3 %collective-permute-start = (bf16[192,8192]{1,0:T(8,128)(2,1)}, bf16[192,8192]{1,0:T(8,128)(2,1)S(1)}, u32[]{:S(2)}, u32[]{:S(2)}) collective-permute-start(bf16[192,8192]{1,0:T(8,128)(2,1)} %own_hbm.1), channel_id=1, source_target_pairs={{0,16},{16,0},{1,17},{17,1},{2,18},{18,2},{3,19},{19,3},{4,20},{20... | collective-permute-start | bytes 9437192 | tf_op jit(solution)/shard_map/ppermute | solution.py:19
  16.0 2.2 %collective-permute-start.1 = (bf16[192,1664]{1,0:T(8,128)(2,1)S(1)}, bf16[192,1664]{1,0:T(8,128)(2,1)S(1)}, u32[]{:S(2)}, u32[]{:S(2)}) collective-permute-start(bf16[192,1664]{1,0:T(8,128)(2,1)S(1)} %get-tuple-element.48.sent_ref), channel_id=1, source_target_pairs={{0,16},{16,0},{1,17},{17,1},{2,18},{18,2},{3,19},{19,3},{4,20},{20... | collective-permute-start | bytes 1916936 | tf_op jit(solution)/shard_map/ppermute | solution.py:19
  18.1 30.6 %collective-permute-start.10 = (bf16[3,16,256,384]{3,2,1,0:T(8,128)(2,1)}, bf16[3,16,256,384]{3,2,1,0:T(8,128)(2,1)S(1)}, u32[]{:S(2)}, u32[]{:S(2)}) collective-permute-start(bf16[3,16,256,384]{3,2,1,0:T(8,128)(2,1)} %get-tuple-element.60), channel_id=1, source_target_pairs={{0,16},{16,0},{1,17},{17,1},{2,18},{18,2},{3,19},{19,3},{4,20},{20... | collective-permute-start | bytes 28311560 | tf_op jit(solution)/shard_map/ppermute | solution.py:19
  19.2 8.8 %collective-permute-start.3 = (bf16[2,192,512]{2,1,0:T(8,128)(2,1)S(1)}, bf16[2,192,512]{2,1,0:T(8,128)(2,1)S(1)}, u32[]{:S(2)}, u32[]{:S(2)}) collective-permute-start(bf16[2,192,512]{2,1,0:T(8,128)(2,1)S(1)} %get-tuple-element.54), channel_id=1, source_target_pairs={{0,32},{32,64},{48,16},{80,48},{96,0},{112,80},{1,33},{33,65},{49,... | collective-permute-start | bytes 1179656 | tf_op jit(solution)/shard_map/ppermute | solution.py:561
  20.5 14.2 %collective-permute-start.2 = (bf16[192,512]{1,0:T(8,128)(2,1)S(1)}, bf16[192,512]{1,0:T(8,128)(2,1)S(1)}, u32[]{:S(2)}, u32[]{:S(2)}) collective-permute-start(bf16[192,512]{1,0:T(8,128)(2,1)S(1)} %get-tuple-element.53), channel_id=1, source_target_pairs={{0,64},{64,0},{96,32},{1,65},{65,1},{97,33},{2,66},{66,2},{98,34},... | collective-permute-start | bytes 589832 | tf_op jit(solution)/shard_map/ppermute | solution.py:562
  28.0 8.6 %collective-permute-start.6 = (bf16[2,192,512]{2,1,0:T(8,128)(2,1)S(1)}, bf16[2,192,512]{2,1,0:T(8,128)(2,1)S(1)}, u32[]{:S(2)}, u32[]{:S(2)}) collective-permute-start(bf16[2,192,512]{2,1,0:T(8,128)(2,1)S(1)} %collective-permute-done.3.pair), channel_id=1, source_target_pairs={{0,16},{16,0},{1,17},{17,1},{2,18},{18,2},{3,19},{19,3},{4,20},{20... | collective-permute-start | bytes 1179656 | tf_op jit(solution)/shard_map/ppermute | solution.py:19
  34.6 1.6 %collective-permute-start.4 = (bf16[192,512]{1,0:T(8,128)(2,1)S(1)}, bf16[192,512]{1,0:T(8,128)(2,1)S(1)}, u32[]{:S(2)}, u32[]{:S(2)}) collective-permute-start(bf16[192,512]{1,0:T(8,128)(2,1)S(1)} %get-tuple-element.52.stay), channel_id=1, source_target_pairs={{0,16},{16,0},{1,17},{17,1},{2,18},{18,2},{3,19},{19,3},{4,20},{20... | collective-permute-start | bytes 589832 | tf_op jit(solution)/shard_map/ppermute | solution.py:19
  34.6 1.9 %collective-permute-start.5 = (bf16[192,512]{1,0:T(8,128)(2,1)S(1)}, bf16[192,512]{1,0:T(8,128)(2,1)S(1)}, u32[]{:S(2)}, u32[]{:S(2)}) collective-permute-start(bf16[192,512]{1,0:T(8,128)(2,1)S(1)} %collective-permute-done.2.far), channel_id=1, source_target_pairs={{0,16},{16,0},{1,17},{17,1},{2,18},{18,2},{3,19},{19,3},{4,20},{20... | collective-permute-start | bytes 589832 | tf_op jit(solution)/shard_map/ppermute | solution.py:19
  41.3 1.9 %collective-permute-start.7 = (bf16[192,1152]{1,0:T(8,128)(2,1)S(1)}, bf16[192,1152]{1,0:T(8,128)(2,1)S(1)}, u32[]{:S(2)}, u32[]{:S(2)}) collective-permute-start(bf16[192,1152]{1,0:T(8,128)(2,1)S(1)} %get-tuple-element.56), channel_id=1, source_target_pairs={{0,16},{16,0},{1,17},{17,1},{2,18},{18,2},{3,19},{19,3},{4,20},{20... | collective-permute-start | bytes 1327112 | tf_op jit(solution)/shard_map/ppermute | solution.py:19
  43.8 9.1 %collective-permute-start.8 = (bf16[2,192,384]{2,1,0:T(8,128)(2,1)S(1)}, bf16[2,192,384]{2,1,0:T(8,128)(2,1)S(1)}, u32[]{:S(2)}, u32[]{:S(2)}) collective-permute-start(bf16[2,192,384]{2,1,0:T(8,128)(2,1)S(1)} %get-tuple-element.58), channel_id=1, source_target_pairs={{0,96},{16,48},{32,0},{48,80},{64,32},{80,112},{1,97},{17,49},{33,... | collective-permute-start | bytes 884744 | tf_op jit(solution)/shard_map/ppermute | solution.py:569
  45.1 7.8 %collective-permute-start.9 = (bf16[192,384]{1,0:T(8,128)(2,1)S(1)}, bf16[192,384]{1,0:T(8,128)(2,1)S(1)}, u32[]{:S(2)}, u32[]{:S(2)}) collective-permute-start(bf16[192,384]{1,0:T(8,128)(2,1)S(1)} %get-tuple-element.59), channel_id=1, source_target_pairs={{0,64},{32,96},{64,0},{1,65},{33,97},{65,1},{2,66},{34,98},{66,2},... | collective-permute-start | bytes 442376 | tf_op jit(solution)/shard_map/ppermute | solution.py:570
  52.9 3.5 %collective-permute-start.13 = (bf16[2,192,384]{2,1,0:T(8,128)(2,1)S(1)}, bf16[2,192,384]{2,1,0:T(8,128)(2,1)S(1)}, u32[]{:S(2)}, u32[]{:S(2)}) collective-permute-start(bf16[2,192,384]{2,1,0:T(8,128)(2,1)S(1)} %collective-permute-done.8.refs_2_), channel_id=1, source_target_pairs={{0,16},{16,0},{1,17},{17,1},{2,18},{18,2},{3,19},{19,3},{4,20},{20... | collective-permute-start | bytes 884744 | tf_op jit(solution)/shard_map/ppermute | solution.py:19
  54.8 1.4 %collective-permute-start.11 = (bf16[192,384]{1,0:T(8,128)(2,1)S(1)}, bf16[192,384]{1,0:T(8,128)(2,1)S(1)}, u32[]{:S(2)}, u32[]{:S(2)}) collective-permute-start(bf16[192,384]{1,0:T(8,128)(2,1)S(1)} %get-tuple-element.57.after_ref.refs_0_), channel_id=1, source_target_pairs={{0,16},{16,0},{1,17},{17,1},{2,18},{18,2},{3,19},{19,3},{4,20},{20... | collective-permute-start | bytes 442376 | tf_op jit(solution)/shard_map/ppermute | solution.py:19
  54.8 1.6 %collective-permute-start.12 = (bf16[192,384]{1,0:T(8,128)(2,1)S(1)}, bf16[192,384]{1,0:T(8,128)(2,1)S(1)}, u32[]{:S(2)}, u32[]{:S(2)}) collective-permute-start(bf16[192,384]{1,0:T(8,128)(2,1)S(1)} %collective-permute-done.9.refs_1_), channel_id=1, source_target_pairs={{0,16},{16,0},{1,17},{17,1},{2,18},{18,2},{3,19},{19,3},{4,20},{20... | collective-permute-start | bytes 442376 | tf_op jit(solution)/shard_map/ppermute | solution.py:19
  59.6 9.8 %collective-permute-start.14 = (bf16[2,384,256]{2,1,0:T(8,128)(2,1)S(1)}, bf16[2,384,256]{2,1,0:T(8,128)(2,1)S(1)}, u32[]{:S(2)}, u32[]{:S(2)}) collective-permute-start(bf16[2,384,256]{2,1,0:T(8,128)(2,1)S(1)} %get-tuple-element.70), channel_id=1, source_target_pairs={{0,1},{1,2},{2,3},{3,0},{4,5},{5,6},{6,7},{7,4},{8,9},{9,10},{10,1... | collective-permute-start | bytes 1179656 | tf_op jit(solution)/shard_map/ppermute | solution.py:466
  61.1 8.8 %collective-permute-start.15 = (bf16[2,384,256]{2,1,0:T(8,128)(2,1)S(1)}, bf16[2,384,256]{2,1,0:T(8,128)(2,1)S(1)}, u32[]{:S(2)}, u32[]{:S(2)}) collective-permute-start(bf16[2,384,256]{2,1,0:T(8,128)(2,1)S(1)} %get-tuple-element.73), channel_id=1, source_target_pairs={{0,3},{1,0},{2,1},{3,2},{4,7},{5,4},{6,5},{7,6},{8,11},{9,8},{10,9... | collective-permute-start | bytes 1179656 | tf_op jit(solution)/shard_map/ppermute | solution.py:469
  64.6 10.1 %collective-permute-start.16 = (bf16[2,384,256]{2,1,0:T(8,128)(2,1)S(1)}, bf16[2,384,256]{2,1,0:T(8,128)(2,1)S(1)}, u32[]{:S(2)}, u32[]{:S(2)}) collective-permute-start(bf16[2,384,256]{2,1,0:T(8,128)(2,1)S(1)} %get-tuple-element.77), channel_id=1, source_target_pairs={{0,1},{1,2},{2,3},{3,0},{4,5},{5,6},{6,7},{7,4},{8,9},{9,10},{10,1... | collective-permute-start | bytes 1179656 | tf_op jit(solution)/shard_map/ppermute | solution.py:466
  66.7 8.1 %collective-permute-start.17 = (bf16[2,384,256]{2,1,0:T(8,128)(2,1)S(1)}, bf16[2,384,256]{2,1,0:T(8,128)(2,1)S(1)}, u32[]{:S(2)}, u32[]{:S(2)}) collective-permute-start(bf16[2,384,256]{2,1,0:T(8,128)(2,1)S(1)} %get-tuple-element.79), channel_id=1, source_target_pairs={{0,3},{1,0},{2,1},{3,2},{4,7},{5,4},{6,5},{7,6},{8,11},{9,8},{10,9... | collective-permute-start | bytes 1179656 | tf_op jit(solution)/shard_map/ppermute | solution.py:469
  69.5 8.4 %collective-permute-start.18 = (bf16[2,384,256]{2,1,0:T(8,128)(2,1)S(1)}, bf16[2,384,256]{2,1,0:T(8,128)(2,1)S(1)}, u32[]{:S(2)}, u32[]{:S(2)}) collective-permute-start(bf16[2,384,256]{2,1,0:T(8,128)(2,1)S(1)} %add.41.after_a), channel_id=1, source_target_pairs={{0,1},{1,2},{2,3},{3,0},{4,5},{5,6},{6,7},{7,4},{8,9},{9,10},{10,1... | collective-permute-start | bytes 1179656 | tf_op jit(solution)/shard_map/ppermute | solution.py:466
  70.0 9.6 %collective-permute-start.20 = (bf16[2,384,256]{2,1,0:T(8,128)(2,1)S(1)}, bf16[2,384,256]{2,1,0:T(8,128)(2,1)S(1)}, u32[]{:S(2)}, u32[]{:S(2)}) collective-permute-start(bf16[2,384,256]{2,1,0:T(8,128)(2,1)S(1)} %add.42.after_b), channel_id=1, source_target_pairs={{0,3},{1,0},{2,1},{3,2},{4,7},{5,4},{6,5},{7,6},{8,11},{9,8},{10,9... | collective-permute-start | bytes 1179656 | tf_op jit(solution)/shard_map/ppermute | solution.py:469
  78.1 6.9 %collective-permute-start.19 = (bf16[384,256]{1,0:T(8,128)(2,1)S(1)}, bf16[384,256]{1,0:T(8,128)(2,1)S(1)}, u32[]{:S(2)}, u32[]{:S(2)}) collective-permute-start(bf16[384,256]{1,0:T(8,128)(2,1)S(1)} %fusion), channel_id=1, source_target_pairs={{0,4},{1,5},{2,6},{3,7},{4,8},{5,9},{6,10},{7,11},{8,12},{9,13},{1... | collective-permute-start | bytes 589832 | tf_op jit(solution)/shard_map/ppermute | solution.py:578
  79.7 8.6 %collective-permute-start.22 = (bf16[384,256]{1,0:T(8,128)(2,1)S(1)}, bf16[384,256]{1,0:T(8,128)(2,1)S(1)}, u32[]{:S(2)}, u32[]{:S(2)}) collective-permute-start(bf16[384,256]{1,0:T(8,128)(2,1)S(1)} %get-tuple-element.85), channel_id=1, source_target_pairs={{0,8},{1,9},{2,10},{3,11},{4,12},{5,13},{6,14},{7,15},{8,0},{9,1},... | collective-permute-start | bytes 589832 | tf_op jit(solution)/shard_map/ppermute | solution.py:578
  83.3 4.7 %collective-permute-start.21 = (bf16[384,256]{1,0:T(8,128)(2,1)S(1)}, bf16[384,256]{1,0:T(8,128)(2,1)S(1)}, u32[]{:S(2)}, u32[]{:S(2)}) collective-permute-start(bf16[384,256]{1,0:T(8,128)(2,1)S(1)} %get-tuple-element.86), channel_id=1, source_target_pairs={{0,12},{1,13},{2,14},{3,15},{4,0},{5,1},{6,2},{7,3},{8,4},{9,5},{1... | collective-permute-start | bytes 589832 | tf_op jit(solution)/shard_map/ppermute | solution.py:578
  88.4 4.7 %collective-permute-start.23 = (bf16[192,256]{1,0:T(8,128)(2,1)S(1)}, bf16[192,256]{1,0:T(8,128)(2,1)S(1)}, u32[]{:S(2)}, u32[]{:S(2)}) collective-permute-start(bf16[192,256]{1,0:T(8,128)(2,1)S(1)} %get-tuple-element.88), channel_id=1, source_target_pairs={{0,16},{16,0},{1,17},{17,1},{2,18},{18,2},{3,19},{19,3},{4,20},{20... | collective-permute-start | bytes 294920 | tf_op jit(solution)/shard_map/ppermute | solution.py:19
  (2 other events, 16.8 us)
